TPU v7x, 32 devices: a whole 2x2x4 slice. The times are simulated.
32 devices in a mesh: groups: 2 (over y), tensor: 4 (over z), dp: 2 (over x), section: 2 (over core).
Axes of the slice: x: 2, y: 2, z: 4, core: 2. Of those that a mesh axis runs over, the one named last changes fastest.
Arguments:
- hidden: bfloat16 [64, 53248], P(('groups', 'dp'), ('tensor', 'section')), parts along dimension 0, may hold values from -6 to 6
- down_matrix: bfloat16 [53248, 8192], P(('tensor', 'section'), 'dp'), may hold values from -0.02734375 to 0.02734375
- residual: bfloat16 [64, 8192], P(('groups', 'tensor', 'section'), 'dp'), parts along dimension 0, may hold values from -6 to 6
- next_norm_scale: bfloat16 [8192], replicated, may hold values from 0.099609375 to 1.8984375
- shrink_matrix: bfloat16 [2, 8192, 64], P('dp'), may hold values from -0.0625 to 0.0625
- adapter_index: int32 [64, 1], P(('groups', 'tensor', 'section')), parts along dimension 0, may hold values from 0 to 1; in each aligned block of 4 rows (0 to 3, 4 to 7, ...) at most 2 rows name the same one
Outputs:
- mixed: bfloat16 [64, 8192], P(('groups', 'tensor', 'section'), 'dp'), parts along dimension 0
- shrunk: float32 [2, 16, 2, 64], P('dp', ('groups', 'tensor', 'section')), parts along dimension 1
There are 2 independent parts, one for each index of `groups`. A program takes and returns all parts, laid end to end along the dimension named above; an argument that names none is the same for every part. Nothing has to cross between parts.
Inputs may be any that keep to these rules, and one draw needn't show every extreme that they name: `adapter_index`: in each aligned block of 4 rows no adapter is named by more than 2 rows, a bound that some block reaches.
All inputs are finite; a program needn't handle non-finite values.
Results may differ from a plain program's by a relative error of at most 0.0051.
Values may be sent and summed in bfloat16 or wider, within the bound.
No kernel may reach another device: no remote copies, remote signals or barrier semaphores. Data moves between devices by JAX's collectives and lax.ppermute only.
A program may use at most 128 MiB of HBM per device.

v0:
```python
import jax
import jax.numpy as jnp
from jax import lax
from jax.sharding import PartitionSpec as P

MOST = 2


def body(hidden, down_matrix, residual, next_norm_scale, shrink_matrix, adapter_index):
    gathered = lax.all_gather(hidden, "dp", axis=0, tiled=True)
    projected = lax.psum_scatter(
        jnp.dot(gathered, down_matrix, preferred_element_type=jnp.float32),
        ("tensor", "section"),
        scatter_dimension=0,
        tiled=True,
    )
    mixed = (projected + residual.astype(jnp.float32)).astype(jnp.bfloat16)
    owner_count = lax.axis_size("dp")
    local_row_count = shrink_matrix.shape[0]
    adapter_count = owner_count * local_row_count
    row_adapter = adapter_index[:, 0]
    onehot = (row_adapter[:, None] == jnp.arange(adapter_count, dtype=jnp.int32)[None, :]).astype(
        jnp.int32
    )
    slot_rank = jnp.cumsum(onehot, axis=0) - onehot
    placement = (
        onehot[:, :, None]
        * (slot_rank[:, :, None] == jnp.arange(MOST, dtype=jnp.int32)[None, None, :]).astype(
            jnp.int32
        )
    ).astype(jnp.bfloat16)
    outgoing = jnp.einsum(
        "ram,rc->amc", placement, mixed, preferred_element_type=jnp.float32
    ).astype(jnp.bfloat16)
    outgoing = outgoing.reshape(owner_count, local_row_count, MOST, mixed.shape[1])
    arrived = lax.all_to_all(outgoing, "dp", split_axis=0, concat_axis=3, tiled=True)
    widened = arrived[0].astype(jnp.float32)
    mean_square = jnp.mean(widened * widened, axis=2, keepdims=True)
    normalized_rows = (
        widened * lax.rsqrt(mean_square + 1e-05) * next_norm_scale.astype(jnp.float32)
    ).astype(jnp.bfloat16)
    shrunk = (
        jnp.einsum(
            "fxl,flc->fxc", normalized_rows, shrink_matrix, preferred_element_type=jnp.float32
        )
        * 2.0
    )
    return (mixed, shrunk[:, None])


def solution(mesh):
    placed = (
        P(("groups", "dp"), ("tensor", "section")),
        P(("tensor", "section"), "dp"),
        P(("groups", "tensor", "section"), "dp"),
        P(),
        P("dp", None, None),
        P(("groups", "tensor", "section"), None),
    )
    return jax.shard_map(
        body,
        mesh=mesh,
        in_specs=placed,
        out_specs=(
            P(("groups", "tensor", "section"), "dp"),
            P("dp", ("groups", "tensor", "section"), None, None),
        ),
        check_vma=False,
    )
```

profile of v0, /device:TPU:0, one launch (start us, length us, event | category | flops | bytes accessed | tf_op | source)
XLA Modules:
  0.0 113.7 jit_solution(17363756103460089129)
XLA Ops:
  7.2 0.0 copy-start
  7.2 0.0 copy-start.5
  7.2 0.0 copy-start.4
  7.2 0.0 copy-start.2
  7.2 0.0 copy-start.3
  7.2 0.0 all-reduce.3.cloned.1.call-start
  7.3 9.3 %all_gather.3 = bf16[32,6656]{1,0:T(8,128)(2,1)S(1)} all-gather(bf16[16,6656]{1,0:T(8,128)(2,1)} %param.6), channel_id=1, replica_groups=mesh['groups'=2,'tensor'=4,'dp'=2,'section'=2] {'dp'}, dimensions={0}, use_global_device_ids=true | all-gather | bytes 638976 | tf_op jit(solution)/shard_map/all_gather | solution.py:10
  16.5 22.4 %fusion.15 = f32[32,4096]{1,0:T(8,128)} fusion(bf16[32,6656]{1,0:T(8,128)(2,1)S(1)} %all_gather.3, bf16[6656,4096]{1,0:T(8,128)(2,1)} %param.7), kind=kOutput, calls=%fused_computation.22 | convolution fusion | flops 1744830464 | bytes 55476224 | tf_op jit(solution)/shard_map/dot_general | solution.py:12
  38.9 0.0 all-reduce.3.cloned.1.call-update
  38.9 0.0 copy-done.4
  38.9 0.0 copy-done.5
  38.9 0.6 dynamic-slice
  40.2 0.2 reduce_window_sum.11
  40.4 56.3 %all-reduce.3.cloned.1.call-done = f32[32,4096]{1,0:T(8,128)} async-done(((f32[32,4096]{1,0:T(8,128)}), f32[32,4096]{1,0:T(8,128)}) %all-reduce.3.cloned.1.call-update) | async-done | bytes 524304
  96.7 0.0 copy-done.2
  96.7 0.9 fusion.6
  97.6 0.0 copy-start.1
  97.6 0.8 fusion
  98.4 3.3 %all-to-all-start = ((bf16[2,1,2,4096]{3,2,1,0:T(2,128)(2,1)}), bf16[2,1,2,4096]{3,2,1,0:T(2,128)(2,1)S(1)}, u32[]{:S(2)}, u32[]{:S(2)}) async-start(bf16[2,1,2,4096]{3,2,1,0:T(2,128)(2,1)} %fusion), calls=%async_computation | async-start | bytes 65536 | tf_op jit(solution)/shard_map/all_to_all | solution.py:36
  101.6 0.0 copy-done.3
  101.7 3.9 %all-to-all-done = bf16[2,1,2,4096]{3,2,1,0:T(2,128)(2,1)S(1)} async-done(((bf16[2,1,2,4096]{3,2,1,0:T(2,128)(2,1)}), bf16[2,1,2,4096]{3,2,1,0:T(2,128)(2,1)S(1)}, u32[]{:S(2)}, u32[]{:S(2)}) %all-to-all-start) | async-done | bytes 32800 | tf_op jit(solution)/shard_map/all_to_all | solution.py:36
  105.6 0.2 fusion.3
  105.8 0.1 fusion.5
  105.9 0.0 copy-done
  105.9 1.0 fusion.1
  106.8 0.0 copy-done.1
  (4 shorter events, 0.0 us)
Async XLA Ops:
  7.2 98.7 %copy-start = (bf16[1,8192,64]{1,2,0:T(8,128)(2,1)S(1)}, bf16[1,8192,64]{1,2,0:T(8,128)(2,1)}, u32[]{:S(2)}) copy-start(bf16[1,8192,64]{1,2,0:T(8,128)(2,1)} %param.10) | copy-start | bytes 3145732
  7.2 31.8 %copy-start.5 = (u32[32]{0:T(128)S(1)}, u32[32]{0:T(128)}, u32[]{:S(2)}) copy-start(u32[32]{0:T(128)} %constant.19) | copy-start | bytes 388
  7.2 31.7 %copy-start.4 = (s32[4,1]{0,1:T(1,128)S(1)}, s32[4,1]{0,1:T(1,128)}, u32[]{:S(2)}) copy-start(s32[4,1]{0,1:T(1,128)} %param.11) | copy-start | bytes 52
  7.2 89.5 %copy-start.2 = (bf16[4,4096]{1,0:T(4,128)(2,1)S(1)}, bf16[4,4096]{1,0:T(4,128)(2,1)}, u32[]{:S(2)}) copy-start(bf16[4,4096]{1,0:T(4,128)(2,1)} %param.8) | copy-start | bytes 98308
  7.2 94.4 %copy-start.3 = (bf16[8192]{0:T(1024)(128)(2,1)S(1)}, bf16[8192]{0:T(1024)(128)(2,1)}, u32[]{:S(2)}) copy-start(bf16[8192]{0:T(1024)(128)(2,1)} %param.9) | copy-start | bytes 49156
  7.2 89.4 %all-reduce.3.cloned.1.call-start = ((), (), s32[]{:S(2)}) async-start(), calls=%async_computation.1 | async-start | bytes 1048576
  97.6 9.2 %copy-start.1 = (bf16[4,4096]{1,0:T(4,128)(2,1)}, bf16[4,4096]{1,0:T(4,128)(2,1)S(1)}, u32[]{:S(2)}) copy-start(bf16[4,4096]{1,0:T(4,128)(2,1)S(1)} %fusion.6) | copy-start | bytes 98308
  98.4 7.2 %all-to-all-start = ((bf16[2,1,2,4096]{3,2,1,0:T(2,128)(2,1)}), bf16[2,1,2,4096]{3,2,1,0:T(2,128)(2,1)S(1)}, u32[]{:S(2)}, u32[]{:S(2)}) async-start(bf16[2,1,2,4096]{3,2,1,0:T(2,128)(2,1)} %fusion), calls=%async_computation | async-start | bytes 65536 | tf_op jit(solution)/shard_map/all_to_all | solution.py:36
Sparse Core Ops, SparseCore 0:
  39.0 57.5 all-reduce.2
where the time goes:
time: 114 us
  waiting for transfers between devices  60.2 us (53%)
  matrix products  24.1 us (21%)
  between operations  14.8 us (13%)
  blocking collectives  9.25 us (8%)
  starting transfers between devices  3.29 us (3%)
  other arithmetic  1.42 us (1%)
    unnamed x2, waiting for transfers between devices  56.3 us
    dot_general x1, matrix products, body(): jnp.dot(gathered, down_matrix, preferred_element_type=jnp.float32)  22.4 us
    all_gather x1, blocking collectives, body(): gathered = lax.all_gather(hidden, 'dp', axis=0, tiled=True)  9.25 us
    all_to_all x1, waiting for transfers between devices, body(): lax.all_to_all(outgoing, 'dp', split_axis=0, concat_axis=3, tiled=True)  3.89 us
    all_to_all x1, starting transfers between devices, body(): lax.all_to_all(outgoing, 'dp', split_axis=0, concat_axis=3, tiled=True)  3.25 us
  transfers between devices with their start and end apart: 2, of which 2 were waited for; matrix products, arithmetic and copies ran while one was open for 1% of the time, Pallas kernels for 0%

commit v1 on v0

v1 whole, which is shorter than its diff:
```python
import itertools

import jax
import jax.numpy as jnp
from jax import lax
from jax.experimental import pallas as pl
from jax.experimental.pallas import tpu as pltpu
from jax.sharding import PartitionSpec as P

MOST = 2
EPS = 1e-05
REDUCE_AXES = ("tensor", "section")


def project_kernel(place_ref, own_ref, others_ref, weight_ref, out_ref, rows_ref):
    own_rows = own_ref.shape[0]

    @pl.when(pl.program_id(0) == 0)
    def _():
        rows_ref[pl.ds(pl.multiple_of(place_ref[0] * own_rows, own_rows), own_rows), :] = own_ref[...]
        for shift in range(others_ref.shape[0]):
            start = pl.multiple_of(place_ref[shift + 1] * own_rows, own_rows)
            rows_ref[pl.ds(start, own_rows), :] = others_ref[shift]

    out_ref[...] = jnp.dot(
        rows_ref[...], weight_ref[...], preferred_element_type=jnp.float32
    ).astype(out_ref.dtype)


def project(place, own, others, weight, width):
    own_rows, depth = own.shape
    rows = own_rows * (1 + others.shape[0])
    columns = weight.shape[1]
    whole = pl.BlockSpec(memory_space=pltpu.VMEM)
    return pl.pallas_call(
        project_kernel,
        grid=(columns // width,),
        out_shape=jax.ShapeDtypeStruct((rows, columns), jnp.bfloat16),
        in_specs=[
            pl.BlockSpec(memory_space=pltpu.SMEM),
            whole,
            whole,
            pl.BlockSpec((depth, width), lambda n: (0, n)),
        ],
        out_specs=pl.BlockSpec((rows, width), lambda n: (0, n)),
        scratch_shapes=[pltpu.VMEM((rows, depth), jnp.bfloat16)],
        compiler_params=pltpu.CompilerParams(vmem_limit_bytes=32 * 2**20),
        cost_estimate=pl.CostEstimate(
            flops=2 * rows * depth * columns,
            bytes_accessed=depth * columns * 2,
            transcendentals=0,
        ),
        name="project",
    )(place, own, others, weight)


def finish_kernel(
    place_ref, index_ref, parts_ref, residual_ref, gain_ref, shrink_ref, mixed_ref, sent_ref
):
    rows, columns = residual_ref.shape
    owners, local_adapters, _, _ = sent_ref.shape
    rank = shrink_ref.shape[0] // (owners * local_adapters)
    total = residual_ref[...].astype(jnp.float32)
    for source in range(parts_ref.shape[0]):
        total = total + parts_ref[source].astype(jnp.float32)
    mixed = total.astype(jnp.bfloat16)
    mixed_ref[...] = mixed
    widened = mixed.astype(jnp.float32)
    squares = jnp.sum(widened * widened, axis=1, keepdims=True)
    scaled = widened * gain_ref[...].astype(jnp.float32)
    high = scaled.astype(jnp.bfloat16)
    low = (scaled - high.astype(jnp.float32)).astype(jnp.bfloat16)
    against = (((1,), (1,)), ((), ()))
    values = lax.dot_general(
        high, shrink_ref[...], against, preferred_element_type=jnp.float32
    ) + lax.dot_general(low, shrink_ref[...], against, preferred_element_type=jnp.float32)
    named = [index_ref[row, 0] for row in range(rows)]
    for place, local in itertools.product(range(owners), range(local_adapters)):
        adapter = place_ref[place] * local_adapters + local
        first = (place * local_adapters + local) * rank
        own = values[:, first : first + rank]
        filled = jnp.concatenate([own, jnp.broadcast_to(squares, own.shape)], axis=1)
        before = jnp.int32(0)
        slots = [jnp.zeros((1, 2 * rank), jnp.float32) for _ in range(MOST)]
        for row in range(rows):
            hit = named[row] == adapter
            for slot in range(MOST):
                here = jnp.logical_and(hit, before == slot).astype(jnp.float32)
                slots[slot] = slots[slot] + here * filled[row : row + 1, :]
            before = before + hit.astype(jnp.int32)
        for slot in range(MOST):
            sent_ref[place, local, slot : slot + 1, :] = slots[slot]


def finish(place, index, parts, residual, gain, shrink, rank):
    rows, columns = residual.shape
    owners = place.shape[0]
    local_adapters = shrink.shape[0] // (owners * rank)
    whole = pl.BlockSpec(memory_space=pltpu.VMEM)
    return pl.pallas_call(
        finish_kernel,
        out_shape=(
            jax.ShapeDtypeStruct((rows, columns), jnp.bfloat16),
            jax.ShapeDtypeStruct((owners, local_adapters, MOST, 2 * rank), jnp.float32),
        ),
        in_specs=[pl.BlockSpec(memory_space=pltpu.SMEM)] * 2 + [whole] * 4,
        out_specs=(whole, whole),
        compiler_params=pltpu.CompilerParams(vmem_limit_bytes=16 * 2**20),
        name="finish",
    )(place, index, parts, residual, gain, shrink)


def shifted(array, count, shift):
    if shift == 0:
        return array
    return lax.ppermute(array, "dp", [(i, (i + shift) % count) for i in range(count)])


def body(hidden, down_matrix, residual, next_norm_scale, shrink_matrix, adapter_index):
    dp = lax.axis_size("dp")
    me = lax.axis_index("dp")
    blocks = lax.axis_size(REDUCE_AXES)
    columns = down_matrix.shape[1]
    local_adapters, _, rank = shrink_matrix.shape

    others = jnp.stack([shifted(hidden, dp, shift) for shift in range(1, dp)])
    place = jnp.stack([(me - shift) % dp for shift in range(dp)]).astype(jnp.int32)

    by_feature = jnp.swapaxes(shrink_matrix, 1, 2).reshape(local_adapters * rank, dp * columns)
    by_feature, others = lax.optimization_barrier((by_feature, others))
    shrink = jnp.concatenate(
        [
            shifted(
                lax.dynamic_slice_in_dim(by_feature, (me + shift) % dp * columns, columns, 1),
                dp,
                shift,
            )
            for shift in range(dp)
        ]
    )
    gain = lax.dynamic_slice_in_dim(next_norm_scale, me * columns, columns)[None, :]

    partial = project(place, hidden, others, down_matrix, 512)
    rows = partial.shape[0] // blocks
    parts = lax.all_to_all(
        partial.reshape(blocks, rows, columns),
        REDUCE_AXES,
        split_axis=0,
        concat_axis=0,
        tiled=True,
    )
    mixed, sent = finish(place, adapter_index, parts, residual, gain, shrink, rank)

    total = sent[0]
    for back in range(1, dp):
        total = total + shifted(sent[back], dp, dp - back)
    mean_square = total[..., rank:] / (columns * dp)
    shrunk = 2.0 * total[..., :rank] * lax.rsqrt(mean_square + EPS)
    return (mixed, shrunk[:, None])


def solution(mesh):
    placed = (
        P(("groups", "dp"), ("tensor", "section")),
        P(("tensor", "section"), "dp"),
        P(("groups", "tensor", "section"), "dp"),
        P(),
        P("dp", None, None),
        P(("groups", "tensor", "section"), None),
    )
    return jax.shard_map(
        body,
        mesh=mesh,
        in_specs=placed,
        out_specs=(
            P(("groups", "tensor", "section"), "dp"),
            P("dp", ("groups", "tensor", "section"), None, None),
        ),
        check_vma=False,
    )
```

time: 114 us -> 53.7 us (0.47)
  waiting for transfers between devices: 60.2 us -> 18.2 us
  matrix products: 24.1 us -> 0 us
  Pallas kernels: 0 us -> 21.3 us
  between operations: 14.8 us -> 0.71 us
  blocking collectives: 9.25 us -> 0 us
  starting transfers between devices: 3.29 us -> 10.2 us
  local copies, waits for them, and re-layouts: 0.64 us -> 2.21 us
    unnamed x2 -> x0, waiting for transfers between devices: 56.3 us -> none
    dot_general x3 -> x0, matrix products: 24.1 us -> none  [the longest x1 22.4 us: body(): jnp.dot(gathered, down_matrix, preferred_element_type=jnp.float32)]
    pallas_call x0 -> x2, Pallas kernels: none -> 21.3 us  [the longest x1 19.6 us: project(): pl.pallas_call(project_kernel, grid=(columns // width,), out_shape=jax.Sh...]
    all_gather x1 -> x0, blocking collectives: 9.25 us -> none  [body(): gathered = lax.all_gather(hidden, 'dp', axis=0, tiled=True)]
    ppermute x0 -> x3, waiting for transfers between devices: none -> 8.5 us  [shifted(): lax.ppermute(array, 'dp', [(i, (i + shift) % count) for i in range(count)])]
    all_to_all x1, waiting for transfers between devices: 3.89 us -> 9.66 us  [body(): lax.all_to_all(partial.reshape(blocks, rows, columns), REDUCE_AXES, split...]
    ppermute x0 -> x3, starting transfers between devices: none -> 5.34 us  [shifted(): lax.ppermute(array, 'dp', [(i, (i + shift) % count) for i in range(count)])]
    all_to_all x1, starting transfers between devices: 3.25 us -> 4.88 us  [body(): lax.all_to_all(partial.reshape(blocks, rows, columns), REDUCE_AXES, split...]
  transfers between devices with their start and end apart: 2 -> 4, of which waited for: 2 -> 3; matrix products, arithmetic and copies ran while one was open for 1% -> 2% of each run, Pallas kernels for 0% -> 37%
where the time goes in v1:
time: 53.7 us; the launch traced here: 53.4 us
  Pallas kernels  21.3 us (40%)
  waiting for transfers between devices  18.2 us (34%)
  starting transfers between devices  10.2 us (19%)
  local copies, waits for them, and re-layouts  2.21 us (4%)
  other arithmetic  0.79 us (1%)
  between operations  0.71 us (1%)
    pallas_call x1, Pallas kernels, project(): pl.pallas_call(project_kernel, grid=(columns // width,), out_shape=jax.Sh...  19.6 us
    all_to_all x1, waiting for transfers between devices, body(): lax.all_to_all(partial.reshape(blocks, rows, columns), REDUCE_AXES, split...  9.66 us
    ppermute x3, waiting for transfers between devices, shifted(): lax.ppermute(array, 'dp', [(i, (i + shift) % count) for i in range(count)])  8.5 us
    ppermute x3, starting transfers between devices, shifted(): lax.ppermute(array, 'dp', [(i, (i + shift) % count) for i in range(count)])  5.34 us
    all_to_all x1, starting transfers between devices, body(): lax.all_to_all(partial.reshape(blocks, rows, columns), REDUCE_AXES, split...  4.88 us
    pallas_call x1, Pallas kernels, finish(): pl.pallas_call(finish_kernel, out_shape=(jax.ShapeDtypeStruct((rows, colu...  1.69 us
    dynamic_slice x1, local copies, waits for them, and re-layouts, body(): lax.dynamic_slice_in_dim(by_feature, (me + shift) % dp * columns, columns...  1.27 us
  transfers between devices with their start and end apart: 4, of which 3 were waited for; matrix products, arithmetic and copies ran while one was open for 2% of the time, Pallas kernels for 37%

profile of v1, /device:TPU:0, one launch (start us, length us, event | category | flops | bytes accessed | tf_op | source)
XLA Modules:
  0.0 53.4 jit_solution(6432467132921233730)
XLA Ops:
  0.6 0.0 copy-start
  0.6 0.0 copy-start.2
  0.7 0.0 copy-start.3
  0.7 3.0 %collective-permute-start = (bf16[16,6656]{1,0:T(8,128)(2,1)}, bf16[16,6656]{1,0:T(8,128)(2,1)S(1)}, u32[]{:S(2)}, u32[]{:S(2)}) collective-permute-start(bf16[16,6656]{1,0:T(8,128)(2,1)} %own_ref.1), channel_id=1, source_target_pairs={{0,2},{2,0},{1,3},{3,1},{4,6},{6,4},{5,7},{7,5},{8,10},{10,8},{9,1... | collective-permute-start | bytes 638984 | tf_op jit(solution)/shard_map/ppermute | solution.py:116
  3.7 5.5 %collective-permute-done = bf16[16,6656]{1,0:T(8,128)(2,1)S(1)} collective-permute-done((bf16[16,6656]{1,0:T(8,128)(2,1)}, bf16[16,6656]{1,0:T(8,128)(2,1)S(1)}, u32[]{:S(2)}, u32[]{:S(2)}) %collective-permute-start) | collective-permute-done | bytes 213024 | tf_op jit(solution)/shard_map/ppermute | solution.py:116
  9.1 1.3 %constant_dynamic-slice_fusion.1 = (bf16[64,4096]{1,0:T(8,128)(2,1)S(1)}, bf16[64,4096]{1,0:T(8,128)(2,1)S(1)}) fusion(bf16[64,8192]{1,0:T(8,128)(2,1)} %bitcast.13, s32[]{:T(128)S(6)} %select_n.29, s32[]{:T(128)S(6)} %select_n.31), kind=kLoop, calls=%fused_computation.6 | loop fusion | bytes 2097160 | tf_op jit(solution)/shard_map/dynamic_slice | solution.py:134
  10.4 1.8 %collective-permute-start.1 = (bf16[64,4096]{1,0:T(8,128)(2,1)S(1)}, bf16[64,4096]{1,0:T(8,128)(2,1)S(1)}, u32[]{:S(2)}, u32[]{:S(2)}) collective-permute-start(bf16[64,4096]{1,0:T(8,128)(2,1)S(1)} %get-tuple-element.11), channel_id=1, source_target_pairs={{0,2},{2,0},{1,3},{3,1},{4,6},{6,4},{5,7},{7,5},{8,10},{10,8},{9,1... | collective-permute-start | bytes 1572872 | tf_op jit(solution)/shard_map/ppermute | solution.py:116
  12.2 0.0 copy-done.2
  12.2 0.0 copy-done.3
  12.2 0.1 copy.8.index_ref
  12.3 0.1 pad_add_fusion.place_ref
  12.4 0.0 copy-done
  12.4 19.6 %project.1 = bf16[32,4096]{1,0:T(8,128)(2,1)S(1)} custom-call(s32[2]{0:T(128)S(1)} %pad_add_fusion.place_ref, bf16[16,6656]{1,0:T(8,128)(2,1)S(1)} %copy-done, bf16[1,16,6656]{2,1,0:T(8,128)(2,1)S(1)} %bitcast.12, bf16[6656,4096]{1,0:T(8,128)(2,1)} %weight_ref.1), custom_call_target="tpu_custom_call" | custom-call | flops 1744830464 | bytes 54525952 | tf_op jit(solution)/shard_map/project/pallas_call | solution.py:35
  32.0 0.0 copy-start.1
  32.0 0.8 %reshape.11 = bf16[8,4,4096]{2,1,0:T(4,128)(2,1)} reshape(bf16[32,4096]{1,0:T(8,128)(2,1)S(1)} %project.1) | data formatting | bytes 524288 | tf_op jit(solution)/shard_map/reshape | solution.py:146
  32.8 4.9 %all-to-all-start = ((bf16[8,4,4096]{2,1,0:T(4,128)(2,1)}), bf16[8,4,4096]{2,1,0:T(4,128)(2,1)S(1)}, u32[]{:S(2)}, u32[]{:S(2)}) async-start(bf16[8,4,4096]{2,1,0:T(4,128)(2,1)} %reshape.11), calls=%async_computation | async-start | bytes 524288 | tf_op jit(solution)/shard_map/all_to_all | solution.py:145
  37.7 0.0 collective-permute-done.1
  37.7 0.1 pad_maximum_fusion.shrink_ref
  37.8 9.7 %all-to-all-done.parts_ref = bf16[8,4,4096]{2,1,0:T(4,128)(2,1)S(1)} async-done(((bf16[8,4,4096]{2,1,0:T(4,128)(2,1)}), bf16[8,4,4096]{2,1,0:T(4,128)(2,1)S(1)}, u32[]{:S(2)}, u32[]{:S(2)}) %all-to-all-start) | async-done | bytes 262176 | tf_op jit(solution)/shard_map/all_to_all | solution.py:145
  47.4 0.0 copy-done.1
  47.5 1.7 %finish.1 = (bf16[4,4096]{1,0:T(4,128)(2,1)}, f32[2,1,2,128]{3,2,1,0:T(2,128)S(1)}) custom-call(s32[2]{0:T(128)S(1)} %pad_add_fusion.place_ref, s32[4,1]{1,0:T(4,128)S(1)} %copy.8.index_ref, bf16[8,4,4096]{2,1,0:T(4,128)(2,1)S(1)} %all-to-all-done.parts_ref, bf16[4,4096]{1,0:T(4,128)(2,1)S(1)} %copy-done.1, bf16[1,4096]{1,0:T(2,128)(2,1)S(1)} %broadcast_in_dim.6.gain_ref, ...), custom_call_target="tpu_custom_call" | custom-call | tf_op jit(solution)/shard_map/finish/pallas_call | solution.py:100
  49.1 0.5 %collective-permute-start.2 = (f32[1,2,128]{2,1,0:T(2,128)S(1)}, f32[1,2,128]{2,1,0:T(2,128)S(1)}, u32[]{:S(2)}, u32[]{:S(2)}) collective-permute-start(f32[1,2,128]{2,1,0:T(2,128)S(1)} %slice_bitcast_fusion), channel_id=1, source_target_pairs={{0,2},{2,0},{1,3},{3,1},{4,6},{6,4},{5,7},{7,5},{8,10},{10,8},{9,1... | collective-permute-start | bytes 3080 | tf_op jit(solution)/shard_map/ppermute | solution.py:116
  49.7 3.0 %collective-permute-done.2 = f32[1,2,128]{2,1,0:T(2,128)S(1)} collective-permute-done((f32[1,2,128]{2,1,0:T(2,128)S(1)}, f32[1,2,128]{2,1,0:T(2,128)S(1)}, u32[]{:S(2)}, u32[]{:S(2)}) %collective-permute-start.2) | collective-permute-done | bytes 1056 | tf_op jit(solution)/shard_map/ppermute | solution.py:116
  52.7 0.6 %multiply_bitcast_fusion = f32[1,1,2,64]{3,2,1,0:T(2,128)} fusion(f32[1,2,128]{2,1,0:T(2,128)S(1)} %bitcast_add_fusion), kind=kLoop, calls=%fused_computation.2 | loop fusion | flops 512 | bytes 1536 | tf_op jit(solution)/shard_map/broadcast_in_dim | solution.py:159
  (4 shorter events, 0.0 us)
Async XLA Ops:
  0.6 11.8 %copy-start = (bf16[16,6656]{1,0:T(8,128)(2,1)S(1)}, bf16[16,6656]{1,0:T(8,128)(2,1)}, u32[]{:S(2)}) copy-start(bf16[16,6656]{1,0:T(8,128)(2,1)} %own_ref.1) | copy-start | bytes 638980
  0.6 11.6 %copy-start.2 = (bf16[8192]{0:T(1024)(128)(2,1)S(1)}, bf16[8192]{0:T(1024)(128)(2,1)}, u32[]{:S(2)}) copy-start(bf16[8192]{0:T(1024)(128)(2,1)} %param.9) | copy-start | bytes 49156
  0.7 11.6 %copy-start.3 = (s32[4,1]{0,1:T(1,128)S(1)}, s32[4,1]{0,1:T(1,128)}, u32[]{:S(2)}) copy-start(s32[4,1]{0,1:T(1,128)} %param.11) | copy-start | bytes 52
  0.7 8.5 %collective-permute-start = (bf16[16,6656]{1,0:T(8,128)(2,1)}, bf16[16,6656]{1,0:T(8,128)(2,1)S(1)}, u32[]{:S(2)}, u32[]{:S(2)}) collective-permute-start(bf16[16,6656]{1,0:T(8,128)(2,1)} %own_ref.1), channel_id=1, source_target_pairs={{0,2},{2,0},{1,3},{3,1},{4,6},{6,4},{5,7},{7,5},{8,10},{10,8},{9,1... | collective-permute-start | bytes 638984 | tf_op jit(solution)/shard_map/ppermute | solution.py:116
  10.4 27.3 %collective-permute-start.1 = (bf16[64,4096]{1,0:T(8,128)(2,1)S(1)}, bf16[64,4096]{1,0:T(8,128)(2,1)S(1)}, u32[]{:S(2)}, u32[]{:S(2)}) collective-permute-start(bf16[64,4096]{1,0:T(8,128)(2,1)S(1)} %get-tuple-element.11), channel_id=1, source_target_pairs={{0,2},{2,0},{1,3},{3,1},{4,6},{6,4},{5,7},{7,5},{8,10},{10,8},{9,1... | collective-permute-start | bytes 1572872 | tf_op jit(solution)/shard_map/ppermute | solution.py:116
  32.0 15.5 %copy-start.1 = (bf16[4,4096]{1,0:T(4,128)(2,1)S(1)}, bf16[4,4096]{1,0:T(4,128)(2,1)}, u32[]{:S(2)}) copy-start(bf16[4,4096]{1,0:T(4,128)(2,1)} %residual_ref.1) | copy-start | bytes 98308
  32.8 14.6 %all-to-all-start = ((bf16[8,4,4096]{2,1,0:T(4,128)(2,1)}), bf16[8,4,4096]{2,1,0:T(4,128)(2,1)S(1)}, u32[]{:S(2)}, u32[]{:S(2)}) async-start(bf16[8,4,4096]{2,1,0:T(4,128)(2,1)} %reshape.11), calls=%async_computation | async-start | bytes 524288 | tf_op jit(solution)/shard_map/all_to_all | solution.py:145
  49.1 3.6 %collective-permute-start.2 = (f32[1,2,128]{2,1,0:T(2,128)S(1)}, f32[1,2,128]{2,1,0:T(2,128)S(1)}, u32[]{:S(2)}, u32[]{:S(2)}) collective-permute-start(f32[1,2,128]{2,1,0:T(2,128)S(1)} %slice_bitcast_fusion), channel_id=1, source_target_pairs={{0,2},{2,0},{1,3},{3,1},{4,6},{6,4},{5,7},{7,5},{8,10},{10,8},{9,1... | collective-permute-start | bytes 3080 | tf_op jit(solution)/shard_map/ppermute | solution.py:116

commit v2 on v0

v2 whole, which is shorter than its diff:
```python
import jax
import jax.numpy as jnp
from jax import lax
from jax.experimental import pallas as pl
from jax.experimental.pallas import tpu as pltpu
from jax.sharding import PartitionSpec as P

MOST = 2
EPS = 1e-05
DEPTH_STEP = 512
HELD_BYTES = 26 * 2**20
MIB = 2**20
F32 = jnp.float32
BF16 = jnp.bfloat16


def whole():
    return pl.BlockSpec(memory_space=pltpu.VMEM)


def step_of(depth):
    return max(s for s in range(16, DEPTH_STEP + 1, 16) if depth % s == 0)


def fetch_kernel(weight_ref, held_ref, sems):
    count, step, _ = held_ref.shape
    copies = [
        pltpu.make_async_copy(
            weight_ref.at[pl.ds(i * step, step), :], held_ref.at[i], sems.at[i]
        )
        for i in range(count)
    ]
    for copy in copies:
        copy.start()
    for copy in copies:
        copy.wait()


def fetch(weight, count, step):
    columns = weight.shape[1]
    return pl.pallas_call(
        fetch_kernel,
        out_shape=pltpu.VMEM((count, step, columns), weight.dtype),
        in_specs=[pl.BlockSpec(memory_space=pl.ANY)],
        out_specs=whole(),
        scratch_shapes=[pltpu.SemaphoreType.DMA((count,))],
        compiler_params=pltpu.CompilerParams(vmem_limit_bytes=1 * MIB),
        cost_estimate=pl.CostEstimate(
            flops=0, bytes_accessed=2 * count * step * columns, transcendentals=0
        ),
        name="fetch",
    )(weight)


def project_kernel(
    own_ref, others_ref, held_ref, weight_ref, kept_ref, sent_ref, rows_ref, total_ref, rest_ref, sems
):
    held, step, columns = held_ref.shape
    rest = rest_ref.shape[0]
    own_rows = own_ref.shape[0]
    dp = 1 + others_ref.shape[0]
    me = lax.axis_index("dp")
    section = lax.axis_index("section")
    width = min(columns, 1024)

    def copy_of(i):
        return pltpu.make_async_copy(
            weight_ref.at[pl.ds((held + i) * step, step), :], rest_ref.at[i], sems.at[i]
        )

    for i in range(rest):
        copy_of(i).start()

    for i in range(held + rest):
        block = slice(i * step, (i + 1) * step)
        own_first = pl.multiple_of(me * own_rows, own_rows)
        rows_ref[i, pl.ds(own_first, own_rows), :] = own_ref[:, block]
        for shift in range(1, dp):
            first = pl.multiple_of(lax.rem(me + dp - shift, dp) * own_rows, own_rows)
            rows_ref[i, pl.ds(first, own_rows), :] = others_ref[shift - 1, :, block]
    total_ref[...] = jnp.zeros_like(total_ref)

    def add(block_ref, i):
        for n in range(0, columns, width):
            total_ref[:, n : n + width] += jnp.dot(
                rows_ref[i], block_ref[:, n : n + width], preferred_element_type=F32
            )

    def held_step(i, _):
        add(held_ref.at[i], i)
        return 0

    def rest_step(i, _):
        copy_of(i).wait()
        add(rest_ref.at[i], held + i)
        return 0

    lax.fori_loop(0, held, held_step, 0)
    lax.fori_loop(0, rest, rest_step, 0)

    _, tensors, block_rows, _ = kept_ref.shape
    sections = sent_ref.shape[0] + 1
    for s in range(sections):
        for t in range(tensors):
            first = (t * sections + s) * block_rows
            block = total_ref[first : first + block_rows, :]

            @pl.when(section == s)
            def _():
                kept_ref[0, t] = block

            @pl.when(section != s)
            def _():
                sent_ref[lax.rem(s + sections - section, sections) - 1, t] = block.astype(BF16)


def project(own, others, held, weight, tensors, sections):
    own_rows, depth = own.shape
    rows = own_rows * (1 + others.shape[0])
    columns = weight.shape[1]
    count, step, _ = held.shape
    rest = depth // step - count
    block_rows = rows // (tensors * sections)
    return pl.pallas_call(
        project_kernel,
        out_shape=(
            pltpu.VMEM((1, tensors, block_rows, columns), F32),
            pltpu.VMEM((sections - 1, tensors, block_rows, columns), BF16),
        ),
        in_specs=[whole(), whole(), whole(), pl.BlockSpec(memory_space=pl.ANY)],
        out_specs=(whole(), whole()),
        scratch_shapes=[
            pltpu.VMEM((depth // step, rows, step), BF16),
            pltpu.VMEM((rows, columns), F32),
            pltpu.VMEM((rest, step, columns), BF16),
            pltpu.SemaphoreType.DMA((rest,)),
        ],
        compiler_params=pltpu.CompilerParams(vmem_limit_bytes=31 * MIB),
        cost_estimate=pl.CostEstimate(
            flops=2 * rows * depth * columns,
            bytes_accessed=2 * rest * step * columns,
            transcendentals=0,
        ),
        name="project",
    )(own, others, held, weight)


def pair_kernel(kept_ref, *refs):
    tensors = kept_ref.shape[1]
    arrived, outs = refs[:-tensors], refs[-tensors:]
    me = lax.axis_index("tensor")
    for shift, out_ref in enumerate(outs):
        place = lax.rem(me + shift, tensors)
        block = kept_ref[0, place]
        for piece in arrived:
            block = block + piece[place].astype(F32)
        out_ref[...] = block.astype(out_ref.dtype)


def pair(kept, arrived):
    _, tensors, block_rows, columns = kept.shape
    return pl.pallas_call(
        pair_kernel,
        out_shape=[
            jax.ShapeDtypeStruct((block_rows, columns), F32 if shift == 0 else BF16)
            for shift in range(tensors)
        ],
        in_specs=[whole()] * (1 + len(arrived)),
        out_specs=[whole()] * tensors,
        compiler_params=pltpu.CompilerParams(vmem_limit_bytes=8 * MIB),
        name="pair",
    )(kept, *arrived)


def mix_kernel(residual_ref, places_ref, own_ref, *refs):
    arrived, (mixed_ref, kept_ref, sent_ref) = refs[:-3], refs[-3:]
    total = own_ref[...] + residual_ref[...].astype(F32)
    for piece in arrived:
        total = total + piece[...].astype(F32)
    mixed = total.astype(BF16)
    mixed_ref[...] = mixed
    widened = mixed.astype(F32)
    places = places_ref[...]
    slots = kept_ref.shape[0]
    routed = sum(
        places[:, row : row + 1] * widened[row : row + 1, :] for row in range(widened.shape[0])
    )
    kept_ref[...] = routed[:slots]
    for shift in range(sent_ref.shape[0]):
        sent_ref[shift] = routed[(shift + 1) * slots : (shift + 2) * slots].astype(BF16)


def mix(residual, places, own, arrived, slots):
    rows, columns = residual.shape
    owners = places.shape[0] // slots
    return pl.pallas_call(
        mix_kernel,
        out_shape=(
            jax.ShapeDtypeStruct((rows, columns), BF16),
            jax.ShapeDtypeStruct((slots, columns), F32),
            jax.ShapeDtypeStruct((owners - 1, slots, columns), BF16),
        ),
        in_specs=[whole()] * (3 + len(arrived)),
        out_specs=(whole(),) * 3,
        compiler_params=pltpu.CompilerParams(vmem_limit_bytes=8 * MIB),
        name="mix",
    )(residual, places, own, *arrived)


def partial_values(rows, gain_ref, shrink_ref, place, columns, local):
    first = pl.multiple_of(place * columns, columns)
    squares = jnp.sum(rows * rows, axis=1, keepdims=True)
    scaled = rows * gain_ref[:, pl.ds(first, columns)].astype(F32)
    high = scaled.astype(BF16)
    low = (scaled - high.astype(F32)).astype(BF16)
    values = []
    for adapter in range(local):
        mine = slice(adapter * MOST, (adapter + 1) * MOST)
        both = jnp.concatenate([high[mine], low[mine]], axis=0)
        product = lax.dot_general(
            both,
            shrink_ref[adapter, :, pl.ds(first, columns)],
            (((1,), (1,)), ((), ())),
            preferred_element_type=F32,
        )
        values.append(product[:MOST] + product[MOST:])
    return jnp.concatenate(values, axis=0), squares


def own_half_kernel(rows_ref, gain_ref, shrink_ref, values_ref, squares_ref):
    columns = rows_ref.shape[1]
    values, squares = partial_values(
        rows_ref[...], gain_ref, shrink_ref, lax.axis_index("dp"), columns, shrink_ref.shape[0]
    )
    values_ref[...] = values
    squares_ref[...] = jnp.broadcast_to(squares, squares_ref.shape)


def own_half(rows, gain, shrink):
    slots = rows.shape[0]
    rank = shrink.shape[1]
    return pl.pallas_call(
        own_half_kernel,
        out_shape=(
            jax.ShapeDtypeStruct((slots, rank), F32),
            jax.ShapeDtypeStruct((slots, rank), F32),
        ),
        in_specs=[whole()] * 3,
        out_specs=(whole(),) * 2,
        compiler_params=pltpu.CompilerParams(vmem_limit_bytes=8 * MIB),
        cost_estimate=pl.CostEstimate(
            flops=2 * slots * rows.shape[1] * rank, bytes_accessed=2 * MIB, transcendentals=0
        ),
        name="own_half",
    )(rows, gain, shrink)


def finish_kernel(values_ref, squares_ref, gain_ref, shrink_ref, *refs):
    arrived, out_ref = refs[:-1], refs[-1]
    dp = 1 + len(arrived)
    me = lax.axis_index("dp")
    local = shrink_ref.shape[0]
    columns = arrived[0].shape[1]
    values, squares = values_ref[...], squares_ref[:, :1]
    for shift, piece in enumerate(arrived, start=1):
        more, more_squares = partial_values(
            piece[...].astype(F32),
            gain_ref,
            shrink_ref,
            lax.rem(me + dp - shift, dp),
            columns,
            local,
        )
        values, squares = values + more, squares + more_squares
    result = 2.0 * values * lax.rsqrt(squares / (columns * dp) + EPS)
    for adapter in range(local):
        out_ref[adapter, 0] = result[adapter * MOST : (adapter + 1) * MOST]


def finish(values, squares, gain, shrink, arrived):
    local, rank, _ = shrink.shape
    return pl.pallas_call(
        finish_kernel,
        out_shape=jax.ShapeDtypeStruct((local, 1, MOST, rank), F32),
        in_specs=[whole()] * (4 + len(arrived)),
        out_specs=whole(),
        compiler_params=pltpu.CompilerParams(vmem_limit_bytes=8 * MIB),
        name="finish",
    )(values, squares, gain, shrink, *arrived)


def shifted(array, axis, shift):
    count = lax.axis_size(axis)
    return lax.ppermute(array, axis, [(i, (i + shift) % count) for i in range(count)])


def body(hidden, down_matrix, residual, next_norm_scale, shrink_matrix, adapter_index):
    dp, tensors, sections = (lax.axis_size(axis) for axis in ("dp", "tensor", "section"))
    me = lax.axis_index("dp")
    depth, _ = down_matrix.shape
    local = shrink_matrix.shape[0]

    others = jnp.stack([shifted(hidden, "dp", shift) for shift in range(1, dp)])

    step = step_of(depth)
    blocks = depth // step
    held_count = max(1, min(blocks // 2, HELD_BYTES // (2 * step * down_matrix.shape[1])))
    held = fetch(down_matrix, held_count, step)

    row_adapter = adapter_index[:, 0]
    same = row_adapter[:, None] == row_adapter[None, :]
    rows = row_adapter.shape[0]
    earlier = jnp.arange(rows)[:, None] < jnp.arange(rows)[None, :]
    rank_of = jnp.sum(jnp.logical_and(same, earlier), axis=0)
    owners = (me + jnp.arange(dp)) % dp
    adapters = owners[:, None] * local + jnp.arange(local)[None, :]
    places = jnp.logical_and(
        adapters[:, :, None, None] == row_adapter,
        jnp.arange(MOST)[None, None, :, None] == rank_of,
    )
    places = places.astype(F32).reshape(dp * local * MOST, rows)
    shrink = jnp.swapaxes(shrink_matrix, 1, 2)
    gain = next_norm_scale[None, :]

    in_vmem = [pltpu.with_memory_space_constraint(x, pltpu.VMEM) for x in (hidden, others, held)]
    kept, sent = project(*in_vmem, down_matrix, tensors, sections)
    arrived = [shifted(sent[s - 1], "section", s) for s in range(1, sections)]
    own, *sums = pair(kept, arrived)
    arrived = [shifted(piece, "tensor", s) for s, piece in enumerate(sums, start=1)]
    mixed, routed, leaving = mix(residual, places, own, arrived, local * MOST)
    arrived = [shifted(leaving[s - 1], "dp", s) for s in range(1, dp)]
    values, squares = own_half(routed, gain, shrink)
    shrunk = finish(values, squares, gain, shrink, arrived)
    return (mixed, shrunk)


def solution(mesh):
    placed = (
        P(("groups", "dp"), ("tensor", "section")),
        P(("tensor", "section"), "dp"),
        P(("groups", "tensor", "section"), "dp"),
        P(),
        P("dp", None, None),
        P(("groups", "tensor", "section"), None),
    )
    return jax.shard_map(
        body,
        mesh=mesh,
        in_specs=placed,
        out_specs=(
            P(("groups", "tensor", "section"), "dp"),
            P("dp", ("groups", "tensor", "section"), None, None),
        ),
        check_vma=False,
    )
```

time: 114 us -> 38.2 us (0.34)
  waiting for transfers between devices: 60.2 us -> 6.74 us
  matrix products: 24.1 us -> 0 us
  Pallas kernels: 0 us -> 21.2 us
  between operations: 14.8 us -> 0.73 us
  blocking collectives: 9.25 us -> 0 us
  starting transfers between devices: 3.29 us -> 9.17 us
  other arithmetic: 1.42 us -> 0.18 us
    unnamed x2 -> x0, waiting for transfers between devices: 56.3 us -> none
    dot_general x3 -> x0, matrix products: 24.1 us -> none  [the longest x1 22.4 us: body(): jnp.dot(gathered, down_matrix, preferred_element_type=jnp.float32)]
    pallas_call x0 -> x6, Pallas kernels: none -> 21.2 us  [the longest x1 11.1 us: project(): pl.pallas_call(project_kernel, out_shape=(pltpu.VMEM((1, tensors, block_r...]
    all_gather x1 -> x0, blocking collectives: 9.25 us -> none  [body(): gathered = lax.all_gather(hidden, 'dp', axis=0, tiled=True)]
    ppermute x0 -> x6, starting transfers between devices: none -> 9.17 us  [shifted(): lax.ppermute(array, axis, [(i, (i + shift) % count) for i in range(count)])]
    ppermute x0 -> x6, waiting for transfers between devices: none -> 6.74 us  [shifted(): lax.ppermute(array, axis, [(i, (i + shift) % count) for i in range(count)])]
    all_to_all x1 -> x0, waiting for transfers between devices: 3.89 us -> none  [body(): lax.all_to_all(outgoing, 'dp', split_axis=0, concat_axis=3, tiled=True)]
    all_to_all x1 -> x0, starting transfers between devices: 3.25 us -> none  [body(): lax.all_to_all(outgoing, 'dp', split_axis=0, concat_axis=3, tiled=True)]
  transfers between devices with their start and end apart: 2 -> 6, of which waited for: 2 -> 5; matrix products, arithmetic and copies ran while one was open for 1% -> 1% of each run, Pallas kernels for 0% -> 22%
where the time goes in v2:
time: 38.2 us; the launch traced here: 38 us
  Pallas kernels  21.2 us (55%)
  starting transfers between devices  9.17 us (24%)
  waiting for transfers between devices  6.74 us (18%)
  between operations  0.73 us (2%)
    pallas_call x1, Pallas kernels, project(): pl.pallas_call(project_kernel, out_shape=(pltpu.VMEM((1, tensors, block_r...  11.1 us
    ppermute x6, starting transfers between devices, shifted(): lax.ppermute(array, axis, [(i, (i + shift) % count) for i in range(count)])  9.17 us
    pallas_call x1, Pallas kernels, fetch(): pl.pallas_call(fetch_kernel, out_shape=pltpu.VMEM((count, step, columns),...  8.29 us
    ppermute x6, waiting for transfers between devices, shifted(): lax.ppermute(array, axis, [(i, (i + shift) % count) for i in range(count)])  6.74 us
    pallas_call x1, Pallas kernels, finish(): pl.pallas_call(finish_kernel, out_shape=jax.ShapeDtypeStruct((local, 1, M...  0.84 us
  transfers between devices with their start and end apart: 6, of which 5 were waited for; matrix products, arithmetic and copies ran while one was open for 1% of the time, Pallas kernels for 22%

profile of v2, /device:TPU:0, one launch (start us, length us, event | category | flops | bytes accessed | tf_op | source)
XLA Modules:
  0.0 38.0 jit_solution(6906951127792829511)
XLA Ops:
  0.6 0.0 copy-start.1
  0.6 0.0 copy-start.4
  0.6 3.0 %collective-permute-start = (bf16[16,6656]{1,0:T(8,128)(2,1)}, bf16[16,6656]{1,0:T(8,128)(2,1)S(1)}, u32[]{:S(2)}, u32[]{:S(2)}) collective-permute-start(bf16[16,6656]{1,0:T(8,128)(2,1)} %own_ref.1), channel_id=1, source_target_pairs={{0,2},{2,0},{1,3},{3,1},{4,6},{6,4},{5,7},{7,5},{8,10},{10,8},{9,1... | collective-permute-start | bytes 638984 | tf_op jit(solution)/shard_map/ppermute | solution.py:294
  3.7 8.3 %fetch.1.held_ref = bf16[6,512,4096]{2,1,0:T(8,128)(2,1)S(1)} custom-call(bf16[6656,4096]{1,0:T(8,128)(2,1)} %weight_ref.3), custom_call_target="tpu_custom_call" | custom-call | bytes 25165824 | tf_op jit(solution)/shard_map/fetch/pallas_call | solution.py:41
  12.0 0.0 copy-start.2
  12.0 0.0 copy-start.3
  12.0 0.0 copy-start
  12.0 0.0 copy-done.4
  12.0 0.1 convert_reduce_fusion
  12.1 0.0 collective-permute-done
  12.1 0.0 copy-done.1
  12.1 11.1 %project.1 = (f32[1,4,4,4096]{3,2,1,0:T(4,128)S(1)}, bf16[1,4,4,4096]{3,2,1,0:T(4,128)(2,1)S(1)}) custom-call(bf16[16,6656]{1,0:T(8,128)(2,1)S(1)} %copy-done.1, bf16[1,16,6656]{2,1,0:T(8,128)(2,1)S(1)} %bitcast.8, bf16[6,512,4096]{2,1,0:T(8,128)(2,1)S(1)} %fetch.1.held_ref, bf16[6656,4096]{1,0:T(8,128)(2,1)} %weight_ref.3), custom_call_target="tpu_custom_call" | custom-call | flops 1744830464 | bytes 29360128 | tf_op jit(solution)/shard_map/project/pallas_call | solution.py:124
  23.2 0.1 collective-permute-start.1
  23.3 0.1 iota_compare_fusion.1
  23.4 1.3 %collective-permute-done.1.refs_0_ = bf16[4,4,4096]{2,1,0:T(4,128)(2,1)S(1)} collective-permute-done((bf16[4,4,4096]{2,1,0:T(4,128)(2,1)S(1)}, bf16[4,4,4096]{2,1,0:T(4,128)(2,1)S(1)}, u32[]{:S(2)}, u32[]{:S(2)}) %collective-permute-start.1) | collective-permute-done | bytes 131104 | tf_op jit(solution)/shard_map/ppermute | solution.py:294
  24.7 1.6 %collective-permute-start.2 = (bf16[4,4096]{1,0:T(4,128)(2,1)S(1)}, bf16[4,4096]{1,0:T(4,128)(2,1)S(1)}, u32[]{:S(2)}, u32[]{:S(2)}) collective-permute-start(bf16[4,4096]{1,0:T(4,128)(2,1)S(1)} %get-tuple-element.16), channel_id=1, source_target_pairs={{0,4},{4,8},{8,12},{12,0},{1,5},{5,9},{9,13},{13,1},{2,6},{6,10},{... | collective-permute-start | bytes 98312 | tf_op jit(solution)/shard_map/ppermute | solution.py:294
  26.3 2.6 %collective-permute-start.3 = (bf16[4,4096]{1,0:T(4,128)(2,1)S(1)}, bf16[4,4096]{1,0:T(4,128)(2,1)S(1)}, u32[]{:S(2)}, u32[]{:S(2)}) collective-permute-start(bf16[4,4096]{1,0:T(4,128)(2,1)S(1)} %get-tuple-element.17), channel_id=1, source_target_pairs={{0,8},{4,12},{8,0},{12,4},{1,9},{5,13},{9,1},{13,5},{2,10},{6,14},... | collective-permute-start | bytes 98312 | tf_op jit(solution)/shard_map/ppermute | solution.py:294
  28.9 1.3 %collective-permute-start.4 = (bf16[4,4096]{1,0:T(4,128)(2,1)S(1)}, bf16[4,4096]{1,0:T(4,128)(2,1)S(1)}, u32[]{:S(2)}, u32[]{:S(2)}) collective-permute-start(bf16[4,4096]{1,0:T(4,128)(2,1)S(1)} %get-tuple-element.18), channel_id=1, source_target_pairs={{0,12},{4,0},{8,4},{12,8},{1,13},{5,1},{9,5},{13,9},{2,14},{6,2},{... | collective-permute-start | bytes 98312 | tf_op jit(solution)/shard_map/ppermute | solution.py:294
  30.2 0.2 collective-permute-done.2.refs_0_
  30.4 1.3 %collective-permute-done.3.refs_1_ = bf16[4,4096]{1,0:T(4,128)(2,1)S(1)} collective-permute-done((bf16[4,4096]{1,0:T(4,128)(2,1)S(1)}, bf16[4,4096]{1,0:T(4,128)(2,1)S(1)}, u32[]{:S(2)}, u32[]{:S(2)}) %collective-permute-start.3) | collective-permute-done | bytes 32800 | tf_op jit(solution)/shard_map/ppermute | solution.py:294
  31.7 1.1 %collective-permute-done.4.refs_2_ = bf16[4,4096]{1,0:T(4,128)(2,1)S(1)} collective-permute-done((bf16[4,4096]{1,0:T(4,128)(2,1)S(1)}, bf16[4,4096]{1,0:T(4,128)(2,1)S(1)}, u32[]{:S(2)}, u32[]{:S(2)}) %collective-permute-start.4) | collective-permute-done | bytes 32800 | tf_op jit(solution)/shard_map/ppermute | solution.py:294
  32.8 0.0 copy-done.2
  32.8 0.6 %mix.1 = (bf16[4,4096]{1,0:T(4,128)(2,1)}, f32[2,4096]{1,0:T(2,128)S(1)}, bf16[1,2,4096]{2,1,0:T(2,128)(2,1)S(1)}) custom-call(bf16[4,4096]{1,0:T(4,128)(2,1)S(1)} %copy-done.2, f32[4,4]{1,0:T(4,128)S(1)} %bitcast.9, f32[4,4096]{1,0:T(4,128)S(1)} %get-tuple-element.15.own_ref, bf16[4,4096]{1,0:T(4,128)(2,1)S(1)} %collective-permute-done.2.refs_0_, ...), custom_call_target="tpu_custom_call" | custom-call | tf_op jit(solution)/shard_map/mix/pallas_call | solution.py:196
  33.5 0.5 %collective-permute-start.5 = (bf16[2,4096]{1,0:T(2,128)(2,1)S(1)}, bf16[2,4096]{1,0:T(2,128)(2,1)S(1)}, u32[]{:S(2)}, u32[]{:S(2)}) collective-permute-start(bf16[2,4096]{1,0:T(2,128)(2,1)S(1)} %bitcast.11), channel_id=1, source_target_pairs={{0,2},{2,0},{1,3},{3,1},{4,6},{6,4},{5,7},{7,5},{8,10},{10,8},{9,1... | collective-permute-start | bytes 49160 | tf_op jit(solution)/shard_map/ppermute | solution.py:294
  34.0 0.0 copy-done.3
  34.0 0.0 copy-done
  34.0 0.3 own_half.1
  34.3 2.9 %collective-permute-done.5.refs_0_ = bf16[2,4096]{1,0:T(2,128)(2,1)S(1)} collective-permute-done((bf16[2,4096]{1,0:T(2,128)(2,1)S(1)}, bf16[2,4096]{1,0:T(2,128)(2,1)S(1)}, u32[]{:S(2)}, u32[]{:S(2)}) %collective-permute-start.5) | collective-permute-done | bytes 16416 | tf_op jit(solution)/shard_map/ppermute | solution.py:294
  37.2 0.8 %finish.1 = f32[1,1,2,64]{3,2,1,0:T(2,128)} custom-call(f32[2,64]{1,0:T(2,128)S(1)} %get-tuple-element.21.values_ref, f32[2,64]{1,0:T(2,128)S(1)} %get-tuple-element.22.squares_ref, bf16[1,8192]{1,0:T(2,128)(2,1)S(1)} %broadcast_in_dim.2.gain_ref, bf16[1,64,8192]{2,1,0:T(8,128)(2,1)S(1)} %bitcast.7, bf16[2,4096]{1,0:T(2,128)(2,1)S(1)} %collective-permute-done.5.refs_0_), custom_call_target="tpu_custom_call" | custom-call | tf_op jit(solution)/shard_map/finish/pallas_call | solution.py:282
  (4 shorter events, 0.1 us)
Async XLA Ops:
  0.6 11.5 %copy-start.1 = (bf16[16,6656]{1,0:T(8,128)(2,1)S(1)}, bf16[16,6656]{1,0:T(8,128)(2,1)}, u32[]{:S(2)}) copy-start(bf16[16,6656]{1,0:T(8,128)(2,1)} %own_ref.1) | copy-start | bytes 638980
  0.6 11.4 %copy-start.4 = (s32[4,1]{0,1:T(1,128)S(1)}, s32[4,1]{0,1:T(1,128)}, u32[]{:S(2)}) copy-start(s32[4,1]{0,1:T(1,128)} %param.11) | copy-start | bytes 52
  0.6 11.5 %collective-permute-start = (bf16[16,6656]{1,0:T(8,128)(2,1)}, bf16[16,6656]{1,0:T(8,128)(2,1)S(1)}, u32[]{:S(2)}, u32[]{:S(2)}) collective-permute-start(bf16[16,6656]{1,0:T(8,128)(2,1)} %own_ref.1), channel_id=1, source_target_pairs={{0,2},{2,0},{1,3},{3,1},{4,6},{6,4},{5,7},{7,5},{8,10},{10,8},{9,1... | collective-permute-start | bytes 638984 | tf_op jit(solution)/shard_map/ppermute | solution.py:294
  12.0 20.9 %copy-start.2 = (bf16[4,4096]{1,0:T(4,128)(2,1)S(1)}, bf16[4,4096]{1,0:T(4,128)(2,1)}, u32[]{:S(2)}) copy-start(bf16[4,4096]{1,0:T(4,128)(2,1)} %residual_ref.1) | copy-start | bytes 98308
  12.0 22.0 %copy-start.3 = (bf16[8192]{0:T(1024)(128)(2,1)S(1)}, bf16[8192]{0:T(1024)(128)(2,1)}, u32[]{:S(2)}) copy-start(bf16[8192]{0:T(1024)(128)(2,1)} %param.9) | copy-start | bytes 49156
  12.0 22.0 %copy-start = (bf16[1,8192,64]{1,2,0:T(8,128)(2,1)S(1)}, bf16[1,8192,64]{1,2,0:T(8,128)(2,1)}, u32[]{:S(2)}) copy-start(bf16[1,8192,64]{1,2,0:T(8,128)(2,1)} %param.10) | copy-start | bytes 3145732
  23.2 1.4 %collective-permute-start.1 = (bf16[4,4,4096]{2,1,0:T(4,128)(2,1)S(1)}, bf16[4,4,4096]{2,1,0:T(4,128)(2,1)S(1)}, u32[]{:S(2)}, u32[]{:S(2)}) collective-permute-start(bf16[4,4,4096]{2,1,0:T(4,128)(2,1)S(1)} %bitcast.10), channel_id=1, source_target_pairs={{0,1},{1,0},{2,3},{3,2},{4,5},{5,4},{6,7},{7,6},{8,9},{9,8},{10,11... | collective-permute-start | bytes 393224 | tf_op jit(solution)/shard_map/ppermute | solution.py:294
  24.7 5.8 %collective-permute-start.2 = (bf16[4,4096]{1,0:T(4,128)(2,1)S(1)}, bf16[4,4096]{1,0:T(4,128)(2,1)S(1)}, u32[]{:S(2)}, u32[]{:S(2)}) collective-permute-start(bf16[4,4096]{1,0:T(4,128)(2,1)S(1)} %get-tuple-element.16), channel_id=1, source_target_pairs={{0,4},{4,8},{8,12},{12,0},{1,5},{5,9},{9,13},{13,1},{2,6},{6,10},{... | collective-permute-start | bytes 98312 | tf_op jit(solution)/shard_map/ppermute | solution.py:294
  26.3 5.4 %collective-permute-start.3 = (bf16[4,4096]{1,0:T(4,128)(2,1)S(1)}, bf16[4,4096]{1,0:T(4,128)(2,1)S(1)}, u32[]{:S(2)}, u32[]{:S(2)}) collective-permute-start(bf16[4,4096]{1,0:T(4,128)(2,1)S(1)} %get-tuple-element.17), channel_id=1, source_target_pairs={{0,8},{4,12},{8,0},{12,4},{1,9},{5,13},{9,1},{13,5},{2,10},{6,14},... | collective-permute-start | bytes 98312 | tf_op jit(solution)/shard_map/ppermute | solution.py:294
  28.9 3.9 %collective-permute-start.4 = (bf16[4,4096]{1,0:T(4,128)(2,1)S(1)}, bf16[4,4096]{1,0:T(4,128)(2,1)S(1)}, u32[]{:S(2)}, u32[]{:S(2)}) collective-permute-start(bf16[4,4096]{1,0:T(4,128)(2,1)S(1)} %get-tuple-element.18), channel_id=1, source_target_pairs={{0,12},{4,0},{8,4},{12,8},{1,13},{5,1},{9,5},{13,9},{2,14},{6,2},{... | collective-permute-start | bytes 98312 | tf_op jit(solution)/shard_map/ppermute | solution.py:294
  33.5 3.7 %collective-permute-start.5 = (bf16[2,4096]{1,0:T(2,128)(2,1)S(1)}, bf16[2,4096]{1,0:T(2,128)(2,1)S(1)}, u32[]{:S(2)}, u32[]{:S(2)}) collective-permute-start(bf16[2,4096]{1,0:T(2,128)(2,1)S(1)} %bitcast.11), channel_id=1, source_target_pairs={{0,2},{2,0},{1,3},{3,1},{4,6},{6,4},{5,7},{7,5},{8,10},{10,8},{9,1... | collective-permute-start | bytes 49160 | tf_op jit(solution)/shard_map/ppermute | solution.py:294

commit v3 on v2

--- a/solution.py
+++ b/solution.py
@@ -8,7 +8,9 @@
 MOST = 2
 EPS = 1e-05
 DEPTH_STEP = 512
-HELD_BYTES = 26 * 2**20
+HELD_BYTES = 21 * 2**20
+IN_FLIGHT = 4
+HALVES = 2
 MIB = 2**20
 F32 = jnp.float32
 BF16 = jnp.bfloat16
@@ -61,15 +63,20 @@
     dp = 1 + others_ref.shape[0]
     me = lax.axis_index("dp")
     section = lax.axis_index("section")
-    width = min(columns, 1024)
-
-    def copy_of(i):
+    half = columns // HALVES
+    width = min(half, 1024)
+
+    def copy_of(i, part):
+        lanes = pl.ds(part * half, half)
         return pltpu.make_async_copy(
-            weight_ref.at[pl.ds((held + i) * step, step), :], rest_ref.at[i], sems.at[i]
+            weight_ref.at[pl.ds((held + i) * step, step), lanes],
+            rest_ref.at[i, :, lanes],
+            sems.at[i, part],
         )
 
-    for i in range(rest):
-        copy_of(i).start()
+    for i in range(min(rest, IN_FLIGHT)):
+        for part in range(HALVES):
+            copy_of(i, part).start()
 
     for i in range(held + rest):
         block = slice(i * step, (i + 1) * step)
@@ -80,19 +87,26 @@
             rows_ref[i, pl.ds(first, own_rows), :] = others_ref[shift - 1, :, block]
     total_ref[...] = jnp.zeros_like(total_ref)
 
-    def add(block_ref, i):
-        for n in range(0, columns, width):
+    def add(block_ref, i, part):
+        for n in range(part * half, (part + 1) * half, width):
             total_ref[:, n : n + width] += jnp.dot(
                 rows_ref[i], block_ref[:, n : n + width], preferred_element_type=F32
             )
 
     def held_step(i, _):
-        add(held_ref.at[i], i)
+        for part in range(HALVES):
+            add(held_ref.at[i], i, part)
         return 0
 
     def rest_step(i, _):
-        copy_of(i).wait()
-        add(rest_ref.at[i], held + i)
+        for part in range(HALVES):
+            copy_of(i, part).wait()
+
+            @pl.when(i + IN_FLIGHT < rest)
+            def _():
+                copy_of(i + IN_FLIGHT, part).start()
+
+            add(rest_ref.at[i], held + i, part)
         return 0
 
     lax.fori_loop(0, held, held_step, 0)
@@ -133,9 +147,9 @@
             pltpu.VMEM((depth // step, rows, step), BF16),
             pltpu.VMEM((rows, columns), F32),
             pltpu.VMEM((rest, step, columns), BF16),
-            pltpu.SemaphoreType.DMA((rest,)),
+            pltpu.SemaphoreType.DMA((rest, HALVES)),
         ],
-        compiler_params=pltpu.CompilerParams(vmem_limit_bytes=31 * MIB),
+        compiler_params=pltpu.CompilerParams(vmem_limit_bytes=35 * MIB),
         cost_estimate=pl.CostEstimate(
             flops=2 * rows * depth * columns,
             bytes_accessed=2 * rest * step * columns,
@@ -143,6 +157,12 @@
         ),
         name="project",
     )(own, others, held, weight)
+
+
+def partner_of(me, turn, count):
+    if count & (count - 1) == 0:
+        return me ^ turn
+    return (me + turn) % count
 
 
 def pair_kernel(kept_ref, *refs):
@@ -150,7 +170,7 @@
     arrived, outs = refs[:-tensors], refs[-tensors:]
     me = lax.axis_index("tensor")
     for shift, out_ref in enumerate(outs):
-        place = lax.rem(me + shift, tensors)
+        place = partner_of(me, shift, tensors)
         block = kept_ref[0, place]
         for piece in arrived:
             block = block + piece[place].astype(F32)
@@ -196,7 +216,7 @@
     return pl.pallas_call(
         mix_kernel,
         out_shape=(
-            jax.ShapeDtypeStruct((rows, columns), BF16),
+            pltpu.VMEM((rows, columns), BF16),
             jax.ShapeDtypeStruct((slots, columns), F32),
             jax.ShapeDtypeStruct((owners - 1, slots, columns), BF16),
         ),
@@ -294,6 +314,11 @@
     return lax.ppermute(array, axis, [(i, (i + shift) % count) for i in range(count)])
 
 
+def to_partner(array, axis, turn):
+    count = lax.axis_size(axis)
+    return lax.ppermute(array, axis, [(i, partner_of(i, turn, count)) for i in range(count)])
+
+
 def body(hidden, down_matrix, residual, next_norm_scale, shrink_matrix, adapter_index):
     dp, tensors, sections = (lax.axis_size(axis) for axis in ("dp", "tensor", "section"))
     me = lax.axis_index("dp")
@@ -326,7 +351,7 @@
     kept, sent = project(*in_vmem, down_matrix, tensors, sections)
     arrived = [shifted(sent[s - 1], "section", s) for s in range(1, sections)]
     own, *sums = pair(kept, arrived)
-    arrived = [shifted(piece, "tensor", s) for s, piece in enumerate(sums, start=1)]
+    arrived = [to_partner(sums[s - 1], "tensor", s) for s in range(tensors - 1, 0, -1)]
     mixed, routed, leaving = mix(residual, places, own, arrived, local * MOST)
     arrived = [shifted(leaving[s - 1], "dp", s) for s in range(1, dp)]
     values, squares = own_half(routed, gain, shrink)

time: 38.2 us -> 37.9 us (level)
  starting transfers between devices: 9.17 us -> 8.12 us
  waiting for transfers between devices: 6.74 us -> 7.6 us
  Pallas kernels: 21.2 us -> 20.4 us
  local copies, waits for them, and re-layouts: 0.05 us -> 0.66 us
    ppermute x6 -> x3, starting transfers between devices: 9.17 us -> 3.67 us  [shifted(): lax.ppermute(array, axis, [(i, (i + shift) % count) for i in range(count)])]
    ppermute x0 -> x3, starting transfers between devices: none -> 4.45 us  [to_partner(): lax.ppermute(array, axis, [(i, partner_of(i, turn, count)) for i in range...]
    ppermute x0 -> x3, waiting for transfers between devices: none -> 4.03 us  [to_partner(): lax.ppermute(array, axis, [(i, partner_of(i, turn, count)) for i in range...]
    ppermute x6 -> x3, waiting for transfers between devices: 6.74 us -> 3.57 us  [shifted(): lax.ppermute(array, axis, [(i, (i + shift) % count) for i in range(count)])]
    pallas_call x1, Pallas kernels: 8.29 us -> 7.09 us  [fetch(): pl.pallas_call(fetch_kernel, out_shape=pltpu.VMEM((count, step, columns),...]
    pallas_call x1, Pallas kernels: 11.1 us -> 12.1 us  [project(): pl.pallas_call(project_kernel, out_shape=(pltpu.VMEM((1, tensors, block_r...]
    unnamed x10 -> x11, local copies, waits for them, and re-layouts: 0.03 us -> 0.64 us
    pallas_call x1, Pallas kernels: 0.65 us -> 0.13 us  [mix(): pl.pallas_call(mix_kernel, out_shape=(pltpu.VMEM((rows, columns), BF16),...]
  transfers between devices with their start and end apart: 6 -> 6, of which waited for: 5 -> 4; matrix products, arithmetic and copies ran while one was open for 1% -> 2% of each run, Pallas kernels for 22% -> 19%
where the time goes in v3:
time: 37.9 us; the launch traced here: 37.7 us
  Pallas kernels  20.4 us (54%)
  starting transfers between devices  8.12 us (21%)
  waiting for transfers between devices  7.6 us (20%)
  between operations  0.73 us (2%)
  local copies, waits for them, and re-layouts  0.66 us (2%)
    pallas_call x1, Pallas kernels, project(): pl.pallas_call(project_kernel, out_shape=(pltpu.VMEM((1, tensors, block_r...  12.1 us
    pallas_call x1, Pallas kernels, fetch(): pl.pallas_call(fetch_kernel, out_shape=pltpu.VMEM((count, step, columns),...  7.09 us
    ppermute x3, starting transfers between devices, to_partner(): lax.ppermute(array, axis, [(i, partner_of(i, turn, count)) for i in range...  4.45 us
    ppermute x3, waiting for transfers between devices, to_partner(): lax.ppermute(array, axis, [(i, partner_of(i, turn, count)) for i in range...  4.03 us
    ppermute x3, starting transfers between devices, shifted(): lax.ppermute(array, axis, [(i, (i + shift) % count) for i in range(count)])  3.67 us
    ppermute x3, waiting for transfers between devices, shifted(): lax.ppermute(array, axis, [(i, (i + shift) % count) for i in range(count)])  3.57 us
    pallas_call x1, Pallas kernels, finish(): pl.pallas_call(finish_kernel, out_shape=jax.ShapeDtypeStruct((local, 1, M...  0.84 us
  transfers between devices with their start and end apart: 6, of which 4 were waited for; matrix products, arithmetic and copies ran while one was open for 2% of the time, Pallas kernels for 19%

profile of v3, /device:TPU:0, one launch (start us, length us, event | category | flops | bytes accessed | tf_op | source)
XLA Modules:
  0.0 37.7 jit_solution(4593895209406887736)
XLA Ops:
  0.6 0.0 copy-start.1
  0.6 0.0 copy-start.4
  0.6 3.0 %collective-permute-start = (bf16[16,6656]{1,0:T(8,128)(2,1)}, bf16[16,6656]{1,0:T(8,128)(2,1)S(1)}, u32[]{:S(2)}, u32[]{:S(2)}) collective-permute-start(bf16[16,6656]{1,0:T(8,128)(2,1)} %own_ref.1), channel_id=1, source_target_pairs={{0,2},{2,0},{1,3},{3,1},{4,6},{6,4},{5,7},{7,5},{8,10},{10,8},{9,1... | collective-permute-start | bytes 638984 | tf_op jit(solution)/shard_map/ppermute | solution.py:314
  3.7 7.1 %fetch.1.held_ref = bf16[5,512,4096]{2,1,0:T(8,128)(2,1)S(1)} custom-call(bf16[6656,4096]{1,0:T(8,128)(2,1)} %weight_ref.3), custom_call_target="tpu_custom_call" | custom-call | bytes 20971520 | tf_op jit(solution)/shard_map/fetch/pallas_call | solution.py:43
  10.8 0.0 copy-start.2
  10.8 0.0 copy-start.3
  10.8 0.0 copy-start
  10.8 0.0 copy-done.4
  10.8 0.1 convert_reduce_fusion
  10.9 0.0 collective-permute-done
  10.9 0.0 copy-done.1
  10.9 12.1 %project.1 = (f32[1,4,4,4096]{3,2,1,0:T(4,128)S(1)}, bf16[1,4,4,4096]{3,2,1,0:T(4,128)(2,1)S(1)}) custom-call(bf16[16,6656]{1,0:T(8,128)(2,1)S(1)} %copy-done.1, bf16[1,16,6656]{2,1,0:T(8,128)(2,1)S(1)} %bitcast.8, bf16[5,512,4096]{2,1,0:T(8,128)(2,1)S(1)} %fetch.1.held_ref, bf16[6656,4096]{1,0:T(8,128)(2,1)} %weight_ref.3), custom_call_target="tpu_custom_call" | custom-call | flops 1744830464 | bytes 33554432 | tf_op jit(solution)/shard_map/project/pallas_call | solution.py:138
  23.0 0.1 collective-permute-start.1
  23.1 0.1 iota_compare_fusion.1
  23.1 1.3 %collective-permute-done.1.refs_0_ = bf16[4,4,4096]{2,1,0:T(4,128)(2,1)S(1)} collective-permute-done((bf16[4,4,4096]{2,1,0:T(4,128)(2,1)S(1)}, bf16[4,4,4096]{2,1,0:T(4,128)(2,1)S(1)}, u32[]{:S(2)}, u32[]{:S(2)}) %collective-permute-start.1) | collective-permute-done | bytes 131104 | tf_op jit(solution)/shard_map/ppermute | solution.py:314
  24.5 3.7 %collective-permute-start.2 = (bf16[4,4096]{1,0:T(4,128)(2,1)S(1)}, bf16[4,4096]{1,0:T(4,128)(2,1)S(1)}, u32[]{:S(2)}, u32[]{:S(2)}) collective-permute-start(bf16[4,4096]{1,0:T(4,128)(2,1)S(1)} %get-tuple-element.16), channel_id=1, source_target_pairs={{0,12},{4,8},{8,4},{12,0},{1,13},{5,9},{9,5},{13,1},{2,14},{6,10},... | collective-permute-start | bytes 98312 | tf_op jit(solution)/shard_map/ppermute | solution.py:319
  28.1 0.0 collective-permute-start.3
  28.1 0.8 %collective-permute-start.4 = (bf16[4,4096]{1,0:T(4,128)(2,1)S(1)}, bf16[4,4096]{1,0:T(4,128)(2,1)S(1)}, u32[]{:S(2)}, u32[]{:S(2)}) collective-permute-start(bf16[4,4096]{1,0:T(4,128)(2,1)S(1)} %get-tuple-element.18), channel_id=1, source_target_pairs={{0,4},{4,0},{8,12},{12,8},{1,5},{5,1},{9,13},{13,9},{2,6},{6,2},{1... | collective-permute-start | bytes 98312 | tf_op jit(solution)/shard_map/ppermute | solution.py:319
  28.9 1.3 %collective-permute-done.2.refs_0_ = bf16[4,4096]{1,0:T(4,128)(2,1)S(1)} collective-permute-done((bf16[4,4096]{1,0:T(4,128)(2,1)S(1)}, bf16[4,4096]{1,0:T(4,128)(2,1)S(1)}, u32[]{:S(2)}, u32[]{:S(2)}) %collective-permute-start.2) | collective-permute-done | bytes 32800 | tf_op jit(solution)/shard_map/ppermute | solution.py:319
  30.2 2.7 %collective-permute-done.3.refs_1_ = bf16[4,4096]{1,0:T(4,128)(2,1)S(1)} collective-permute-done((bf16[4,4096]{1,0:T(4,128)(2,1)S(1)}, bf16[4,4096]{1,0:T(4,128)(2,1)S(1)}, u32[]{:S(2)}, u32[]{:S(2)}) %collective-permute-start.3) | collective-permute-done | bytes 32800 | tf_op jit(solution)/shard_map/ppermute | solution.py:319
  32.9 0.0 collective-permute-done.4.refs_2_
  32.9 0.0 copy-done.2
  32.9 0.1 mix.1
  33.1 0.6 %collective-permute-start.5 = (bf16[2,4096]{1,0:T(2,128)(2,1)S(1)}, bf16[2,4096]{1,0:T(2,128)(2,1)S(1)}, u32[]{:S(2)}, u32[]{:S(2)}) collective-permute-start(bf16[2,4096]{1,0:T(2,128)(2,1)S(1)} %bitcast.11), channel_id=1, source_target_pairs={{0,2},{2,0},{1,3},{3,1},{4,6},{6,4},{5,7},{7,5},{8,10},{10,8},{9,1... | collective-permute-start | bytes 49160 | tf_op jit(solution)/shard_map/ppermute | solution.py:314
  33.7 0.0 copy-done.3
  33.7 0.6 %copy.8 = bf16[4,4096]{1,0:T(4,128)(2,1)} copy(bf16[4,4096]{1,0:T(4,128)(2,1)S(1)} %get-tuple-element.26) | data formatting | bytes 65536
  34.3 0.0 copy-done
  34.3 0.3 own_half.1
  34.6 2.3 %collective-permute-done.5.refs_0_ = bf16[2,4096]{1,0:T(2,128)(2,1)S(1)} collective-permute-done((bf16[2,4096]{1,0:T(2,128)(2,1)S(1)}, bf16[2,4096]{1,0:T(2,128)(2,1)S(1)}, u32[]{:S(2)}, u32[]{:S(2)}) %collective-permute-start.5) | collective-permute-done | bytes 16416 | tf_op jit(solution)/shard_map/ppermute | solution.py:314
  36.9 0.8 %finish.1 = f32[1,1,2,64]{3,2,1,0:T(2,128)} custom-call(f32[2,64]{1,0:T(2,128)S(1)} %get-tuple-element.21.values_ref, f32[2,64]{1,0:T(2,128)S(1)} %get-tuple-element.22.squares_ref, bf16[1,8192]{1,0:T(2,128)(2,1)S(1)} %broadcast_in_dim.2.gain_ref, bf16[1,64,8192]{2,1,0:T(8,128)(2,1)S(1)} %bitcast.7, bf16[2,4096]{1,0:T(2,128)(2,1)S(1)} %collective-permute-done.5.refs_0_), custom_call_target="tpu_custom_call" | custom-call | tf_op jit(solution)/shard_map/finish/pallas_call | solution.py:302
  (4 shorter events, 0.1 us)
Async XLA Ops:
  0.6 10.3 %copy-start.1 = (bf16[16,6656]{1,0:T(8,128)(2,1)S(1)}, bf16[16,6656]{1,0:T(8,128)(2,1)}, u32[]{:S(2)}) copy-start(bf16[16,6656]{1,0:T(8,128)(2,1)} %own_ref.1) | copy-start | bytes 638980
  0.6 10.2 %copy-start.4 = (s32[4,1]{0,1:T(1,128)S(1)}, s32[4,1]{0,1:T(1,128)}, u32[]{:S(2)}) copy-start(s32[4,1]{0,1:T(1,128)} %param.11) | copy-start | bytes 52
  0.6 10.3 %collective-permute-start = (bf16[16,6656]{1,0:T(8,128)(2,1)}, bf16[16,6656]{1,0:T(8,128)(2,1)S(1)}, u32[]{:S(2)}, u32[]{:S(2)}) collective-permute-start(bf16[16,6656]{1,0:T(8,128)(2,1)} %own_ref.1), channel_id=1, source_target_pairs={{0,2},{2,0},{1,3},{3,1},{4,6},{6,4},{5,7},{7,5},{8,10},{10,8},{9,1... | collective-permute-start | bytes 638984 | tf_op jit(solution)/shard_map/ppermute | solution.py:314
  10.8 22.2 %copy-start.2 = (bf16[4,4096]{1,0:T(4,128)(2,1)S(1)}, bf16[4,4096]{1,0:T(4,128)(2,1)}, u32[]{:S(2)}) copy-start(bf16[4,4096]{1,0:T(4,128)(2,1)} %residual_ref.1) | copy-start | bytes 98308
  10.8 22.9 %copy-start.3 = (bf16[8192]{0:T(1024)(128)(2,1)S(1)}, bf16[8192]{0:T(1024)(128)(2,1)}, u32[]{:S(2)}) copy-start(bf16[8192]{0:T(1024)(128)(2,1)} %param.9) | copy-start | bytes 49156
  10.8 23.6 %copy-start = (bf16[1,8192,64]{1,2,0:T(8,128)(2,1)S(1)}, bf16[1,8192,64]{1,2,0:T(8,128)(2,1)}, u32[]{:S(2)}) copy-start(bf16[1,8192,64]{1,2,0:T(8,128)(2,1)} %param.10) | copy-start | bytes 3145732
  23.0 1.4 %collective-permute-start.1 = (bf16[4,4,4096]{2,1,0:T(4,128)(2,1)S(1)}, bf16[4,4,4096]{2,1,0:T(4,128)(2,1)S(1)}, u32[]{:S(2)}, u32[]{:S(2)}) collective-permute-start(bf16[4,4,4096]{2,1,0:T(4,128)(2,1)S(1)} %bitcast.10), channel_id=1, source_target_pairs={{0,1},{1,0},{2,3},{3,2},{4,5},{5,4},{6,7},{7,6},{8,9},{9,8},{10,11... | collective-permute-start | bytes 393224 | tf_op jit(solution)/shard_map/ppermute | solution.py:314
  24.5 5.8 %collective-permute-start.2 = (bf16[4,4096]{1,0:T(4,128)(2,1)S(1)}, bf16[4,4096]{1,0:T(4,128)(2,1)S(1)}, u32[]{:S(2)}, u32[]{:S(2)}) collective-permute-start(bf16[4,4096]{1,0:T(4,128)(2,1)S(1)} %get-tuple-element.16), channel_id=1, source_target_pairs={{0,12},{4,8},{8,4},{12,0},{1,13},{5,9},{9,5},{13,1},{2,14},{6,10},... | collective-permute-start | bytes 98312 | tf_op jit(solution)/shard_map/ppermute | solution.py:319
  28.1 4.8 %collective-permute-start.3 = (bf16[4,4096]{1,0:T(4,128)(2,1)S(1)}, bf16[4,4096]{1,0:T(4,128)(2,1)S(1)}, u32[]{:S(2)}, u32[]{:S(2)}) collective-permute-start(bf16[4,4096]{1,0:T(4,128)(2,1)S(1)} %get-tuple-element.17), channel_id=1, source_target_pairs={{0,8},{4,12},{8,0},{12,4},{1,9},{5,13},{9,1},{13,5},{2,10},{6,14},... | collective-permute-start | bytes 98312 | tf_op jit(solution)/shard_map/ppermute | solution.py:319
  28.1 4.8 %collective-permute-start.4 = (bf16[4,4096]{1,0:T(4,128)(2,1)S(1)}, bf16[4,4096]{1,0:T(4,128)(2,1)S(1)}, u32[]{:S(2)}, u32[]{:S(2)}) collective-permute-start(bf16[4,4096]{1,0:T(4,128)(2,1)S(1)} %get-tuple-element.18), channel_id=1, source_target_pairs={{0,4},{4,0},{8,12},{12,8},{1,5},{5,1},{9,13},{13,9},{2,6},{6,2},{1... | collective-permute-start | bytes 98312 | tf_op jit(solution)/shard_map/ppermute | solution.py:319
  33.1 3.8 %collective-permute-start.5 = (bf16[2,4096]{1,0:T(2,128)(2,1)S(1)}, bf16[2,4096]{1,0:T(2,128)(2,1)S(1)}, u32[]{:S(2)}, u32[]{:S(2)}) collective-permute-start(bf16[2,4096]{1,0:T(2,128)(2,1)S(1)} %bitcast.11), channel_id=1, source_target_pairs={{0,2},{2,0},{1,3},{3,1},{4,6},{6,4},{5,7},{7,5},{8,10},{10,8},{9,1... | collective-permute-start | bytes 49160 | tf_op jit(solution)/shard_map/ppermute | solution.py:314

commit v4 on v3

--- a/solution.py
+++ b/solution.py
@@ -22,36 +22,6 @@
 
 def step_of(depth):
     return max(s for s in range(16, DEPTH_STEP + 1, 16) if depth % s == 0)
-
-
-def fetch_kernel(weight_ref, held_ref, sems):
-    count, step, _ = held_ref.shape
-    copies = [
-        pltpu.make_async_copy(
-            weight_ref.at[pl.ds(i * step, step), :], held_ref.at[i], sems.at[i]
-        )
-        for i in range(count)
-    ]
-    for copy in copies:
-        copy.start()
-    for copy in copies:
-        copy.wait()
-
-
-def fetch(weight, count, step):
-    columns = weight.shape[1]
-    return pl.pallas_call(
-        fetch_kernel,
-        out_shape=pltpu.VMEM((count, step, columns), weight.dtype),
-        in_specs=[pl.BlockSpec(memory_space=pl.ANY)],
-        out_specs=whole(),
-        scratch_shapes=[pltpu.SemaphoreType.DMA((count,))],
-        compiler_params=pltpu.CompilerParams(vmem_limit_bytes=1 * MIB),
-        cost_estimate=pl.CostEstimate(
-            flops=0, bytes_accessed=2 * count * step * columns, transcendentals=0
-        ),
-        name="fetch",
-    )(weight)
 
 
 def project_kernel(
@@ -330,7 +300,8 @@
     step = step_of(depth)
     blocks = depth // step
     held_count = max(1, min(blocks // 2, HELD_BYTES // (2 * step * down_matrix.shape[1])))
-    held = fetch(down_matrix, held_count, step)
+    held = lax.slice_in_dim(down_matrix, 0, held_count * step)
+    held = held.reshape(held_count, step, -1)
 
     row_adapter = adapter_index[:, 0]
     same = row_adapter[:, None] == row_adapter[None, :]

time: 37.9 us -> 42.9 us (1.13)
  local copies, waits for them, and re-layouts: 0.66 us -> 12 us
  Pallas kernels: 20.4 us -> 13.4 us
  other arithmetic: 0.18 us -> 0.91 us
    slice x0 -> x1, local copies, waits for them, and re-layouts: none -> 10.5 us  [body(): held = lax.slice_in_dim(down_matrix, 0, held_count * step)]
    pallas_call x1 -> x0, Pallas kernels: 7.09 us -> none  [fetch(): pl.pallas_call(fetch_kernel, out_shape=pltpu.VMEM((count, step, columns),...]
    unnamed x11, local copies, waits for them, and re-layouts: 0.64 us -> 1.56 us
    reduce_sum x1, other arithmetic: 0.09 us -> 0.82 us  [body(): rank_of = jnp.sum(jnp.logical_and(same, earlier), axis=0)]
  transfers between devices with their start and end apart: 6 -> 6, of which waited for: 4 -> 4; matrix products, arithmetic and copies ran while one was open for 2% -> 28% of each run, Pallas kernels for 19% -> 1%
where the time goes in v4:
time: 42.9 us; the launch traced here: 42.7 us
  Pallas kernels  13.4 us (31%)
  local copies, waits for them, and re-layouts  12 us (28%)
  starting transfers between devices  8.13 us (19%)
  waiting for transfers between devices  7.57 us (18%)
  other arithmetic  0.91 us (2%)
  between operations  0.7 us (2%)
    pallas_call x1, Pallas kernels, project(): pl.pallas_call(project_kernel, out_shape=(pltpu.VMEM((1, tensors, block_r...  12.1 us
    slice x1, local copies, waits for them, and re-layouts, body(): held = lax.slice_in_dim(down_matrix, 0, held_count * step)  10.5 us
    ppermute x3, starting transfers between devices, to_partner(): lax.ppermute(array, axis, [(i, partner_of(i, turn, count)) for i in range...  4.45 us
    ppermute x3, waiting for transfers between devices, to_partner(): lax.ppermute(array, axis, [(i, partner_of(i, turn, count)) for i in range...  4.02 us
    ppermute x3, starting transfers between devices, shifted(): lax.ppermute(array, axis, [(i, (i + shift) % count) for i in range(count)])  3.68 us
    ppermute x3, waiting for transfers between devices, shifted(): lax.ppermute(array, axis, [(i, (i + shift) % count) for i in range(count)])  3.55 us
    unnamed x11, local copies, waits for them, and re-layouts  1.56 us
  transfers between devices with their start and end apart: 6, of which 4 were waited for; matrix products, arithmetic and copies ran while one was open for 28% of the time, Pallas kernels for 1%

profile of v4, /device:TPU:0, one launch (start us, length us, event | category | flops | bytes accessed | tf_op | source)
XLA Modules:
  0.0 42.7 jit_solution(15506313834029969793)
XLA Ops:
  0.6 3.0 %collective-permute-start = (bf16[16,6656]{1,0:T(8,128)(2,1)}, bf16[16,6656]{1,0:T(8,128)(2,1)S(1)}, u32[]{:S(2)}, u32[]{:S(2)}) collective-permute-start(bf16[16,6656]{1,0:T(8,128)(2,1)} %own_ref.1), channel_id=1, source_target_pairs={{0,2},{2,0},{1,3},{3,1},{4,6},{6,4},{5,7},{7,5},{8,10},{10,8},{9,1... | collective-permute-start | bytes 638984 | tf_op jit(solution)/shard_map/ppermute | solution.py:284
  3.6 0.0 copy-start.4
  3.6 0.0 copy-start.2
  3.6 0.0 copy-start.3
  3.6 0.0 copy-start
  3.6 10.5 %slice.3 = bf16[2560,4096]{1,0:T(8,128)(2,1)S(1)} slice(bf16[6656,4096]{1,0:T(8,128)(2,1)} %weight_ref.1), slice={[0:2560], [0:4096]} | slice | bytes 41943040 | tf_op jit(solution)/shard_map/slice | solution.py:303
  14.1 0.8 %convert_reduce_fusion = s32[4]{0:T(128)S(1)} fusion(s32[4]{0:T(128)} %bitcast.14), kind=kLoop, calls=%fused_computation.3 | loop fusion | flops 76 | bytes 32 | tf_op jit(solution)/shard_map/reduce_sum | solution.py:310
  15.0 0.0 collective-permute-done
  15.0 0.0 copy-start.1
  15.0 0.9 %copy-done.1 = bf16[16,6656]{1,0:T(8,128)(2,1)S(1)} copy-done((bf16[16,6656]{1,0:T(8,128)(2,1)S(1)}, bf16[16,6656]{1,0:T(8,128)(2,1)}, u32[]{:S(2)}) %copy-start.1) | copy-done | bytes 213016
  15.9 12.1 %project.1 = (f32[1,4,4,4096]{3,2,1,0:T(4,128)S(1)}, bf16[1,4,4,4096]{3,2,1,0:T(4,128)(2,1)S(1)}) custom-call(bf16[16,6656]{1,0:T(8,128)(2,1)S(1)} %copy-done.1, bf16[1,16,6656]{2,1,0:T(8,128)(2,1)S(1)} %bitcast.10, bf16[5,512,4096]{2,1,0:T(8,128)(2,1)S(1)} %bitcast.7, bf16[6656,4096]{1,0:T(8,128)(2,1)} %weight_ref.1), custom_call_target="tpu_custom_call" | custom-call | flops 1744830464 | bytes 33554432 | tf_op jit(solution)/shard_map/project/pallas_call | solution.py:108
  28.0 0.1 collective-permute-start.1
  28.1 0.0 copy-done.4
  28.1 0.1 iota_compare_fusion.1
  28.1 1.2 %collective-permute-done.1.refs_0_ = bf16[4,4,4096]{2,1,0:T(4,128)(2,1)S(1)} collective-permute-done((bf16[4,4,4096]{2,1,0:T(4,128)(2,1)S(1)}, bf16[4,4,4096]{2,1,0:T(4,128)(2,1)S(1)}, u32[]{:S(2)}, u32[]{:S(2)}) %collective-permute-start.1) | collective-permute-done | bytes 131104 | tf_op jit(solution)/shard_map/ppermute | solution.py:284
  29.4 0.1 pair.1
  29.4 3.7 %collective-permute-start.2 = (bf16[4,4096]{1,0:T(4,128)(2,1)S(1)}, bf16[4,4096]{1,0:T(4,128)(2,1)S(1)}, u32[]{:S(2)}, u32[]{:S(2)}) collective-permute-start(bf16[4,4096]{1,0:T(4,128)(2,1)S(1)} %get-tuple-element.16), channel_id=1, source_target_pairs={{0,12},{4,8},{8,4},{12,0},{1,13},{5,9},{9,5},{13,1},{2,14},{6,10},... | collective-permute-start | bytes 98312 | tf_op jit(solution)/shard_map/ppermute | solution.py:289
  33.1 0.0 collective-permute-start.3
  33.1 0.8 %collective-permute-start.4 = (bf16[4,4096]{1,0:T(4,128)(2,1)S(1)}, bf16[4,4096]{1,0:T(4,128)(2,1)S(1)}, u32[]{:S(2)}, u32[]{:S(2)}) collective-permute-start(bf16[4,4096]{1,0:T(4,128)(2,1)S(1)} %get-tuple-element.18), channel_id=1, source_target_pairs={{0,4},{4,0},{8,12},{12,8},{1,5},{5,1},{9,13},{13,9},{2,6},{6,2},{1... | collective-permute-start | bytes 98312 | tf_op jit(solution)/shard_map/ppermute | solution.py:289
  33.9 1.3 %collective-permute-done.2.refs_0_ = bf16[4,4096]{1,0:T(4,128)(2,1)S(1)} collective-permute-done((bf16[4,4096]{1,0:T(4,128)(2,1)S(1)}, bf16[4,4096]{1,0:T(4,128)(2,1)S(1)}, u32[]{:S(2)}, u32[]{:S(2)}) %collective-permute-start.2) | collective-permute-done | bytes 32800 | tf_op jit(solution)/shard_map/ppermute | solution.py:289
  35.2 2.7 %collective-permute-done.3.refs_1_ = bf16[4,4096]{1,0:T(4,128)(2,1)S(1)} collective-permute-done((bf16[4,4096]{1,0:T(4,128)(2,1)S(1)}, bf16[4,4096]{1,0:T(4,128)(2,1)S(1)}, u32[]{:S(2)}, u32[]{:S(2)}) %collective-permute-start.3) | collective-permute-done | bytes 32800 | tf_op jit(solution)/shard_map/ppermute | solution.py:289
  37.9 0.0 collective-permute-done.4.refs_2_
  37.9 0.0 copy-done.2
  37.9 0.1 mix.1
  38.1 0.6 %collective-permute-start.5 = (bf16[2,4096]{1,0:T(2,128)(2,1)S(1)}, bf16[2,4096]{1,0:T(2,128)(2,1)S(1)}, u32[]{:S(2)}, u32[]{:S(2)}) collective-permute-start(bf16[2,4096]{1,0:T(2,128)(2,1)S(1)} %bitcast.13), channel_id=1, source_target_pairs={{0,2},{2,0},{1,3},{3,1},{4,6},{6,4},{5,7},{7,5},{8,10},{10,8},{9,1... | collective-permute-start | bytes 49160 | tf_op jit(solution)/shard_map/ppermute | solution.py:284
  38.7 0.0 copy-done.3
  38.7 0.6 %copy.8 = bf16[4,4096]{1,0:T(4,128)(2,1)} copy(bf16[4,4096]{1,0:T(4,128)(2,1)S(1)} %get-tuple-element.26) | data formatting | bytes 65536
  39.3 0.0 copy-done
  39.3 0.3 own_half.1
  39.6 2.3 %collective-permute-done.5.refs_0_ = bf16[2,4096]{1,0:T(2,128)(2,1)S(1)} collective-permute-done((bf16[2,4096]{1,0:T(2,128)(2,1)S(1)}, bf16[2,4096]{1,0:T(2,128)(2,1)S(1)}, u32[]{:S(2)}, u32[]{:S(2)}) %collective-permute-start.5) | collective-permute-done | bytes 16416 | tf_op jit(solution)/shard_map/ppermute | solution.py:284
  41.9 0.8 %finish.1 = f32[1,1,2,64]{3,2,1,0:T(2,128)} custom-call(f32[2,64]{1,0:T(2,128)S(1)} %get-tuple-element.21.values_ref, f32[2,64]{1,0:T(2,128)S(1)} %get-tuple-element.22.squares_ref, bf16[1,8192]{1,0:T(2,128)(2,1)S(1)} %broadcast_in_dim.2.gain_ref, bf16[1,64,8192]{2,1,0:T(8,128)(2,1)S(1)} %bitcast.9, bf16[2,4096]{1,0:T(2,128)(2,1)S(1)} %collective-permute-done.5.refs_0_), custom_call_target="tpu_custom_call" | custom-call | tf_op jit(solution)/shard_map/finish/pallas_call | solution.py:272
  (3 shorter events, 0.0 us)
Async XLA Ops:
  0.6 14.3 %collective-permute-start = (bf16[16,6656]{1,0:T(8,128)(2,1)}, bf16[16,6656]{1,0:T(8,128)(2,1)S(1)}, u32[]{:S(2)}, u32[]{:S(2)}) collective-permute-start(bf16[16,6656]{1,0:T(8,128)(2,1)} %own_ref.1), channel_id=1, source_target_pairs={{0,2},{2,0},{1,3},{3,1},{4,6},{6,4},{5,7},{7,5},{8,10},{10,8},{9,1... | collective-permute-start | bytes 638984 | tf_op jit(solution)/shard_map/ppermute | solution.py:284
  3.6 24.4 %copy-start.4 = (s32[4,1]{0,1:T(1,128)S(1)}, s32[4,1]{0,1:T(1,128)}, u32[]{:S(2)}) copy-start(s32[4,1]{0,1:T(1,128)} %param.11) | copy-start | bytes 52
  3.6 34.3 %copy-start.2 = (bf16[4,4096]{1,0:T(4,128)(2,1)S(1)}, bf16[4,4096]{1,0:T(4,128)(2,1)}, u32[]{:S(2)}) copy-start(bf16[4,4096]{1,0:T(4,128)(2,1)} %residual_ref.1) | copy-start | bytes 98308
  3.6 35.0 %copy-start.3 = (bf16[8192]{0:T(1024)(128)(2,1)S(1)}, bf16[8192]{0:T(1024)(128)(2,1)}, u32[]{:S(2)}) copy-start(bf16[8192]{0:T(1024)(128)(2,1)} %param.9) | copy-start | bytes 49156
  3.6 35.7 %copy-start = (bf16[1,8192,64]{1,2,0:T(8,128)(2,1)S(1)}, bf16[1,8192,64]{1,2,0:T(8,128)(2,1)}, u32[]{:S(2)}) copy-start(bf16[1,8192,64]{1,2,0:T(8,128)(2,1)} %param.10) | copy-start | bytes 3145732
  15.0 0.9 %copy-start.1 = (bf16[16,6656]{1,0:T(8,128)(2,1)S(1)}, bf16[16,6656]{1,0:T(8,128)(2,1)}, u32[]{:S(2)}) copy-start(bf16[16,6656]{1,0:T(8,128)(2,1)} %own_ref.1) | copy-start | bytes 638980
  28.0 1.4 %collective-permute-start.1 = (bf16[4,4,4096]{2,1,0:T(4,128)(2,1)S(1)}, bf16[4,4,4096]{2,1,0:T(4,128)(2,1)S(1)}, u32[]{:S(2)}, u32[]{:S(2)}) collective-permute-start(bf16[4,4,4096]{2,1,0:T(4,128)(2,1)S(1)} %bitcast.12), channel_id=1, source_target_pairs={{0,1},{1,0},{2,3},{3,2},{4,5},{5,4},{6,7},{7,6},{8,9},{9,8},{10,11... | collective-permute-start | bytes 393224 | tf_op jit(solution)/shard_map/ppermute | solution.py:284
  29.4 5.8 %collective-permute-start.2 = (bf16[4,4096]{1,0:T(4,128)(2,1)S(1)}, bf16[4,4096]{1,0:T(4,128)(2,1)S(1)}, u32[]{:S(2)}, u32[]{:S(2)}) collective-permute-start(bf16[4,4096]{1,0:T(4,128)(2,1)S(1)} %get-tuple-element.16), channel_id=1, source_target_pairs={{0,12},{4,8},{8,4},{12,0},{1,13},{5,9},{9,5},{13,1},{2,14},{6,10},... | collective-permute-start | bytes 98312 | tf_op jit(solution)/shard_map/ppermute | solution.py:289
  33.1 4.8 %collective-permute-start.3 = (bf16[4,4096]{1,0:T(4,128)(2,1)S(1)}, bf16[4,4096]{1,0:T(4,128)(2,1)S(1)}, u32[]{:S(2)}, u32[]{:S(2)}) collective-permute-start(bf16[4,4096]{1,0:T(4,128)(2,1)S(1)} %get-tuple-element.17), channel_id=1, source_target_pairs={{0,8},{4,12},{8,0},{12,4},{1,9},{5,13},{9,1},{13,5},{2,10},{6,14},... | collective-permute-start | bytes 98312 | tf_op jit(solution)/shard_map/ppermute | solution.py:289
  33.1 4.8 %collective-permute-start.4 = (bf16[4,4096]{1,0:T(4,128)(2,1)S(1)}, bf16[4,4096]{1,0:T(4,128)(2,1)S(1)}, u32[]{:S(2)}, u32[]{:S(2)}) collective-permute-start(bf16[4,4096]{1,0:T(4,128)(2,1)S(1)} %get-tuple-element.18), channel_id=1, source_target_pairs={{0,4},{4,0},{8,12},{12,8},{1,5},{5,1},{9,13},{13,9},{2,6},{6,2},{1... | collective-permute-start | bytes 98312 | tf_op jit(solution)/shard_map/ppermute | solution.py:289
  38.1 3.8 %collective-permute-start.5 = (bf16[2,4096]{1,0:T(2,128)(2,1)S(1)}, bf16[2,4096]{1,0:T(2,128)(2,1)S(1)}, u32[]{:S(2)}, u32[]{:S(2)}) collective-permute-start(bf16[2,4096]{1,0:T(2,128)(2,1)S(1)} %bitcast.13), channel_id=1, source_target_pairs={{0,2},{2,0},{1,3},{3,1},{4,6},{6,4},{5,7},{7,5},{8,10},{10,8},{9,1... | collective-permute-start | bytes 49160 | tf_op jit(solution)/shard_map/ppermute | solution.py:284

commit v5 on v3

--- a/solution.py
+++ b/solution.py
@@ -1,3 +1,5 @@
+import functools
+
 import jax
 import jax.numpy as jnp
 from jax import lax
@@ -10,7 +12,7 @@
 DEPTH_STEP = 512
 HELD_BYTES = 21 * 2**20
 IN_FLIGHT = 4
-HALVES = 2
+PIECES = 4
 MIB = 2**20
 F32 = jnp.float32
 BF16 = jnp.bfloat16
@@ -54,20 +56,43 @@
     )(weight)
 
 
+def exchange_order(own_rows, dp, tensors, sections):
+    rows = own_rows * dp
+    block_rows = rows // (tensors * sections)
+    me, tensor, section = (lax.axis_index(axis) for axis in ("dp", "tensor", "section"))
+    target = lax.broadcasted_iota(jnp.int32, (rows, rows), 0)
+    source = lax.broadcasted_iota(jnp.int32, (rows, rows), 1)
+    s = (section + target // (tensors * block_rows)) % sections
+    t = partner_of(tensor, target // block_rows % tensors, tensors)
+    wanted = (t * sections + s) * block_rows + target % block_rows
+    owner = (me + dp - source // own_rows) % dp
+    return (wanted == owner * own_rows + source % own_rows).astype(BF16)
+
+
 def project_kernel(
-    own_ref, others_ref, held_ref, weight_ref, kept_ref, sent_ref, rows_ref, total_ref, rest_ref, sems
+    own_ref,
+    others_ref,
+    held_ref,
+    weight_ref,
+    kept_ref,
+    sent_ref,
+    rows_ref,
+    total_ref,
+    rest_ref,
+    sems,
+    *,
+    tensors,
+    sections,
 ):
     held, step, columns = held_ref.shape
     rest = rest_ref.shape[0]
     own_rows = own_ref.shape[0]
     dp = 1 + others_ref.shape[0]
-    me = lax.axis_index("dp")
-    section = lax.axis_index("section")
-    half = columns // HALVES
-    width = min(half, 1024)
+    piece = columns // PIECES
+    width = min(piece, 1024)
 
     def copy_of(i, part):
-        lanes = pl.ds(part * half, half)
+        lanes = pl.ds(part * piece, piece)
         return pltpu.make_async_copy(
             weight_ref.at[pl.ds((held + i) * step, step), lanes],
             rest_ref.at[i, :, lanes],
@@ -75,31 +100,31 @@
         )
 
     for i in range(min(rest, IN_FLIGHT)):
-        for part in range(HALVES):
+        for part in range(PIECES):
             copy_of(i, part).start()
 
+    order = exchange_order(own_rows, dp, tensors, sections)
     for i in range(held + rest):
         block = slice(i * step, (i + 1) * step)
-        own_first = pl.multiple_of(me * own_rows, own_rows)
-        rows_ref[i, pl.ds(own_first, own_rows), :] = own_ref[:, block]
-        for shift in range(1, dp):
-            first = pl.multiple_of(lax.rem(me + dp - shift, dp) * own_rows, own_rows)
-            rows_ref[i, pl.ds(first, own_rows), :] = others_ref[shift - 1, :, block]
+        stacked = [own_ref[:, block]] + [others_ref[k, :, block] for k in range(dp - 1)]
+        rows_ref[i] = jnp.dot(
+            order, jnp.concatenate(stacked, axis=0), preferred_element_type=F32
+        ).astype(BF16)
     total_ref[...] = jnp.zeros_like(total_ref)
 
     def add(block_ref, i, part):
-        for n in range(part * half, (part + 1) * half, width):
+        for n in range(part * piece, (part + 1) * piece, width):
             total_ref[:, n : n + width] += jnp.dot(
                 rows_ref[i], block_ref[:, n : n + width], preferred_element_type=F32
             )
 
     def held_step(i, _):
-        for part in range(HALVES):
+        for part in range(PIECES):
             add(held_ref.at[i], i, part)
         return 0
 
     def rest_step(i, _):
-        for part in range(HALVES):
+        for part in range(PIECES):
             copy_of(i, part).wait()
 
             @pl.when(i + IN_FLIGHT < rest)
@@ -112,20 +137,10 @@
     lax.fori_loop(0, held, held_step, 0)
     lax.fori_loop(0, rest, rest_step, 0)
 
-    _, tensors, block_rows, _ = kept_ref.shape
-    sections = sent_ref.shape[0] + 1
-    for s in range(sections):
-        for t in range(tensors):
-            first = (t * sections + s) * block_rows
-            block = total_ref[first : first + block_rows, :]
-
-            @pl.when(section == s)
-            def _():
-                kept_ref[0, t] = block
-
-            @pl.when(section != s)
-            def _():
-                sent_ref[lax.rem(s + sections - section, sections) - 1, t] = block.astype(BF16)
+    each = kept_ref.shape[0]
+    kept_ref[...] = total_ref[:each]
+    for turn in range(sections - 1):
+        sent_ref[turn] = total_ref[(turn + 1) * each : (turn + 2) * each].astype(BF16)
 
 
 def project(own, others, held, weight, tensors, sections):
@@ -134,12 +149,11 @@
     columns = weight.shape[1]
     count, step, _ = held.shape
     rest = depth // step - count
-    block_rows = rows // (tensors * sections)
-    return pl.pallas_call(
-        project_kernel,
+    return pl.pallas_call(
+        functools.partial(project_kernel, tensors=tensors, sections=sections),
         out_shape=(
-            pltpu.VMEM((1, tensors, block_rows, columns), F32),
-            pltpu.VMEM((sections - 1, tensors, block_rows, columns), BF16),
+            pltpu.VMEM((rows // sections, columns), F32),
+            pltpu.VMEM((sections - 1, rows // sections, columns), BF16),
         ),
         in_specs=[whole(), whole(), whole(), pl.BlockSpec(memory_space=pl.ANY)],
         out_specs=(whole(), whole()),
@@ -147,9 +161,9 @@
             pltpu.VMEM((depth // step, rows, step), BF16),
             pltpu.VMEM((rows, columns), F32),
             pltpu.VMEM((rest, step, columns), BF16),
-            pltpu.SemaphoreType.DMA((rest, HALVES)),
+            pltpu.SemaphoreType.DMA((rest, PIECES)),
         ],
-        compiler_params=pltpu.CompilerParams(vmem_limit_bytes=35 * MIB),
+        compiler_params=pltpu.CompilerParams(vmem_limit_bytes=36 * MIB),
         cost_estimate=pl.CostEstimate(
             flops=2 * rows * depth * columns,
             bytes_accessed=2 * rest * step * columns,
@@ -166,24 +180,24 @@
 
 
 def pair_kernel(kept_ref, *refs):
-    tensors = kept_ref.shape[1]
-    arrived, outs = refs[:-tensors], refs[-tensors:]
-    me = lax.axis_index("tensor")
-    for shift, out_ref in enumerate(outs):
-        place = partner_of(me, shift, tensors)
-        block = kept_ref[0, place]
+    outs = refs[-(kept_ref.shape[0] // refs[-1].shape[0]) :]
+    arrived = refs[: -len(outs)]
+    for turn, out_ref in enumerate(outs):
+        block_rows = out_ref.shape[0]
+        mine = slice(turn * block_rows, (turn + 1) * block_rows)
+        block = kept_ref[mine, :]
         for piece in arrived:
-            block = block + piece[place].astype(F32)
+            block = block + piece[mine, :].astype(F32)
         out_ref[...] = block.astype(out_ref.dtype)
 
 
-def pair(kept, arrived):
-    _, tensors, block_rows, columns = kept.shape
+def pair(kept, arrived, tensors):
+    rows, columns = kept.shape
     return pl.pallas_call(
         pair_kernel,
         out_shape=[
-            jax.ShapeDtypeStruct((block_rows, columns), F32 if shift == 0 else BF16)
-            for shift in range(tensors)
+            jax.ShapeDtypeStruct((rows // tensors, columns), F32 if turn == 0 else BF16)
+            for turn in range(tensors)
         ],
         in_specs=[whole()] * (1 + len(arrived)),
         out_specs=[whole()] * tensors,
@@ -192,27 +206,39 @@
     )(kept, *arrived)
 
 
-def mix_kernel(residual_ref, places_ref, own_ref, *refs):
+def places_of(row, slots, owners, local):
+    rows = row.shape[1]
+    upper = lax.broadcasted_iota(jnp.int32, (rows, rows), 0)
+    lower = lax.broadcasted_iota(jnp.int32, (rows, rows), 1)
+    column = jnp.sum(jnp.where(upper == lower, row, 0), axis=1, keepdims=True)
+    before = jnp.logical_and(column == row, upper < lower)
+    rank_of = jnp.sum(before.astype(jnp.int32), axis=0, keepdims=True)
+    slot = lax.broadcasted_iota(jnp.int32, (slots * owners, rows), 0)
+    owner = (lax.axis_index("dp") + slot // slots) % owners
+    adapter = owner * local + slot // MOST % local
+    return jnp.logical_and(row == adapter, rank_of == slot % MOST).astype(F32)
+
+
+def mix_kernel(residual_ref, index_ref, own_ref, *refs):
     arrived, (mixed_ref, kept_ref, sent_ref) = refs[:-3], refs[-3:]
+    slots = kept_ref.shape[0]
+    places = places_of(index_ref[...], slots, 1 + sent_ref.shape[0], slots // MOST)
     total = own_ref[...] + residual_ref[...].astype(F32)
     for piece in arrived:
         total = total + piece[...].astype(F32)
     mixed = total.astype(BF16)
     mixed_ref[...] = mixed
     widened = mixed.astype(F32)
-    places = places_ref[...]
-    slots = kept_ref.shape[0]
     routed = sum(
         places[:, row : row + 1] * widened[row : row + 1, :] for row in range(widened.shape[0])
     )
     kept_ref[...] = routed[:slots]
-    for shift in range(sent_ref.shape[0]):
-        sent_ref[shift] = routed[(shift + 1) * slots : (shift + 2) * slots].astype(BF16)
-
-
-def mix(residual, places, own, arrived, slots):
+    for turn in range(sent_ref.shape[0]):
+        sent_ref[turn] = routed[(turn + 1) * slots : (turn + 2) * slots].astype(BF16)
+
+
+def mix(residual, index, own, arrived, slots, owners):
     rows, columns = residual.shape
-    owners = places.shape[0] // slots
     return pl.pallas_call(
         mix_kernel,
         out_shape=(
@@ -224,7 +250,7 @@
         out_specs=(whole(),) * 3,
         compiler_params=pltpu.CompilerParams(vmem_limit_bytes=8 * MIB),
         name="mix",
-    )(residual, places, own, *arrived)
+    )(residual, index, own, *arrived)
 
 
 def partial_values(rows, gain_ref, shrink_ref, place, columns, local):
@@ -321,7 +347,6 @@
 
 def body(hidden, down_matrix, residual, next_norm_scale, shrink_matrix, adapter_index):
     dp, tensors, sections = (lax.axis_size(axis) for axis in ("dp", "tensor", "section"))
-    me = lax.axis_index("dp")
     depth, _ = down_matrix.shape
     local = shrink_matrix.shape[0]
 
@@ -332,27 +357,16 @@
     held_count = max(1, min(blocks // 2, HELD_BYTES // (2 * step * down_matrix.shape[1])))
     held = fetch(down_matrix, held_count, step)
 
-    row_adapter = adapter_index[:, 0]
-    same = row_adapter[:, None] == row_adapter[None, :]
-    rows = row_adapter.shape[0]
-    earlier = jnp.arange(rows)[:, None] < jnp.arange(rows)[None, :]
-    rank_of = jnp.sum(jnp.logical_and(same, earlier), axis=0)
-    owners = (me + jnp.arange(dp)) % dp
-    adapters = owners[:, None] * local + jnp.arange(local)[None, :]
-    places = jnp.logical_and(
-        adapters[:, :, None, None] == row_adapter,
-        jnp.arange(MOST)[None, None, :, None] == rank_of,
-    )
-    places = places.astype(F32).reshape(dp * local * MOST, rows)
     shrink = jnp.swapaxes(shrink_matrix, 1, 2)
     gain = next_norm_scale[None, :]
 
     in_vmem = [pltpu.with_memory_space_constraint(x, pltpu.VMEM) for x in (hidden, others, held)]
     kept, sent = project(*in_vmem, down_matrix, tensors, sections)
     arrived = [shifted(sent[s - 1], "section", s) for s in range(1, sections)]
-    own, *sums = pair(kept, arrived)
+    own, *sums = pair(kept, arrived, tensors)
     arrived = [to_partner(sums[s - 1], "tensor", s) for s in range(tensors - 1, 0, -1)]
-    mixed, routed, leaving = mix(residual, places, own, arrived, local * MOST)
+    index = adapter_index.reshape(1, -1)
+    mixed, routed, leaving = mix(residual, index, own, arrived, local * MOST, dp)
     arrived = [shifted(leaving[s - 1], "dp", s) for s in range(1, dp)]
     values, squares = own_half(routed, gain, shrink)
     shrunk = finish(values, squares, gain, shrink, arrived)

time: 37.9 us -> 40 us (1.055)
  Pallas kernels: 20.4 us -> 22.6 us
    pallas_call x2, Pallas kernels: 12.1 us -> 14.2 us  [the longest x1 14.2 us: project(): pl.pallas_call(functools.partial(project_kernel, tensors=tensors, section...]
  transfers between devices with their start and end apart: 6 -> 6, of which waited for: 4 -> 4; matrix products, arithmetic and copies ran while one was open for 2% -> 2% of each run, Pallas kernels for 19% -> 18%
where the time goes in v5:
time: 40 us; the launch traced here: 39.8 us
  Pallas kernels  22.6 us (56%)
  starting transfers between devices  8.12 us (20%)
  waiting for transfers between devices  7.65 us (19%)
  between operations  0.73 us (2%)
  local copies, waits for them, and re-layouts  0.67 us (2%)
    pallas_call x1, Pallas kernels, project(): pl.pallas_call(functools.partial(project_kernel, tensors=tensors, section...  14.2 us
    pallas_call x1, Pallas kernels, fetch(): pl.pallas_call(fetch_kernel, out_shape=pltpu.VMEM((count, step, columns),...  7.09 us
    ppermute x3, starting transfers between devices, to_partner(): lax.ppermute(array, axis, [(i, partner_of(i, turn, count)) for i in range...  4.45 us
    ppermute x3, waiting for transfers between devices, to_partner(): lax.ppermute(array, axis, [(i, partner_of(i, turn, count)) for i in range...  4.01 us
    ppermute x3, starting transfers between devices, shifted(): lax.ppermute(array, axis, [(i, (i + shift) % count) for i in range(count)])  3.67 us
    ppermute x3, waiting for transfers between devices, shifted(): lax.ppermute(array, axis, [(i, (i + shift) % count) for i in range(count)])  3.65 us
    pallas_call x1, Pallas kernels, finish(): pl.pallas_call(finish_kernel, out_shape=jax.ShapeDtypeStruct((local, 1, M...  0.84 us
  transfers between devices with their start and end apart: 6, of which 4 were waited for; matrix products, arithmetic and copies ran while one was open for 2% of the time, Pallas kernels for 18%

profile of v5, /device:TPU:0, one launch (start us, length us, event | category | flops | bytes accessed | tf_op | source)
XLA Modules:
  0.0 39.8 jit_solution(5256316375839431399)
XLA Ops:
  0.6 0.0 copy-start.1
  0.6 3.0 %collective-permute-start = (bf16[16,6656]{1,0:T(8,128)(2,1)}, bf16[16,6656]{1,0:T(8,128)(2,1)S(1)}, u32[]{:S(2)}, u32[]{:S(2)}) collective-permute-start(bf16[16,6656]{1,0:T(8,128)(2,1)} %own_ref.1), channel_id=1, source_target_pairs={{0,2},{2,0},{1,3},{3,1},{4,6},{6,4},{5,7},{7,5},{8,10},{10,8},{9,1... | collective-permute-start | bytes 638984 | tf_op jit(solution)/shard_map/ppermute | solution.py:340
  3.6 7.1 %fetch.1.held_ref = bf16[5,512,4096]{2,1,0:T(8,128)(2,1)S(1)} custom-call(bf16[6656,4096]{1,0:T(8,128)(2,1)} %weight_ref.3), custom_call_target="tpu_custom_call" | custom-call | bytes 20971520 | tf_op jit(solution)/shard_map/fetch/pallas_call | solution.py:45
  10.7 0.0 copy-start.2
  10.8 0.0 copy-start.3
  10.8 0.0 copy-start.4
  10.8 0.0 copy-start
  10.8 0.0 collective-permute-done
  10.8 0.0 copy-done.1
  10.8 14.2 %project.1 = (f32[16,4096]{1,0:T(8,128)S(1)}, bf16[1,16,4096]{2,1,0:T(8,128)(2,1)S(1)}) custom-call(bf16[16,6656]{1,0:T(8,128)(2,1)S(1)} %copy-done.1, bf16[1,16,6656]{2,1,0:T(8,128)(2,1)S(1)} %bitcast.7, bf16[5,512,4096]{2,1,0:T(8,128)(2,1)S(1)} %fetch.1.held_ref, bf16[6656,4096]{1,0:T(8,128)(2,1)} %weight_ref.3), custom_call_target="tpu_custom_call" | custom-call | flops 1744830464 | bytes 33554432 | tf_op jit(solution)/shard_map/project/pallas_call | solution.py:152
  25.0 0.1 collective-permute-start.1
  25.1 1.3 %collective-permute-done.1.refs_0_ = bf16[16,4096]{1,0:T(8,128)(2,1)S(1)} collective-permute-done((bf16[16,4096]{1,0:T(8,128)(2,1)S(1)}, bf16[16,4096]{1,0:T(8,128)(2,1)S(1)}, u32[]{:S(2)}, u32[]{:S(2)}) %collective-permute-start.1) | collective-permute-done | bytes 131104 | tf_op jit(solution)/shard_map/ppermute | solution.py:340
  26.4 0.1 pair.1
  26.5 3.6 %collective-permute-start.2 = (bf16[4,4096]{1,0:T(4,128)(2,1)S(1)}, bf16[4,4096]{1,0:T(4,128)(2,1)S(1)}, u32[]{:S(2)}, u32[]{:S(2)}) collective-permute-start(bf16[4,4096]{1,0:T(4,128)(2,1)S(1)} %get-tuple-element.16), channel_id=1, source_target_pairs={{0,12},{4,8},{8,4},{12,0},{1,13},{5,9},{9,5},{13,1},{2,14},{6,10},... | collective-permute-start | bytes 98312 | tf_op jit(solution)/shard_map/ppermute | solution.py:345
  30.1 0.0 collective-permute-start.3
  30.1 0.8 %collective-permute-start.4 = (bf16[4,4096]{1,0:T(4,128)(2,1)S(1)}, bf16[4,4096]{1,0:T(4,128)(2,1)S(1)}, u32[]{:S(2)}, u32[]{:S(2)}) collective-permute-start(bf16[4,4096]{1,0:T(4,128)(2,1)S(1)} %get-tuple-element.18), channel_id=1, source_target_pairs={{0,4},{4,0},{8,12},{12,8},{1,5},{5,1},{9,13},{13,9},{2,6},{6,2},{1... | collective-permute-start | bytes 98312 | tf_op jit(solution)/shard_map/ppermute | solution.py:345
  30.9 1.3 %collective-permute-done.2.refs_0_ = bf16[4,4096]{1,0:T(4,128)(2,1)S(1)} collective-permute-done((bf16[4,4096]{1,0:T(4,128)(2,1)S(1)}, bf16[4,4096]{1,0:T(4,128)(2,1)S(1)}, u32[]{:S(2)}, u32[]{:S(2)}) %collective-permute-start.2) | collective-permute-done | bytes 32800 | tf_op jit(solution)/shard_map/ppermute | solution.py:345
  32.2 2.7 %collective-permute-done.3.refs_1_ = bf16[4,4096]{1,0:T(4,128)(2,1)S(1)} collective-permute-done((bf16[4,4096]{1,0:T(4,128)(2,1)S(1)}, bf16[4,4096]{1,0:T(4,128)(2,1)S(1)}, u32[]{:S(2)}, u32[]{:S(2)}) %collective-permute-start.3) | collective-permute-done | bytes 32800 | tf_op jit(solution)/shard_map/ppermute | solution.py:345
  34.9 0.0 collective-permute-done.4.refs_2_
  34.9 0.0 copy-done.2
  34.9 0.0 copy-done.3
  34.9 0.2 mix.1
  35.2 0.6 %collective-permute-start.5 = (bf16[2,4096]{1,0:T(2,128)(2,1)S(1)}, bf16[2,4096]{1,0:T(2,128)(2,1)S(1)}, u32[]{:S(2)}, u32[]{:S(2)}) collective-permute-start(bf16[2,4096]{1,0:T(2,128)(2,1)S(1)} %bitcast.10), channel_id=1, source_target_pairs={{0,2},{2,0},{1,3},{3,1},{4,6},{6,4},{5,7},{7,5},{8,10},{10,8},{9,1... | collective-permute-start | bytes 49160 | tf_op jit(solution)/shard_map/ppermute | solution.py:340
  35.8 0.0 copy-done.4
  35.8 0.6 %copy.8 = bf16[4,4096]{1,0:T(4,128)(2,1)} copy(bf16[4,4096]{1,0:T(4,128)(2,1)S(1)} %get-tuple-element.24) | data formatting | bytes 65536
  36.4 0.0 copy-done
  36.4 0.3 own_half.1
  36.7 2.3 %collective-permute-done.5.refs_0_ = bf16[2,4096]{1,0:T(2,128)(2,1)S(1)} collective-permute-done((bf16[2,4096]{1,0:T(2,128)(2,1)S(1)}, bf16[2,4096]{1,0:T(2,128)(2,1)S(1)}, u32[]{:S(2)}, u32[]{:S(2)}) %collective-permute-start.5) | collective-permute-done | bytes 16416 | tf_op jit(solution)/shard_map/ppermute | solution.py:340
  39.0 0.8 %finish.1 = f32[1,1,2,64]{3,2,1,0:T(2,128)} custom-call(f32[2,64]{1,0:T(2,128)S(1)} %get-tuple-element.21.values_ref, f32[2,64]{1,0:T(2,128)S(1)} %get-tuple-element.22.squares_ref, bf16[1,8192]{1,0:T(2,128)(2,1)S(1)} %broadcast_in_dim.3.gain_ref, bf16[1,64,8192]{2,1,0:T(8,128)(2,1)S(1)} %bitcast.6, bf16[2,4096]{1,0:T(2,128)(2,1)S(1)} %collective-permute-done.5.refs_0_), custom_call_target="tpu_custom_call" | custom-call | tf_op jit(solution)/shard_map/finish/pallas_call | solution.py:328
  (1 shorter events, 0.0 us)
Async XLA Ops:
  0.6 10.2 %copy-start.1 = (bf16[16,6656]{1,0:T(8,128)(2,1)S(1)}, bf16[16,6656]{1,0:T(8,128)(2,1)}, u32[]{:S(2)}) copy-start(bf16[16,6656]{1,0:T(8,128)(2,1)} %own_ref.1) | copy-start | bytes 638980
  0.6 10.2 %collective-permute-start = (bf16[16,6656]{1,0:T(8,128)(2,1)}, bf16[16,6656]{1,0:T(8,128)(2,1)S(1)}, u32[]{:S(2)}, u32[]{:S(2)}) collective-permute-start(bf16[16,6656]{1,0:T(8,128)(2,1)} %own_ref.1), channel_id=1, source_target_pairs={{0,2},{2,0},{1,3},{3,1},{4,6},{6,4},{5,7},{7,5},{8,10},{10,8},{9,1... | collective-permute-start | bytes 638984 | tf_op jit(solution)/shard_map/ppermute | solution.py:340
  10.7 24.2 %copy-start.2 = (bf16[4,4096]{1,0:T(4,128)(2,1)S(1)}, bf16[4,4096]{1,0:T(4,128)(2,1)}, u32[]{:S(2)}) copy-start(bf16[4,4096]{1,0:T(4,128)(2,1)} %residual_ref.1) | copy-start | bytes 98308
  10.8 24.2 %copy-start.3 = (s32[4,1]{0,1:T(1,128)S(1)}, s32[4,1]{0,1:T(1,128)}, u32[]{:S(2)}) copy-start(s32[4,1]{0,1:T(1,128)} %param.11) | copy-start | bytes 52
  10.8 25.0 %copy-start.4 = (bf16[8192]{0:T(1024)(128)(2,1)S(1)}, bf16[8192]{0:T(1024)(128)(2,1)}, u32[]{:S(2)}) copy-start(bf16[8192]{0:T(1024)(128)(2,1)} %param.9) | copy-start | bytes 49156
  10.8 25.6 %copy-start = (bf16[1,8192,64]{1,2,0:T(8,128)(2,1)S(1)}, bf16[1,8192,64]{1,2,0:T(8,128)(2,1)}, u32[]{:S(2)}) copy-start(bf16[1,8192,64]{1,2,0:T(8,128)(2,1)} %param.10) | copy-start | bytes 3145732
  25.0 1.4 %collective-permute-start.1 = (bf16[16,4096]{1,0:T(8,128)(2,1)S(1)}, bf16[16,4096]{1,0:T(8,128)(2,1)S(1)}, u32[]{:S(2)}, u32[]{:S(2)}) collective-permute-start(bf16[16,4096]{1,0:T(8,128)(2,1)S(1)} %bitcast.9), channel_id=1, source_target_pairs={{0,1},{1,0},{2,3},{3,2},{4,5},{5,4},{6,7},{7,6},{8,9},{9,8},{10,11... | collective-permute-start | bytes 393224 | tf_op jit(solution)/shard_map/ppermute | solution.py:340
  26.5 5.8 %collective-permute-start.2 = (bf16[4,4096]{1,0:T(4,128)(2,1)S(1)}, bf16[4,4096]{1,0:T(4,128)(2,1)S(1)}, u32[]{:S(2)}, u32[]{:S(2)}) collective-permute-start(bf16[4,4096]{1,0:T(4,128)(2,1)S(1)} %get-tuple-element.16), channel_id=1, source_target_pairs={{0,12},{4,8},{8,4},{12,0},{1,13},{5,9},{9,5},{13,1},{2,14},{6,10},... | collective-permute-start | bytes 98312 | tf_op jit(solution)/shard_map/ppermute | solution.py:345
  30.1 4.8 %collective-permute-start.3 = (bf16[4,4096]{1,0:T(4,128)(2,1)S(1)}, bf16[4,4096]{1,0:T(4,128)(2,1)S(1)}, u32[]{:S(2)}, u32[]{:S(2)}) collective-permute-start(bf16[4,4096]{1,0:T(4,128)(2,1)S(1)} %get-tuple-element.17), channel_id=1, source_target_pairs={{0,8},{4,12},{8,0},{12,4},{1,9},{5,13},{9,1},{13,5},{2,10},{6,14},... | collective-permute-start | bytes 98312 | tf_op jit(solution)/shard_map/ppermute | solution.py:345
  30.1 4.8 %collective-permute-start.4 = (bf16[4,4096]{1,0:T(4,128)(2,1)S(1)}, bf16[4,4096]{1,0:T(4,128)(2,1)S(1)}, u32[]{:S(2)}, u32[]{:S(2)}) collective-permute-start(bf16[4,4096]{1,0:T(4,128)(2,1)S(1)} %get-tuple-element.18), channel_id=1, source_target_pairs={{0,4},{4,0},{8,12},{12,8},{1,5},{5,1},{9,13},{13,9},{2,6},{6,2},{1... | collective-permute-start | bytes 98312 | tf_op jit(solution)/shard_map/ppermute | solution.py:345
  35.2 3.8 %collective-permute-start.5 = (bf16[2,4096]{1,0:T(2,128)(2,1)S(1)}, bf16[2,4096]{1,0:T(2,128)(2,1)S(1)}, u32[]{:S(2)}, u32[]{:S(2)}) collective-permute-start(bf16[2,4096]{1,0:T(2,128)(2,1)S(1)} %bitcast.10), channel_id=1, source_target_pairs={{0,2},{2,0},{1,3},{3,1},{4,6},{6,4},{5,7},{7,5},{8,10},{10,8},{9,1... | collective-permute-start | bytes 49160 | tf_op jit(solution)/shard_map/ppermute | solution.py:340

commit v6 on v5

--- a/solution.py
+++ b/solution.py
@@ -11,8 +11,7 @@
 EPS = 1e-05
 DEPTH_STEP = 512
 HELD_BYTES = 21 * 2**20
-IN_FLIGHT = 4
-PIECES = 4
+WIDTH = 1024
 MIB = 2**20
 F32 = jnp.float32
 BF16 = jnp.bfloat16
@@ -54,19 +53,6 @@
         ),
         name="fetch",
     )(weight)
-
-
-def exchange_order(own_rows, dp, tensors, sections):
-    rows = own_rows * dp
-    block_rows = rows // (tensors * sections)
-    me, tensor, section = (lax.axis_index(axis) for axis in ("dp", "tensor", "section"))
-    target = lax.broadcasted_iota(jnp.int32, (rows, rows), 0)
-    source = lax.broadcasted_iota(jnp.int32, (rows, rows), 1)
-    s = (section + target // (tensors * block_rows)) % sections
-    t = partner_of(tensor, target // block_rows % tensors, tensors)
-    wanted = (t * sections + s) * block_rows + target % block_rows
-    owner = (me + dp - source // own_rows) % dp
-    return (wanted == owner * own_rows + source % own_rows).astype(BF16)
 
 
 def project_kernel(
@@ -88,59 +74,72 @@
     rest = rest_ref.shape[0]
     own_rows = own_ref.shape[0]
     dp = 1 + others_ref.shape[0]
-    piece = columns // PIECES
-    width = min(piece, 1024)
-
-    def copy_of(i, part):
-        lanes = pl.ds(part * piece, piece)
+    me, tensor, section = (lax.axis_index(axis) for axis in ("dp", "tensor", "section"))
+    width = min(columns, WIDTH)
+    half = step // 2
+
+    def copy_of(i, sem, first=0, size=step):
         return pltpu.make_async_copy(
-            weight_ref.at[pl.ds((held + i) * step, step), lanes],
-            rest_ref.at[i, :, lanes],
-            sems.at[i, part],
+            weight_ref.at[pl.ds((held + i) * step + first, size), :],
+            rest_ref.at[i, pl.ds(first, size), :],
+            sems.at[sem],
         )
 
-    for i in range(min(rest, IN_FLIGHT)):
-        for part in range(PIECES):
-            copy_of(i, part).start()
-
-    order = exchange_order(own_rows, dp, tensors, sections)
+    last = [copy_of(rest - 1, rest - 1, 0, half), copy_of(rest - 1, rest, half, half)]
+    for i in range(rest - 1):
+        copy_of(i, i).start()
+    for copy in last:
+        copy.start()
+
     for i in range(held + rest):
         block = slice(i * step, (i + 1) * step)
-        stacked = [own_ref[:, block]] + [others_ref[k, :, block] for k in range(dp - 1)]
-        rows_ref[i] = jnp.dot(
-            order, jnp.concatenate(stacked, axis=0), preferred_element_type=F32
-        ).astype(BF16)
-    total_ref[...] = jnp.zeros_like(total_ref)
-
-    def add(block_ref, i, part):
-        for n in range(part * piece, (part + 1) * piece, width):
-            total_ref[:, n : n + width] += jnp.dot(
-                rows_ref[i], block_ref[:, n : n + width], preferred_element_type=F32
+        for shift in range(dp):
+            first = pl.multiple_of((me + dp - shift) % dp * own_rows, own_rows)
+            source = own_ref[:, block] if shift == 0 else others_ref[shift - 1, :, block]
+            rows_ref[i, pl.ds(first, own_rows), :] = source
+
+    def held_step(n, _):
+        lanes = pl.ds(pl.multiple_of(n * width, width), width)
+        total_ref[:, lanes] = sum(
+            jnp.dot(rows_ref[i], held_ref[i, :, lanes], preferred_element_type=F32)
+            for i in range(held)
+        )
+        return 0
+
+    def add(i, part=slice(None)):
+        for n in range(0, columns, width):
+            lanes = slice(n, n + width)
+            total_ref[:, lanes] += jnp.dot(
+                rows_ref[held + i, :, part], rest_ref[i, part, lanes], preferred_element_type=F32
             )
 
-    def held_step(i, _):
-        for part in range(PIECES):
-            add(held_ref.at[i], i, part)
+    def rest_step(i, _):
+        copy_of(i, i).wait()
+        add(i)
         return 0
 
-    def rest_step(i, _):
-        for part in range(PIECES):
-            copy_of(i, part).wait()
-
-            @pl.when(i + IN_FLIGHT < rest)
-            def _():
-                copy_of(i + IN_FLIGHT, part).start()
-
-            add(rest_ref.at[i], held + i, part)
-        return 0
-
-    lax.fori_loop(0, held, held_step, 0)
-    lax.fori_loop(0, rest, rest_step, 0)
-
-    each = kept_ref.shape[0]
-    kept_ref[...] = total_ref[:each]
-    for turn in range(sections - 1):
-        sent_ref[turn] = total_ref[(turn + 1) * each : (turn + 2) * each].astype(BF16)
+    lax.fori_loop(0, columns // width, held_step, 0)
+    lax.fori_loop(0, rest - 1, rest_step, 0)
+    for copy, part in zip(last, (slice(0, half), slice(half, step))):
+        copy.wait()
+        add(rest - 1, part)
+
+    block_rows = kept_ref.shape[0] // tensors
+    group = sections * block_rows
+    for n in range(0, columns, width):
+        lanes = slice(n, n + width)
+        turned = []
+        for turn in range(tensors):
+            first = pl.multiple_of(partner_of(tensor, turn, tensors) * group, group)
+            rows = total_ref[pl.ds(first, group), lanes]
+            turned.append(pltpu.roll(rows, (sections - section) % sections * block_rows, 0))
+        for s in range(sections):
+            part = slice(s * block_rows, (s + 1) * block_rows)
+            rows = jnp.concatenate([block[part] for block in turned], axis=0)
+            if s == 0:
+                kept_ref[:, lanes] = rows
+            else:
+                sent_ref[s - 1, :, lanes] = rows.astype(BF16)
 
 
 def project(own, others, held, weight, tensors, sections):
@@ -161,7 +160,7 @@
             pltpu.VMEM((depth // step, rows, step), BF16),
             pltpu.VMEM((rows, columns), F32),
             pltpu.VMEM((rest, step, columns), BF16),
-            pltpu.SemaphoreType.DMA((rest, PIECES)),
+            pltpu.SemaphoreType.DMA((rest + 1,)),
         ],
         compiler_params=pltpu.CompilerParams(vmem_limit_bytes=36 * MIB),
         cost_estimate=pl.CostEstimate(
@@ -182,12 +181,12 @@
 def pair_kernel(kept_ref, *refs):
     outs = refs[-(kept_ref.shape[0] // refs[-1].shape[0]) :]
     arrived = refs[: -len(outs)]
+    total = kept_ref[...]
+    for piece in arrived:
+        total = total + piece[...].astype(F32)
     for turn, out_ref in enumerate(outs):
         block_rows = out_ref.shape[0]
-        mine = slice(turn * block_rows, (turn + 1) * block_rows)
-        block = kept_ref[mine, :]
-        for piece in arrived:
-            block = block + piece[mine, :].astype(F32)
+        block = total[turn * block_rows : (turn + 1) * block_rows]
         out_ref[...] = block.astype(out_ref.dtype)
 
 
@@ -219,10 +218,25 @@
     return jnp.logical_and(row == adapter, rank_of == slot % MOST).astype(F32)
 
 
-def mix_kernel(residual_ref, index_ref, own_ref, *refs):
+def places_kernel(index_ref, places_ref, *, slots, owners):
+    places_ref[...] = places_of(index_ref[...], slots, owners, slots // MOST)
+
+
+def find_places(index, slots, owners):
+    return pl.pallas_call(
+        functools.partial(places_kernel, slots=slots, owners=owners),
+        out_shape=jax.ShapeDtypeStruct((slots * owners, index.shape[1]), F32),
+        in_specs=[whole()],
+        out_specs=whole(),
+        compiler_params=pltpu.CompilerParams(vmem_limit_bytes=1 * MIB),
+        name="find_places",
+    )(index)
+
+
+def mix_kernel(residual_ref, places_ref, own_ref, *refs):
     arrived, (mixed_ref, kept_ref, sent_ref) = refs[:-3], refs[-3:]
     slots = kept_ref.shape[0]
-    places = places_of(index_ref[...], slots, 1 + sent_ref.shape[0], slots // MOST)
+    places = places_ref[...]
     total = own_ref[...] + residual_ref[...].astype(F32)
     for piece in arrived:
         total = total + piece[...].astype(F32)
@@ -237,7 +251,7 @@
         sent_ref[turn] = routed[(turn + 1) * slots : (turn + 2) * slots].astype(BF16)
 
 
-def mix(residual, index, own, arrived, slots, owners):
+def mix(residual, places, own, arrived, slots, owners):
     rows, columns = residual.shape
     return pl.pallas_call(
         mix_kernel,
@@ -250,7 +264,7 @@
         out_specs=(whole(),) * 3,
         compiler_params=pltpu.CompilerParams(vmem_limit_bytes=8 * MIB),
         name="mix",
-    )(residual, index, own, *arrived)
+    )(residual, places, own, *arrived)
 
 
 def partial_values(rows, gain_ref, shrink_ref, place, columns, local):
@@ -362,11 +376,12 @@
 
     in_vmem = [pltpu.with_memory_space_constraint(x, pltpu.VMEM) for x in (hidden, others, held)]
     kept, sent = project(*in_vmem, down_matrix, tensors, sections)
+    index, kept = lax.optimization_barrier((adapter_index.reshape(1, -1), kept))
+    places = find_places(index, local * MOST, dp)
     arrived = [shifted(sent[s - 1], "section", s) for s in range(1, sections)]
     own, *sums = pair(kept, arrived, tensors)
     arrived = [to_partner(sums[s - 1], "tensor", s) for s in range(tensors - 1, 0, -1)]
-    index = adapter_index.reshape(1, -1)
-    mixed, routed, leaving = mix(residual, index, own, arrived, local * MOST, dp)
+    mixed, routed, leaving = mix(residual, places, own, arrived, local * MOST, dp)
     arrived = [shifted(leaving[s - 1], "dp", s) for s in range(1, dp)]
     values, squares = own_half(routed, gain, shrink)
     shrunk = finish(values, squares, gain, shrink, arrived)

time: 40 us -> 37 us (0.925)
  Pallas kernels: 22.6 us -> 19.8 us
    pallas_call x1, Pallas kernels: 14.2 us -> 11.3 us  [project(): pl.pallas_call(functools.partial(project_kernel, tensors=tensors, section...]
  transfers between devices with their start and end apart: 6 -> 6, of which waited for: 4 -> 4; matrix products, arithmetic and copies ran while one was open for 2% -> 2% of each run, Pallas kernels for 18% -> 20%
where the time goes in v6:
time: 37 us; the launch traced here: 36.9 us
  Pallas kernels  19.8 us (54%)
  starting transfers between devices  8.13 us (22%)
  waiting for transfers between devices  7.57 us (20%)
  between operations  0.73 us (2%)
  local copies, waits for them, and re-layouts  0.67 us (2%)
    pallas_call x1, Pallas kernels, project(): pl.pallas_call(functools.partial(project_kernel, tensors=tensors, section...  11.3 us
    pallas_call x1, Pallas kernels, fetch(): pl.pallas_call(fetch_kernel, out_shape=pltpu.VMEM((count, step, columns),...  7.09 us
    ppermute x3, starting transfers between devices, to_partner(): lax.ppermute(array, axis, [(i, partner_of(i, turn, count)) for i in range...  4.45 us
    ppermute x3, waiting for transfers between devices, to_partner(): lax.ppermute(array, axis, [(i, partner_of(i, turn, count)) for i in range...  3.93 us
    ppermute x3, starting transfers between devices, shifted(): lax.ppermute(array, axis, [(i, (i + shift) % count) for i in range(count)])  3.68 us
    ppermute x3, waiting for transfers between devices, shifted(): lax.ppermute(array, axis, [(i, (i + shift) % count) for i in range(count)])  3.64 us
    pallas_call x1, Pallas kernels, finish(): pl.pallas_call(finish_kernel, out_shape=jax.ShapeDtypeStruct((local, 1, M...  0.84 us
  transfers between devices with their start and end apart: 6, of which 4 were waited for; matrix products, arithmetic and copies ran while one was open for 2% of the time, Pallas kernels for 20%

profile of v6, /device:TPU:0, one launch (start us, length us, event | category | flops | bytes accessed | tf_op | source)
XLA Modules:
  0.0 36.9 jit_solution(6524932457827604167)
XLA Ops:
  0.6 0.0 copy-start.1
  0.6 3.0 %collective-permute-start = (bf16[16,6656]{1,0:T(8,128)(2,1)}, bf16[16,6656]{1,0:T(8,128)(2,1)S(1)}, u32[]{:S(2)}, u32[]{:S(2)}) collective-permute-start(bf16[16,6656]{1,0:T(8,128)(2,1)} %own_ref.1), channel_id=1, source_target_pairs={{0,2},{2,0},{1,3},{3,1},{4,6},{6,4},{5,7},{7,5},{8,10},{10,8},{9,1... | collective-permute-start | bytes 638984 | tf_op jit(solution)/shard_map/ppermute | solution.py:354
  3.6 7.1 %fetch.1.held_ref = bf16[5,512,4096]{2,1,0:T(8,128)(2,1)S(1)} custom-call(bf16[6656,4096]{1,0:T(8,128)(2,1)} %weight_ref.3), custom_call_target="tpu_custom_call" | custom-call | bytes 20971520 | tf_op jit(solution)/shard_map/fetch/pallas_call | solution.py:44
  10.7 0.0 copy-start.3
  10.8 0.0 copy-start.2
  10.8 0.0 copy-start.4
  10.8 0.0 copy-start
  10.8 0.0 collective-permute-done
  10.8 0.0 copy-done.1
  10.8 11.3 %project.1 = (f32[16,4096]{1,0:T(8,128)S(1)}, bf16[1,16,4096]{2,1,0:T(8,128)(2,1)S(1)}) custom-call(bf16[16,6656]{1,0:T(8,128)(2,1)S(1)} %copy-done.1, bf16[1,16,6656]{2,1,0:T(8,128)(2,1)S(1)} %bitcast.7, bf16[5,512,4096]{2,1,0:T(8,128)(2,1)S(1)} %fetch.1.held_ref, bf16[6656,4096]{1,0:T(8,128)(2,1)} %weight_ref.3), custom_call_target="tpu_custom_call" | custom-call | flops 1744830464 | bytes 33554432 | tf_op jit(solution)/shard_map/project/pallas_call | solution.py:151
  22.1 0.1 collective-permute-start.1
  22.2 1.3 %collective-permute-done.1.refs_0_ = bf16[16,4096]{1,0:T(8,128)(2,1)S(1)} collective-permute-done((bf16[16,4096]{1,0:T(8,128)(2,1)S(1)}, bf16[16,4096]{1,0:T(8,128)(2,1)S(1)}, u32[]{:S(2)}, u32[]{:S(2)}) %collective-permute-start.1) | collective-permute-done | bytes 131104 | tf_op jit(solution)/shard_map/ppermute | solution.py:354
  23.6 3.7 %collective-permute-start.2 = (bf16[4,4096]{1,0:T(4,128)(2,1)S(1)}, bf16[4,4096]{1,0:T(4,128)(2,1)S(1)}, u32[]{:S(2)}, u32[]{:S(2)}) collective-permute-start(bf16[4,4096]{1,0:T(4,128)(2,1)S(1)} %get-tuple-element.20), channel_id=1, source_target_pairs={{0,12},{4,8},{8,4},{12,0},{1,13},{5,9},{9,5},{13,1},{2,14},{6,10},... | collective-permute-start | bytes 98312 | tf_op jit(solution)/shard_map/ppermute | solution.py:359
  27.3 0.0 collective-permute-start.3
  27.3 0.8 %collective-permute-start.4 = (bf16[4,4096]{1,0:T(4,128)(2,1)S(1)}, bf16[4,4096]{1,0:T(4,128)(2,1)S(1)}, u32[]{:S(2)}, u32[]{:S(2)}) collective-permute-start(bf16[4,4096]{1,0:T(4,128)(2,1)S(1)} %get-tuple-element.22), channel_id=1, source_target_pairs={{0,4},{4,0},{8,12},{12,8},{1,5},{5,1},{9,13},{13,9},{2,6},{6,2},{1... | collective-permute-start | bytes 98312 | tf_op jit(solution)/shard_map/ppermute | solution.py:359
  28.1 0.0 copy-done.3
  28.1 0.1 find_places.1.places_ref
  28.2 1.2 %collective-permute-done.2.refs_0_ = bf16[4,4096]{1,0:T(4,128)(2,1)S(1)} collective-permute-done((bf16[4,4096]{1,0:T(4,128)(2,1)S(1)}, bf16[4,4096]{1,0:T(4,128)(2,1)S(1)}, u32[]{:S(2)}, u32[]{:S(2)}) %collective-permute-start.2) | collective-permute-done | bytes 32800 | tf_op jit(solution)/shard_map/ppermute | solution.py:359
  29.4 2.7 %collective-permute-done.3.refs_1_ = bf16[4,4096]{1,0:T(4,128)(2,1)S(1)} collective-permute-done((bf16[4,4096]{1,0:T(4,128)(2,1)S(1)}, bf16[4,4096]{1,0:T(4,128)(2,1)S(1)}, u32[]{:S(2)}, u32[]{:S(2)}) %collective-permute-start.3) | collective-permute-done | bytes 32800 | tf_op jit(solution)/shard_map/ppermute | solution.py:359
  32.1 0.0 collective-permute-done.4.refs_2_
  32.1 0.0 copy-done.2
  32.1 0.1 mix.1
  32.2 0.6 %collective-permute-start.5 = (bf16[2,4096]{1,0:T(2,128)(2,1)S(1)}, bf16[2,4096]{1,0:T(2,128)(2,1)S(1)}, u32[]{:S(2)}, u32[]{:S(2)}) collective-permute-start(bf16[2,4096]{1,0:T(2,128)(2,1)S(1)} %bitcast.10), channel_id=1, source_target_pairs={{0,2},{2,0},{1,3},{3,1},{4,6},{6,4},{5,7},{7,5},{8,10},{10,8},{9,1... | collective-permute-start | bytes 49160 | tf_op jit(solution)/shard_map/ppermute | solution.py:354
  32.8 0.0 copy-done.4
  32.9 0.6 %copy.8 = bf16[4,4096]{1,0:T(4,128)(2,1)} copy(bf16[4,4096]{1,0:T(4,128)(2,1)S(1)} %get-tuple-element.28) | data formatting | bytes 65536
  33.5 0.0 copy-done
  33.5 0.3 own_half.1
  33.7 2.3 %collective-permute-done.5.refs_0_ = bf16[2,4096]{1,0:T(2,128)(2,1)S(1)} collective-permute-done((bf16[2,4096]{1,0:T(2,128)(2,1)S(1)}, bf16[2,4096]{1,0:T(2,128)(2,1)S(1)}, u32[]{:S(2)}, u32[]{:S(2)}) %collective-permute-start.5) | collective-permute-done | bytes 16416 | tf_op jit(solution)/shard_map/ppermute | solution.py:354
  36.0 0.8 %finish.1 = f32[1,1,2,64]{3,2,1,0:T(2,128)} custom-call(f32[2,64]{1,0:T(2,128)S(1)} %get-tuple-element.25.values_ref, f32[2,64]{1,0:T(2,128)S(1)} %get-tuple-element.26.squares_ref, bf16[1,8192]{1,0:T(2,128)(2,1)S(1)} %broadcast_in_dim.3.gain_ref, bf16[1,64,8192]{2,1,0:T(8,128)(2,1)S(1)} %bitcast.6, bf16[2,4096]{1,0:T(2,128)(2,1)S(1)} %collective-permute-done.5.refs_0_), custom_call_target="tpu_custom_call" | custom-call | tf_op jit(solution)/shard_map/finish/pallas_call | solution.py:342
  (2 shorter events, 0.1 us)
Async XLA Ops:
  0.6 10.2 %copy-start.1 = (bf16[16,6656]{1,0:T(8,128)(2,1)S(1)}, bf16[16,6656]{1,0:T(8,128)(2,1)}, u32[]{:S(2)}) copy-start(bf16[16,6656]{1,0:T(8,128)(2,1)} %own_ref.1) | copy-start | bytes 638980
  0.6 10.2 %collective-permute-start = (bf16[16,6656]{1,0:T(8,128)(2,1)}, bf16[16,6656]{1,0:T(8,128)(2,1)S(1)}, u32[]{:S(2)}, u32[]{:S(2)}) collective-permute-start(bf16[16,6656]{1,0:T(8,128)(2,1)} %own_ref.1), channel_id=1, source_target_pairs={{0,2},{2,0},{1,3},{3,1},{4,6},{6,4},{5,7},{7,5},{8,10},{10,8},{9,1... | collective-permute-start | bytes 638984 | tf_op jit(solution)/shard_map/ppermute | solution.py:354
  10.7 17.3 %copy-start.3 = (s32[4,1]{0,1:T(1,128)S(1)}, s32[4,1]{0,1:T(1,128)}, u32[]{:S(2)}) copy-start(s32[4,1]{0,1:T(1,128)} %param.11) | copy-start | bytes 52
  10.8 21.3 %copy-start.2 = (bf16[4,4096]{1,0:T(4,128)(2,1)S(1)}, bf16[4,4096]{1,0:T(4,128)(2,1)}, u32[]{:S(2)}) copy-start(bf16[4,4096]{1,0:T(4,128)(2,1)} %residual_ref.1) | copy-start | bytes 98308
  10.8 22.1 %copy-start.4 = (bf16[8192]{0:T(1024)(128)(2,1)S(1)}, bf16[8192]{0:T(1024)(128)(2,1)}, u32[]{:S(2)}) copy-start(bf16[8192]{0:T(1024)(128)(2,1)} %param.9) | copy-start | bytes 49156
  10.8 22.7 %copy-start = (bf16[1,8192,64]{1,2,0:T(8,128)(2,1)S(1)}, bf16[1,8192,64]{1,2,0:T(8,128)(2,1)}, u32[]{:S(2)}) copy-start(bf16[1,8192,64]{1,2,0:T(8,128)(2,1)} %param.10) | copy-start | bytes 3145732
  22.1 1.4 %collective-permute-start.1 = (bf16[16,4096]{1,0:T(8,128)(2,1)S(1)}, bf16[16,4096]{1,0:T(8,128)(2,1)S(1)}, u32[]{:S(2)}, u32[]{:S(2)}) collective-permute-start(bf16[16,4096]{1,0:T(8,128)(2,1)S(1)} %bitcast.9), channel_id=1, source_target_pairs={{0,1},{1,0},{2,3},{3,2},{4,5},{5,4},{6,7},{7,6},{8,9},{9,8},{10,11... | collective-permute-start | bytes 393224 | tf_op jit(solution)/shard_map/ppermute | solution.py:354
  23.6 5.8 %collective-permute-start.2 = (bf16[4,4096]{1,0:T(4,128)(2,1)S(1)}, bf16[4,4096]{1,0:T(4,128)(2,1)S(1)}, u32[]{:S(2)}, u32[]{:S(2)}) collective-permute-start(bf16[4,4096]{1,0:T(4,128)(2,1)S(1)} %get-tuple-element.20), channel_id=1, source_target_pairs={{0,12},{4,8},{8,4},{12,0},{1,13},{5,9},{9,5},{13,1},{2,14},{6,10},... | collective-permute-start | bytes 98312 | tf_op jit(solution)/shard_map/ppermute | solution.py:359
  27.3 4.8 %collective-permute-start.3 = (bf16[4,4096]{1,0:T(4,128)(2,1)S(1)}, bf16[4,4096]{1,0:T(4,128)(2,1)S(1)}, u32[]{:S(2)}, u32[]{:S(2)}) collective-permute-start(bf16[4,4096]{1,0:T(4,128)(2,1)S(1)} %get-tuple-element.21), channel_id=1, source_target_pairs={{0,8},{4,12},{8,0},{12,4},{1,9},{5,13},{9,1},{13,5},{2,10},{6,14},... | collective-permute-start | bytes 98312 | tf_op jit(solution)/shard_map/ppermute | solution.py:359
  27.3 4.8 %collective-permute-start.4 = (bf16[4,4096]{1,0:T(4,128)(2,1)S(1)}, bf16[4,4096]{1,0:T(4,128)(2,1)S(1)}, u32[]{:S(2)}, u32[]{:S(2)}) collective-permute-start(bf16[4,4096]{1,0:T(4,128)(2,1)S(1)} %get-tuple-element.22), channel_id=1, source_target_pairs={{0,4},{4,0},{8,12},{12,8},{1,5},{5,1},{9,13},{13,9},{2,6},{6,2},{1... | collective-permute-start | bytes 98312 | tf_op jit(solution)/shard_map/ppermute | solution.py:359
  32.2 3.8 %collective-permute-start.5 = (bf16[2,4096]{1,0:T(2,128)(2,1)S(1)}, bf16[2,4096]{1,0:T(2,128)(2,1)S(1)}, u32[]{:S(2)}, u32[]{:S(2)}) collective-permute-start(bf16[2,4096]{1,0:T(2,128)(2,1)S(1)} %bitcast.10), channel_id=1, source_target_pairs={{0,2},{2,0},{1,3},{3,1},{4,6},{6,4},{5,7},{7,5},{8,10},{10,8},{9,1... | collective-permute-start | bytes 49160 | tf_op jit(solution)/shard_map/ppermute | solution.py:354

commit v7 on v6

--- a/solution.py
+++ b/solution.py
@@ -178,28 +178,50 @@
     return (me + turn) % count
 
 
-def pair_kernel(kept_ref, *refs):
-    outs = refs[-(kept_ref.shape[0] // refs[-1].shape[0]) :]
-    arrived = refs[: -len(outs)]
+def turn_of(me, partner, count):
+    if count & (count - 1) == 0:
+        return me ^ partner
+    return (partner - me) % count
+
+
+def exchange_plan(count):
+    if count == 4:
+        return [
+            {2: 1, 3: 0},
+            {0: 1, 2: 0},
+            {0: 2, 1: 0, 2: 3, 3: 1},
+            {0: 3, 1: 2},
+            {1: 3, 3: 2},
+        ]
+    return [{i: partner_of(i, turn, count) for i in range(count)} for turn in range(count - 1, 0, -1)]
+
+
+def pair_kernel(kept_ref, *refs, plan, tensors):
+    arrived, (own_ref, *outs) = refs[: -1 - len(plan)], refs[-1 - len(plan) :]
+    me = lax.axis_index("tensor")
+    block_rows = own_ref.shape[0]
     total = kept_ref[...]
     for piece in arrived:
         total = total + piece[...].astype(F32)
-    for turn, out_ref in enumerate(outs):
-        block_rows = out_ref.shape[0]
-        block = total[turn * block_rows : (turn + 1) * block_rows]
+    blocks = [total[turn * block_rows : (turn + 1) * block_rows] for turn in range(tensors)]
+    own_ref[...] = blocks[0]
+    for sends, out_ref in zip(plan, outs):
+        turns = {i: turn_of(i, j, tensors) for i, j in sends.items()}
+        block = blocks[turns[min(turns)]]
+        for i, turn in turns.items():
+            if turn != turns[min(turns)]:
+                block = jnp.where(me == i, blocks[turn], block)
         out_ref[...] = block.astype(out_ref.dtype)
 
 
-def pair(kept, arrived, tensors):
+def pair(kept, arrived, plan, tensors):
     rows, columns = kept.shape
-    return pl.pallas_call(
-        pair_kernel,
-        out_shape=[
-            jax.ShapeDtypeStruct((rows // tensors, columns), F32 if turn == 0 else BF16)
-            for turn in range(tensors)
-        ],
+    block = (rows // tensors, columns)
+    return pl.pallas_call(
+        functools.partial(pair_kernel, plan=plan, tensors=tensors),
+        out_shape=[jax.ShapeDtypeStruct(block, F32)] + [jax.ShapeDtypeStruct(block, BF16)] * len(plan),
         in_specs=[whole()] * (1 + len(arrived)),
-        out_specs=[whole()] * tensors,
+        out_specs=[whole()] * (1 + len(plan)),
         compiler_params=pltpu.CompilerParams(vmem_limit_bytes=8 * MIB),
         name="pair",
     )(kept, *arrived)
@@ -354,11 +376,6 @@
     return lax.ppermute(array, axis, [(i, (i + shift) % count) for i in range(count)])
 
 
-def to_partner(array, axis, turn):
-    count = lax.axis_size(axis)
-    return lax.ppermute(array, axis, [(i, partner_of(i, turn, count)) for i in range(count)])
-
-
 def body(hidden, down_matrix, residual, next_norm_scale, shrink_matrix, adapter_index):
     dp, tensors, sections = (lax.axis_size(axis) for axis in ("dp", "tensor", "section"))
     depth, _ = down_matrix.shape
@@ -379,8 +396,9 @@
     index, kept = lax.optimization_barrier((adapter_index.reshape(1, -1), kept))
     places = find_places(index, local * MOST, dp)
     arrived = [shifted(sent[s - 1], "section", s) for s in range(1, sections)]
-    own, *sums = pair(kept, arrived, tensors)
-    arrived = [to_partner(sums[s - 1], "tensor", s) for s in range(tensors - 1, 0, -1)]
+    plan = exchange_plan(tensors)
+    own, *sums = pair(kept, arrived, plan, tensors)
+    arrived = [lax.ppermute(x, "tensor", list(sends.items())) for x, sends in zip(sums, plan)]
     mixed, routed, leaving = mix(residual, places, own, arrived, local * MOST, dp)
     arrived = [shifted(leaving[s - 1], "dp", s) for s in range(1, dp)]
     values, squares = own_half(routed, gain, shrink)

time: 37 us -> 38.7 us (1.046)
  starting transfers between devices: 8.13 us -> 12.8 us
  waiting for transfers between devices: 7.57 us -> 4.42 us
    ppermute x3 -> x5, starting transfers between devices: 4.45 us -> 9.13 us  [body(): lax.ppermute(x, 'tensor', list(sends.items()))]
    ppermute x3 -> x5, waiting for transfers between devices: 3.93 us -> 0.78 us  [body(): lax.ppermute(x, 'tensor', list(sends.items()))]
  transfers between devices with their start and end apart: 6 -> 8, of which waited for: 4 -> 3; matrix products, arithmetic and copies ran while one was open for 2% -> 2% of each run, Pallas kernels for 20% -> 19%
where the time goes in v7:
time: 38.7 us; the launch traced here: 38.5 us
  Pallas kernels  19.8 us (51%)
  starting transfers between devices  12.8 us (33%)
  waiting for transfers between devices  4.42 us (11%)
  between operations  0.79 us (2%)
  local copies, waits for them, and re-layouts  0.67 us (2%)
    pallas_call x1, Pallas kernels, project(): pl.pallas_call(functools.partial(project_kernel, tensors=tensors, section...  11.3 us
    ppermute x5, starting transfers between devices, body(): lax.ppermute(x, 'tensor', list(sends.items()))  9.13 us
    pallas_call x1, Pallas kernels, fetch(): pl.pallas_call(fetch_kernel, out_shape=pltpu.VMEM((count, step, columns),...  7.09 us
    ppermute x3, starting transfers between devices, shifted(): lax.ppermute(array, axis, [(i, (i + shift) % count) for i in range(count)])  3.67 us
    ppermute x3, waiting for transfers between devices, shifted(): lax.ppermute(array, axis, [(i, (i + shift) % count) for i in range(count)])  3.64 us
    pallas_call x1, Pallas kernels, finish(): pl.pallas_call(finish_kernel, out_shape=jax.ShapeDtypeStruct((local, 1, M...  0.84 us
    ppermute x5, waiting for transfers between devices, body(): lax.ppermute(x, 'tensor', list(sends.items()))  0.78 us
  transfers between devices with their start and end apart: 8, of which 3 were waited for; matrix products, arithmetic and copies ran while one was open for 2% of the time, Pallas kernels for 19%

profile of v7, /device:TPU:0, one launch (start us, length us, event | category | flops | bytes accessed | tf_op | source)
XLA Modules:
  0.0 38.5 jit_solution(15713702109207082278)
XLA Ops:
  0.6 0.0 copy-start.1
  0.6 3.0 %collective-permute-start = (bf16[16,6656]{1,0:T(8,128)(2,1)}, bf16[16,6656]{1,0:T(8,128)(2,1)S(1)}, u32[]{:S(2)}, u32[]{:S(2)}) collective-permute-start(bf16[16,6656]{1,0:T(8,128)(2,1)} %own_ref.1), channel_id=1, source_target_pairs={{0,2},{2,0},{1,3},{3,1},{4,6},{6,4},{5,7},{7,5},{8,10},{10,8},{9,1... | collective-permute-start | bytes 638984 | tf_op jit(solution)/shard_map/ppermute | solution.py:376
  3.6 7.1 %fetch.1.held_ref = bf16[5,512,4096]{2,1,0:T(8,128)(2,1)S(1)} custom-call(bf16[6656,4096]{1,0:T(8,128)(2,1)} %weight_ref.3), custom_call_target="tpu_custom_call" | custom-call | bytes 20971520 | tf_op jit(solution)/shard_map/fetch/pallas_call | solution.py:44
  10.7 0.0 copy-start.3
  10.8 0.0 copy-start.2
  10.8 0.0 copy-start.4
  10.8 0.0 copy-start
  10.8 0.0 collective-permute-done
  10.8 0.0 copy-done.1
  10.8 11.3 %project.1 = (f32[16,4096]{1,0:T(8,128)S(1)}, bf16[1,16,4096]{2,1,0:T(8,128)(2,1)S(1)}) custom-call(bf16[16,6656]{1,0:T(8,128)(2,1)S(1)} %copy-done.1, bf16[1,16,6656]{2,1,0:T(8,128)(2,1)S(1)} %bitcast.7, bf16[5,512,4096]{2,1,0:T(8,128)(2,1)S(1)} %fetch.1.held_ref, bf16[6656,4096]{1,0:T(8,128)(2,1)} %weight_ref.3), custom_call_target="tpu_custom_call" | custom-call | flops 1744830464 | bytes 33554432 | tf_op jit(solution)/shard_map/project/pallas_call | solution.py:151
  22.1 0.1 collective-permute-start.1
  22.2 1.3 %collective-permute-done.1.refs_0_ = bf16[16,4096]{1,0:T(8,128)(2,1)S(1)} collective-permute-done((bf16[16,4096]{1,0:T(8,128)(2,1)S(1)}, bf16[16,4096]{1,0:T(8,128)(2,1)S(1)}, u32[]{:S(2)}, u32[]{:S(2)}) %collective-permute-start.1) | collective-permute-done | bytes 131104 | tf_op jit(solution)/shard_map/ppermute | solution.py:376
  23.6 0.1 pair.1
  23.6 1.3 %collective-permute-start.2 = (bf16[4,4096]{1,0:T(4,128)(2,1)S(1)}, bf16[4,4096]{1,0:T(4,128)(2,1)S(1)}, u32[]{:S(2)}, u32[]{:S(2)}) collective-permute-start(bf16[4,4096]{1,0:T(4,128)(2,1)S(1)} %get-tuple-element.22), channel_id=1, source_target_pairs={{8,4},{12,0},{9,5},{13,1},{10,6},{14,2},{11,7},{15,3},{24,20},{28,... | collective-permute-start | bytes 98312 | tf_op jit(solution)/shard_map/ppermute | solution.py:401
  24.9 3.5 %collective-permute-start.3 = (bf16[4,4096]{1,0:T(4,128)(2,1)S(1)}, bf16[4,4096]{1,0:T(4,128)(2,1)S(1)}, u32[]{:S(2)}, u32[]{:S(2)}) collective-permute-start(bf16[4,4096]{1,0:T(4,128)(2,1)S(1)} %get-tuple-element.23), channel_id=1, source_target_pairs={{0,4},{8,0},{1,5},{9,1},{2,6},{10,2},{3,7},{11,3},{16,20},{24,16},... | collective-permute-start | bytes 98312 | tf_op jit(solution)/shard_map/ppermute | solution.py:401
  28.4 1.5 %collective-permute-start.4 = (bf16[4,4096]{1,0:T(4,128)(2,1)S(1)}, bf16[4,4096]{1,0:T(4,128)(2,1)S(1)}, u32[]{:S(2)}, u32[]{:S(2)}) collective-permute-start(bf16[4,4096]{1,0:T(4,128)(2,1)S(1)} %get-tuple-element.24), channel_id=1, source_target_pairs={{0,8},{4,0},{8,12},{12,4},{1,9},{5,1},{9,13},{13,5},{2,10},{6,2},{... | collective-permute-start | bytes 98312 | tf_op jit(solution)/shard_map/ppermute | solution.py:401
  29.9 2.2 %collective-permute-start.5 = (bf16[4,4096]{1,0:T(4,128)(2,1)S(1)}, bf16[4,4096]{1,0:T(4,128)(2,1)S(1)}, u32[]{:S(2)}, u32[]{:S(2)}) collective-permute-start(bf16[4,4096]{1,0:T(4,128)(2,1)S(1)} %get-tuple-element.25), channel_id=1, source_target_pairs={{0,12},{4,8},{1,13},{5,9},{2,14},{6,10},{3,15},{7,11},{16,28},{20,... | collective-permute-start | bytes 98312 | tf_op jit(solution)/shard_map/ppermute | solution.py:401
  32.1 0.7 %collective-permute-start.6 = (bf16[4,4096]{1,0:T(4,128)(2,1)S(1)}, bf16[4,4096]{1,0:T(4,128)(2,1)S(1)}, u32[]{:S(2)}, u32[]{:S(2)}) collective-permute-start(bf16[4,4096]{1,0:T(4,128)(2,1)S(1)} %get-tuple-element.26), channel_id=1, source_target_pairs={{4,12},{12,8},{5,13},{13,9},{6,14},{14,10},{7,15},{15,11},{20,28},... | collective-permute-start | bytes 98312 | tf_op jit(solution)/shard_map/ppermute | solution.py:401
  32.8 0.0 copy-done.3
  32.8 0.1 find_places.1.places_ref
  32.9 0.0 collective-permute-done.2.refs_0_
  32.9 0.0 collective-permute-done.3.refs_1_
  32.9 0.0 collective-permute-done.4.refs_2_
  32.9 0.8 %collective-permute-done.5.refs_3_ = bf16[4,4096]{1,0:T(4,128)(2,1)S(1)} collective-permute-done((bf16[4,4096]{1,0:T(4,128)(2,1)S(1)}, bf16[4,4096]{1,0:T(4,128)(2,1)S(1)}, u32[]{:S(2)}, u32[]{:S(2)}) %collective-permute-start.5) | collective-permute-done | bytes 32800 | tf_op jit(solution)/shard_map/ppermute | solution.py:401
  33.7 0.0 collective-permute-done.6.refs_4_
  33.7 0.0 copy-done.2
  33.7 0.1 mix.1
  33.9 0.6 %collective-permute-start.7 = (bf16[2,4096]{1,0:T(2,128)(2,1)S(1)}, bf16[2,4096]{1,0:T(2,128)(2,1)S(1)}, u32[]{:S(2)}, u32[]{:S(2)}) collective-permute-start(bf16[2,4096]{1,0:T(2,128)(2,1)S(1)} %bitcast.10), channel_id=1, source_target_pairs={{0,2},{2,0},{1,3},{3,1},{4,6},{6,4},{5,7},{7,5},{8,10},{10,8},{9,1... | collective-permute-start | bytes 49160 | tf_op jit(solution)/shard_map/ppermute | solution.py:376
  34.5 0.6 %copy.8 = bf16[4,4096]{1,0:T(4,128)(2,1)} copy(bf16[4,4096]{1,0:T(4,128)(2,1)S(1)} %get-tuple-element.32) | data formatting | bytes 65536
  35.1 0.3 own_half.1
  35.4 2.3 %collective-permute-done.7.refs_0_ = bf16[2,4096]{1,0:T(2,128)(2,1)S(1)} collective-permute-done((bf16[2,4096]{1,0:T(2,128)(2,1)S(1)}, bf16[2,4096]{1,0:T(2,128)(2,1)S(1)}, u32[]{:S(2)}, u32[]{:S(2)}) %collective-permute-start.7) | collective-permute-done | bytes 16416 | tf_op jit(solution)/shard_map/ppermute | solution.py:376
  37.7 0.8 %finish.1 = f32[1,1,2,64]{3,2,1,0:T(2,128)} custom-call(f32[2,64]{1,0:T(2,128)S(1)} %get-tuple-element.29.values_ref, f32[2,64]{1,0:T(2,128)S(1)} %get-tuple-element.30.squares_ref, bf16[1,8192]{1,0:T(2,128)(2,1)S(1)} %broadcast_in_dim.3.gain_ref, bf16[1,64,8192]{2,1,0:T(8,128)(2,1)S(1)} %bitcast.6, bf16[2,4096]{1,0:T(2,128)(2,1)S(1)} %collective-permute-done.7.refs_0_), custom_call_target="tpu_custom_call" | custom-call | tf_op jit(solution)/shard_map/finish/pallas_call | solution.py:364
  (3 shorter events, 0.0 us)
Async XLA Ops:
  0.6 10.2 %copy-start.1 = (bf16[16,6656]{1,0:T(8,128)(2,1)S(1)}, bf16[16,6656]{1,0:T(8,128)(2,1)}, u32[]{:S(2)}) copy-start(bf16[16,6656]{1,0:T(8,128)(2,1)} %own_ref.1) | copy-start | bytes 638980
  0.6 10.2 %collective-permute-start = (bf16[16,6656]{1,0:T(8,128)(2,1)}, bf16[16,6656]{1,0:T(8,128)(2,1)S(1)}, u32[]{:S(2)}, u32[]{:S(2)}) collective-permute-start(bf16[16,6656]{1,0:T(8,128)(2,1)} %own_ref.1), channel_id=1, source_target_pairs={{0,2},{2,0},{1,3},{3,1},{4,6},{6,4},{5,7},{7,5},{8,10},{10,8},{9,1... | collective-permute-start | bytes 638984 | tf_op jit(solution)/shard_map/ppermute | solution.py:376
  10.7 22.1 %copy-start.3 = (s32[4,1]{0,1:T(1,128)S(1)}, s32[4,1]{0,1:T(1,128)}, u32[]{:S(2)}) copy-start(s32[4,1]{0,1:T(1,128)} %param.11) | copy-start | bytes 52
  10.8 23.0 %copy-start.2 = (bf16[4,4096]{1,0:T(4,128)(2,1)S(1)}, bf16[4,4096]{1,0:T(4,128)(2,1)}, u32[]{:S(2)}) copy-start(bf16[4,4096]{1,0:T(4,128)(2,1)} %residual_ref.1) | copy-start | bytes 98308
  10.8 23.7 %copy-start.4 = (bf16[8192]{0:T(1024)(128)(2,1)S(1)}, bf16[8192]{0:T(1024)(128)(2,1)}, u32[]{:S(2)}) copy-start(bf16[8192]{0:T(1024)(128)(2,1)} %param.9) | copy-start | bytes 49156
  10.8 24.3 %copy-start = (bf16[1,8192,64]{1,2,0:T(8,128)(2,1)S(1)}, bf16[1,8192,64]{1,2,0:T(8,128)(2,1)}, u32[]{:S(2)}) copy-start(bf16[1,8192,64]{1,2,0:T(8,128)(2,1)} %param.10) | copy-start | bytes 3145732
  22.1 1.4 %collective-permute-start.1 = (bf16[16,4096]{1,0:T(8,128)(2,1)S(1)}, bf16[16,4096]{1,0:T(8,128)(2,1)S(1)}, u32[]{:S(2)}, u32[]{:S(2)}) collective-permute-start(bf16[16,4096]{1,0:T(8,128)(2,1)S(1)} %bitcast.9), channel_id=1, source_target_pairs={{0,1},{1,0},{2,3},{3,2},{4,5},{5,4},{6,7},{7,6},{8,9},{9,8},{10,11... | collective-permute-start | bytes 393224 | tf_op jit(solution)/shard_map/ppermute | solution.py:376
  23.6 9.3 %collective-permute-start.2 = (bf16[4,4096]{1,0:T(4,128)(2,1)S(1)}, bf16[4,4096]{1,0:T(4,128)(2,1)S(1)}, u32[]{:S(2)}, u32[]{:S(2)}) collective-permute-start(bf16[4,4096]{1,0:T(4,128)(2,1)S(1)} %get-tuple-element.22), channel_id=1, source_target_pairs={{8,4},{12,0},{9,5},{13,1},{10,6},{14,2},{11,7},{15,3},{24,20},{28,... | collective-permute-start | bytes 98312 | tf_op jit(solution)/shard_map/ppermute | solution.py:401
  24.9 8.0 %collective-permute-start.3 = (bf16[4,4096]{1,0:T(4,128)(2,1)S(1)}, bf16[4,4096]{1,0:T(4,128)(2,1)S(1)}, u32[]{:S(2)}, u32[]{:S(2)}) collective-permute-start(bf16[4,4096]{1,0:T(4,128)(2,1)S(1)} %get-tuple-element.23), channel_id=1, source_target_pairs={{0,4},{8,0},{1,5},{9,1},{2,6},{10,2},{3,7},{11,3},{16,20},{24,16},... | collective-permute-start | bytes 98312 | tf_op jit(solution)/shard_map/ppermute | solution.py:401
  28.4 4.5 %collective-permute-start.4 = (bf16[4,4096]{1,0:T(4,128)(2,1)S(1)}, bf16[4,4096]{1,0:T(4,128)(2,1)S(1)}, u32[]{:S(2)}, u32[]{:S(2)}) collective-permute-start(bf16[4,4096]{1,0:T(4,128)(2,1)S(1)} %get-tuple-element.24), channel_id=1, source_target_pairs={{0,8},{4,0},{8,12},{12,4},{1,9},{5,1},{9,13},{13,5},{2,10},{6,2},{... | collective-permute-start | bytes 98312 | tf_op jit(solution)/shard_map/ppermute | solution.py:401
  29.9 3.8 %collective-permute-start.5 = (bf16[4,4096]{1,0:T(4,128)(2,1)S(1)}, bf16[4,4096]{1,0:T(4,128)(2,1)S(1)}, u32[]{:S(2)}, u32[]{:S(2)}) collective-permute-start(bf16[4,4096]{1,0:T(4,128)(2,1)S(1)} %get-tuple-element.25), channel_id=1, source_target_pairs={{0,12},{4,8},{1,13},{5,9},{2,14},{6,10},{3,15},{7,11},{16,28},{20,... | collective-permute-start | bytes 98312 | tf_op jit(solution)/shard_map/ppermute | solution.py:401
  32.1 1.6 %collective-permute-start.6 = (bf16[4,4096]{1,0:T(4,128)(2,1)S(1)}, bf16[4,4096]{1,0:T(4,128)(2,1)S(1)}, u32[]{:S(2)}, u32[]{:S(2)}) collective-permute-start(bf16[4,4096]{1,0:T(4,128)(2,1)S(1)} %get-tuple-element.26), channel_id=1, source_target_pairs={{4,12},{12,8},{5,13},{13,9},{6,14},{14,10},{7,15},{15,11},{20,28},... | collective-permute-start | bytes 98312 | tf_op jit(solution)/shard_map/ppermute | solution.py:401
  33.9 3.8 %collective-permute-start.7 = (bf16[2,4096]{1,0:T(2,128)(2,1)S(1)}, bf16[2,4096]{1,0:T(2,128)(2,1)S(1)}, u32[]{:S(2)}, u32[]{:S(2)}) collective-permute-start(bf16[2,4096]{1,0:T(2,128)(2,1)S(1)} %bitcast.10), channel_id=1, source_target_pairs={{0,2},{2,0},{1,3},{3,1},{4,6},{6,4},{5,7},{7,5},{8,10},{10,8},{9,1... | collective-permute-start | bytes 49160 | tf_op jit(solution)/shard_map/ppermute | solution.py:376

commit v8 on v7

--- a/solution.py
+++ b/solution.py
@@ -186,14 +186,9 @@
 
 def exchange_plan(count):
     if count == 4:
-        return [
-            {2: 1, 3: 0},
-            {0: 1, 2: 0},
-            {0: 2, 1: 0, 2: 3, 3: 1},
-            {0: 3, 1: 2},
-            {1: 3, 3: 2},
-        ]
-    return [{i: partner_of(i, turn, count) for i in range(count)} for turn in range(count - 1, 0, -1)]
+        return [(1, 3, 2, 0), (2, 1, 0, 3), (3, 0, 1, 2), (0, 2, 3, 1)]
+    turns = range(count - 1, 0, -1)
+    return [tuple(partner_of(i, turn, count) for i in range(count)) for turn in turns]
 
 
 def pair_kernel(kept_ref, *refs, plan, tensors):
@@ -205,11 +200,12 @@
         total = total + piece[...].astype(F32)
     blocks = [total[turn * block_rows : (turn + 1) * block_rows] for turn in range(tensors)]
     own_ref[...] = blocks[0]
-    for sends, out_ref in zip(plan, outs):
-        turns = {i: turn_of(i, j, tensors) for i, j in sends.items()}
-        block = blocks[turns[min(turns)]]
-        for i, turn in turns.items():
-            if turn != turns[min(turns)]:
+    blocks[0] = jnp.zeros_like(blocks[0])
+    for receivers, out_ref in zip(plan, outs):
+        turns = [turn_of(i, j, tensors) for i, j in enumerate(receivers)]
+        block = blocks[turns[0]]
+        for i, turn in enumerate(turns):
+            if turn != turns[0]:
                 block = jnp.where(me == i, blocks[turn], block)
         out_ref[...] = block.astype(out_ref.dtype)
 
@@ -398,7 +394,7 @@
     arrived = [shifted(sent[s - 1], "section", s) for s in range(1, sections)]
     plan = exchange_plan(tensors)
     own, *sums = pair(kept, arrived, plan, tensors)
-    arrived = [lax.ppermute(x, "tensor", list(sends.items())) for x, sends in zip(sums, plan)]
+    arrived = [lax.ppermute(x, "tensor", list(enumerate(p))) for x, p in zip(sums, plan)]
     mixed, routed, leaving = mix(residual, places, own, arrived, local * MOST, dp)
     arrived = [shifted(leaving[s - 1], "dp", s) for s in range(1, dp)]
     values, squares = own_half(routed, gain, shrink)

time: 38.7 us -> 39.8 us (1.028)
  the two profiles are of different devices: /device:TPU:0 before, /device:TPU:8 now
where the time goes in v8:
time: 39.8 us; the launch traced here: 39.6 us
  Pallas kernels  19.8 us (50%)
  starting transfers between devices  11.5 us (29%)
  waiting for transfers between devices  6.83 us (17%)
  between operations  0.77 us (2%)
  local copies, waits for them, and re-layouts  0.67 us (2%)
    pallas_call x1, Pallas kernels, project(): pl.pallas_call(functools.partial(project_kernel, tensors=tensors, section...  11.3 us
    ppermute x4, starting transfers between devices, body(): lax.ppermute(x, 'tensor', list(enumerate(p)))  9.28 us
    pallas_call x1, Pallas kernels, fetch(): pl.pallas_call(fetch_kernel, out_shape=pltpu.VMEM((count, step, columns),...  7.09 us
    ppermute x3, waiting for transfers between devices, shifted(): lax.ppermute(array, axis, [(i, (i + shift) % count) for i in range(count)])  3.64 us
    ppermute x4, waiting for transfers between devices, body(): lax.ppermute(x, 'tensor', list(enumerate(p)))  3.19 us
    ppermute x3, starting transfers between devices, shifted(): lax.ppermute(array, axis, [(i, (i + shift) % count) for i in range(count)])  2.23 us
    pallas_call x1, Pallas kernels, finish(): pl.pallas_call(finish_kernel, out_shape=jax.ShapeDtypeStruct((local, 1, M...  0.84 us
  transfers between devices with their start and end apart: 7, of which 4 were waited for; matrix products, arithmetic and copies ran while one was open for 2% of the time, Pallas kernels for 19%

profile of v8, /device:TPU:8, one launch (start us, length us, event | category | flops | bytes accessed | tf_op | source)
XLA Modules:
  0.0 39.6 jit_solution(4738808674658519153)
XLA Ops:
  0.6 0.0 copy-start.1
  0.6 1.6 %collective-permute-start = (bf16[16,6656]{1,0:T(8,128)(2,1)}, bf16[16,6656]{1,0:T(8,128)(2,1)S(1)}, u32[]{:S(2)}, u32[]{:S(2)}) collective-permute-start(bf16[16,6656]{1,0:T(8,128)(2,1)} %own_ref.1), channel_id=1, source_target_pairs={{0,2},{2,0},{1,3},{3,1},{4,6},{6,4},{5,7},{7,5},{8,10},{10,8},{9,1... | collective-permute-start | bytes 638984 | tf_op jit(solution)/shard_map/ppermute | solution.py:372
  2.2 7.1 %fetch.1.held_ref = bf16[5,512,4096]{2,1,0:T(8,128)(2,1)S(1)} custom-call(bf16[6656,4096]{1,0:T(8,128)(2,1)} %weight_ref.3), custom_call_target="tpu_custom_call" | custom-call | bytes 20971520 | tf_op jit(solution)/shard_map/fetch/pallas_call | solution.py:44
  9.3 0.0 copy-start.3
  9.3 0.0 copy-start.2
  9.3 0.0 copy-start.4
  9.3 0.0 copy-start
  9.3 0.0 collective-permute-done
  9.4 0.0 copy-done.1
  9.4 11.3 %project.1 = (f32[16,4096]{1,0:T(8,128)S(1)}, bf16[1,16,4096]{2,1,0:T(8,128)(2,1)S(1)}) custom-call(bf16[16,6656]{1,0:T(8,128)(2,1)S(1)} %copy-done.1, bf16[1,16,6656]{2,1,0:T(8,128)(2,1)S(1)} %bitcast.7, bf16[5,512,4096]{2,1,0:T(8,128)(2,1)S(1)} %fetch.1.held_ref, bf16[6656,4096]{1,0:T(8,128)(2,1)} %weight_ref.3), custom_call_target="tpu_custom_call" | custom-call | flops 1744830464 | bytes 33554432 | tf_op jit(solution)/shard_map/project/pallas_call | solution.py:151
  20.7 0.1 collective-permute-start.1
  20.8 1.3 %collective-permute-done.1.refs_0_ = bf16[16,4096]{1,0:T(8,128)(2,1)S(1)} collective-permute-done((bf16[16,4096]{1,0:T(8,128)(2,1)S(1)}, bf16[16,4096]{1,0:T(8,128)(2,1)S(1)}, u32[]{:S(2)}, u32[]{:S(2)}) %collective-permute-start.1) | collective-permute-done | bytes 131104 | tf_op jit(solution)/shard_map/ppermute | solution.py:372
  22.1 0.1 pair.1
  22.2 4.5 %collective-permute-start.2 = (bf16[4,4096]{1,0:T(4,128)(2,1)S(1)}, bf16[4,4096]{1,0:T(4,128)(2,1)S(1)}, u32[]{:S(2)}, u32[]{:S(2)}) collective-permute-start(bf16[4,4096]{1,0:T(4,128)(2,1)S(1)} %get-tuple-element.21), channel_id=1, source_target_pairs={{0,4},{4,12},{8,8},{12,0},{1,5},{5,13},{9,9},{13,1},{2,6},{6,14},{... | collective-permute-start | bytes 98312 | tf_op jit(solution)/shard_map/ppermute | solution.py:397
  26.7 0.7 %collective-permute-start.3 = (bf16[4,4096]{1,0:T(4,128)(2,1)S(1)}, bf16[4,4096]{1,0:T(4,128)(2,1)S(1)}, u32[]{:S(2)}, u32[]{:S(2)}) collective-permute-start(bf16[4,4096]{1,0:T(4,128)(2,1)S(1)} %get-tuple-element.22), channel_id=1, source_target_pairs={{0,8},{4,4},{8,0},{12,12},{1,9},{5,5},{9,1},{13,13},{2,10},{6,6},{... | collective-permute-start | bytes 98312 | tf_op jit(solution)/shard_map/ppermute | solution.py:397
  27.4 0.7 %collective-permute-start.4 = (bf16[4,4096]{1,0:T(4,128)(2,1)S(1)}, bf16[4,4096]{1,0:T(4,128)(2,1)S(1)}, u32[]{:S(2)}, u32[]{:S(2)}) collective-permute-start(bf16[4,4096]{1,0:T(4,128)(2,1)S(1)} %get-tuple-element.23), channel_id=1, source_target_pairs={{0,12},{4,0},{8,4},{12,8},{1,13},{5,1},{9,5},{13,9},{2,14},{6,2},{... | collective-permute-start | bytes 98312 | tf_op jit(solution)/shard_map/ppermute | solution.py:397
  28.1 3.4 %collective-permute-start.5 = (bf16[4,4096]{1,0:T(4,128)(2,1)S(1)}, bf16[4,4096]{1,0:T(4,128)(2,1)S(1)}, u32[]{:S(2)}, u32[]{:S(2)}) collective-permute-start(bf16[4,4096]{1,0:T(4,128)(2,1)S(1)} %get-tuple-element.24), channel_id=1, source_target_pairs={{0,0},{4,8},{8,12},{12,4},{1,1},{5,9},{9,13},{13,5},{2,2},{6,10},{... | collective-permute-start | bytes 98312 | tf_op jit(solution)/shard_map/ppermute | solution.py:397
  31.5 0.0 copy-done.3
  31.5 0.1 find_places.1.places_ref
  31.6 0.0 collective-permute-done.2.refs_0_
  31.6 0.0 collective-permute-done.3.refs_1_
  31.6 0.1 collective-permute-done.4.refs_2_
  31.8 3.1 %collective-permute-done.5.refs_3_ = bf16[4,4096]{1,0:T(4,128)(2,1)S(1)} collective-permute-done((bf16[4,4096]{1,0:T(4,128)(2,1)S(1)}, bf16[4,4096]{1,0:T(4,128)(2,1)S(1)}, u32[]{:S(2)}, u32[]{:S(2)}) %collective-permute-start.5) | collective-permute-done | bytes 32800 | tf_op jit(solution)/shard_map/ppermute | solution.py:397
  34.8 0.0 copy-done.2
  34.8 0.1 mix.1
  35.0 0.6 %collective-permute-start.6 = (bf16[2,4096]{1,0:T(2,128)(2,1)S(1)}, bf16[2,4096]{1,0:T(2,128)(2,1)S(1)}, u32[]{:S(2)}, u32[]{:S(2)}) collective-permute-start(bf16[2,4096]{1,0:T(2,128)(2,1)S(1)} %bitcast.10), channel_id=1, source_target_pairs={{0,2},{2,0},{1,3},{3,1},{4,6},{6,4},{5,7},{7,5},{8,10},{10,8},{9,1... | collective-permute-start | bytes 49160 | tf_op jit(solution)/shard_map/ppermute | solution.py:372
  35.6 0.0 copy-done.4
  35.6 0.6 %copy.8 = bf16[4,4096]{1,0:T(4,128)(2,1)} copy(bf16[4,4096]{1,0:T(4,128)(2,1)S(1)} %get-tuple-element.30) | data formatting | bytes 65536
  36.2 0.0 copy-done
  36.2 0.3 own_half.1
  36.5 2.3 %collective-permute-done.6.refs_0_ = bf16[2,4096]{1,0:T(2,128)(2,1)S(1)} collective-permute-done((bf16[2,4096]{1,0:T(2,128)(2,1)S(1)}, bf16[2,4096]{1,0:T(2,128)(2,1)S(1)}, u32[]{:S(2)}, u32[]{:S(2)}) %collective-permute-start.6) | collective-permute-done | bytes 16416 | tf_op jit(solution)/shard_map/ppermute | solution.py:372
  38.8 0.8 %finish.1 = f32[1,1,2,64]{3,2,1,0:T(2,128)} custom-call(f32[2,64]{1,0:T(2,128)S(1)} %get-tuple-element.27.values_ref, f32[2,64]{1,0:T(2,128)S(1)} %get-tuple-element.28.squares_ref, bf16[1,8192]{1,0:T(2,128)(2,1)S(1)} %broadcast_in_dim.3.gain_ref, bf16[1,64,8192]{2,1,0:T(8,128)(2,1)S(1)} %bitcast.6, bf16[2,4096]{1,0:T(2,128)(2,1)S(1)} %collective-permute-done.6.refs_0_), custom_call_target="tpu_custom_call" | custom-call | tf_op jit(solution)/shard_map/finish/pallas_call | solution.py:360
  (1 shorter events, 0.0 us)
Async XLA Ops:
  0.6 8.7 %copy-start.1 = (bf16[16,6656]{1,0:T(8,128)(2,1)S(1)}, bf16[16,6656]{1,0:T(8,128)(2,1)}, u32[]{:S(2)}) copy-start(bf16[16,6656]{1,0:T(8,128)(2,1)} %own_ref.1) | copy-start | bytes 638980
  0.6 8.7 %collective-permute-start = (bf16[16,6656]{1,0:T(8,128)(2,1)}, bf16[16,6656]{1,0:T(8,128)(2,1)S(1)}, u32[]{:S(2)}, u32[]{:S(2)}) collective-permute-start(bf16[16,6656]{1,0:T(8,128)(2,1)} %own_ref.1), channel_id=1, source_target_pairs={{0,2},{2,0},{1,3},{3,1},{4,6},{6,4},{5,7},{7,5},{8,10},{10,8},{9,1... | collective-permute-start | bytes 638984 | tf_op jit(solution)/shard_map/ppermute | solution.py:372
  9.3 22.2 %copy-start.3 = (s32[4,1]{0,1:T(1,128)S(1)}, s32[4,1]{0,1:T(1,128)}, u32[]{:S(2)}) copy-start(s32[4,1]{0,1:T(1,128)} %param.11) | copy-start | bytes 52
  9.3 25.5 %copy-start.2 = (bf16[4,4096]{1,0:T(4,128)(2,1)S(1)}, bf16[4,4096]{1,0:T(4,128)(2,1)}, u32[]{:S(2)}) copy-start(bf16[4,4096]{1,0:T(4,128)(2,1)} %residual_ref.1) | copy-start | bytes 98308
  9.3 26.3 %copy-start.4 = (bf16[8192]{0:T(1024)(128)(2,1)S(1)}, bf16[8192]{0:T(1024)(128)(2,1)}, u32[]{:S(2)}) copy-start(bf16[8192]{0:T(1024)(128)(2,1)} %param.9) | copy-start | bytes 49156
  9.3 26.9 %copy-start = (bf16[1,8192,64]{1,2,0:T(8,128)(2,1)S(1)}, bf16[1,8192,64]{1,2,0:T(8,128)(2,1)}, u32[]{:S(2)}) copy-start(bf16[1,8192,64]{1,2,0:T(8,128)(2,1)} %param.10) | copy-start | bytes 3145732
  20.7 1.4 %collective-permute-start.1 = (bf16[16,4096]{1,0:T(8,128)(2,1)S(1)}, bf16[16,4096]{1,0:T(8,128)(2,1)S(1)}, u32[]{:S(2)}, u32[]{:S(2)}) collective-permute-start(bf16[16,4096]{1,0:T(8,128)(2,1)S(1)} %bitcast.9), channel_id=1, source_target_pairs={{0,1},{1,0},{2,3},{3,2},{4,5},{5,4},{6,7},{7,6},{8,9},{9,8},{10,11... | collective-permute-start | bytes 393224 | tf_op jit(solution)/shard_map/ppermute | solution.py:372
  22.2 9.4 %collective-permute-start.2 = (bf16[4,4096]{1,0:T(4,128)(2,1)S(1)}, bf16[4,4096]{1,0:T(4,128)(2,1)S(1)}, u32[]{:S(2)}, u32[]{:S(2)}) collective-permute-start(bf16[4,4096]{1,0:T(4,128)(2,1)S(1)} %get-tuple-element.21), channel_id=1, source_target_pairs={{0,4},{4,12},{8,8},{12,0},{1,5},{5,13},{9,9},{13,1},{2,6},{6,14},{... | collective-permute-start | bytes 98312 | tf_op jit(solution)/shard_map/ppermute | solution.py:397
  26.7 4.9 %collective-permute-start.3 = (bf16[4,4096]{1,0:T(4,128)(2,1)S(1)}, bf16[4,4096]{1,0:T(4,128)(2,1)S(1)}, u32[]{:S(2)}, u32[]{:S(2)}) collective-permute-start(bf16[4,4096]{1,0:T(4,128)(2,1)S(1)} %get-tuple-element.22), channel_id=1, source_target_pairs={{0,8},{4,4},{8,0},{12,12},{1,9},{5,5},{9,1},{13,13},{2,10},{6,6},{... | collective-permute-start | bytes 98312 | tf_op jit(solution)/shard_map/ppermute | solution.py:397
  27.4 4.4 %collective-permute-start.4 = (bf16[4,4096]{1,0:T(4,128)(2,1)S(1)}, bf16[4,4096]{1,0:T(4,128)(2,1)S(1)}, u32[]{:S(2)}, u32[]{:S(2)}) collective-permute-start(bf16[4,4096]{1,0:T(4,128)(2,1)S(1)} %get-tuple-element.23), channel_id=1, source_target_pairs={{0,12},{4,0},{8,4},{12,8},{1,13},{5,1},{9,5},{13,9},{2,14},{6,2},{... | collective-permute-start | bytes 98312 | tf_op jit(solution)/shard_map/ppermute | solution.py:397
  28.1 6.7 %collective-permute-start.5 = (bf16[4,4096]{1,0:T(4,128)(2,1)S(1)}, bf16[4,4096]{1,0:T(4,128)(2,1)S(1)}, u32[]{:S(2)}, u32[]{:S(2)}) collective-permute-start(bf16[4,4096]{1,0:T(4,128)(2,1)S(1)} %get-tuple-element.24), channel_id=1, source_target_pairs={{0,0},{4,8},{8,12},{12,4},{1,1},{5,9},{9,13},{13,5},{2,2},{6,10},{... | collective-permute-start | bytes 98312 | tf_op jit(solution)/shard_map/ppermute | solution.py:397
  35.0 3.8 %collective-permute-start.6 = (bf16[2,4096]{1,0:T(2,128)(2,1)S(1)}, bf16[2,4096]{1,0:T(2,128)(2,1)S(1)}, u32[]{:S(2)}, u32[]{:S(2)}) collective-permute-start(bf16[2,4096]{1,0:T(2,128)(2,1)S(1)} %bitcast.10), channel_id=1, source_target_pairs={{0,2},{2,0},{1,3},{3,1},{4,6},{6,4},{5,7},{7,5},{8,10},{10,8},{9,1... | collective-permute-start | bytes 49160 | tf_op jit(solution)/shard_map/ppermute | solution.py:372

commit v9 on v8

--- a/solution.py
+++ b/solution.py
@@ -134,8 +134,11 @@
             rows = total_ref[pl.ds(first, group), lanes]
             turned.append(pltpu.roll(rows, (sections - section) % sections * block_rows, 0))
         for s in range(sections):
-            part = slice(s * block_rows, (s + 1) * block_rows)
-            rows = jnp.concatenate([block[part] for block in turned], axis=0)
+            parts = [s] + [(s + 1) % sections] * (tensors - 1)
+            rows = jnp.concatenate(
+                [block[p * block_rows : (p + 1) * block_rows] for p, block in zip(parts, turned)],
+                axis=0,
+            )
             if s == 0:
                 kept_ref[:, lanes] = rows
             else:
@@ -186,7 +189,7 @@
 
 def exchange_plan(count):
     if count == 4:
-        return [(1, 3, 2, 0), (2, 1, 0, 3), (3, 0, 1, 2), (0, 2, 3, 1)]
+        return [(2, 3, 1, 0), (3, 2, 0, 1), (1, 0, 3, 2)]
     turns = range(count - 1, 0, -1)
     return [tuple(partner_of(i, turn, count) for i in range(count)) for turn in turns]
 
@@ -200,7 +203,6 @@
         total = total + piece[...].astype(F32)
     blocks = [total[turn * block_rows : (turn + 1) * block_rows] for turn in range(tensors)]
     own_ref[...] = blocks[0]
-    blocks[0] = jnp.zeros_like(blocks[0])
     for receivers, out_ref in zip(plan, outs):
         turns = [turn_of(i, j, tensors) for i, j in enumerate(receivers)]
         block = blocks[turns[0]]
@@ -236,19 +238,26 @@
     return jnp.logical_and(row == adapter, rank_of == slot % MOST).astype(F32)
 
 
-def places_kernel(index_ref, places_ref, *, slots, owners):
+def prepare_kernel(index_ref, shrink_ref, places_ref, out_ref, sem, *, slots, owners):
+    copy = pltpu.make_async_copy(shrink_ref, out_ref, sem)
+    copy.start()
     places_ref[...] = places_of(index_ref[...], slots, owners, slots // MOST)
-
-
-def find_places(index, slots, owners):
-    return pl.pallas_call(
-        functools.partial(places_kernel, slots=slots, owners=owners),
-        out_shape=jax.ShapeDtypeStruct((slots * owners, index.shape[1]), F32),
-        in_specs=[whole()],
-        out_specs=whole(),
+    copy.wait()
+
+
+def prepare(index, shrink, slots, owners):
+    return pl.pallas_call(
+        functools.partial(prepare_kernel, slots=slots, owners=owners),
+        out_shape=(
+            jax.ShapeDtypeStruct((slots * owners, index.shape[1]), F32),
+            pltpu.VMEM(shrink.shape, shrink.dtype),
+        ),
+        in_specs=[whole(), pl.BlockSpec(memory_space=pl.ANY)],
+        out_specs=(whole(), whole()),
+        scratch_shapes=[pltpu.SemaphoreType.DMA],
         compiler_params=pltpu.CompilerParams(vmem_limit_bytes=1 * MIB),
-        name="find_places",
-    )(index)
+        name="prepare",
+    )(index, pltpu.with_memory_space_constraint(shrink, pltpu.HBM))
 
 
 def mix_kernel(residual_ref, places_ref, own_ref, *refs):
@@ -372,6 +381,16 @@
     return lax.ppermute(array, axis, [(i, (i + shift) % count) for i in range(count)])
 
 
+def across(array, receivers):
+    sections = lax.axis_size("section")
+    pairs = [
+        (i * sections + s, j * sections + (s + 1) % sections)
+        for i, j in enumerate(receivers)
+        for s in range(sections)
+    ]
+    return lax.ppermute(array, ("tensor", "section"), pairs)
+
+
 def body(hidden, down_matrix, residual, next_norm_scale, shrink_matrix, adapter_index):
     dp, tensors, sections = (lax.axis_size(axis) for axis in ("dp", "tensor", "section"))
     depth, _ = down_matrix.shape
@@ -390,11 +409,11 @@
     in_vmem = [pltpu.with_memory_space_constraint(x, pltpu.VMEM) for x in (hidden, others, held)]
     kept, sent = project(*in_vmem, down_matrix, tensors, sections)
     index, kept = lax.optimization_barrier((adapter_index.reshape(1, -1), kept))
-    places = find_places(index, local * MOST, dp)
+    places, shrink = prepare(index, shrink, local * MOST, dp)
     arrived = [shifted(sent[s - 1], "section", s) for s in range(1, sections)]
     plan = exchange_plan(tensors)
     own, *sums = pair(kept, arrived, plan, tensors)
-    arrived = [lax.ppermute(x, "tensor", list(enumerate(p))) for x, p in zip(sums, plan)]
+    arrived = [across(x, receivers) for x, receivers in zip(sums, plan)]
     mixed, routed, leaving = mix(residual, places, own, arrived, local * MOST, dp)
     arrived = [shifted(leaving[s - 1], "dp", s) for s in range(1, dp)]
     values, squares = own_half(routed, gain, shrink)

time: 39.8 us -> 36 us (0.905)
  the two profiles are of different devices: /device:TPU:8 before, /device:TPU:0 now
where the time goes in v9:
time: 36 us; the launch traced here: 35.8 us
  Pallas kernels  20.9 us (58%)
  starting transfers between devices  7.62 us (21%)
  waiting for transfers between devices  5.95 us (17%)
  between operations  0.73 us (2%)
  local copies, waits for them, and re-layouts  0.66 us (2%)
    pallas_call x1, Pallas kernels, project(): pl.pallas_call(functools.partial(project_kernel, tensors=tensors, section...  11.3 us
    pallas_call x1, Pallas kernels, fetch(): pl.pallas_call(fetch_kernel, out_shape=pltpu.VMEM((count, step, columns),...  7.09 us
    ppermute x3, starting transfers between devices, across(): return lax.ppermute(array, ('tensor', 'section'), pairs)  3.94 us
    ppermute x3, starting transfers between devices, shifted(): lax.ppermute(array, axis, [(i, (i + shift) % count) for i in range(count)])  3.67 us
    ppermute x3, waiting for transfers between devices, shifted(): lax.ppermute(array, axis, [(i, (i + shift) % count) for i in range(count)])  3.64 us
    ppermute x3, waiting for transfers between devices, across(): return lax.ppermute(array, ('tensor', 'section'), pairs)  2.31 us
    pallas_call x1, Pallas kernels, prepare(): pl.pallas_call(functools.partial(prepare_kernel, slots=slots, owners=owne...  1.23 us
    pallas_call x1, Pallas kernels, finish(): pl.pallas_call(finish_kernel, out_shape=jax.ShapeDtypeStruct((local, 1, M...  0.84 us
  transfers between devices with their start and end apart: 6, of which 4 were waited for; matrix products, arithmetic and copies ran while one was open for 2% of the time, Pallas kernels for 24%

profile of v9, /device:TPU:0, one launch (start us, length us, event | category | flops | bytes accessed | tf_op | source)
XLA Modules:
  0.0 35.8 jit_solution(16487563736736033159)
XLA Ops:
  0.6 0.0 copy-start
  0.6 3.0 %collective-permute-start = (bf16[16,6656]{1,0:T(8,128)(2,1)}, bf16[16,6656]{1,0:T(8,128)(2,1)S(1)}, u32[]{:S(2)}, u32[]{:S(2)}) collective-permute-start(bf16[16,6656]{1,0:T(8,128)(2,1)} %own_ref.1), channel_id=1, source_target_pairs={{0,2},{2,0},{1,3},{3,1},{4,6},{6,4},{5,7},{7,5},{8,10},{10,8},{9,1... | collective-permute-start | bytes 638984 | tf_op jit(solution)/shard_map/ppermute | solution.py:381
  3.6 7.1 %fetch.1.held_ref = bf16[5,512,4096]{2,1,0:T(8,128)(2,1)S(1)} custom-call(bf16[6656,4096]{1,0:T(8,128)(2,1)} %weight_ref.3), custom_call_target="tpu_custom_call" | custom-call | bytes 20971520 | tf_op jit(solution)/shard_map/fetch/pallas_call | solution.py:44
  10.7 0.0 copy-start.2
  10.8 0.0 copy-start.1
  10.8 0.0 copy-start.3
  10.8 0.0 collective-permute-done
  10.8 0.0 copy-done
  10.8 11.3 %project.1 = (f32[16,4096]{1,0:T(8,128)S(1)}, bf16[1,16,4096]{2,1,0:T(8,128)(2,1)S(1)}) custom-call(bf16[16,6656]{1,0:T(8,128)(2,1)S(1)} %copy-done, bf16[1,16,6656]{2,1,0:T(8,128)(2,1)S(1)} %bitcast.5, bf16[5,512,4096]{2,1,0:T(8,128)(2,1)S(1)} %fetch.1.held_ref, bf16[6656,4096]{1,0:T(8,128)(2,1)} %weight_ref.3), custom_call_target="tpu_custom_call" | custom-call | flops 1744830464 | bytes 33554432 | tf_op jit(solution)/shard_map/project/pallas_call | solution.py:154
  22.1 0.1 collective-permute-start.1
  22.1 1.3 %collective-permute-done.1.refs_0_ = bf16[16,4096]{1,0:T(8,128)(2,1)S(1)} collective-permute-done((bf16[16,4096]{1,0:T(8,128)(2,1)S(1)}, bf16[16,4096]{1,0:T(8,128)(2,1)S(1)}, u32[]{:S(2)}, u32[]{:S(2)}) %collective-permute-start.1) | collective-permute-done | bytes 131104 | tf_op jit(solution)/shard_map/ppermute | solution.py:381
  23.5 2.4 %collective-permute-start.2 = (bf16[4,4096]{1,0:T(4,128)(2,1)S(1)}, bf16[4,4096]{1,0:T(4,128)(2,1)S(1)}, u32[]{:S(2)}, u32[]{:S(2)}) collective-permute-start(bf16[4,4096]{1,0:T(4,128)(2,1)S(1)} %get-tuple-element.23), channel_id=1, source_target_pairs={{0,9},{1,8},{4,13},{5,12},{8,5},{9,4},{12,1},{13,0},{2,11},{3,10},... | collective-permute-start | bytes 98312 | tf_op jit(solution)/shard_map/ppermute | solution.py:391
  25.9 1.2 %collective-permute-start.3 = (bf16[4,4096]{1,0:T(4,128)(2,1)S(1)}, bf16[4,4096]{1,0:T(4,128)(2,1)S(1)}, u32[]{:S(2)}, u32[]{:S(2)}) collective-permute-start(bf16[4,4096]{1,0:T(4,128)(2,1)S(1)} %get-tuple-element.24), channel_id=1, source_target_pairs={{0,13},{1,12},{4,9},{5,8},{8,1},{9,0},{12,5},{13,4},{2,15},{3,14},... | collective-permute-start | bytes 98312 | tf_op jit(solution)/shard_map/ppermute | solution.py:391
  27.1 0.3 collective-permute-start.4
  27.5 0.0 copy-done.2
  27.5 1.2 %prepare.1 = (f32[4,4]{1,0:T(4,128)S(1)}, bf16[1,64,8192]{2,1,0:T(8,128)(2,1)S(1)}) custom-call(s32[1,4]{1,0:T(1,128)S(1)} %bitcast.6, bf16[1,64,8192]{2,1,0:T(8,128)(2,1)} %bitcast.9), custom_call_target="tpu_custom_call" | custom-call | tf_op jit(solution)/shard_map/prepare/pallas_call | solution.py:249
  28.7 0.0 collective-permute-done.2.refs_0_
  28.7 1.5 %collective-permute-done.3.refs_1_ = bf16[4,4096]{1,0:T(4,128)(2,1)S(1)} collective-permute-done((bf16[4,4096]{1,0:T(4,128)(2,1)S(1)}, bf16[4,4096]{1,0:T(4,128)(2,1)S(1)}, u32[]{:S(2)}, u32[]{:S(2)}) %collective-permute-start.3) | collective-permute-done | bytes 32800 | tf_op jit(solution)/shard_map/ppermute | solution.py:391
  30.2 0.8 %collective-permute-done.4.refs_2_ = bf16[4,4096]{1,0:T(4,128)(2,1)S(1)} collective-permute-done((bf16[4,4096]{1,0:T(4,128)(2,1)S(1)}, bf16[4,4096]{1,0:T(4,128)(2,1)S(1)}, u32[]{:S(2)}, u32[]{:S(2)}) %collective-permute-start.4) | collective-permute-done | bytes 32800 | tf_op jit(solution)/shard_map/ppermute | solution.py:391
  31.0 0.0 copy-done.1
  31.0 0.1 mix.1
  31.2 0.6 %collective-permute-start.5 = (bf16[2,4096]{1,0:T(2,128)(2,1)S(1)}, bf16[2,4096]{1,0:T(2,128)(2,1)S(1)}, u32[]{:S(2)}, u32[]{:S(2)}) collective-permute-start(bf16[2,4096]{1,0:T(2,128)(2,1)S(1)} %bitcast.8), channel_id=1, source_target_pairs={{0,2},{2,0},{1,3},{3,1},{4,6},{6,4},{5,7},{7,5},{8,10},{10,8},{9,1... | collective-permute-start | bytes 49160 | tf_op jit(solution)/shard_map/ppermute | solution.py:381
  31.8 0.0 copy-done.3
  31.8 0.6 %copy.8 = bf16[4,4096]{1,0:T(4,128)(2,1)} copy(bf16[4,4096]{1,0:T(4,128)(2,1)S(1)} %get-tuple-element.32) | data formatting | bytes 65536
  32.4 0.3 own_half.1
  32.7 2.3 %collective-permute-done.5.refs_0_ = bf16[2,4096]{1,0:T(2,128)(2,1)S(1)} collective-permute-done((bf16[2,4096]{1,0:T(2,128)(2,1)S(1)}, bf16[2,4096]{1,0:T(2,128)(2,1)S(1)}, u32[]{:S(2)}, u32[]{:S(2)}) %collective-permute-start.5) | collective-permute-done | bytes 16416 | tf_op jit(solution)/shard_map/ppermute | solution.py:381
  35.0 0.8 %finish.1 = f32[1,1,2,64]{3,2,1,0:T(2,128)} custom-call(f32[2,64]{1,0:T(2,128)S(1)} %get-tuple-element.29.values_ref, f32[2,64]{1,0:T(2,128)S(1)} %get-tuple-element.30.squares_ref, bf16[1,8192]{1,0:T(2,128)(2,1)S(1)} %broadcast_in_dim.3.gain_ref, bf16[1,64,8192]{2,1,0:T(8,128)(2,1)S(1)} %get-tuple-element.28.shrink_ref, ...), custom_call_target="tpu_custom_call" | custom-call | tf_op jit(solution)/shard_map/finish/pallas_call | solution.py:369
  (2 shorter events, 0.1 us)
Async XLA Ops:
  0.6 10.2 %copy-start = (bf16[16,6656]{1,0:T(8,128)(2,1)S(1)}, bf16[16,6656]{1,0:T(8,128)(2,1)}, u32[]{:S(2)}) copy-start(bf16[16,6656]{1,0:T(8,128)(2,1)} %own_ref.1) | copy-start | bytes 638980
  0.6 10.1 %collective-permute-start = (bf16[16,6656]{1,0:T(8,128)(2,1)}, bf16[16,6656]{1,0:T(8,128)(2,1)S(1)}, u32[]{:S(2)}, u32[]{:S(2)}) collective-permute-start(bf16[16,6656]{1,0:T(8,128)(2,1)} %own_ref.1), channel_id=1, source_target_pairs={{0,2},{2,0},{1,3},{3,1},{4,6},{6,4},{5,7},{7,5},{8,10},{10,8},{9,1... | collective-permute-start | bytes 638984 | tf_op jit(solution)/shard_map/ppermute | solution.py:381
  10.7 16.7 %copy-start.2 = (s32[4,1]{0,1:T(1,128)S(1)}, s32[4,1]{0,1:T(1,128)}, u32[]{:S(2)}) copy-start(s32[4,1]{0,1:T(1,128)} %param.11) | copy-start | bytes 52
  10.8 20.3 %copy-start.1 = (bf16[4,4096]{1,0:T(4,128)(2,1)S(1)}, bf16[4,4096]{1,0:T(4,128)(2,1)}, u32[]{:S(2)}) copy-start(bf16[4,4096]{1,0:T(4,128)(2,1)} %residual_ref.1) | copy-start | bytes 98308
  10.8 21.0 %copy-start.3 = (bf16[8192]{0:T(1024)(128)(2,1)S(1)}, bf16[8192]{0:T(1024)(128)(2,1)}, u32[]{:S(2)}) copy-start(bf16[8192]{0:T(1024)(128)(2,1)} %param.9) | copy-start | bytes 49156
  22.1 1.4 %collective-permute-start.1 = (bf16[16,4096]{1,0:T(8,128)(2,1)S(1)}, bf16[16,4096]{1,0:T(8,128)(2,1)S(1)}, u32[]{:S(2)}, u32[]{:S(2)}) collective-permute-start(bf16[16,4096]{1,0:T(8,128)(2,1)S(1)} %bitcast.7), channel_id=1, source_target_pairs={{0,1},{1,0},{2,3},{3,2},{4,5},{5,4},{6,7},{7,6},{8,9},{9,8},{10,11... | collective-permute-start | bytes 393224 | tf_op jit(solution)/shard_map/ppermute | solution.py:381
  23.5 5.2 %collective-permute-start.2 = (bf16[4,4096]{1,0:T(4,128)(2,1)S(1)}, bf16[4,4096]{1,0:T(4,128)(2,1)S(1)}, u32[]{:S(2)}, u32[]{:S(2)}) collective-permute-start(bf16[4,4096]{1,0:T(4,128)(2,1)S(1)} %get-tuple-element.23), channel_id=1, source_target_pairs={{0,9},{1,8},{4,13},{5,12},{8,5},{9,4},{12,1},{13,0},{2,11},{3,10},... | collective-permute-start | bytes 98312 | tf_op jit(solution)/shard_map/ppermute | solution.py:391
  25.9 4.3 %collective-permute-start.3 = (bf16[4,4096]{1,0:T(4,128)(2,1)S(1)}, bf16[4,4096]{1,0:T(4,128)(2,1)S(1)}, u32[]{:S(2)}, u32[]{:S(2)}) collective-permute-start(bf16[4,4096]{1,0:T(4,128)(2,1)S(1)} %get-tuple-element.24), channel_id=1, source_target_pairs={{0,13},{1,12},{4,9},{5,8},{8,1},{9,0},{12,5},{13,4},{2,15},{3,14},... | collective-permute-start | bytes 98312 | tf_op jit(solution)/shard_map/ppermute | solution.py:391
  27.1 3.9 %collective-permute-start.4 = (bf16[4,4096]{1,0:T(4,128)(2,1)S(1)}, bf16[4,4096]{1,0:T(4,128)(2,1)S(1)}, u32[]{:S(2)}, u32[]{:S(2)}) collective-permute-start(bf16[4,4096]{1,0:T(4,128)(2,1)S(1)} %get-tuple-element.25), channel_id=1, source_target_pairs={{0,5},{1,4},{4,1},{5,0},{8,13},{9,12},{12,9},{13,8},{2,7},{3,6},{6... | collective-permute-start | bytes 98312 | tf_op jit(solution)/shard_map/ppermute | solution.py:391
  31.2 3.8 %collective-permute-start.5 = (bf16[2,4096]{1,0:T(2,128)(2,1)S(1)}, bf16[2,4096]{1,0:T(2,128)(2,1)S(1)}, u32[]{:S(2)}, u32[]{:S(2)}) collective-permute-start(bf16[2,4096]{1,0:T(2,128)(2,1)S(1)} %bitcast.8), channel_id=1, source_target_pairs={{0,2},{2,0},{1,3},{3,1},{4,6},{6,4},{5,7},{7,5},{8,10},{10,8},{9,1... | collective-permute-start | bytes 49160 | tf_op jit(solution)/shard_map/ppermute | solution.py:381

commit v10 on v9

--- a/solution.py
+++ b/solution.py
@@ -27,11 +27,16 @@
 
 def fetch_kernel(weight_ref, held_ref, sems):
     count, step, _ = held_ref.shape
+    parts = sems.shape[1]
+    size = step // parts
     copies = [
         pltpu.make_async_copy(
-            weight_ref.at[pl.ds(i * step, step), :], held_ref.at[i], sems.at[i]
+            weight_ref.at[pl.ds(i * step + part * size, size), :],
+            held_ref.at[i, pl.ds(part * size, size), :],
+            sems.at[i, part],
         )
         for i in range(count)
+        for part in range(parts)
     ]
     for copy in copies:
         copy.start()
@@ -46,13 +51,19 @@
         out_shape=pltpu.VMEM((count, step, columns), weight.dtype),
         in_specs=[pl.BlockSpec(memory_space=pl.ANY)],
         out_specs=whole(),
-        scratch_shapes=[pltpu.SemaphoreType.DMA((count,))],
+        scratch_shapes=[pltpu.SemaphoreType.DMA((count, 4 if step % 64 == 0 else 1))],
         compiler_params=pltpu.CompilerParams(vmem_limit_bytes=1 * MIB),
         cost_estimate=pl.CostEstimate(
             flops=0, bytes_accessed=2 * count * step * columns, transcendentals=0
         ),
         name="fetch",
     )(weight)
+
+
+def last_parts(step):
+    if step % 64:
+        return [(0, step)]
+    return [(0, step // 2), (step // 2, step // 4), (step // 4 * 3, step // 4)]
 
 
 def project_kernel(
@@ -76,7 +87,6 @@
     dp = 1 + others_ref.shape[0]
     me, tensor, section = (lax.axis_index(axis) for axis in ("dp", "tensor", "section"))
     width = min(columns, WIDTH)
-    half = step // 2
 
     def copy_of(i, sem, first=0, size=step):
         return pltpu.make_async_copy(
@@ -85,7 +95,8 @@
             sems.at[sem],
         )
 
-    last = [copy_of(rest - 1, rest - 1, 0, half), copy_of(rest - 1, rest, half, half)]
+    parts = last_parts(step)
+    last = [copy_of(rest - 1, rest - 1 + k, *part) for k, part in enumerate(parts)]
     for i in range(rest - 1):
         copy_of(i, i).start()
     for copy in last:
@@ -120,9 +131,9 @@
 
     lax.fori_loop(0, columns // width, held_step, 0)
     lax.fori_loop(0, rest - 1, rest_step, 0)
-    for copy, part in zip(last, (slice(0, half), slice(half, step))):
+    for copy, (first, size) in zip(last, parts):
         copy.wait()
-        add(rest - 1, part)
+        add(rest - 1, slice(first, first + size))
 
     block_rows = kept_ref.shape[0] // tensors
     group = sections * block_rows
@@ -163,7 +174,7 @@
             pltpu.VMEM((depth // step, rows, step), BF16),
             pltpu.VMEM((rows, columns), F32),
             pltpu.VMEM((rest, step, columns), BF16),
-            pltpu.SemaphoreType.DMA((rest + 1,)),
+            pltpu.SemaphoreType.DMA((rest - 1 + len(last_parts(step)),)),
         ],
         compiler_params=pltpu.CompilerParams(vmem_limit_bytes=36 * MIB),
         cost_estimate=pl.CostEstimate(

time: 36 us -> 36 us (level)
  no operation moved by 1% of the time
where the time goes in v10:
time: 36 us; the launch traced here: 35.8 us
  Pallas kernels  20.9 us (58%)
  starting transfers between devices  7.62 us (21%)
  waiting for transfers between devices  5.95 us (17%)
  between operations  0.73 us (2%)
  local copies, waits for them, and re-layouts  0.66 us (2%)
    pallas_call x1, Pallas kernels, project(): pl.pallas_call(functools.partial(project_kernel, tensors=tensors, section...  11.2 us
    pallas_call x1, Pallas kernels, fetch(): pl.pallas_call(fetch_kernel, out_shape=pltpu.VMEM((count, step, columns),...  7.16 us
    ppermute x3, starting transfers between devices, across(): return lax.ppermute(array, ('tensor', 'section'), pairs)  3.94 us
    ppermute x3, starting transfers between devices, shifted(): lax.ppermute(array, axis, [(i, (i + shift) % count) for i in range(count)])  3.68 us
    ppermute x3, waiting for transfers between devices, shifted(): lax.ppermute(array, axis, [(i, (i + shift) % count) for i in range(count)])  3.64 us
    ppermute x3, waiting for transfers between devices, across(): return lax.ppermute(array, ('tensor', 'section'), pairs)  2.31 us
    pallas_call x1, Pallas kernels, prepare(): pl.pallas_call(functools.partial(prepare_kernel, slots=slots, owners=owne...  1.23 us
    pallas_call x1, Pallas kernels, finish(): pl.pallas_call(finish_kernel, out_shape=jax.ShapeDtypeStruct((local, 1, M...  0.84 us
  transfers between devices with their start and end apart: 6, of which 4 were waited for; matrix products, arithmetic and copies ran while one was open for 2% of the time, Pallas kernels for 24%

profile of v10, /device:TPU:0, one launch (start us, length us, event | category | flops | bytes accessed | tf_op | source)
XLA Modules:
  0.0 35.8 jit_solution(6590361984056921982)
XLA Ops:
  0.6 0.0 copy-start
  0.6 3.0 %collective-permute-start = (bf16[16,6656]{1,0:T(8,128)(2,1)}, bf16[16,6656]{1,0:T(8,128)(2,1)S(1)}, u32[]{:S(2)}, u32[]{:S(2)}) collective-permute-start(bf16[16,6656]{1,0:T(8,128)(2,1)} %own_ref.1), channel_id=1, source_target_pairs={{0,2},{2,0},{1,3},{3,1},{4,6},{6,4},{5,7},{7,5},{8,10},{10,8},{9,1... | collective-permute-start | bytes 638984 | tf_op jit(solution)/shard_map/ppermute | solution.py:392
  3.6 7.2 %fetch.1.held_ref = bf16[5,512,4096]{2,1,0:T(8,128)(2,1)S(1)} custom-call(bf16[6656,4096]{1,0:T(8,128)(2,1)} %weight_ref.3), custom_call_target="tpu_custom_call" | custom-call | bytes 20971520 | tf_op jit(solution)/shard_map/fetch/pallas_call | solution.py:49
  10.8 0.0 copy-start.2
  10.8 0.0 copy-start.1
  10.8 0.0 copy-start.3
  10.8 0.0 collective-permute-done
  10.9 0.0 copy-done
  10.9 11.2 %project.1 = (f32[16,4096]{1,0:T(8,128)S(1)}, bf16[1,16,4096]{2,1,0:T(8,128)(2,1)S(1)}) custom-call(bf16[16,6656]{1,0:T(8,128)(2,1)S(1)} %copy-done, bf16[1,16,6656]{2,1,0:T(8,128)(2,1)S(1)} %bitcast.5, bf16[5,512,4096]{2,1,0:T(8,128)(2,1)S(1)} %fetch.1.held_ref, bf16[6656,4096]{1,0:T(8,128)(2,1)} %weight_ref.3), custom_call_target="tpu_custom_call" | custom-call | flops 1744830464 | bytes 33554432 | tf_op jit(solution)/shard_map/project/pallas_call | solution.py:165
  22.1 0.1 collective-permute-start.1
  22.2 1.3 %collective-permute-done.1.refs_0_ = bf16[16,4096]{1,0:T(8,128)(2,1)S(1)} collective-permute-done((bf16[16,4096]{1,0:T(8,128)(2,1)S(1)}, bf16[16,4096]{1,0:T(8,128)(2,1)S(1)}, u32[]{:S(2)}, u32[]{:S(2)}) %collective-permute-start.1) | collective-permute-done | bytes 131104 | tf_op jit(solution)/shard_map/ppermute | solution.py:392
  23.6 2.4 %collective-permute-start.2 = (bf16[4,4096]{1,0:T(4,128)(2,1)S(1)}, bf16[4,4096]{1,0:T(4,128)(2,1)S(1)}, u32[]{:S(2)}, u32[]{:S(2)}) collective-permute-start(bf16[4,4096]{1,0:T(4,128)(2,1)S(1)} %get-tuple-element.23), channel_id=1, source_target_pairs={{0,9},{1,8},{4,13},{5,12},{8,5},{9,4},{12,1},{13,0},{2,11},{3,10},... | collective-permute-start | bytes 98312 | tf_op jit(solution)/shard_map/ppermute | solution.py:402
  26.0 1.2 %collective-permute-start.3 = (bf16[4,4096]{1,0:T(4,128)(2,1)S(1)}, bf16[4,4096]{1,0:T(4,128)(2,1)S(1)}, u32[]{:S(2)}, u32[]{:S(2)}) collective-permute-start(bf16[4,4096]{1,0:T(4,128)(2,1)S(1)} %get-tuple-element.24), channel_id=1, source_target_pairs={{0,13},{1,12},{4,9},{5,8},{8,1},{9,0},{12,5},{13,4},{2,15},{3,14},... | collective-permute-start | bytes 98312 | tf_op jit(solution)/shard_map/ppermute | solution.py:402
  27.2 0.3 collective-permute-start.4
  27.5 0.0 copy-done.2
  27.5 1.2 %prepare.1 = (f32[4,4]{1,0:T(4,128)S(1)}, bf16[1,64,8192]{2,1,0:T(8,128)(2,1)S(1)}) custom-call(s32[1,4]{1,0:T(1,128)S(1)} %bitcast.6, bf16[1,64,8192]{2,1,0:T(8,128)(2,1)} %bitcast.9), custom_call_target="tpu_custom_call" | custom-call | tf_op jit(solution)/shard_map/prepare/pallas_call | solution.py:260
  28.7 0.0 collective-permute-done.2.refs_0_
  28.8 1.4 %collective-permute-done.3.refs_1_ = bf16[4,4096]{1,0:T(4,128)(2,1)S(1)} collective-permute-done((bf16[4,4096]{1,0:T(4,128)(2,1)S(1)}, bf16[4,4096]{1,0:T(4,128)(2,1)S(1)}, u32[]{:S(2)}, u32[]{:S(2)}) %collective-permute-start.3) | collective-permute-done | bytes 32800 | tf_op jit(solution)/shard_map/ppermute | solution.py:402
  30.2 0.9 %collective-permute-done.4.refs_2_ = bf16[4,4096]{1,0:T(4,128)(2,1)S(1)} collective-permute-done((bf16[4,4096]{1,0:T(4,128)(2,1)S(1)}, bf16[4,4096]{1,0:T(4,128)(2,1)S(1)}, u32[]{:S(2)}, u32[]{:S(2)}) %collective-permute-start.4) | collective-permute-done | bytes 32800 | tf_op jit(solution)/shard_map/ppermute | solution.py:402
  31.1 0.0 copy-done.1
  31.1 0.1 mix.1
  31.2 0.6 %collective-permute-start.5 = (bf16[2,4096]{1,0:T(2,128)(2,1)S(1)}, bf16[2,4096]{1,0:T(2,128)(2,1)S(1)}, u32[]{:S(2)}, u32[]{:S(2)}) collective-permute-start(bf16[2,4096]{1,0:T(2,128)(2,1)S(1)} %bitcast.8), channel_id=1, source_target_pairs={{0,2},{2,0},{1,3},{3,1},{4,6},{6,4},{5,7},{7,5},{8,10},{10,8},{9,1... | collective-permute-start | bytes 49160 | tf_op jit(solution)/shard_map/ppermute | solution.py:392
  31.8 0.0 copy-done.3
  31.8 0.6 %copy.8 = bf16[4,4096]{1,0:T(4,128)(2,1)} copy(bf16[4,4096]{1,0:T(4,128)(2,1)S(1)} %get-tuple-element.32) | data formatting | bytes 65536
  32.4 0.3 own_half.1
  32.7 2.3 %collective-permute-done.5.refs_0_ = bf16[2,4096]{1,0:T(2,128)(2,1)S(1)} collective-permute-done((bf16[2,4096]{1,0:T(2,128)(2,1)S(1)}, bf16[2,4096]{1,0:T(2,128)(2,1)S(1)}, u32[]{:S(2)}, u32[]{:S(2)}) %collective-permute-start.5) | collective-permute-done | bytes 16416 | tf_op jit(solution)/shard_map/ppermute | solution.py:392
  35.0 0.8 %finish.1 = f32[1,1,2,64]{3,2,1,0:T(2,128)} custom-call(f32[2,64]{1,0:T(2,128)S(1)} %get-tuple-element.29.values_ref, f32[2,64]{1,0:T(2,128)S(1)} %get-tuple-element.30.squares_ref, bf16[1,8192]{1,0:T(2,128)(2,1)S(1)} %broadcast_in_dim.3.gain_ref, bf16[1,64,8192]{2,1,0:T(8,128)(2,1)S(1)} %get-tuple-element.28.shrink_ref, ...), custom_call_target="tpu_custom_call" | custom-call | tf_op jit(solution)/shard_map/finish/pallas_call | solution.py:380
  (2 shorter events, 0.1 us)
Async XLA Ops:
  0.6 10.2 %copy-start = (bf16[16,6656]{1,0:T(8,128)(2,1)S(1)}, bf16[16,6656]{1,0:T(8,128)(2,1)}, u32[]{:S(2)}) copy-start(bf16[16,6656]{1,0:T(8,128)(2,1)} %own_ref.1) | copy-start | bytes 638980
  0.6 10.2 %collective-permute-start = (bf16[16,6656]{1,0:T(8,128)(2,1)}, bf16[16,6656]{1,0:T(8,128)(2,1)S(1)}, u32[]{:S(2)}, u32[]{:S(2)}) collective-permute-start(bf16[16,6656]{1,0:T(8,128)(2,1)} %own_ref.1), channel_id=1, source_target_pairs={{0,2},{2,0},{1,3},{3,1},{4,6},{6,4},{5,7},{7,5},{8,10},{10,8},{9,1... | collective-permute-start | bytes 638984 | tf_op jit(solution)/shard_map/ppermute | solution.py:392
  10.8 16.7 %copy-start.2 = (s32[4,1]{0,1:T(1,128)S(1)}, s32[4,1]{0,1:T(1,128)}, u32[]{:S(2)}) copy-start(s32[4,1]{0,1:T(1,128)} %param.11) | copy-start | bytes 52
  10.8 20.2 %copy-start.1 = (bf16[4,4096]{1,0:T(4,128)(2,1)S(1)}, bf16[4,4096]{1,0:T(4,128)(2,1)}, u32[]{:S(2)}) copy-start(bf16[4,4096]{1,0:T(4,128)(2,1)} %residual_ref.1) | copy-start | bytes 98308
  10.8 21.0 %copy-start.3 = (bf16[8192]{0:T(1024)(128)(2,1)S(1)}, bf16[8192]{0:T(1024)(128)(2,1)}, u32[]{:S(2)}) copy-start(bf16[8192]{0:T(1024)(128)(2,1)} %param.9) | copy-start | bytes 49156
  22.1 1.4 %collective-permute-start.1 = (bf16[16,4096]{1,0:T(8,128)(2,1)S(1)}, bf16[16,4096]{1,0:T(8,128)(2,1)S(1)}, u32[]{:S(2)}, u32[]{:S(2)}) collective-permute-start(bf16[16,4096]{1,0:T(8,128)(2,1)S(1)} %bitcast.7), channel_id=1, source_target_pairs={{0,1},{1,0},{2,3},{3,2},{4,5},{5,4},{6,7},{7,6},{8,9},{9,8},{10,11... | collective-permute-start | bytes 393224 | tf_op jit(solution)/shard_map/ppermute | solution.py:392
  23.6 5.2 %collective-permute-start.2 = (bf16[4,4096]{1,0:T(4,128)(2,1)S(1)}, bf16[4,4096]{1,0:T(4,128)(2,1)S(1)}, u32[]{:S(2)}, u32[]{:S(2)}) collective-permute-start(bf16[4,4096]{1,0:T(4,128)(2,1)S(1)} %get-tuple-element.23), channel_id=1, source_target_pairs={{0,9},{1,8},{4,13},{5,12},{8,5},{9,4},{12,1},{13,0},{2,11},{3,10},... | collective-permute-start | bytes 98312 | tf_op jit(solution)/shard_map/ppermute | solution.py:402
  26.0 4.3 %collective-permute-start.3 = (bf16[4,4096]{1,0:T(4,128)(2,1)S(1)}, bf16[4,4096]{1,0:T(4,128)(2,1)S(1)}, u32[]{:S(2)}, u32[]{:S(2)}) collective-permute-start(bf16[4,4096]{1,0:T(4,128)(2,1)S(1)} %get-tuple-element.24), channel_id=1, source_target_pairs={{0,13},{1,12},{4,9},{5,8},{8,1},{9,0},{12,5},{13,4},{2,15},{3,14},... | collective-permute-start | bytes 98312 | tf_op jit(solution)/shard_map/ppermute | solution.py:402
  27.2 3.9 %collective-permute-start.4 = (bf16[4,4096]{1,0:T(4,128)(2,1)S(1)}, bf16[4,4096]{1,0:T(4,128)(2,1)S(1)}, u32[]{:S(2)}, u32[]{:S(2)}) collective-permute-start(bf16[4,4096]{1,0:T(4,128)(2,1)S(1)} %get-tuple-element.25), channel_id=1, source_target_pairs={{0,5},{1,4},{4,1},{5,0},{8,13},{9,12},{12,9},{13,8},{2,7},{3,6},{6... | collective-permute-start | bytes 98312 | tf_op jit(solution)/shard_map/ppermute | solution.py:402
  31.2 3.8 %collective-permute-start.5 = (bf16[2,4096]{1,0:T(2,128)(2,1)S(1)}, bf16[2,4096]{1,0:T(2,128)(2,1)S(1)}, u32[]{:S(2)}, u32[]{:S(2)}) collective-permute-start(bf16[2,4096]{1,0:T(2,128)(2,1)S(1)} %bitcast.8), channel_id=1, source_target_pairs={{0,2},{2,0},{1,3},{3,1},{4,6},{6,4},{5,7},{7,5},{8,10},{10,8},{9,1... | collective-permute-start | bytes 49160 | tf_op jit(solution)/shard_map/ppermute | solution.py:392

commit v11 on v10

--- a/solution.py
+++ b/solution.py
@@ -27,16 +27,11 @@
 
 def fetch_kernel(weight_ref, held_ref, sems):
     count, step, _ = held_ref.shape
-    parts = sems.shape[1]
-    size = step // parts
     copies = [
         pltpu.make_async_copy(
-            weight_ref.at[pl.ds(i * step + part * size, size), :],
-            held_ref.at[i, pl.ds(part * size, size), :],
-            sems.at[i, part],
+            weight_ref.at[pl.ds(i * step, step), :], held_ref.at[i], sems.at[i]
         )
         for i in range(count)
-        for part in range(parts)
     ]
     for copy in copies:
         copy.start()
@@ -51,7 +46,7 @@
         out_shape=pltpu.VMEM((count, step, columns), weight.dtype),
         in_specs=[pl.BlockSpec(memory_space=pl.ANY)],
         out_specs=whole(),
-        scratch_shapes=[pltpu.SemaphoreType.DMA((count, 4 if step % 64 == 0 else 1))],
+        scratch_shapes=[pltpu.SemaphoreType.DMA((count,))],
         compiler_params=pltpu.CompilerParams(vmem_limit_bytes=1 * MIB),
         cost_estimate=pl.CostEstimate(
             flops=0, bytes_accessed=2 * count * step * columns, transcendentals=0
@@ -71,10 +66,9 @@
     others_ref,
     held_ref,
     weight_ref,
-    kept_ref,
+    total_ref,
     sent_ref,
     rows_ref,
-    total_ref,
     rest_ref,
     sems,
     *,
@@ -85,7 +79,7 @@
     rest = rest_ref.shape[0]
     own_rows = own_ref.shape[0]
     dp = 1 + others_ref.shape[0]
-    me, tensor, section = (lax.axis_index(axis) for axis in ("dp", "tensor", "section"))
+    me = lax.axis_index("dp")
     width = min(columns, WIDTH)
 
     def copy_of(i, sem, first=0, size=step):
@@ -109,14 +103,6 @@
             source = own_ref[:, block] if shift == 0 else others_ref[shift - 1, :, block]
             rows_ref[i, pl.ds(first, own_rows), :] = source
 
-    def held_step(n, _):
-        lanes = pl.ds(pl.multiple_of(n * width, width), width)
-        total_ref[:, lanes] = sum(
-            jnp.dot(rows_ref[i], held_ref[i, :, lanes], preferred_element_type=F32)
-            for i in range(held)
-        )
-        return 0
-
     def add(i, part=slice(None)):
         for n in range(0, columns, width):
             lanes = slice(n, n + width)
@@ -129,31 +115,56 @@
         add(i)
         return 0
 
-    lax.fori_loop(0, columns // width, held_step, 0)
+    for n in range(0, columns, width):
+        lanes = slice(n, n + width)
+        total_ref[:, lanes] = sum(
+            jnp.dot(rows_ref[i], held_ref[i, :, lanes], preferred_element_type=F32)
+            for i in range(held)
+        )
     lax.fori_loop(0, rest - 1, rest_step, 0)
     for copy, (first, size) in zip(last, parts):
         copy.wait()
         add(rest - 1, slice(first, first + size))
 
-    block_rows = kept_ref.shape[0] // tensors
+    for turn in range(1, sections):
+        for n in range(0, columns, width):
+            lanes = slice(n, n + width)
+            rows = rows_of(turn, total_ref, lanes, tensors, sections)
+            sent_ref[turn - 1, :, lanes] = rows.astype(BF16)
+
+
+def rows_of(turn, total_ref, lanes, tensors, sections):
+    tensor, section = lax.axis_index("tensor"), lax.axis_index("section")
+    block_rows = total_ref.shape[0] // (tensors * sections)
     group = sections * block_rows
+    blocks = []
+    for k in range(tensors):
+        first = pl.multiple_of(partner_of(tensor, k, tensors) * group, group)
+        rows = total_ref[pl.ds(first, group), lanes]
+        rows = pltpu.roll(rows, (sections - section) % sections * block_rows, 0)
+        part = (turn + (k > 0)) % sections
+        blocks.append(rows[part * block_rows : (part + 1) * block_rows])
+    return jnp.concatenate(blocks, axis=0)
+
+
+def keep_kernel(total_ref, kept_ref, *, tensors, sections):
+    columns = total_ref.shape[1]
+    width = min(columns, WIDTH)
     for n in range(0, columns, width):
         lanes = slice(n, n + width)
-        turned = []
-        for turn in range(tensors):
-            first = pl.multiple_of(partner_of(tensor, turn, tensors) * group, group)
-            rows = total_ref[pl.ds(first, group), lanes]
-            turned.append(pltpu.roll(rows, (sections - section) % sections * block_rows, 0))
-        for s in range(sections):
-            parts = [s] + [(s + 1) % sections] * (tensors - 1)
-            rows = jnp.concatenate(
-                [block[p * block_rows : (p + 1) * block_rows] for p, block in zip(parts, turned)],
-                axis=0,
-            )
-            if s == 0:
-                kept_ref[:, lanes] = rows
-            else:
-                sent_ref[s - 1, :, lanes] = rows.astype(BF16)
+        kept_ref[:, lanes] = rows_of(0, total_ref, lanes, tensors, sections)
+
+
+def keep(total, tensors, sections):
+    rows, columns = total.shape
+    return pl.pallas_call(
+        functools.partial(keep_kernel, tensors=tensors, sections=sections),
+        out_shape=jax.ShapeDtypeStruct((rows // sections, columns), F32),
+        in_specs=[whole()],
+        out_specs=whole(),
+        compiler_params=pltpu.CompilerParams(vmem_limit_bytes=4 * MIB),
+        name="keep",
+    )(total)
 
 
 def project(own, others, held, weight, tensors, sections):
@@ -165,14 +176,13 @@
     return pl.pallas_call(
         functools.partial(project_kernel, tensors=tensors, sections=sections),
         out_shape=(
-            pltpu.VMEM((rows // sections, columns), F32),
+            pltpu.VMEM((rows, columns), F32),
             pltpu.VMEM((sections - 1, rows // sections, columns), BF16),
         ),
         in_specs=[whole(), whole(), whole(), pl.BlockSpec(memory_space=pl.ANY)],
         out_specs=(whole(), whole()),
         scratch_shapes=[
             pltpu.VMEM((depth // step, rows, step), BF16),
-            pltpu.VMEM((rows, columns), F32),
             pltpu.VMEM((rest, step, columns), BF16),
             pltpu.SemaphoreType.DMA((rest - 1 + len(last_parts(step)),)),
         ],
@@ -418,8 +428,9 @@
     gain = next_norm_scale[None, :]
 
     in_vmem = [pltpu.with_memory_space_constraint(x, pltpu.VMEM) for x in (hidden, others, held)]
-    kept, sent = project(*in_vmem, down_matrix, tensors, sections)
-    index, kept = lax.optimization_barrier((adapter_index.reshape(1, -1), kept))
+    total, sent = project(*in_vmem, down_matrix, tensors, sections)
+    index, total = lax.optimization_barrier((adapter_index.reshape(1, -1), total))
+    kept = keep(total, tensors, sections)
     places, shrink = prepare(index, shrink, local * MOST, dp)
     arrived = [shifted(sent[s - 1], "section", s) for s in range(1, sections)]
     plan = exchange_plan(tensors)

time: 36 us -> 36.9 us (1.025)
  Pallas kernels: 20.9 us -> 21.8 us
    pallas_call x1, Pallas kernels: 11.2 us -> 12.2 us  [project(): pl.pallas_call(functools.partial(project_kernel, tensors=tensors, section...]
where the time goes in v11:
time: 36.9 us; the launch traced here: 36.7 us
  Pallas kernels  21.8 us (59%)
  starting transfers between devices  7.61 us (21%)
  waiting for transfers between devices  5.91 us (16%)
  between operations  0.74 us (2%)
  local copies, waits for them, and re-layouts  0.66 us (2%)
    pallas_call x1, Pallas kernels, project(): pl.pallas_call(functools.partial(project_kernel, tensors=tensors, section...  12.2 us
    pallas_call x1, Pallas kernels, fetch(): pl.pallas_call(fetch_kernel, out_shape=pltpu.VMEM((count, step, columns),...  7.09 us
    ppermute x3, starting transfers between devices, across(): return lax.ppermute(array, ('tensor', 'section'), pairs)  3.94 us
    ppermute x3, starting transfers between devices, shifted(): lax.ppermute(array, axis, [(i, (i + shift) % count) for i in range(count)])  3.67 us
    ppermute x3, waiting for transfers between devices, shifted(): lax.ppermute(array, axis, [(i, (i + shift) % count) for i in range(count)])  3.59 us
    ppermute x3, waiting for transfers between devices, across(): return lax.ppermute(array, ('tensor', 'section'), pairs)  2.32 us
    pallas_call x1, Pallas kernels, prepare(): pl.pallas_call(functools.partial(prepare_kernel, slots=slots, owners=owne...  1.23 us
    pallas_call x1, Pallas kernels, finish(): pl.pallas_call(finish_kernel, out_shape=jax.ShapeDtypeStruct((local, 1, M...  0.84 us
  transfers between devices with their start and end apart: 6, of which 4 were waited for; matrix products, arithmetic and copies ran while one was open for 2% of the time, Pallas kernels for 24%

profile of v11, /device:TPU:0, one launch (start us, length us, event | category | flops | bytes accessed | tf_op | source)
XLA Modules:
  0.0 36.7 jit_solution(8439346502257497838)
XLA Ops:
  0.6 0.0 copy-start
  0.6 3.0 %collective-permute-start = (bf16[16,6656]{1,0:T(8,128)(2,1)}, bf16[16,6656]{1,0:T(8,128)(2,1)S(1)}, u32[]{:S(2)}, u32[]{:S(2)}) collective-permute-start(bf16[16,6656]{1,0:T(8,128)(2,1)} %own_ref.1), channel_id=1, source_target_pairs={{0,2},{2,0},{1,3},{3,1},{4,6},{6,4},{5,7},{7,5},{8,10},{10,8},{9,1... | collective-permute-start | bytes 638984 | tf_op jit(solution)/shard_map/ppermute | solution.py:402
  3.6 7.1 %fetch.1.held_ref = bf16[5,512,4096]{2,1,0:T(8,128)(2,1)S(1)} custom-call(bf16[6656,4096]{1,0:T(8,128)(2,1)} %weight_ref.3), custom_call_target="tpu_custom_call" | custom-call | bytes 20971520 | tf_op jit(solution)/shard_map/fetch/pallas_call | solution.py:44
  10.7 0.0 copy-start.2
  10.8 0.0 copy-start.1
  10.8 0.0 copy-start.3
  10.8 0.0 collective-permute-done
  10.8 0.0 copy-done
  10.8 12.2 %project.1 = (f32[32,4096]{1,0:T(8,128)S(1)}, bf16[1,16,4096]{2,1,0:T(8,128)(2,1)S(1)}) custom-call(bf16[16,6656]{1,0:T(8,128)(2,1)S(1)} %copy-done, bf16[1,16,6656]{2,1,0:T(8,128)(2,1)S(1)} %bitcast.5, bf16[5,512,4096]{2,1,0:T(8,128)(2,1)S(1)} %fetch.1.held_ref, bf16[6656,4096]{1,0:T(8,128)(2,1)} %weight_ref.3), custom_call_target="tpu_custom_call" | custom-call | flops 1744830464 | bytes 33554432 | tf_op jit(solution)/shard_map/project/pallas_call | solution.py:176
  23.0 0.1 collective-permute-start.1
  23.1 1.3 %collective-permute-done.1.refs_0_ = bf16[16,4096]{1,0:T(8,128)(2,1)S(1)} collective-permute-done((bf16[16,4096]{1,0:T(8,128)(2,1)S(1)}, bf16[16,4096]{1,0:T(8,128)(2,1)S(1)}, u32[]{:S(2)}, u32[]{:S(2)}) %collective-permute-start.1) | collective-permute-done | bytes 131104 | tf_op jit(solution)/shard_map/ppermute | solution.py:402
  24.4 2.4 %collective-permute-start.2 = (bf16[4,4096]{1,0:T(4,128)(2,1)S(1)}, bf16[4,4096]{1,0:T(4,128)(2,1)S(1)}, u32[]{:S(2)}, u32[]{:S(2)}) collective-permute-start(bf16[4,4096]{1,0:T(4,128)(2,1)S(1)} %get-tuple-element.23), channel_id=1, source_target_pairs={{0,9},{1,8},{4,13},{5,12},{8,5},{9,4},{12,1},{13,0},{2,11},{3,10},... | collective-permute-start | bytes 98312 | tf_op jit(solution)/shard_map/ppermute | solution.py:412
  26.8 1.2 %collective-permute-start.3 = (bf16[4,4096]{1,0:T(4,128)(2,1)S(1)}, bf16[4,4096]{1,0:T(4,128)(2,1)S(1)}, u32[]{:S(2)}, u32[]{:S(2)}) collective-permute-start(bf16[4,4096]{1,0:T(4,128)(2,1)S(1)} %get-tuple-element.24), channel_id=1, source_target_pairs={{0,13},{1,12},{4,9},{5,8},{8,1},{9,0},{12,5},{13,4},{2,15},{3,14},... | collective-permute-start | bytes 98312 | tf_op jit(solution)/shard_map/ppermute | solution.py:412
  28.0 0.3 collective-permute-start.4
  28.4 0.0 copy-done.2
  28.4 1.2 %prepare.1 = (f32[4,4]{1,0:T(4,128)S(1)}, bf16[1,64,8192]{2,1,0:T(8,128)(2,1)S(1)}) custom-call(s32[1,4]{1,0:T(1,128)S(1)} %bitcast.6, bf16[1,64,8192]{2,1,0:T(8,128)(2,1)} %bitcast.9), custom_call_target="tpu_custom_call" | custom-call | tf_op jit(solution)/shard_map/prepare/pallas_call | solution.py:270
  29.6 0.0 collective-permute-done.2.refs_0_
  29.6 1.5 %collective-permute-done.3.refs_1_ = bf16[4,4096]{1,0:T(4,128)(2,1)S(1)} collective-permute-done((bf16[4,4096]{1,0:T(4,128)(2,1)S(1)}, bf16[4,4096]{1,0:T(4,128)(2,1)S(1)}, u32[]{:S(2)}, u32[]{:S(2)}) %collective-permute-start.3) | collective-permute-done | bytes 32800 | tf_op jit(solution)/shard_map/ppermute | solution.py:412
  31.1 0.8 %collective-permute-done.4.refs_2_ = bf16[4,4096]{1,0:T(4,128)(2,1)S(1)} collective-permute-done((bf16[4,4096]{1,0:T(4,128)(2,1)S(1)}, bf16[4,4096]{1,0:T(4,128)(2,1)S(1)}, u32[]{:S(2)}, u32[]{:S(2)}) %collective-permute-start.4) | collective-permute-done | bytes 32800 | tf_op jit(solution)/shard_map/ppermute | solution.py:412
  31.9 0.0 copy-done.1
  31.9 0.1 mix.1
  32.1 0.6 %collective-permute-start.5 = (bf16[2,4096]{1,0:T(2,128)(2,1)S(1)}, bf16[2,4096]{1,0:T(2,128)(2,1)S(1)}, u32[]{:S(2)}, u32[]{:S(2)}) collective-permute-start(bf16[2,4096]{1,0:T(2,128)(2,1)S(1)} %bitcast.8), channel_id=1, source_target_pairs={{0,2},{2,0},{1,3},{3,1},{4,6},{6,4},{5,7},{7,5},{8,10},{10,8},{9,1... | collective-permute-start | bytes 49160 | tf_op jit(solution)/shard_map/ppermute | solution.py:402
  32.7 0.0 copy-done.3
  32.7 0.6 %copy.8 = bf16[4,4096]{1,0:T(4,128)(2,1)} copy(bf16[4,4096]{1,0:T(4,128)(2,1)S(1)} %get-tuple-element.32) | data formatting | bytes 65536
  33.3 0.3 own_half.1
  33.6 2.3 %collective-permute-done.5.refs_0_ = bf16[2,4096]{1,0:T(2,128)(2,1)S(1)} collective-permute-done((bf16[2,4096]{1,0:T(2,128)(2,1)S(1)}, bf16[2,4096]{1,0:T(2,128)(2,1)S(1)}, u32[]{:S(2)}, u32[]{:S(2)}) %collective-permute-start.5) | collective-permute-done | bytes 16416 | tf_op jit(solution)/shard_map/ppermute | solution.py:402
  35.9 0.8 %finish.1 = f32[1,1,2,64]{3,2,1,0:T(2,128)} custom-call(f32[2,64]{1,0:T(2,128)S(1)} %get-tuple-element.29.values_ref, f32[2,64]{1,0:T(2,128)S(1)} %get-tuple-element.30.squares_ref, bf16[1,8192]{1,0:T(2,128)(2,1)S(1)} %broadcast_in_dim.3.gain_ref, bf16[1,64,8192]{2,1,0:T(8,128)(2,1)S(1)} %get-tuple-element.28.shrink_ref, ...), custom_call_target="tpu_custom_call" | custom-call | tf_op jit(solution)/shard_map/finish/pallas_call | solution.py:390
  (3 shorter events, 0.1 us)
Async XLA Ops:
  0.6 10.2 %copy-start = (bf16[16,6656]{1,0:T(8,128)(2,1)S(1)}, bf16[16,6656]{1,0:T(8,128)(2,1)}, u32[]{:S(2)}) copy-start(bf16[16,6656]{1,0:T(8,128)(2,1)} %own_ref.1) | copy-start | bytes 638980
  0.6 10.1 %collective-permute-start = (bf16[16,6656]{1,0:T(8,128)(2,1)}, bf16[16,6656]{1,0:T(8,128)(2,1)S(1)}, u32[]{:S(2)}, u32[]{:S(2)}) collective-permute-start(bf16[16,6656]{1,0:T(8,128)(2,1)} %own_ref.1), channel_id=1, source_target_pairs={{0,2},{2,0},{1,3},{3,1},{4,6},{6,4},{5,7},{7,5},{8,10},{10,8},{9,1... | collective-permute-start | bytes 638984 | tf_op jit(solution)/shard_map/ppermute | solution.py:402
  10.7 17.6 %copy-start.2 = (s32[4,1]{0,1:T(1,128)S(1)}, s32[4,1]{0,1:T(1,128)}, u32[]{:S(2)}) copy-start(s32[4,1]{0,1:T(1,128)} %param.11) | copy-start | bytes 52
  10.8 21.2 %copy-start.1 = (bf16[4,4096]{1,0:T(4,128)(2,1)S(1)}, bf16[4,4096]{1,0:T(4,128)(2,1)}, u32[]{:S(2)}) copy-start(bf16[4,4096]{1,0:T(4,128)(2,1)} %residual_ref.1) | copy-start | bytes 98308
  10.8 21.9 %copy-start.3 = (bf16[8192]{0:T(1024)(128)(2,1)S(1)}, bf16[8192]{0:T(1024)(128)(2,1)}, u32[]{:S(2)}) copy-start(bf16[8192]{0:T(1024)(128)(2,1)} %param.9) | copy-start | bytes 49156
  23.0 1.4 %collective-permute-start.1 = (bf16[16,4096]{1,0:T(8,128)(2,1)S(1)}, bf16[16,4096]{1,0:T(8,128)(2,1)S(1)}, u32[]{:S(2)}, u32[]{:S(2)}) collective-permute-start(bf16[16,4096]{1,0:T(8,128)(2,1)S(1)} %bitcast.7), channel_id=1, source_target_pairs={{0,1},{1,0},{2,3},{3,2},{4,5},{5,4},{6,7},{7,6},{8,9},{9,8},{10,11... | collective-permute-start | bytes 393224 | tf_op jit(solution)/shard_map/ppermute | solution.py:402
  24.4 5.2 %collective-permute-start.2 = (bf16[4,4096]{1,0:T(4,128)(2,1)S(1)}, bf16[4,4096]{1,0:T(4,128)(2,1)S(1)}, u32[]{:S(2)}, u32[]{:S(2)}) collective-permute-start(bf16[4,4096]{1,0:T(4,128)(2,1)S(1)} %get-tuple-element.23), channel_id=1, source_target_pairs={{0,9},{1,8},{4,13},{5,12},{8,5},{9,4},{12,1},{13,0},{2,11},{3,10},... | collective-permute-start | bytes 98312 | tf_op jit(solution)/shard_map/ppermute | solution.py:412
  26.8 4.3 %collective-permute-start.3 = (bf16[4,4096]{1,0:T(4,128)(2,1)S(1)}, bf16[4,4096]{1,0:T(4,128)(2,1)S(1)}, u32[]{:S(2)}, u32[]{:S(2)}) collective-permute-start(bf16[4,4096]{1,0:T(4,128)(2,1)S(1)} %get-tuple-element.24), channel_id=1, source_target_pairs={{0,13},{1,12},{4,9},{5,8},{8,1},{9,0},{12,5},{13,4},{2,15},{3,14},... | collective-permute-start | bytes 98312 | tf_op jit(solution)/shard_map/ppermute | solution.py:412
  28.0 3.9 %collective-permute-start.4 = (bf16[4,4096]{1,0:T(4,128)(2,1)S(1)}, bf16[4,4096]{1,0:T(4,128)(2,1)S(1)}, u32[]{:S(2)}, u32[]{:S(2)}) collective-permute-start(bf16[4,4096]{1,0:T(4,128)(2,1)S(1)} %get-tuple-element.25), channel_id=1, source_target_pairs={{0,5},{1,4},{4,1},{5,0},{8,13},{9,12},{12,9},{13,8},{2,7},{3,6},{6... | collective-permute-start | bytes 98312 | tf_op jit(solution)/shard_map/ppermute | solution.py:412
  32.1 3.8 %collective-permute-start.5 = (bf16[2,4096]{1,0:T(2,128)(2,1)S(1)}, bf16[2,4096]{1,0:T(2,128)(2,1)S(1)}, u32[]{:S(2)}, u32[]{:S(2)}) collective-permute-start(bf16[2,4096]{1,0:T(2,128)(2,1)S(1)} %bitcast.8), channel_id=1, source_target_pairs={{0,2},{2,0},{1,3},{3,1},{4,6},{6,4},{5,7},{7,5},{8,10},{10,8},{9,1... | collective-permute-start | bytes 49160 | tf_op jit(solution)/shard_map/ppermute | solution.py:402

commit v12 on v11

--- a/solution.py
+++ b/solution.py
@@ -55,12 +55,6 @@
     )(weight)
 
 
-def last_parts(step):
-    if step % 64:
-        return [(0, step)]
-    return [(0, step // 2), (step // 2, step // 4), (step // 4 * 3, step // 4)]
-
-
 def project_kernel(
     own_ref,
     others_ref,
@@ -69,6 +63,7 @@
     total_ref,
     sent_ref,
     rows_ref,
+    halves_ref,
     rest_ref,
     sems,
     *,
@@ -89,48 +84,59 @@
             sems.at[sem],
         )
 
-    parts = last_parts(step)
-    last = [copy_of(rest - 1, rest - 1 + k, *part) for k, part in enumerate(parts)]
+    half = step // 2
     for i in range(rest - 1):
         copy_of(i, i).start()
-    for copy in last:
-        copy.start()
-
-    for i in range(held + rest):
-        block = slice(i * step, (i + 1) * step)
+    for part in range(2):
+        copy_of(rest - 1, rest - 1 + part, part * half, half).start()
+
+    def fill(target, block):
         for shift in range(dp):
             first = pl.multiple_of((me + dp - shift) % dp * own_rows, own_rows)
             source = own_ref[:, block] if shift == 0 else others_ref[shift - 1, :, block]
-            rows_ref[i, pl.ds(first, own_rows), :] = source
-
-    def add(i, part=slice(None)):
-        for n in range(0, columns, width):
-            lanes = slice(n, n + width)
-            total_ref[:, lanes] += jnp.dot(
-                rows_ref[held + i, :, part], rest_ref[i, part, lanes], preferred_element_type=F32
-            )
-
-    def rest_step(i, _):
-        copy_of(i, i).wait()
-        add(i)
-        return 0
-
-    for n in range(0, columns, width):
-        lanes = slice(n, n + width)
+            target[pl.ds(first, own_rows), :] = source
+
+    for i in range(held + rest - 1):
+        fill(rows_ref.at[i], slice(i * step, (i + 1) * step))
+    for part in range(2):
+        first = (held + rest - 1) * step + part * half
+        fill(halves_ref.at[part], slice(first, first + half))
+
+    def held_step(n, _):
+        lanes = pl.ds(pl.multiple_of(n * width, width), width)
         total_ref[:, lanes] = sum(
             jnp.dot(rows_ref[i], held_ref[i, :, lanes], preferred_element_type=F32)
             for i in range(held)
         )
-    lax.fori_loop(0, rest - 1, rest_step, 0)
-    for copy, (first, size) in zip(last, parts):
-        copy.wait()
-        add(rest - 1, slice(first, first + size))
-
-    for turn in range(1, sections):
+        return 0
+
+    def add(rows, block_ref):
         for n in range(0, columns, width):
             lanes = slice(n, n + width)
+            total_ref[:, lanes] += jnp.dot(rows, block_ref[:, lanes], preferred_element_type=F32)
+
+    def rest_step(i, _):
+        copy_of(i, i).wait()
+        add(rows_ref[held + i], rest_ref.at[i])
+        return 0
+
+    def half_step(part, _):
+        first = pl.multiple_of(part * half, half)
+        copy_of(rest - 1, rest - 1 + part, first, half).wait()
+        add(halves_ref[part], rest_ref.at[rest - 1, pl.ds(first, half), :])
+        return 0
+
+    def sent_step(n, _):
+        lanes = pl.ds(pl.multiple_of(n * width, width), width)
+        for turn in range(1, sections):
             rows = rows_of(turn, total_ref, lanes, tensors, sections)
             sent_ref[turn - 1, :, lanes] = rows.astype(BF16)
+        return 0
+
+    lax.fori_loop(0, columns // width, held_step, 0)
+    lax.fori_loop(0, rest - 1, rest_step, 0)
+    lax.fori_loop(0, 2, half_step, 0)
+    lax.fori_loop(0, columns // width, sent_step, 0)
 
 
 def rows_of(turn, total_ref, lanes, tensors, sections):
@@ -182,9 +188,10 @@
         in_specs=[whole(), whole(), whole(), pl.BlockSpec(memory_space=pl.ANY)],
         out_specs=(whole(), whole()),
         scratch_shapes=[
-            pltpu.VMEM((depth // step, rows, step), BF16),
+            pltpu.VMEM((depth // step - 1, rows, step), BF16),
+            pltpu.VMEM((2, rows, step // 2), BF16),
             pltpu.VMEM((rest, step, columns), BF16),
-            pltpu.SemaphoreType.DMA((rest - 1 + len(last_parts(step)),)),
+            pltpu.SemaphoreType.DMA((rest + 1,)),
         ],
         compiler_params=pltpu.CompilerParams(vmem_limit_bytes=36 * MIB),
         cost_estimate=pl.CostEstimate(

time: 36.9 us -> 36.1 us (0.978)
  Pallas kernels: 21.8 us -> 21 us
    pallas_call x1, Pallas kernels: 12.2 us -> 11.4 us  [project(): pl.pallas_call(functools.partial(project_kernel, tensors=tensors, section...]
where the time goes in v12:
time: 36.1 us; the launch traced here: 35.9 us
  Pallas kernels  21 us (58%)
  starting transfers between devices  7.61 us (21%)
  waiting for transfers between devices  5.9 us (16%)
  between operations  0.74 us (2%)
  local copies, waits for them, and re-layouts  0.66 us (2%)
    pallas_call x1, Pallas kernels, project(): pl.pallas_call(functools.partial(project_kernel, tensors=tensors, section...  11.4 us
    pallas_call x1, Pallas kernels, fetch(): pl.pallas_call(fetch_kernel, out_shape=pltpu.VMEM((count, step, columns),...  7.09 us
    ppermute x3, starting transfers between devices, across(): return lax.ppermute(array, ('tensor', 'section'), pairs)  3.94 us
    ppermute x3, starting transfers between devices, shifted(): lax.ppermute(array, axis, [(i, (i + shift) % count) for i in range(count)])  3.67 us
    ppermute x3, waiting for transfers between devices, shifted(): lax.ppermute(array, axis, [(i, (i + shift) % count) for i in range(count)])  3.59 us
    ppermute x3, waiting for transfers between devices, across(): return lax.ppermute(array, ('tensor', 'section'), pairs)  2.31 us
    pallas_call x1, Pallas kernels, prepare(): pl.pallas_call(functools.partial(prepare_kernel, slots=slots, owners=owne...  1.23 us
    pallas_call x1, Pallas kernels, finish(): pl.pallas_call(finish_kernel, out_shape=jax.ShapeDtypeStruct((local, 1, M...  0.84 us
  transfers between devices with their start and end apart: 6, of which 4 were waited for; matrix products, arithmetic and copies ran while one was open for 2% of the time, Pallas kernels for 24%

profile of v12, /device:TPU:0, one launch (start us, length us, event | category | flops | bytes accessed | tf_op | source)
XLA Modules:
  0.0 35.9 jit_solution(15667036745963270887)
XLA Ops:
  0.6 0.0 copy-start
  0.6 3.0 %collective-permute-start = (bf16[16,6656]{1,0:T(8,128)(2,1)}, bf16[16,6656]{1,0:T(8,128)(2,1)S(1)}, u32[]{:S(2)}, u32[]{:S(2)}) collective-permute-start(bf16[16,6656]{1,0:T(8,128)(2,1)} %own_ref.1), channel_id=1, source_target_pairs={{0,2},{2,0},{1,3},{3,1},{4,6},{6,4},{5,7},{7,5},{8,10},{10,8},{9,1... | collective-permute-start | bytes 638984 | tf_op jit(solution)/shard_map/ppermute | solution.py:409
  3.6 7.1 %fetch.1.held_ref = bf16[5,512,4096]{2,1,0:T(8,128)(2,1)S(1)} custom-call(bf16[6656,4096]{1,0:T(8,128)(2,1)} %weight_ref.3), custom_call_target="tpu_custom_call" | custom-call | bytes 20971520 | tf_op jit(solution)/shard_map/fetch/pallas_call | solution.py:44
  10.7 0.0 copy-start.2
  10.8 0.0 copy-start.1
  10.8 0.0 copy-start.3
  10.8 0.0 collective-permute-done
  10.8 0.0 copy-done
  10.8 11.4 %project.1 = (f32[32,4096]{1,0:T(8,128)S(1)}, bf16[1,16,4096]{2,1,0:T(8,128)(2,1)S(1)}) custom-call(bf16[16,6656]{1,0:T(8,128)(2,1)S(1)} %copy-done, bf16[1,16,6656]{2,1,0:T(8,128)(2,1)S(1)} %bitcast.5, bf16[5,512,4096]{2,1,0:T(8,128)(2,1)S(1)} %fetch.1.held_ref, bf16[6656,4096]{1,0:T(8,128)(2,1)} %weight_ref.3), custom_call_target="tpu_custom_call" | custom-call | flops 1744830464 | bytes 33554432 | tf_op jit(solution)/shard_map/project/pallas_call | solution.py:182
  22.2 0.1 collective-permute-start.1
  22.3 1.3 %collective-permute-done.1.refs_0_ = bf16[16,4096]{1,0:T(8,128)(2,1)S(1)} collective-permute-done((bf16[16,4096]{1,0:T(8,128)(2,1)S(1)}, bf16[16,4096]{1,0:T(8,128)(2,1)S(1)}, u32[]{:S(2)}, u32[]{:S(2)}) %collective-permute-start.1) | collective-permute-done | bytes 131104 | tf_op jit(solution)/shard_map/ppermute | solution.py:409
  23.7 2.4 %collective-permute-start.2 = (bf16[4,4096]{1,0:T(4,128)(2,1)S(1)}, bf16[4,4096]{1,0:T(4,128)(2,1)S(1)}, u32[]{:S(2)}, u32[]{:S(2)}) collective-permute-start(bf16[4,4096]{1,0:T(4,128)(2,1)S(1)} %get-tuple-element.23), channel_id=1, source_target_pairs={{0,9},{1,8},{4,13},{5,12},{8,5},{9,4},{12,1},{13,0},{2,11},{3,10},... | collective-permute-start | bytes 98312 | tf_op jit(solution)/shard_map/ppermute | solution.py:419
  26.1 1.2 %collective-permute-start.3 = (bf16[4,4096]{1,0:T(4,128)(2,1)S(1)}, bf16[4,4096]{1,0:T(4,128)(2,1)S(1)}, u32[]{:S(2)}, u32[]{:S(2)}) collective-permute-start(bf16[4,4096]{1,0:T(4,128)(2,1)S(1)} %get-tuple-element.24), channel_id=1, source_target_pairs={{0,13},{1,12},{4,9},{5,8},{8,1},{9,0},{12,5},{13,4},{2,15},{3,14},... | collective-permute-start | bytes 98312 | tf_op jit(solution)/shard_map/ppermute | solution.py:419
  27.3 0.3 collective-permute-start.4
  27.6 0.0 copy-done.2
  27.6 1.2 %prepare.1 = (f32[4,4]{1,0:T(4,128)S(1)}, bf16[1,64,8192]{2,1,0:T(8,128)(2,1)S(1)}) custom-call(s32[1,4]{1,0:T(1,128)S(1)} %bitcast.6, bf16[1,64,8192]{2,1,0:T(8,128)(2,1)} %bitcast.9), custom_call_target="tpu_custom_call" | custom-call | tf_op jit(solution)/shard_map/prepare/pallas_call | solution.py:277
  28.8 0.0 collective-permute-done.2.refs_0_
  28.9 1.5 %collective-permute-done.3.refs_1_ = bf16[4,4096]{1,0:T(4,128)(2,1)S(1)} collective-permute-done((bf16[4,4096]{1,0:T(4,128)(2,1)S(1)}, bf16[4,4096]{1,0:T(4,128)(2,1)S(1)}, u32[]{:S(2)}, u32[]{:S(2)}) %collective-permute-start.3) | collective-permute-done | bytes 32800 | tf_op jit(solution)/shard_map/ppermute | solution.py:419
  30.3 0.8 %collective-permute-done.4.refs_2_ = bf16[4,4096]{1,0:T(4,128)(2,1)S(1)} collective-permute-done((bf16[4,4096]{1,0:T(4,128)(2,1)S(1)}, bf16[4,4096]{1,0:T(4,128)(2,1)S(1)}, u32[]{:S(2)}, u32[]{:S(2)}) %collective-permute-start.4) | collective-permute-done | bytes 32800 | tf_op jit(solution)/shard_map/ppermute | solution.py:419
  31.2 0.0 copy-done.1
  31.2 0.1 mix.1
  31.3 0.6 %collective-permute-start.5 = (bf16[2,4096]{1,0:T(2,128)(2,1)S(1)}, bf16[2,4096]{1,0:T(2,128)(2,1)S(1)}, u32[]{:S(2)}, u32[]{:S(2)}) collective-permute-start(bf16[2,4096]{1,0:T(2,128)(2,1)S(1)} %bitcast.8), channel_id=1, source_target_pairs={{0,2},{2,0},{1,3},{3,1},{4,6},{6,4},{5,7},{7,5},{8,10},{10,8},{9,1... | collective-permute-start | bytes 49160 | tf_op jit(solution)/shard_map/ppermute | solution.py:409
  31.9 0.0 copy-done.3
  31.9 0.6 %copy.8 = bf16[4,4096]{1,0:T(4,128)(2,1)} copy(bf16[4,4096]{1,0:T(4,128)(2,1)S(1)} %get-tuple-element.32) | data formatting | bytes 65536
  32.5 0.3 own_half.1
  32.8 2.3 %collective-permute-done.5.refs_0_ = bf16[2,4096]{1,0:T(2,128)(2,1)S(1)} collective-permute-done((bf16[2,4096]{1,0:T(2,128)(2,1)S(1)}, bf16[2,4096]{1,0:T(2,128)(2,1)S(1)}, u32[]{:S(2)}, u32[]{:S(2)}) %collective-permute-start.5) | collective-permute-done | bytes 16416 | tf_op jit(solution)/shard_map/ppermute | solution.py:409
  35.1 0.8 %finish.1 = f32[1,1,2,64]{3,2,1,0:T(2,128)} custom-call(f32[2,64]{1,0:T(2,128)S(1)} %get-tuple-element.29.values_ref, f32[2,64]{1,0:T(2,128)S(1)} %get-tuple-element.30.squares_ref, bf16[1,8192]{1,0:T(2,128)(2,1)S(1)} %broadcast_in_dim.3.gain_ref, bf16[1,64,8192]{2,1,0:T(8,128)(2,1)S(1)} %get-tuple-element.28.shrink_ref, ...), custom_call_target="tpu_custom_call" | custom-call | tf_op jit(solution)/shard_map/finish/pallas_call | solution.py:397
  (3 shorter events, 0.1 us)
Async XLA Ops:
  0.6 10.2 %copy-start = (bf16[16,6656]{1,0:T(8,128)(2,1)S(1)}, bf16[16,6656]{1,0:T(8,128)(2,1)}, u32[]{:S(2)}) copy-start(bf16[16,6656]{1,0:T(8,128)(2,1)} %own_ref.1) | copy-start | bytes 638980
  0.6 10.1 %collective-permute-start = (bf16[16,6656]{1,0:T(8,128)(2,1)}, bf16[16,6656]{1,0:T(8,128)(2,1)S(1)}, u32[]{:S(2)}, u32[]{:S(2)}) collective-permute-start(bf16[16,6656]{1,0:T(8,128)(2,1)} %own_ref.1), channel_id=1, source_target_pairs={{0,2},{2,0},{1,3},{3,1},{4,6},{6,4},{5,7},{7,5},{8,10},{10,8},{9,1... | collective-permute-start | bytes 638984 | tf_op jit(solution)/shard_map/ppermute | solution.py:409
  10.7 16.9 %copy-start.2 = (s32[4,1]{0,1:T(1,128)S(1)}, s32[4,1]{0,1:T(1,128)}, u32[]{:S(2)}) copy-start(s32[4,1]{0,1:T(1,128)} %param.11) | copy-start | bytes 52
  10.8 20.4 %copy-start.1 = (bf16[4,4096]{1,0:T(4,128)(2,1)S(1)}, bf16[4,4096]{1,0:T(4,128)(2,1)}, u32[]{:S(2)}) copy-start(bf16[4,4096]{1,0:T(4,128)(2,1)} %residual_ref.1) | copy-start | bytes 98308
  10.8 21.1 %copy-start.3 = (bf16[8192]{0:T(1024)(128)(2,1)S(1)}, bf16[8192]{0:T(1024)(128)(2,1)}, u32[]{:S(2)}) copy-start(bf16[8192]{0:T(1024)(128)(2,1)} %param.9) | copy-start | bytes 49156
  22.2 1.4 %collective-permute-start.1 = (bf16[16,4096]{1,0:T(8,128)(2,1)S(1)}, bf16[16,4096]{1,0:T(8,128)(2,1)S(1)}, u32[]{:S(2)}, u32[]{:S(2)}) collective-permute-start(bf16[16,4096]{1,0:T(8,128)(2,1)S(1)} %bitcast.7), channel_id=1, source_target_pairs={{0,1},{1,0},{2,3},{3,2},{4,5},{5,4},{6,7},{7,6},{8,9},{9,8},{10,11... | collective-permute-start | bytes 393224 | tf_op jit(solution)/shard_map/ppermute | solution.py:409
  23.7 5.2 %collective-permute-start.2 = (bf16[4,4096]{1,0:T(4,128)(2,1)S(1)}, bf16[4,4096]{1,0:T(4,128)(2,1)S(1)}, u32[]{:S(2)}, u32[]{:S(2)}) collective-permute-start(bf16[4,4096]{1,0:T(4,128)(2,1)S(1)} %get-tuple-element.23), channel_id=1, source_target_pairs={{0,9},{1,8},{4,13},{5,12},{8,5},{9,4},{12,1},{13,0},{2,11},{3,10},... | collective-permute-start | bytes 98312 | tf_op jit(solution)/shard_map/ppermute | solution.py:419
  26.1 4.3 %collective-permute-start.3 = (bf16[4,4096]{1,0:T(4,128)(2,1)S(1)}, bf16[4,4096]{1,0:T(4,128)(2,1)S(1)}, u32[]{:S(2)}, u32[]{:S(2)}) collective-permute-start(bf16[4,4096]{1,0:T(4,128)(2,1)S(1)} %get-tuple-element.24), channel_id=1, source_target_pairs={{0,13},{1,12},{4,9},{5,8},{8,1},{9,0},{12,5},{13,4},{2,15},{3,14},... | collective-permute-start | bytes 98312 | tf_op jit(solution)/shard_map/ppermute | solution.py:419
  27.3 3.9 %collective-permute-start.4 = (bf16[4,4096]{1,0:T(4,128)(2,1)S(1)}, bf16[4,4096]{1,0:T(4,128)(2,1)S(1)}, u32[]{:S(2)}, u32[]{:S(2)}) collective-permute-start(bf16[4,4096]{1,0:T(4,128)(2,1)S(1)} %get-tuple-element.25), channel_id=1, source_target_pairs={{0,5},{1,4},{4,1},{5,0},{8,13},{9,12},{12,9},{13,8},{2,7},{3,6},{6... | collective-permute-start | bytes 98312 | tf_op jit(solution)/shard_map/ppermute | solution.py:419
  31.3 3.8 %collective-permute-start.5 = (bf16[2,4096]{1,0:T(2,128)(2,1)S(1)}, bf16[2,4096]{1,0:T(2,128)(2,1)S(1)}, u32[]{:S(2)}, u32[]{:S(2)}) collective-permute-start(bf16[2,4096]{1,0:T(2,128)(2,1)S(1)} %bitcast.8), channel_id=1, source_target_pairs={{0,2},{2,0},{1,3},{3,1},{4,6},{6,4},{5,7},{7,5},{8,10},{10,8},{9,1... | collective-permute-start | bytes 49160 | tf_op jit(solution)/shard_map/ppermute | solution.py:409

commit v13 on v11

--- a/solution.py
+++ b/solution.py
@@ -103,6 +103,14 @@
             source = own_ref[:, block] if shift == 0 else others_ref[shift - 1, :, block]
             rows_ref[i, pl.ds(first, own_rows), :] = source
 
+    def held_step(n, _):
+        lanes = pl.ds(pl.multiple_of(n * width, width), width)
+        total_ref[:, lanes] = sum(
+            jnp.dot(rows_ref[i], held_ref[i, :, lanes], preferred_element_type=F32)
+            for i in range(held)
+        )
+        return 0
+
     def add(i, part=slice(None)):
         for n in range(0, columns, width):
             lanes = slice(n, n + width)
@@ -115,12 +123,7 @@
         add(i)
         return 0
 
-    for n in range(0, columns, width):
-        lanes = slice(n, n + width)
-        total_ref[:, lanes] = sum(
-            jnp.dot(rows_ref[i], held_ref[i, :, lanes], preferred_element_type=F32)
-            for i in range(held)
-        )
+    lax.fori_loop(0, columns // width, held_step, 0)
     lax.fori_loop(0, rest - 1, rest_step, 0)
     for copy, (first, size) in zip(last, parts):
         copy.wait()
@@ -210,7 +213,7 @@
 
 def exchange_plan(count):
     if count == 4:
-        return [(2, 3, 1, 0), (3, 2, 0, 1), (1, 0, 3, 2)]
+        return [(1, 3, 0, 2), (3, 2, 1, 0), (2, 0, 3, 1)]
     turns = range(count - 1, 0, -1)
     return [tuple(partner_of(i, turn, count) for i in range(count)) for turn in turns]
 

time: 36.9 us -> 36.1 us (0.978)
  starting transfers between devices: 7.61 us -> 8.81 us
  waiting for transfers between devices: 5.91 us -> 4.89 us
  Pallas kernels: 21.8 us -> 20.9 us
    ppermute x3, starting transfers between devices: 3.94 us -> 5.16 us  [across(): return lax.ppermute(array, ('tensor', 'section'), pairs)]
    ppermute x3, waiting for transfers between devices: 2.32 us -> 1.28 us  [across(): return lax.ppermute(array, ('tensor', 'section'), pairs)]
    pallas_call x1, Pallas kernels: 12.2 us -> 11.2 us  [project(): pl.pallas_call(functools.partial(project_kernel, tensors=tensors, section...]
where the time goes in v13:
time: 36.1 us; the launch traced here: 36 us
  Pallas kernels  20.9 us (58%)
  starting transfers between devices  8.81 us (24%)
  waiting for transfers between devices  4.89 us (14%)
  between operations  0.74 us (2%)
  local copies, waits for them, and re-layouts  0.66 us (2%)
    pallas_call x1, Pallas kernels, project(): pl.pallas_call(functools.partial(project_kernel, tensors=tensors, section...  11.2 us
    pallas_call x1, Pallas kernels, fetch(): pl.pallas_call(fetch_kernel, out_shape=pltpu.VMEM((count, step, columns),...  7.09 us
    ppermute x3, starting transfers between devices, across(): return lax.ppermute(array, ('tensor', 'section'), pairs)  5.16 us
    ppermute x3, starting transfers between devices, shifted(): lax.ppermute(array, axis, [(i, (i + shift) % count) for i in range(count)])  3.65 us
    ppermute x3, waiting for transfers between devices, shifted(): lax.ppermute(array, axis, [(i, (i + shift) % count) for i in range(count)])  3.61 us
    ppermute x3, waiting for transfers between devices, across(): return lax.ppermute(array, ('tensor', 'section'), pairs)  1.28 us
    pallas_call x1, Pallas kernels, prepare(): pl.pallas_call(functools.partial(prepare_kernel, slots=slots, owners=owne...  1.23 us
    pallas_call x1, Pallas kernels, finish(): pl.pallas_call(finish_kernel, out_shape=jax.ShapeDtypeStruct((local, 1, M...  0.84 us
  transfers between devices with their start and end apart: 6, of which 4 were waited for; matrix products, arithmetic and copies ran while one was open for 2% of the time, Pallas kernels for 24%

profile of v13, /device:TPU:0, one launch (start us, length us, event | category | flops | bytes accessed | tf_op | source)
XLA Modules:
  0.0 36.0 jit_solution(16764683197472381947)
XLA Ops:
  0.6 0.0 copy-start
  0.6 3.0 %collective-permute-start = (bf16[16,6656]{1,0:T(8,128)(2,1)}, bf16[16,6656]{1,0:T(8,128)(2,1)S(1)}, u32[]{:S(2)}, u32[]{:S(2)}) collective-permute-start(bf16[16,6656]{1,0:T(8,128)(2,1)} %own_ref.1), channel_id=1, source_target_pairs={{0,2},{2,0},{1,3},{3,1},{4,6},{6,4},{5,7},{7,5},{8,10},{10,8},{9,1... | collective-permute-start | bytes 638984 | tf_op jit(solution)/shard_map/ppermute | solution.py:405
  3.6 7.1 %fetch.1.held_ref = bf16[5,512,4096]{2,1,0:T(8,128)(2,1)S(1)} custom-call(bf16[6656,4096]{1,0:T(8,128)(2,1)} %weight_ref.3), custom_call_target="tpu_custom_call" | custom-call | bytes 20971520 | tf_op jit(solution)/shard_map/fetch/pallas_call | solution.py:44
  10.7 0.0 copy-start.2
  10.8 0.0 copy-start.1
  10.8 0.0 copy-start.3
  10.8 0.0 collective-permute-done
  10.8 0.0 copy-done
  10.8 11.2 %project.1 = (f32[32,4096]{1,0:T(8,128)S(1)}, bf16[1,16,4096]{2,1,0:T(8,128)(2,1)S(1)}) custom-call(bf16[16,6656]{1,0:T(8,128)(2,1)S(1)} %copy-done, bf16[1,16,6656]{2,1,0:T(8,128)(2,1)S(1)} %bitcast.5, bf16[5,512,4096]{2,1,0:T(8,128)(2,1)S(1)} %fetch.1.held_ref, bf16[6656,4096]{1,0:T(8,128)(2,1)} %weight_ref.3), custom_call_target="tpu_custom_call" | custom-call | flops 1744830464 | bytes 33554432 | tf_op jit(solution)/shard_map/project/pallas_call | solution.py:179
  22.0 0.1 collective-permute-start.1
  22.2 1.3 %collective-permute-done.1.refs_0_ = bf16[16,4096]{1,0:T(8,128)(2,1)S(1)} collective-permute-done((bf16[16,4096]{1,0:T(8,128)(2,1)S(1)}, bf16[16,4096]{1,0:T(8,128)(2,1)S(1)}, u32[]{:S(2)}, u32[]{:S(2)}) %collective-permute-start.1) | collective-permute-done | bytes 131104 | tf_op jit(solution)/shard_map/ppermute | solution.py:405
  23.4 0.1 pair.1
  23.5 1.4 %collective-permute-start.2 = (bf16[4,4096]{1,0:T(4,128)(2,1)S(1)}, bf16[4,4096]{1,0:T(4,128)(2,1)S(1)}, u32[]{:S(2)}, u32[]{:S(2)}) collective-permute-start(bf16[4,4096]{1,0:T(4,128)(2,1)S(1)} %get-tuple-element.23), channel_id=1, source_target_pairs={{0,5},{1,4},{4,13},{5,12},{8,1},{9,0},{12,9},{13,8},{2,7},{3,6},{6... | collective-permute-start | bytes 98312 | tf_op jit(solution)/shard_map/ppermute | solution.py:415
  24.9 2.4 %collective-permute-start.3 = (bf16[4,4096]{1,0:T(4,128)(2,1)S(1)}, bf16[4,4096]{1,0:T(4,128)(2,1)S(1)}, u32[]{:S(2)}, u32[]{:S(2)}) collective-permute-start(bf16[4,4096]{1,0:T(4,128)(2,1)S(1)} %get-tuple-element.24), channel_id=1, source_target_pairs={{0,13},{1,12},{4,9},{5,8},{8,5},{9,4},{12,1},{13,0},{2,15},{3,14},... | collective-permute-start | bytes 98312 | tf_op jit(solution)/shard_map/ppermute | solution.py:415
  27.3 1.3 %collective-permute-start.4 = (bf16[4,4096]{1,0:T(4,128)(2,1)S(1)}, bf16[4,4096]{1,0:T(4,128)(2,1)S(1)}, u32[]{:S(2)}, u32[]{:S(2)}) collective-permute-start(bf16[4,4096]{1,0:T(4,128)(2,1)S(1)} %get-tuple-element.25), channel_id=1, source_target_pairs={{0,9},{1,8},{4,1},{5,0},{8,13},{9,12},{12,5},{13,4},{2,11},{3,10},... | collective-permute-start | bytes 98312 | tf_op jit(solution)/shard_map/ppermute | solution.py:415
  28.7 0.0 copy-done.2
  28.7 1.2 %prepare.1 = (f32[4,4]{1,0:T(4,128)S(1)}, bf16[1,64,8192]{2,1,0:T(8,128)(2,1)S(1)}) custom-call(s32[1,4]{1,0:T(1,128)S(1)} %bitcast.6, bf16[1,64,8192]{2,1,0:T(8,128)(2,1)} %bitcast.9), custom_call_target="tpu_custom_call" | custom-call | tf_op jit(solution)/shard_map/prepare/pallas_call | solution.py:273
  29.9 0.0 collective-permute-done.2.refs_0_
  29.9 0.1 collective-permute-done.3.refs_1_
  30.0 1.1 %collective-permute-done.4.refs_2_ = bf16[4,4096]{1,0:T(4,128)(2,1)S(1)} collective-permute-done((bf16[4,4096]{1,0:T(4,128)(2,1)S(1)}, bf16[4,4096]{1,0:T(4,128)(2,1)S(1)}, u32[]{:S(2)}, u32[]{:S(2)}) %collective-permute-start.4) | collective-permute-done | bytes 32800 | tf_op jit(solution)/shard_map/ppermute | solution.py:415
  31.2 0.0 copy-done.1
  31.2 0.1 mix.1
  31.3 0.6 %collective-permute-start.5 = (bf16[2,4096]{1,0:T(2,128)(2,1)S(1)}, bf16[2,4096]{1,0:T(2,128)(2,1)S(1)}, u32[]{:S(2)}, u32[]{:S(2)}) collective-permute-start(bf16[2,4096]{1,0:T(2,128)(2,1)S(1)} %bitcast.8), channel_id=1, source_target_pairs={{0,2},{2,0},{1,3},{3,1},{4,6},{6,4},{5,7},{7,5},{8,10},{10,8},{9,1... | collective-permute-start | bytes 49160 | tf_op jit(solution)/shard_map/ppermute | solution.py:405
  31.9 0.0 copy-done.3
  31.9 0.6 %copy.8 = bf16[4,4096]{1,0:T(4,128)(2,1)} copy(bf16[4,4096]{1,0:T(4,128)(2,1)S(1)} %get-tuple-element.32) | data formatting | bytes 65536
  32.5 0.3 own_half.1
  32.8 2.3 %collective-permute-done.5.refs_0_ = bf16[2,4096]{1,0:T(2,128)(2,1)S(1)} collective-permute-done((bf16[2,4096]{1,0:T(2,128)(2,1)S(1)}, bf16[2,4096]{1,0:T(2,128)(2,1)S(1)}, u32[]{:S(2)}, u32[]{:S(2)}) %collective-permute-start.5) | collective-permute-done | bytes 16416 | tf_op jit(solution)/shard_map/ppermute | solution.py:405
  35.1 0.8 %finish.1 = f32[1,1,2,64]{3,2,1,0:T(2,128)} custom-call(f32[2,64]{1,0:T(2,128)S(1)} %get-tuple-element.29.values_ref, f32[2,64]{1,0:T(2,128)S(1)} %get-tuple-element.30.squares_ref, bf16[1,8192]{1,0:T(2,128)(2,1)S(1)} %broadcast_in_dim.3.gain_ref, bf16[1,64,8192]{2,1,0:T(8,128)(2,1)S(1)} %get-tuple-element.28.shrink_ref, ...), custom_call_target="tpu_custom_call" | custom-call | tf_op jit(solution)/shard_map/finish/pallas_call | solution.py:393
  (2 shorter events, 0.1 us)
Async XLA Ops:
  0.6 10.2 %copy-start = (bf16[16,6656]{1,0:T(8,128)(2,1)S(1)}, bf16[16,6656]{1,0:T(8,128)(2,1)}, u32[]{:S(2)}) copy-start(bf16[16,6656]{1,0:T(8,128)(2,1)} %own_ref.1) | copy-start | bytes 638980
  0.6 10.1 %collective-permute-start = (bf16[16,6656]{1,0:T(8,128)(2,1)}, bf16[16,6656]{1,0:T(8,128)(2,1)S(1)}, u32[]{:S(2)}, u32[]{:S(2)}) collective-permute-start(bf16[16,6656]{1,0:T(8,128)(2,1)} %own_ref.1), channel_id=1, source_target_pairs={{0,2},{2,0},{1,3},{3,1},{4,6},{6,4},{5,7},{7,5},{8,10},{10,8},{9,1... | collective-permute-start | bytes 638984 | tf_op jit(solution)/shard_map/ppermute | solution.py:405
  10.7 17.9 %copy-start.2 = (s32[4,1]{0,1:T(1,128)S(1)}, s32[4,1]{0,1:T(1,128)}, u32[]{:S(2)}) copy-start(s32[4,1]{0,1:T(1,128)} %param.11) | copy-start | bytes 52
  10.8 20.4 %copy-start.1 = (bf16[4,4096]{1,0:T(4,128)(2,1)S(1)}, bf16[4,4096]{1,0:T(4,128)(2,1)}, u32[]{:S(2)}) copy-start(bf16[4,4096]{1,0:T(4,128)(2,1)} %residual_ref.1) | copy-start | bytes 98308
  10.8 21.1 %copy-start.3 = (bf16[8192]{0:T(1024)(128)(2,1)S(1)}, bf16[8192]{0:T(1024)(128)(2,1)}, u32[]{:S(2)}) copy-start(bf16[8192]{0:T(1024)(128)(2,1)} %param.9) | copy-start | bytes 49156
  22.0 1.4 %collective-permute-start.1 = (bf16[16,4096]{1,0:T(8,128)(2,1)S(1)}, bf16[16,4096]{1,0:T(8,128)(2,1)S(1)}, u32[]{:S(2)}, u32[]{:S(2)}) collective-permute-start(bf16[16,4096]{1,0:T(8,128)(2,1)S(1)} %bitcast.7), channel_id=1, source_target_pairs={{0,1},{1,0},{2,3},{3,2},{4,5},{5,4},{6,7},{7,6},{8,9},{9,8},{10,11... | collective-permute-start | bytes 393224 | tf_op jit(solution)/shard_map/ppermute | solution.py:405
  23.5 6.4 %collective-permute-start.2 = (bf16[4,4096]{1,0:T(4,128)(2,1)S(1)}, bf16[4,4096]{1,0:T(4,128)(2,1)S(1)}, u32[]{:S(2)}, u32[]{:S(2)}) collective-permute-start(bf16[4,4096]{1,0:T(4,128)(2,1)S(1)} %get-tuple-element.23), channel_id=1, source_target_pairs={{0,5},{1,4},{4,13},{5,12},{8,1},{9,0},{12,9},{13,8},{2,7},{3,6},{6... | collective-permute-start | bytes 98312 | tf_op jit(solution)/shard_map/ppermute | solution.py:415
  24.9 5.2 %collective-permute-start.3 = (bf16[4,4096]{1,0:T(4,128)(2,1)S(1)}, bf16[4,4096]{1,0:T(4,128)(2,1)S(1)}, u32[]{:S(2)}, u32[]{:S(2)}) collective-permute-start(bf16[4,4096]{1,0:T(4,128)(2,1)S(1)} %get-tuple-element.24), channel_id=1, source_target_pairs={{0,13},{1,12},{4,9},{5,8},{8,5},{9,4},{12,1},{13,0},{2,15},{3,14},... | collective-permute-start | bytes 98312 | tf_op jit(solution)/shard_map/ppermute | solution.py:415
  27.3 3.9 %collective-permute-start.4 = (bf16[4,4096]{1,0:T(4,128)(2,1)S(1)}, bf16[4,4096]{1,0:T(4,128)(2,1)S(1)}, u32[]{:S(2)}, u32[]{:S(2)}) collective-permute-start(bf16[4,4096]{1,0:T(4,128)(2,1)S(1)} %get-tuple-element.25), channel_id=1, source_target_pairs={{0,9},{1,8},{4,1},{5,0},{8,13},{9,12},{12,5},{13,4},{2,11},{3,10},... | collective-permute-start | bytes 98312 | tf_op jit(solution)/shard_map/ppermute | solution.py:415
  31.3 3.8 %collective-permute-start.5 = (bf16[2,4096]{1,0:T(2,128)(2,1)S(1)}, bf16[2,4096]{1,0:T(2,128)(2,1)S(1)}, u32[]{:S(2)}, u32[]{:S(2)}) collective-permute-start(bf16[2,4096]{1,0:T(2,128)(2,1)S(1)} %bitcast.8), channel_id=1, source_target_pairs={{0,2},{2,0},{1,3},{3,1},{4,6},{6,4},{5,7},{7,5},{8,10},{10,8},{9,1... | collective-permute-start | bytes 49160 | tf_op jit(solution)/shard_map/ppermute | solution.py:405

commit v14 on v13

--- a/solution.py
+++ b/solution.py
@@ -213,7 +213,7 @@
 
 def exchange_plan(count):
     if count == 4:
-        return [(1, 3, 0, 2), (3, 2, 1, 0), (2, 0, 3, 1)]
+        return [(2, 3, 1, 0), (3, 2, 0, 1), (1, 0, 3, 2)]
     turns = range(count - 1, 0, -1)
     return [tuple(partner_of(i, turn, count) for i in range(count)) for turn in turns]
 

time: 36.1 us -> 35.9 us (level)
  starting transfers between devices: 8.81 us -> 7.61 us
  waiting for transfers between devices: 4.89 us -> 5.9 us
    ppermute x3, starting transfers between devices: 5.16 us -> 3.94 us  [across(): return lax.ppermute(array, ('tensor', 'section'), pairs)]
    ppermute x3, waiting for transfers between devices: 1.28 us -> 2.31 us  [across(): return lax.ppermute(array, ('tensor', 'section'), pairs)]
where the time goes in v14:
time: 35.9 us; the launch traced here: 35.8 us
  Pallas kernels  20.9 us (58%)
  starting transfers between devices  7.61 us (21%)
  waiting for transfers between devices  5.9 us (16%)
  between operations  0.74 us (2%)
  local copies, waits for them, and re-layouts  0.66 us (2%)
    pallas_call x1, Pallas kernels, project(): pl.pallas_call(functools.partial(project_kernel, tensors=tensors, section...  11.2 us
    pallas_call x1, Pallas kernels, fetch(): pl.pallas_call(fetch_kernel, out_shape=pltpu.VMEM((count, step, columns),...  7.09 us
    ppermute x3, starting transfers between devices, across(): return lax.ppermute(array, ('tensor', 'section'), pairs)  3.94 us
    ppermute x3, starting transfers between devices, shifted(): lax.ppermute(array, axis, [(i, (i + shift) % count) for i in range(count)])  3.68 us
    ppermute x3, waiting for transfers between devices, shifted(): lax.ppermute(array, axis, [(i, (i + shift) % count) for i in range(count)])  3.58 us
    ppermute x3, waiting for transfers between devices, across(): return lax.ppermute(array, ('tensor', 'section'), pairs)  2.31 us
    pallas_call x1, Pallas kernels, prepare(): pl.pallas_call(functools.partial(prepare_kernel, slots=slots, owners=owne...  1.23 us
    pallas_call x1, Pallas kernels, finish(): pl.pallas_call(finish_kernel, out_shape=jax.ShapeDtypeStruct((local, 1, M...  0.84 us
  transfers between devices with their start and end apart: 6, of which 4 were waited for; matrix products, arithmetic and copies ran while one was open for 2% of the time, Pallas kernels for 24%

profile of v14, /device:TPU:0, one launch (start us, length us, event | category | flops | bytes accessed | tf_op | source)
XLA Modules:
  0.0 35.8 jit_solution(15934867741159665891)
XLA Ops:
  0.6 0.0 copy-start
  0.6 3.0 %collective-permute-start = (bf16[16,6656]{1,0:T(8,128)(2,1)}, bf16[16,6656]{1,0:T(8,128)(2,1)S(1)}, u32[]{:S(2)}, u32[]{:S(2)}) collective-permute-start(bf16[16,6656]{1,0:T(8,128)(2,1)} %own_ref.1), channel_id=1, source_target_pairs={{0,2},{2,0},{1,3},{3,1},{4,6},{6,4},{5,7},{7,5},{8,10},{10,8},{9,1... | collective-permute-start | bytes 638984 | tf_op jit(solution)/shard_map/ppermute | solution.py:405
  3.6 7.1 %fetch.1.held_ref = bf16[5,512,4096]{2,1,0:T(8,128)(2,1)S(1)} custom-call(bf16[6656,4096]{1,0:T(8,128)(2,1)} %weight_ref.3), custom_call_target="tpu_custom_call" | custom-call | bytes 20971520 | tf_op jit(solution)/shard_map/fetch/pallas_call | solution.py:44
  10.7 0.0 copy-start.2
  10.8 0.0 copy-start.1
  10.8 0.0 copy-start.3
  10.8 0.0 collective-permute-done
  10.8 0.0 copy-done
  10.8 11.2 %project.1 = (f32[32,4096]{1,0:T(8,128)S(1)}, bf16[1,16,4096]{2,1,0:T(8,128)(2,1)S(1)}) custom-call(bf16[16,6656]{1,0:T(8,128)(2,1)S(1)} %copy-done, bf16[1,16,6656]{2,1,0:T(8,128)(2,1)S(1)} %bitcast.5, bf16[5,512,4096]{2,1,0:T(8,128)(2,1)S(1)} %fetch.1.held_ref, bf16[6656,4096]{1,0:T(8,128)(2,1)} %weight_ref.3), custom_call_target="tpu_custom_call" | custom-call | flops 1744830464 | bytes 33554432 | tf_op jit(solution)/shard_map/project/pallas_call | solution.py:179
  22.0 0.1 collective-permute-start.1
  22.2 1.3 %collective-permute-done.1.refs_0_ = bf16[16,4096]{1,0:T(8,128)(2,1)S(1)} collective-permute-done((bf16[16,4096]{1,0:T(8,128)(2,1)S(1)}, bf16[16,4096]{1,0:T(8,128)(2,1)S(1)}, u32[]{:S(2)}, u32[]{:S(2)}) %collective-permute-start.1) | collective-permute-done | bytes 131104 | tf_op jit(solution)/shard_map/ppermute | solution.py:405
  23.5 2.4 %collective-permute-start.2 = (bf16[4,4096]{1,0:T(4,128)(2,1)S(1)}, bf16[4,4096]{1,0:T(4,128)(2,1)S(1)}, u32[]{:S(2)}, u32[]{:S(2)}) collective-permute-start(bf16[4,4096]{1,0:T(4,128)(2,1)S(1)} %get-tuple-element.23), channel_id=1, source_target_pairs={{0,9},{1,8},{4,13},{5,12},{8,5},{9,4},{12,1},{13,0},{2,11},{3,10},... | collective-permute-start | bytes 98312 | tf_op jit(solution)/shard_map/ppermute | solution.py:415
  25.9 1.2 %collective-permute-start.3 = (bf16[4,4096]{1,0:T(4,128)(2,1)S(1)}, bf16[4,4096]{1,0:T(4,128)(2,1)S(1)}, u32[]{:S(2)}, u32[]{:S(2)}) collective-permute-start(bf16[4,4096]{1,0:T(4,128)(2,1)S(1)} %get-tuple-element.24), channel_id=1, source_target_pairs={{0,13},{1,12},{4,9},{5,8},{8,1},{9,0},{12,5},{13,4},{2,15},{3,14},... | collective-permute-start | bytes 98312 | tf_op jit(solution)/shard_map/ppermute | solution.py:415
  27.1 0.3 collective-permute-start.4
  27.4 0.0 copy-done.2
  27.4 1.2 %prepare.1 = (f32[4,4]{1,0:T(4,128)S(1)}, bf16[1,64,8192]{2,1,0:T(8,128)(2,1)S(1)}) custom-call(s32[1,4]{1,0:T(1,128)S(1)} %bitcast.6, bf16[1,64,8192]{2,1,0:T(8,128)(2,1)} %bitcast.9), custom_call_target="tpu_custom_call" | custom-call | tf_op jit(solution)/shard_map/prepare/pallas_call | solution.py:273
  28.7 0.0 collective-permute-done.2.refs_0_
  28.7 1.4 %collective-permute-done.3.refs_1_ = bf16[4,4096]{1,0:T(4,128)(2,1)S(1)} collective-permute-done((bf16[4,4096]{1,0:T(4,128)(2,1)S(1)}, bf16[4,4096]{1,0:T(4,128)(2,1)S(1)}, u32[]{:S(2)}, u32[]{:S(2)}) %collective-permute-start.3) | collective-permute-done | bytes 32800 | tf_op jit(solution)/shard_map/ppermute | solution.py:415
  30.1 0.9 %collective-permute-done.4.refs_2_ = bf16[4,4096]{1,0:T(4,128)(2,1)S(1)} collective-permute-done((bf16[4,4096]{1,0:T(4,128)(2,1)S(1)}, bf16[4,4096]{1,0:T(4,128)(2,1)S(1)}, u32[]{:S(2)}, u32[]{:S(2)}) %collective-permute-start.4) | collective-permute-done | bytes 32800 | tf_op jit(solution)/shard_map/ppermute | solution.py:415
  31.0 0.0 copy-done.1
  31.0 0.1 mix.1
  31.1 0.6 %collective-permute-start.5 = (bf16[2,4096]{1,0:T(2,128)(2,1)S(1)}, bf16[2,4096]{1,0:T(2,128)(2,1)S(1)}, u32[]{:S(2)}, u32[]{:S(2)}) collective-permute-start(bf16[2,4096]{1,0:T(2,128)(2,1)S(1)} %bitcast.8), channel_id=1, source_target_pairs={{0,2},{2,0},{1,3},{3,1},{4,6},{6,4},{5,7},{7,5},{8,10},{10,8},{9,1... | collective-permute-start | bytes 49160 | tf_op jit(solution)/shard_map/ppermute | solution.py:405
  31.7 0.0 copy-done.3
  31.8 0.6 %copy.8 = bf16[4,4096]{1,0:T(4,128)(2,1)} copy(bf16[4,4096]{1,0:T(4,128)(2,1)S(1)} %get-tuple-element.32) | data formatting | bytes 65536
  32.4 0.3 own_half.1
  32.6 2.3 %collective-permute-done.5.refs_0_ = bf16[2,4096]{1,0:T(2,128)(2,1)S(1)} collective-permute-done((bf16[2,4096]{1,0:T(2,128)(2,1)S(1)}, bf16[2,4096]{1,0:T(2,128)(2,1)S(1)}, u32[]{:S(2)}, u32[]{:S(2)}) %collective-permute-start.5) | collective-permute-done | bytes 16416 | tf_op jit(solution)/shard_map/ppermute | solution.py:405
  34.9 0.8 %finish.1 = f32[1,1,2,64]{3,2,1,0:T(2,128)} custom-call(f32[2,64]{1,0:T(2,128)S(1)} %get-tuple-element.29.values_ref, f32[2,64]{1,0:T(2,128)S(1)} %get-tuple-element.30.squares_ref, bf16[1,8192]{1,0:T(2,128)(2,1)S(1)} %broadcast_in_dim.3.gain_ref, bf16[1,64,8192]{2,1,0:T(8,128)(2,1)S(1)} %get-tuple-element.28.shrink_ref, ...), custom_call_target="tpu_custom_call" | custom-call | tf_op jit(solution)/shard_map/finish/pallas_call | solution.py:393
  (3 shorter events, 0.1 us)
Async XLA Ops:
  0.6 10.2 %copy-start = (bf16[16,6656]{1,0:T(8,128)(2,1)S(1)}, bf16[16,6656]{1,0:T(8,128)(2,1)}, u32[]{:S(2)}) copy-start(bf16[16,6656]{1,0:T(8,128)(2,1)} %own_ref.1) | copy-start | bytes 638980
  0.6 10.1 %collective-permute-start = (bf16[16,6656]{1,0:T(8,128)(2,1)}, bf16[16,6656]{1,0:T(8,128)(2,1)S(1)}, u32[]{:S(2)}, u32[]{:S(2)}) collective-permute-start(bf16[16,6656]{1,0:T(8,128)(2,1)} %own_ref.1), channel_id=1, source_target_pairs={{0,2},{2,0},{1,3},{3,1},{4,6},{6,4},{5,7},{7,5},{8,10},{10,8},{9,1... | collective-permute-start | bytes 638984 | tf_op jit(solution)/shard_map/ppermute | solution.py:405
  10.7 16.7 %copy-start.2 = (s32[4,1]{0,1:T(1,128)S(1)}, s32[4,1]{0,1:T(1,128)}, u32[]{:S(2)}) copy-start(s32[4,1]{0,1:T(1,128)} %param.11) | copy-start | bytes 52
  10.8 20.2 %copy-start.1 = (bf16[4,4096]{1,0:T(4,128)(2,1)S(1)}, bf16[4,4096]{1,0:T(4,128)(2,1)}, u32[]{:S(2)}) copy-start(bf16[4,4096]{1,0:T(4,128)(2,1)} %residual_ref.1) | copy-start | bytes 98308
  10.8 21.0 %copy-start.3 = (bf16[8192]{0:T(1024)(128)(2,1)S(1)}, bf16[8192]{0:T(1024)(128)(2,1)}, u32[]{:S(2)}) copy-start(bf16[8192]{0:T(1024)(128)(2,1)} %param.9) | copy-start | bytes 49156
  22.0 1.4 %collective-permute-start.1 = (bf16[16,4096]{1,0:T(8,128)(2,1)S(1)}, bf16[16,4096]{1,0:T(8,128)(2,1)S(1)}, u32[]{:S(2)}, u32[]{:S(2)}) collective-permute-start(bf16[16,4096]{1,0:T(8,128)(2,1)S(1)} %bitcast.7), channel_id=1, source_target_pairs={{0,1},{1,0},{2,3},{3,2},{4,5},{5,4},{6,7},{7,6},{8,9},{9,8},{10,11... | collective-permute-start | bytes 393224 | tf_op jit(solution)/shard_map/ppermute | solution.py:405
  23.5 5.2 %collective-permute-start.2 = (bf16[4,4096]{1,0:T(4,128)(2,1)S(1)}, bf16[4,4096]{1,0:T(4,128)(2,1)S(1)}, u32[]{:S(2)}, u32[]{:S(2)}) collective-permute-start(bf16[4,4096]{1,0:T(4,128)(2,1)S(1)} %get-tuple-element.23), channel_id=1, source_target_pairs={{0,9},{1,8},{4,13},{5,12},{8,5},{9,4},{12,1},{13,0},{2,11},{3,10},... | collective-permute-start | bytes 98312 | tf_op jit(solution)/shard_map/ppermute | solution.py:415
  25.9 4.3 %collective-permute-start.3 = (bf16[4,4096]{1,0:T(4,128)(2,1)S(1)}, bf16[4,4096]{1,0:T(4,128)(2,1)S(1)}, u32[]{:S(2)}, u32[]{:S(2)}) collective-permute-start(bf16[4,4096]{1,0:T(4,128)(2,1)S(1)} %get-tuple-element.24), channel_id=1, source_target_pairs={{0,13},{1,12},{4,9},{5,8},{8,1},{9,0},{12,5},{13,4},{2,15},{3,14},... | collective-permute-start | bytes 98312 | tf_op jit(solution)/shard_map/ppermute | solution.py:415
  27.1 3.9 %collective-permute-start.4 = (bf16[4,4096]{1,0:T(4,128)(2,1)S(1)}, bf16[4,4096]{1,0:T(4,128)(2,1)S(1)}, u32[]{:S(2)}, u32[]{:S(2)}) collective-permute-start(bf16[4,4096]{1,0:T(4,128)(2,1)S(1)} %get-tuple-element.25), channel_id=1, source_target_pairs={{0,5},{1,4},{4,1},{5,0},{8,13},{9,12},{12,9},{13,8},{2,7},{3,6},{6... | collective-permute-start | bytes 98312 | tf_op jit(solution)/shard_map/ppermute | solution.py:415
  31.1 3.8 %collective-permute-start.5 = (bf16[2,4096]{1,0:T(2,128)(2,1)S(1)}, bf16[2,4096]{1,0:T(2,128)(2,1)S(1)}, u32[]{:S(2)}, u32[]{:S(2)}) collective-permute-start(bf16[2,4096]{1,0:T(2,128)(2,1)S(1)} %bitcast.8), channel_id=1, source_target_pairs={{0,2},{2,0},{1,3},{3,1},{4,6},{6,4},{5,7},{7,5},{8,10},{10,8},{9,1... | collective-permute-start | bytes 49160 | tf_op jit(solution)/shard_map/ppermute | solution.py:405

commit v15 on v14

--- a/solution.py
+++ b/solution.py
@@ -25,31 +25,25 @@
     return max(s for s in range(16, DEPTH_STEP + 1, 16) if depth % s == 0)
 
 
-def fetch_kernel(weight_ref, held_ref, sems):
-    count, step, _ = held_ref.shape
-    copies = [
-        pltpu.make_async_copy(
-            weight_ref.at[pl.ds(i * step, step), :], held_ref.at[i], sems.at[i]
-        )
-        for i in range(count)
-    ]
-    for copy in copies:
-        copy.start()
-    for copy in copies:
-        copy.wait()
-
-
-def fetch(weight, count, step):
+def fetch_kernel(weight_ref, held_ref, sem):
+    copy = pltpu.make_async_copy(
+        weight_ref.at[pl.ds(0, held_ref.shape[0]), :], held_ref, sem
+    )
+    copy.start()
+    copy.wait()
+
+
+def fetch(weight, rows):
     columns = weight.shape[1]
     return pl.pallas_call(
         fetch_kernel,
-        out_shape=pltpu.VMEM((count, step, columns), weight.dtype),
+        out_shape=pltpu.VMEM((rows, columns), weight.dtype),
         in_specs=[pl.BlockSpec(memory_space=pl.ANY)],
         out_specs=whole(),
-        scratch_shapes=[pltpu.SemaphoreType.DMA((count,))],
+        scratch_shapes=[pltpu.SemaphoreType.DMA],
         compiler_params=pltpu.CompilerParams(vmem_limit_bytes=1 * MIB),
         cost_estimate=pl.CostEstimate(
-            flops=0, bytes_accessed=2 * count * step * columns, transcendentals=0
+            flops=0, bytes_accessed=2 * rows * columns, transcendentals=0
         ),
         name="fetch",
     )(weight)
@@ -75,8 +69,8 @@
     tensors,
     sections,
 ):
-    held, step, columns = held_ref.shape
-    rest = rest_ref.shape[0]
+    rest, step, columns = rest_ref.shape
+    held = held_ref.shape[0] // step
     own_rows = own_ref.shape[0]
     dp = 1 + others_ref.shape[0]
     me = lax.axis_index("dp")
@@ -106,7 +100,9 @@
     def held_step(n, _):
         lanes = pl.ds(pl.multiple_of(n * width, width), width)
         total_ref[:, lanes] = sum(
-            jnp.dot(rows_ref[i], held_ref[i, :, lanes], preferred_element_type=F32)
+            jnp.dot(
+                rows_ref[i], held_ref[i * step : (i + 1) * step, lanes], preferred_element_type=F32
+            )
             for i in range(held)
         )
         return 0
@@ -174,8 +170,8 @@
     own_rows, depth = own.shape
     rows = own_rows * (1 + others.shape[0])
     columns = weight.shape[1]
-    count, step, _ = held.shape
-    rest = depth // step - count
+    step = step_of(depth)
+    rest = (depth - held.shape[0]) // step
     return pl.pallas_call(
         functools.partial(project_kernel, tensors=tensors, sections=sections),
         out_shape=(
@@ -425,7 +421,7 @@
     step = step_of(depth)
     blocks = depth // step
     held_count = max(1, min(blocks // 2, HELD_BYTES // (2 * step * down_matrix.shape[1])))
-    held = fetch(down_matrix, held_count, step)
+    held = fetch(down_matrix, held_count * step)
 
     shrink = jnp.swapaxes(shrink_matrix, 1, 2)
     gain = next_norm_scale[None, :]

time: 35.9 us -> 35.8 us (level)
  no operation moved by 1% of the time
where the time goes in v15:
time: 35.8 us; the launch traced here: 35.6 us
  Pallas kernels  20.7 us (58%)
  starting transfers between devices  7.61 us (21%)
  waiting for transfers between devices  5.9 us (16%)
  between operations  0.73 us (2%)
  local copies, waits for them, and re-layouts  0.66 us (2%)
    pallas_call x1, Pallas kernels, project(): pl.pallas_call(functools.partial(project_kernel, tensors=tensors, section...  11.2 us
    pallas_call x1, Pallas kernels, fetch(): pl.pallas_call(fetch_kernel, out_shape=pltpu.VMEM((rows, columns), weight...  6.97 us
    ppermute x3, starting transfers between devices, across(): return lax.ppermute(array, ('tensor', 'section'), pairs)  3.93 us
    ppermute x3, starting transfers between devices, shifted(): lax.ppermute(array, axis, [(i, (i + shift) % count) for i in range(count)])  3.68 us
    ppermute x3, waiting for transfers between devices, shifted(): lax.ppermute(array, axis, [(i, (i + shift) % count) for i in range(count)])  3.58 us
    ppermute x3, waiting for transfers between devices, across(): return lax.ppermute(array, ('tensor', 'section'), pairs)  2.32 us
    pallas_call x1, Pallas kernels, prepare(): pl.pallas_call(functools.partial(prepare_kernel, slots=slots, owners=owne...  1.23 us
    pallas_call x1, Pallas kernels, finish(): pl.pallas_call(finish_kernel, out_shape=jax.ShapeDtypeStruct((local, 1, M...  0.84 us
  transfers between devices with their start and end apart: 6, of which 4 were waited for; matrix products, arithmetic and copies ran while one was open for 2% of the time, Pallas kernels for 24%

profile of v15, /device:TPU:0, one launch (start us, length us, event | category | flops | bytes accessed | tf_op | source)
XLA Modules:
  0.0 35.6 jit_solution(12331148489068102491)
XLA Ops:
  0.6 0.0 copy-start
  0.6 3.0 %collective-permute-start = (bf16[16,6656]{1,0:T(8,128)(2,1)}, bf16[16,6656]{1,0:T(8,128)(2,1)S(1)}, u32[]{:S(2)}, u32[]{:S(2)}) collective-permute-start(bf16[16,6656]{1,0:T(8,128)(2,1)} %own_ref.1), channel_id=1, source_target_pairs={{0,2},{2,0},{1,3},{3,1},{4,6},{6,4},{5,7},{7,5},{8,10},{10,8},{9,1... | collective-permute-start | bytes 638984 | tf_op jit(solution)/shard_map/ppermute | solution.py:401
  3.6 7.0 %fetch.1.held_ref = bf16[2560,4096]{1,0:T(8,128)(2,1)S(1)} custom-call(bf16[6656,4096]{1,0:T(8,128)(2,1)} %weight_ref.3), custom_call_target="tpu_custom_call" | custom-call | bytes 20971520 | tf_op jit(solution)/shard_map/fetch/pallas_call | solution.py:38
  10.6 0.0 copy-start.2
  10.6 0.0 copy-start.1
  10.6 0.0 copy-start.3
  10.7 0.0 collective-permute-done
  10.7 0.0 copy-done
  10.7 11.2 %project.1 = (f32[32,4096]{1,0:T(8,128)S(1)}, bf16[1,16,4096]{2,1,0:T(8,128)(2,1)S(1)}) custom-call(bf16[16,6656]{1,0:T(8,128)(2,1)S(1)} %copy-done, bf16[1,16,6656]{2,1,0:T(8,128)(2,1)S(1)} %bitcast.5, bf16[2560,4096]{1,0:T(8,128)(2,1)S(1)} %fetch.1.held_ref, bf16[6656,4096]{1,0:T(8,128)(2,1)} %weight_ref.3), custom_call_target="tpu_custom_call" | custom-call | flops 1744830464 | bytes 33554432 | tf_op jit(solution)/shard_map/project/pallas_call | solution.py:175
  21.9 0.1 collective-permute-start.1
  22.0 1.3 %collective-permute-done.1.refs_0_ = bf16[16,4096]{1,0:T(8,128)(2,1)S(1)} collective-permute-done((bf16[16,4096]{1,0:T(8,128)(2,1)S(1)}, bf16[16,4096]{1,0:T(8,128)(2,1)S(1)}, u32[]{:S(2)}, u32[]{:S(2)}) %collective-permute-start.1) | collective-permute-done | bytes 131104 | tf_op jit(solution)/shard_map/ppermute | solution.py:401
  23.4 2.4 %collective-permute-start.2 = (bf16[4,4096]{1,0:T(4,128)(2,1)S(1)}, bf16[4,4096]{1,0:T(4,128)(2,1)S(1)}, u32[]{:S(2)}, u32[]{:S(2)}) collective-permute-start(bf16[4,4096]{1,0:T(4,128)(2,1)S(1)} %get-tuple-element.23), channel_id=1, source_target_pairs={{0,9},{1,8},{4,13},{5,12},{8,5},{9,4},{12,1},{13,0},{2,11},{3,10},... | collective-permute-start | bytes 98312 | tf_op jit(solution)/shard_map/ppermute | solution.py:411
  25.8 1.2 %collective-permute-start.3 = (bf16[4,4096]{1,0:T(4,128)(2,1)S(1)}, bf16[4,4096]{1,0:T(4,128)(2,1)S(1)}, u32[]{:S(2)}, u32[]{:S(2)}) collective-permute-start(bf16[4,4096]{1,0:T(4,128)(2,1)S(1)} %get-tuple-element.24), channel_id=1, source_target_pairs={{0,13},{1,12},{4,9},{5,8},{8,1},{9,0},{12,5},{13,4},{2,15},{3,14},... | collective-permute-start | bytes 98312 | tf_op jit(solution)/shard_map/ppermute | solution.py:411
  27.0 0.3 collective-permute-start.4
  27.3 0.0 copy-done.2
  27.3 1.2 %prepare.1 = (f32[4,4]{1,0:T(4,128)S(1)}, bf16[1,64,8192]{2,1,0:T(8,128)(2,1)S(1)}) custom-call(s32[1,4]{1,0:T(1,128)S(1)} %bitcast.6, bf16[1,64,8192]{2,1,0:T(8,128)(2,1)} %bitcast.9), custom_call_target="tpu_custom_call" | custom-call | tf_op jit(solution)/shard_map/prepare/pallas_call | solution.py:269
  28.5 0.0 collective-permute-done.2.refs_0_
  28.6 1.5 %collective-permute-done.3.refs_1_ = bf16[4,4096]{1,0:T(4,128)(2,1)S(1)} collective-permute-done((bf16[4,4096]{1,0:T(4,128)(2,1)S(1)}, bf16[4,4096]{1,0:T(4,128)(2,1)S(1)}, u32[]{:S(2)}, u32[]{:S(2)}) %collective-permute-start.3) | collective-permute-done | bytes 32800 | tf_op jit(solution)/shard_map/ppermute | solution.py:411
  30.0 0.9 %collective-permute-done.4.refs_2_ = bf16[4,4096]{1,0:T(4,128)(2,1)S(1)} collective-permute-done((bf16[4,4096]{1,0:T(4,128)(2,1)S(1)}, bf16[4,4096]{1,0:T(4,128)(2,1)S(1)}, u32[]{:S(2)}, u32[]{:S(2)}) %collective-permute-start.4) | collective-permute-done | bytes 32800 | tf_op jit(solution)/shard_map/ppermute | solution.py:411
  30.9 0.0 copy-done.1
  30.9 0.1 mix.1
  31.0 0.6 %collective-permute-start.5 = (bf16[2,4096]{1,0:T(2,128)(2,1)S(1)}, bf16[2,4096]{1,0:T(2,128)(2,1)S(1)}, u32[]{:S(2)}, u32[]{:S(2)}) collective-permute-start(bf16[2,4096]{1,0:T(2,128)(2,1)S(1)} %bitcast.8), channel_id=1, source_target_pairs={{0,2},{2,0},{1,3},{3,1},{4,6},{6,4},{5,7},{7,5},{8,10},{10,8},{9,1... | collective-permute-start | bytes 49160 | tf_op jit(solution)/shard_map/ppermute | solution.py:401
  31.6 0.0 copy-done.3
  31.6 0.6 %copy.8 = bf16[4,4096]{1,0:T(4,128)(2,1)} copy(bf16[4,4096]{1,0:T(4,128)(2,1)S(1)} %get-tuple-element.32) | data formatting | bytes 65536
  32.3 0.3 own_half.1
  32.5 2.3 %collective-permute-done.5.refs_0_ = bf16[2,4096]{1,0:T(2,128)(2,1)S(1)} collective-permute-done((bf16[2,4096]{1,0:T(2,128)(2,1)S(1)}, bf16[2,4096]{1,0:T(2,128)(2,1)S(1)}, u32[]{:S(2)}, u32[]{:S(2)}) %collective-permute-start.5) | collective-permute-done | bytes 16416 | tf_op jit(solution)/shard_map/ppermute | solution.py:401
  34.8 0.8 %finish.1 = f32[1,1,2,64]{3,2,1,0:T(2,128)} custom-call(f32[2,64]{1,0:T(2,128)S(1)} %get-tuple-element.29.values_ref, f32[2,64]{1,0:T(2,128)S(1)} %get-tuple-element.30.squares_ref, bf16[1,8192]{1,0:T(2,128)(2,1)S(1)} %broadcast_in_dim.3.gain_ref, bf16[1,64,8192]{2,1,0:T(8,128)(2,1)S(1)} %get-tuple-element.28.shrink_ref, ...), custom_call_target="tpu_custom_call" | custom-call | tf_op jit(solution)/shard_map/finish/pallas_call | solution.py:389
  (3 shorter events, 0.1 us)
Async XLA Ops:
  0.6 10.0 %copy-start = (bf16[16,6656]{1,0:T(8,128)(2,1)S(1)}, bf16[16,6656]{1,0:T(8,128)(2,1)}, u32[]{:S(2)}) copy-start(bf16[16,6656]{1,0:T(8,128)(2,1)} %own_ref.1) | copy-start | bytes 638980
  0.6 10.0 %collective-permute-start = (bf16[16,6656]{1,0:T(8,128)(2,1)}, bf16[16,6656]{1,0:T(8,128)(2,1)S(1)}, u32[]{:S(2)}, u32[]{:S(2)}) collective-permute-start(bf16[16,6656]{1,0:T(8,128)(2,1)} %own_ref.1), channel_id=1, source_target_pairs={{0,2},{2,0},{1,3},{3,1},{4,6},{6,4},{5,7},{7,5},{8,10},{10,8},{9,1... | collective-permute-start | bytes 638984 | tf_op jit(solution)/shard_map/ppermute | solution.py:401
  10.6 16.7 %copy-start.2 = (s32[4,1]{0,1:T(1,128)S(1)}, s32[4,1]{0,1:T(1,128)}, u32[]{:S(2)}) copy-start(s32[4,1]{0,1:T(1,128)} %param.11) | copy-start | bytes 52
  10.6 20.2 %copy-start.1 = (bf16[4,4096]{1,0:T(4,128)(2,1)S(1)}, bf16[4,4096]{1,0:T(4,128)(2,1)}, u32[]{:S(2)}) copy-start(bf16[4,4096]{1,0:T(4,128)(2,1)} %residual_ref.1) | copy-start | bytes 98308
  10.6 21.0 %copy-start.3 = (bf16[8192]{0:T(1024)(128)(2,1)S(1)}, bf16[8192]{0:T(1024)(128)(2,1)}, u32[]{:S(2)}) copy-start(bf16[8192]{0:T(1024)(128)(2,1)} %param.9) | copy-start | bytes 49156
  21.9 1.4 %collective-permute-start.1 = (bf16[16,4096]{1,0:T(8,128)(2,1)S(1)}, bf16[16,4096]{1,0:T(8,128)(2,1)S(1)}, u32[]{:S(2)}, u32[]{:S(2)}) collective-permute-start(bf16[16,4096]{1,0:T(8,128)(2,1)S(1)} %bitcast.7), channel_id=1, source_target_pairs={{0,1},{1,0},{2,3},{3,2},{4,5},{5,4},{6,7},{7,6},{8,9},{9,8},{10,11... | collective-permute-start | bytes 393224 | tf_op jit(solution)/shard_map/ppermute | solution.py:401
  23.4 5.2 %collective-permute-start.2 = (bf16[4,4096]{1,0:T(4,128)(2,1)S(1)}, bf16[4,4096]{1,0:T(4,128)(2,1)S(1)}, u32[]{:S(2)}, u32[]{:S(2)}) collective-permute-start(bf16[4,4096]{1,0:T(4,128)(2,1)S(1)} %get-tuple-element.23), channel_id=1, source_target_pairs={{0,9},{1,8},{4,13},{5,12},{8,5},{9,4},{12,1},{13,0},{2,11},{3,10},... | collective-permute-start | bytes 98312 | tf_op jit(solution)/shard_map/ppermute | solution.py:411
  25.8 4.3 %collective-permute-start.3 = (bf16[4,4096]{1,0:T(4,128)(2,1)S(1)}, bf16[4,4096]{1,0:T(4,128)(2,1)S(1)}, u32[]{:S(2)}, u32[]{:S(2)}) collective-permute-start(bf16[4,4096]{1,0:T(4,128)(2,1)S(1)} %get-tuple-element.24), channel_id=1, source_target_pairs={{0,13},{1,12},{4,9},{5,8},{8,1},{9,0},{12,5},{13,4},{2,15},{3,14},... | collective-permute-start | bytes 98312 | tf_op jit(solution)/shard_map/ppermute | solution.py:411
  27.0 3.9 %collective-permute-start.4 = (bf16[4,4096]{1,0:T(4,128)(2,1)S(1)}, bf16[4,4096]{1,0:T(4,128)(2,1)S(1)}, u32[]{:S(2)}, u32[]{:S(2)}) collective-permute-start(bf16[4,4096]{1,0:T(4,128)(2,1)S(1)} %get-tuple-element.25), channel_id=1, source_target_pairs={{0,5},{1,4},{4,1},{5,0},{8,13},{9,12},{12,9},{13,8},{2,7},{3,6},{6... | collective-permute-start | bytes 98312 | tf_op jit(solution)/shard_map/ppermute | solution.py:411
  31.0 3.8 %collective-permute-start.5 = (bf16[2,4096]{1,0:T(2,128)(2,1)S(1)}, bf16[2,4096]{1,0:T(2,128)(2,1)S(1)}, u32[]{:S(2)}, u32[]{:S(2)}) collective-permute-start(bf16[2,4096]{1,0:T(2,128)(2,1)S(1)} %bitcast.8), channel_id=1, source_target_pairs={{0,2},{2,0},{1,3},{3,1},{4,6},{6,4},{5,7},{7,5},{8,10},{10,8},{9,1... | collective-permute-start | bytes 49160 | tf_op jit(solution)/shard_map/ppermute | solution.py:401

commit v16 on v15

--- a/solution.py
+++ b/solution.py
@@ -85,10 +85,10 @@
 
     parts = last_parts(step)
     last = [copy_of(rest - 1, rest - 1 + k, *part) for k, part in enumerate(parts)]
-    for i in range(rest - 1):
+    steps = columns // width
+    early = rest - 1 - steps if rest > steps else rest - 1
+    for i in range(early):
         copy_of(i, i).start()
-    for copy in last:
-        copy.start()
 
     for i in range(held + rest):
         block = slice(i * step, (i + 1) * step)
@@ -98,6 +98,8 @@
             rows_ref[i, pl.ds(first, own_rows), :] = source
 
     def held_step(n, _):
+        if rest > steps:
+            copy_of(early + n, early + n).start()
         lanes = pl.ds(pl.multiple_of(n * width, width), width)
         total_ref[:, lanes] = sum(
             jnp.dot(
@@ -119,7 +121,9 @@
         add(i)
         return 0
 
-    lax.fori_loop(0, columns // width, held_step, 0)
+    lax.fori_loop(0, steps, held_step, 0)
+    for copy in last:
+        copy.start()
     lax.fori_loop(0, rest - 1, rest_step, 0)
     for copy, (first, size) in zip(last, parts):
         copy.wait()

time: 35.8 us -> 36.1 us (level)
  no operation moved by 1% of the time
where the time goes in v16:
time: 36.1 us; the launch traced here: 35.9 us
  Pallas kernels  21 us (58%)
  starting transfers between devices  7.62 us (21%)
  waiting for transfers between devices  5.89 us (16%)
  between operations  0.74 us (2%)
  local copies, waits for them, and re-layouts  0.66 us (2%)
    pallas_call x1, Pallas kernels, project(): pl.pallas_call(functools.partial(project_kernel, tensors=tensors, section...  11.4 us
    pallas_call x1, Pallas kernels, fetch(): pl.pallas_call(fetch_kernel, out_shape=pltpu.VMEM((rows, columns), weight...  6.97 us
    ppermute x3, starting transfers between devices, across(): return lax.ppermute(array, ('tensor', 'section'), pairs)  3.94 us
    ppermute x3, starting transfers between devices, shifted(): lax.ppermute(array, axis, [(i, (i + shift) % count) for i in range(count)])  3.68 us
    ppermute x3, waiting for transfers between devices, shifted(): lax.ppermute(array, axis, [(i, (i + shift) % count) for i in range(count)])  3.59 us
    ppermute x3, waiting for transfers between devices, across(): return lax.ppermute(array, ('tensor', 'section'), pairs)  2.31 us
    pallas_call x1, Pallas kernels, prepare(): pl.pallas_call(functools.partial(prepare_kernel, slots=slots, owners=owne...  1.23 us
    pallas_call x1, Pallas kernels, finish(): pl.pallas_call(finish_kernel, out_shape=jax.ShapeDtypeStruct((local, 1, M...  0.84 us
  transfers between devices with their start and end apart: 6, of which 4 were waited for; matrix products, arithmetic and copies ran while one was open for 2% of the time, Pallas kernels for 24%

profile of v16, /device:TPU:0, one launch (start us, length us, event | category | flops | bytes accessed | tf_op | source)
XLA Modules:
  0.0 35.9 jit_solution(16228246987018360669)
XLA Ops:
  0.6 0.0 copy-start
  0.6 3.0 %collective-permute-start = (bf16[16,6656]{1,0:T(8,128)(2,1)}, bf16[16,6656]{1,0:T(8,128)(2,1)S(1)}, u32[]{:S(2)}, u32[]{:S(2)}) collective-permute-start(bf16[16,6656]{1,0:T(8,128)(2,1)} %own_ref.1), channel_id=1, source_target_pairs={{0,2},{2,0},{1,3},{3,1},{4,6},{6,4},{5,7},{7,5},{8,10},{10,8},{9,1... | collective-permute-start | bytes 638984 | tf_op jit(solution)/shard_map/ppermute | solution.py:405
  3.6 7.0 %fetch.1.held_ref = bf16[2560,4096]{1,0:T(8,128)(2,1)S(1)} custom-call(bf16[6656,4096]{1,0:T(8,128)(2,1)} %weight_ref.3), custom_call_target="tpu_custom_call" | custom-call | bytes 20971520 | tf_op jit(solution)/shard_map/fetch/pallas_call | solution.py:38
  10.6 0.0 copy-start.2
  10.6 0.0 copy-start.1
  10.6 0.0 copy-start.3
  10.7 0.0 collective-permute-done
  10.7 0.0 copy-done
  10.7 11.4 %project.1 = (f32[32,4096]{1,0:T(8,128)S(1)}, bf16[1,16,4096]{2,1,0:T(8,128)(2,1)S(1)}) custom-call(bf16[16,6656]{1,0:T(8,128)(2,1)S(1)} %copy-done, bf16[1,16,6656]{2,1,0:T(8,128)(2,1)S(1)} %bitcast.5, bf16[2560,4096]{1,0:T(8,128)(2,1)S(1)} %fetch.1.held_ref, bf16[6656,4096]{1,0:T(8,128)(2,1)} %weight_ref.3), custom_call_target="tpu_custom_call" | custom-call | flops 1744830464 | bytes 33554432 | tf_op jit(solution)/shard_map/project/pallas_call | solution.py:179
  22.1 0.1 collective-permute-start.1
  22.3 1.3 %collective-permute-done.1.refs_0_ = bf16[16,4096]{1,0:T(8,128)(2,1)S(1)} collective-permute-done((bf16[16,4096]{1,0:T(8,128)(2,1)S(1)}, bf16[16,4096]{1,0:T(8,128)(2,1)S(1)}, u32[]{:S(2)}, u32[]{:S(2)}) %collective-permute-start.1) | collective-permute-done | bytes 131104 | tf_op jit(solution)/shard_map/ppermute | solution.py:405
  23.6 2.4 %collective-permute-start.2 = (bf16[4,4096]{1,0:T(4,128)(2,1)S(1)}, bf16[4,4096]{1,0:T(4,128)(2,1)S(1)}, u32[]{:S(2)}, u32[]{:S(2)}) collective-permute-start(bf16[4,4096]{1,0:T(4,128)(2,1)S(1)} %get-tuple-element.23), channel_id=1, source_target_pairs={{0,9},{1,8},{4,13},{5,12},{8,5},{9,4},{12,1},{13,0},{2,11},{3,10},... | collective-permute-start | bytes 98312 | tf_op jit(solution)/shard_map/ppermute | solution.py:415
  26.0 1.2 %collective-permute-start.3 = (bf16[4,4096]{1,0:T(4,128)(2,1)S(1)}, bf16[4,4096]{1,0:T(4,128)(2,1)S(1)}, u32[]{:S(2)}, u32[]{:S(2)}) collective-permute-start(bf16[4,4096]{1,0:T(4,128)(2,1)S(1)} %get-tuple-element.24), channel_id=1, source_target_pairs={{0,13},{1,12},{4,9},{5,8},{8,1},{9,0},{12,5},{13,4},{2,15},{3,14},... | collective-permute-start | bytes 98312 | tf_op jit(solution)/shard_map/ppermute | solution.py:415
  27.2 0.3 collective-permute-start.4
  27.5 0.0 copy-done.2
  27.5 1.2 %prepare.1 = (f32[4,4]{1,0:T(4,128)S(1)}, bf16[1,64,8192]{2,1,0:T(8,128)(2,1)S(1)}) custom-call(s32[1,4]{1,0:T(1,128)S(1)} %bitcast.6, bf16[1,64,8192]{2,1,0:T(8,128)(2,1)} %bitcast.9), custom_call_target="tpu_custom_call" | custom-call | tf_op jit(solution)/shard_map/prepare/pallas_call | solution.py:273
  28.8 0.0 collective-permute-done.2.refs_0_
  28.8 1.5 %collective-permute-done.3.refs_1_ = bf16[4,4096]{1,0:T(4,128)(2,1)S(1)} collective-permute-done((bf16[4,4096]{1,0:T(4,128)(2,1)S(1)}, bf16[4,4096]{1,0:T(4,128)(2,1)S(1)}, u32[]{:S(2)}, u32[]{:S(2)}) %collective-permute-start.3) | collective-permute-done | bytes 32800 | tf_op jit(solution)/shard_map/ppermute | solution.py:415
  30.2 0.8 %collective-permute-done.4.refs_2_ = bf16[4,4096]{1,0:T(4,128)(2,1)S(1)} collective-permute-done((bf16[4,4096]{1,0:T(4,128)(2,1)S(1)}, bf16[4,4096]{1,0:T(4,128)(2,1)S(1)}, u32[]{:S(2)}, u32[]{:S(2)}) %collective-permute-start.4) | collective-permute-done | bytes 32800 | tf_op jit(solution)/shard_map/ppermute | solution.py:415
  31.1 0.0 copy-done.1
  31.1 0.1 mix.1
  31.2 0.6 %collective-permute-start.5 = (bf16[2,4096]{1,0:T(2,128)(2,1)S(1)}, bf16[2,4096]{1,0:T(2,128)(2,1)S(1)}, u32[]{:S(2)}, u32[]{:S(2)}) collective-permute-start(bf16[2,4096]{1,0:T(2,128)(2,1)S(1)} %bitcast.8), channel_id=1, source_target_pairs={{0,2},{2,0},{1,3},{3,1},{4,6},{6,4},{5,7},{7,5},{8,10},{10,8},{9,1... | collective-permute-start | bytes 49160 | tf_op jit(solution)/shard_map/ppermute | solution.py:405
  31.8 0.0 copy-done.3
  31.9 0.6 %copy.8 = bf16[4,4096]{1,0:T(4,128)(2,1)} copy(bf16[4,4096]{1,0:T(4,128)(2,1)S(1)} %get-tuple-element.32) | data formatting | bytes 65536
  32.5 0.3 own_half.1
  32.7 2.3 %collective-permute-done.5.refs_0_ = bf16[2,4096]{1,0:T(2,128)(2,1)S(1)} collective-permute-done((bf16[2,4096]{1,0:T(2,128)(2,1)S(1)}, bf16[2,4096]{1,0:T(2,128)(2,1)S(1)}, u32[]{:S(2)}, u32[]{:S(2)}) %collective-permute-start.5) | collective-permute-done | bytes 16416 | tf_op jit(solution)/shard_map/ppermute | solution.py:405
  35.0 0.8 %finish.1 = f32[1,1,2,64]{3,2,1,0:T(2,128)} custom-call(f32[2,64]{1,0:T(2,128)S(1)} %get-tuple-element.29.values_ref, f32[2,64]{1,0:T(2,128)S(1)} %get-tuple-element.30.squares_ref, bf16[1,8192]{1,0:T(2,128)(2,1)S(1)} %broadcast_in_dim.3.gain_ref, bf16[1,64,8192]{2,1,0:T(8,128)(2,1)S(1)} %get-tuple-element.28.shrink_ref, ...), custom_call_target="tpu_custom_call" | custom-call | tf_op jit(solution)/shard_map/finish/pallas_call | solution.py:393
  (3 shorter events, 0.1 us)
Async XLA Ops:
  0.6 10.0 %copy-start = (bf16[16,6656]{1,0:T(8,128)(2,1)S(1)}, bf16[16,6656]{1,0:T(8,128)(2,1)}, u32[]{:S(2)}) copy-start(bf16[16,6656]{1,0:T(8,128)(2,1)} %own_ref.1) | copy-start | bytes 638980
  0.6 10.0 %collective-permute-start = (bf16[16,6656]{1,0:T(8,128)(2,1)}, bf16[16,6656]{1,0:T(8,128)(2,1)S(1)}, u32[]{:S(2)}, u32[]{:S(2)}) collective-permute-start(bf16[16,6656]{1,0:T(8,128)(2,1)} %own_ref.1), channel_id=1, source_target_pairs={{0,2},{2,0},{1,3},{3,1},{4,6},{6,4},{5,7},{7,5},{8,10},{10,8},{9,1... | collective-permute-start | bytes 638984 | tf_op jit(solution)/shard_map/ppermute | solution.py:405
  10.6 16.9 %copy-start.2 = (s32[4,1]{0,1:T(1,128)S(1)}, s32[4,1]{0,1:T(1,128)}, u32[]{:S(2)}) copy-start(s32[4,1]{0,1:T(1,128)} %param.11) | copy-start | bytes 52
  10.6 20.5 %copy-start.1 = (bf16[4,4096]{1,0:T(4,128)(2,1)S(1)}, bf16[4,4096]{1,0:T(4,128)(2,1)}, u32[]{:S(2)}) copy-start(bf16[4,4096]{1,0:T(4,128)(2,1)} %residual_ref.1) | copy-start | bytes 98308
  10.6 21.2 %copy-start.3 = (bf16[8192]{0:T(1024)(128)(2,1)S(1)}, bf16[8192]{0:T(1024)(128)(2,1)}, u32[]{:S(2)}) copy-start(bf16[8192]{0:T(1024)(128)(2,1)} %param.9) | copy-start | bytes 49156
  22.1 1.4 %collective-permute-start.1 = (bf16[16,4096]{1,0:T(8,128)(2,1)S(1)}, bf16[16,4096]{1,0:T(8,128)(2,1)S(1)}, u32[]{:S(2)}, u32[]{:S(2)}) collective-permute-start(bf16[16,4096]{1,0:T(8,128)(2,1)S(1)} %bitcast.7), channel_id=1, source_target_pairs={{0,1},{1,0},{2,3},{3,2},{4,5},{5,4},{6,7},{7,6},{8,9},{9,8},{10,11... | collective-permute-start | bytes 393224 | tf_op jit(solution)/shard_map/ppermute | solution.py:405
  23.6 5.2 %collective-permute-start.2 = (bf16[4,4096]{1,0:T(4,128)(2,1)S(1)}, bf16[4,4096]{1,0:T(4,128)(2,1)S(1)}, u32[]{:S(2)}, u32[]{:S(2)}) collective-permute-start(bf16[4,4096]{1,0:T(4,128)(2,1)S(1)} %get-tuple-element.23), channel_id=1, source_target_pairs={{0,9},{1,8},{4,13},{5,12},{8,5},{9,4},{12,1},{13,0},{2,11},{3,10},... | collective-permute-start | bytes 98312 | tf_op jit(solution)/shard_map/ppermute | solution.py:415
  26.0 4.3 %collective-permute-start.3 = (bf16[4,4096]{1,0:T(4,128)(2,1)S(1)}, bf16[4,4096]{1,0:T(4,128)(2,1)S(1)}, u32[]{:S(2)}, u32[]{:S(2)}) collective-permute-start(bf16[4,4096]{1,0:T(4,128)(2,1)S(1)} %get-tuple-element.24), channel_id=1, source_target_pairs={{0,13},{1,12},{4,9},{5,8},{8,1},{9,0},{12,5},{13,4},{2,15},{3,14},... | collective-permute-start | bytes 98312 | tf_op jit(solution)/shard_map/ppermute | solution.py:415
  27.2 3.9 %collective-permute-start.4 = (bf16[4,4096]{1,0:T(4,128)(2,1)S(1)}, bf16[4,4096]{1,0:T(4,128)(2,1)S(1)}, u32[]{:S(2)}, u32[]{:S(2)}) collective-permute-start(bf16[4,4096]{1,0:T(4,128)(2,1)S(1)} %get-tuple-element.25), channel_id=1, source_target_pairs={{0,5},{1,4},{4,1},{5,0},{8,13},{9,12},{12,9},{13,8},{2,7},{3,6},{6... | collective-permute-start | bytes 98312 | tf_op jit(solution)/shard_map/ppermute | solution.py:415
  31.2 3.8 %collective-permute-start.5 = (bf16[2,4096]{1,0:T(2,128)(2,1)S(1)}, bf16[2,4096]{1,0:T(2,128)(2,1)S(1)}, u32[]{:S(2)}, u32[]{:S(2)}) collective-permute-start(bf16[2,4096]{1,0:T(2,128)(2,1)S(1)} %bitcast.8), channel_id=1, source_target_pairs={{0,2},{2,0},{1,3},{3,1},{4,6},{6,4},{5,7},{7,5},{8,10},{10,8},{9,1... | collective-permute-start | bytes 49160 | tf_op jit(solution)/shard_map/ppermute | solution.py:405

commit v17 on v15

--- a/solution.py
+++ b/solution.py
@@ -11,7 +11,7 @@
 EPS = 1e-05
 DEPTH_STEP = 512
 HELD_BYTES = 21 * 2**20
-WIDTH = 1024
+WIDTH = 2048
 MIB = 2**20
 F32 = jnp.float32
 BF16 = jnp.bfloat16

time: 35.8 us -> 35.8 us (level)
  no operation moved by 1% of the time
where the time goes in v17:
time: 35.8 us; the launch traced here: 35.7 us
  Pallas kernels  20.8 us (58%)
  starting transfers between devices  7.61 us (21%)
  waiting for transfers between devices  5.9 us (16%)
  between operations  0.74 us (2%)
  local copies, waits for them, and re-layouts  0.66 us (2%)
    pallas_call x1, Pallas kernels, project(): pl.pallas_call(functools.partial(project_kernel, tensors=tensors, section...  11.2 us
    pallas_call x1, Pallas kernels, fetch(): pl.pallas_call(fetch_kernel, out_shape=pltpu.VMEM((rows, columns), weight...  6.97 us
    ppermute x3, starting transfers between devices, across(): return lax.ppermute(array, ('tensor', 'section'), pairs)  3.94 us
    ppermute x3, starting transfers between devices, shifted(): lax.ppermute(array, axis, [(i, (i + shift) % count) for i in range(count)])  3.68 us
    ppermute x3, waiting for transfers between devices, shifted(): lax.ppermute(array, axis, [(i, (i + shift) % count) for i in range(count)])  3.58 us
    ppermute x3, waiting for transfers between devices, across(): return lax.ppermute(array, ('tensor', 'section'), pairs)  2.31 us
    pallas_call x1, Pallas kernels, prepare(): pl.pallas_call(functools.partial(prepare_kernel, slots=slots, owners=owne...  1.23 us
    pallas_call x1, Pallas kernels, finish(): pl.pallas_call(finish_kernel, out_shape=jax.ShapeDtypeStruct((local, 1, M...  0.84 us
  transfers between devices with their start and end apart: 6, of which 4 were waited for; matrix products, arithmetic and copies ran while one was open for 2% of the time, Pallas kernels for 24%

profile of v17, /device:TPU:0, one launch (start us, length us, event | category | flops | bytes accessed | tf_op | source)
XLA Modules:
  0.0 35.7 jit_solution(8973153212700874258)
XLA Ops:
  0.6 0.0 copy-start
  0.6 3.0 %collective-permute-start = (bf16[16,6656]{1,0:T(8,128)(2,1)}, bf16[16,6656]{1,0:T(8,128)(2,1)S(1)}, u32[]{:S(2)}, u32[]{:S(2)}) collective-permute-start(bf16[16,6656]{1,0:T(8,128)(2,1)} %own_ref.1), channel_id=1, source_target_pairs={{0,2},{2,0},{1,3},{3,1},{4,6},{6,4},{5,7},{7,5},{8,10},{10,8},{9,1... | collective-permute-start | bytes 638984 | tf_op jit(solution)/shard_map/ppermute | solution.py:401
  3.6 7.0 %fetch.1.held_ref = bf16[2560,4096]{1,0:T(8,128)(2,1)S(1)} custom-call(bf16[6656,4096]{1,0:T(8,128)(2,1)} %weight_ref.3), custom_call_target="tpu_custom_call" | custom-call | bytes 20971520 | tf_op jit(solution)/shard_map/fetch/pallas_call | solution.py:38
  10.6 0.0 copy-start.2
  10.6 0.0 copy-start.1
  10.6 0.0 copy-start.3
  10.7 0.0 collective-permute-done
  10.7 0.0 copy-done
  10.7 11.2 %project.1 = (f32[32,4096]{1,0:T(8,128)S(1)}, bf16[1,16,4096]{2,1,0:T(8,128)(2,1)S(1)}) custom-call(bf16[16,6656]{1,0:T(8,128)(2,1)S(1)} %copy-done, bf16[1,16,6656]{2,1,0:T(8,128)(2,1)S(1)} %bitcast.5, bf16[2560,4096]{1,0:T(8,128)(2,1)S(1)} %fetch.1.held_ref, bf16[6656,4096]{1,0:T(8,128)(2,1)} %weight_ref.3), custom_call_target="tpu_custom_call" | custom-call | flops 1744830464 | bytes 33554432 | tf_op jit(solution)/shard_map/project/pallas_call | solution.py:175
  21.9 0.1 collective-permute-start.1
  22.0 1.3 %collective-permute-done.1.refs_0_ = bf16[16,4096]{1,0:T(8,128)(2,1)S(1)} collective-permute-done((bf16[16,4096]{1,0:T(8,128)(2,1)S(1)}, bf16[16,4096]{1,0:T(8,128)(2,1)S(1)}, u32[]{:S(2)}, u32[]{:S(2)}) %collective-permute-start.1) | collective-permute-done | bytes 131104 | tf_op jit(solution)/shard_map/ppermute | solution.py:401
  23.4 2.4 %collective-permute-start.2 = (bf16[4,4096]{1,0:T(4,128)(2,1)S(1)}, bf16[4,4096]{1,0:T(4,128)(2,1)S(1)}, u32[]{:S(2)}, u32[]{:S(2)}) collective-permute-start(bf16[4,4096]{1,0:T(4,128)(2,1)S(1)} %get-tuple-element.23), channel_id=1, source_target_pairs={{0,9},{1,8},{4,13},{5,12},{8,5},{9,4},{12,1},{13,0},{2,11},{3,10},... | collective-permute-start | bytes 98312 | tf_op jit(solution)/shard_map/ppermute | solution.py:411
  25.8 1.2 %collective-permute-start.3 = (bf16[4,4096]{1,0:T(4,128)(2,1)S(1)}, bf16[4,4096]{1,0:T(4,128)(2,1)S(1)}, u32[]{:S(2)}, u32[]{:S(2)}) collective-permute-start(bf16[4,4096]{1,0:T(4,128)(2,1)S(1)} %get-tuple-element.24), channel_id=1, source_target_pairs={{0,13},{1,12},{4,9},{5,8},{8,1},{9,0},{12,5},{13,4},{2,15},{3,14},... | collective-permute-start | bytes 98312 | tf_op jit(solution)/shard_map/ppermute | solution.py:411
  27.0 0.3 collective-permute-start.4
  27.3 0.0 copy-done.2
  27.3 1.2 %prepare.1 = (f32[4,4]{1,0:T(4,128)S(1)}, bf16[1,64,8192]{2,1,0:T(8,128)(2,1)S(1)}) custom-call(s32[1,4]{1,0:T(1,128)S(1)} %bitcast.6, bf16[1,64,8192]{2,1,0:T(8,128)(2,1)} %bitcast.9), custom_call_target="tpu_custom_call" | custom-call | tf_op jit(solution)/shard_map/prepare/pallas_call | solution.py:269
  28.6 0.0 collective-permute-done.2.refs_0_
  28.6 1.4 %collective-permute-done.3.refs_1_ = bf16[4,4096]{1,0:T(4,128)(2,1)S(1)} collective-permute-done((bf16[4,4096]{1,0:T(4,128)(2,1)S(1)}, bf16[4,4096]{1,0:T(4,128)(2,1)S(1)}, u32[]{:S(2)}, u32[]{:S(2)}) %collective-permute-start.3) | collective-permute-done | bytes 32800 | tf_op jit(solution)/shard_map/ppermute | solution.py:411
  30.0 0.9 %collective-permute-done.4.refs_2_ = bf16[4,4096]{1,0:T(4,128)(2,1)S(1)} collective-permute-done((bf16[4,4096]{1,0:T(4,128)(2,1)S(1)}, bf16[4,4096]{1,0:T(4,128)(2,1)S(1)}, u32[]{:S(2)}, u32[]{:S(2)}) %collective-permute-start.4) | collective-permute-done | bytes 32800 | tf_op jit(solution)/shard_map/ppermute | solution.py:411
  30.9 0.0 copy-done.1
  30.9 0.1 mix.1
  31.0 0.6 %collective-permute-start.5 = (bf16[2,4096]{1,0:T(2,128)(2,1)S(1)}, bf16[2,4096]{1,0:T(2,128)(2,1)S(1)}, u32[]{:S(2)}, u32[]{:S(2)}) collective-permute-start(bf16[2,4096]{1,0:T(2,128)(2,1)S(1)} %bitcast.8), channel_id=1, source_target_pairs={{0,2},{2,0},{1,3},{3,1},{4,6},{6,4},{5,7},{7,5},{8,10},{10,8},{9,1... | collective-permute-start | bytes 49160 | tf_op jit(solution)/shard_map/ppermute | solution.py:401
  31.6 0.0 copy-done.3
  31.6 0.6 %copy.8 = bf16[4,4096]{1,0:T(4,128)(2,1)} copy(bf16[4,4096]{1,0:T(4,128)(2,1)S(1)} %get-tuple-element.32) | data formatting | bytes 65536
  32.3 0.3 own_half.1
  32.5 2.3 %collective-permute-done.5.refs_0_ = bf16[2,4096]{1,0:T(2,128)(2,1)S(1)} collective-permute-done((bf16[2,4096]{1,0:T(2,128)(2,1)S(1)}, bf16[2,4096]{1,0:T(2,128)(2,1)S(1)}, u32[]{:S(2)}, u32[]{:S(2)}) %collective-permute-start.5) | collective-permute-done | bytes 16416 | tf_op jit(solution)/shard_map/ppermute | solution.py:401
  34.8 0.8 %finish.1 = f32[1,1,2,64]{3,2,1,0:T(2,128)} custom-call(f32[2,64]{1,0:T(2,128)S(1)} %get-tuple-element.29.values_ref, f32[2,64]{1,0:T(2,128)S(1)} %get-tuple-element.30.squares_ref, bf16[1,8192]{1,0:T(2,128)(2,1)S(1)} %broadcast_in_dim.3.gain_ref, bf16[1,64,8192]{2,1,0:T(8,128)(2,1)S(1)} %get-tuple-element.28.shrink_ref, ...), custom_call_target="tpu_custom_call" | custom-call | tf_op jit(solution)/shard_map/finish/pallas_call | solution.py:389
  (3 shorter events, 0.1 us)
Async XLA Ops:
  0.6 10.0 %copy-start = (bf16[16,6656]{1,0:T(8,128)(2,1)S(1)}, bf16[16,6656]{1,0:T(8,128)(2,1)}, u32[]{:S(2)}) copy-start(bf16[16,6656]{1,0:T(8,128)(2,1)} %own_ref.1) | copy-start | bytes 638980
  0.6 10.0 %collective-permute-start = (bf16[16,6656]{1,0:T(8,128)(2,1)}, bf16[16,6656]{1,0:T(8,128)(2,1)S(1)}, u32[]{:S(2)}, u32[]{:S(2)}) collective-permute-start(bf16[16,6656]{1,0:T(8,128)(2,1)} %own_ref.1), channel_id=1, source_target_pairs={{0,2},{2,0},{1,3},{3,1},{4,6},{6,4},{5,7},{7,5},{8,10},{10,8},{9,1... | collective-permute-start | bytes 638984 | tf_op jit(solution)/shard_map/ppermute | solution.py:401
  10.6 16.7 %copy-start.2 = (s32[4,1]{0,1:T(1,128)S(1)}, s32[4,1]{0,1:T(1,128)}, u32[]{:S(2)}) copy-start(s32[4,1]{0,1:T(1,128)} %param.11) | copy-start | bytes 52
  10.6 20.2 %copy-start.1 = (bf16[4,4096]{1,0:T(4,128)(2,1)S(1)}, bf16[4,4096]{1,0:T(4,128)(2,1)}, u32[]{:S(2)}) copy-start(bf16[4,4096]{1,0:T(4,128)(2,1)} %residual_ref.1) | copy-start | bytes 98308
  10.6 21.0 %copy-start.3 = (bf16[8192]{0:T(1024)(128)(2,1)S(1)}, bf16[8192]{0:T(1024)(128)(2,1)}, u32[]{:S(2)}) copy-start(bf16[8192]{0:T(1024)(128)(2,1)} %param.9) | copy-start | bytes 49156
  21.9 1.4 %collective-permute-start.1 = (bf16[16,4096]{1,0:T(8,128)(2,1)S(1)}, bf16[16,4096]{1,0:T(8,128)(2,1)S(1)}, u32[]{:S(2)}, u32[]{:S(2)}) collective-permute-start(bf16[16,4096]{1,0:T(8,128)(2,1)S(1)} %bitcast.7), channel_id=1, source_target_pairs={{0,1},{1,0},{2,3},{3,2},{4,5},{5,4},{6,7},{7,6},{8,9},{9,8},{10,11... | collective-permute-start | bytes 393224 | tf_op jit(solution)/shard_map/ppermute | solution.py:401
  23.4 5.2 %collective-permute-start.2 = (bf16[4,4096]{1,0:T(4,128)(2,1)S(1)}, bf16[4,4096]{1,0:T(4,128)(2,1)S(1)}, u32[]{:S(2)}, u32[]{:S(2)}) collective-permute-start(bf16[4,4096]{1,0:T(4,128)(2,1)S(1)} %get-tuple-element.23), channel_id=1, source_target_pairs={{0,9},{1,8},{4,13},{5,12},{8,5},{9,4},{12,1},{13,0},{2,11},{3,10},... | collective-permute-start | bytes 98312 | tf_op jit(solution)/shard_map/ppermute | solution.py:411
  25.8 4.3 %collective-permute-start.3 = (bf16[4,4096]{1,0:T(4,128)(2,1)S(1)}, bf16[4,4096]{1,0:T(4,128)(2,1)S(1)}, u32[]{:S(2)}, u32[]{:S(2)}) collective-permute-start(bf16[4,4096]{1,0:T(4,128)(2,1)S(1)} %get-tuple-element.24), channel_id=1, source_target_pairs={{0,13},{1,12},{4,9},{5,8},{8,1},{9,0},{12,5},{13,4},{2,15},{3,14},... | collective-permute-start | bytes 98312 | tf_op jit(solution)/shard_map/ppermute | solution.py:411
  27.0 3.9 %collective-permute-start.4 = (bf16[4,4096]{1,0:T(4,128)(2,1)S(1)}, bf16[4,4096]{1,0:T(4,128)(2,1)S(1)}, u32[]{:S(2)}, u32[]{:S(2)}) collective-permute-start(bf16[4,4096]{1,0:T(4,128)(2,1)S(1)} %get-tuple-element.25), channel_id=1, source_target_pairs={{0,5},{1,4},{4,1},{5,0},{8,13},{9,12},{12,9},{13,8},{2,7},{3,6},{6... | collective-permute-start | bytes 98312 | tf_op jit(solution)/shard_map/ppermute | solution.py:411
  31.0 3.8 %collective-permute-start.5 = (bf16[2,4096]{1,0:T(2,128)(2,1)S(1)}, bf16[2,4096]{1,0:T(2,128)(2,1)S(1)}, u32[]{:S(2)}, u32[]{:S(2)}) collective-permute-start(bf16[2,4096]{1,0:T(2,128)(2,1)S(1)} %bitcast.8), channel_id=1, source_target_pairs={{0,2},{2,0},{1,3},{3,1},{4,6},{6,4},{5,7},{7,5},{8,10},{10,8},{9,1... | collective-permute-start | bytes 49160 | tf_op jit(solution)/shard_map/ppermute | solution.py:401

commit v18 on v15

--- a/solution.py
+++ b/solution.py
@@ -10,7 +10,7 @@
 MOST = 2
 EPS = 1e-05
 DEPTH_STEP = 512
-HELD_BYTES = 21 * 2**20
+HELD_BYTES = 17 * 2**20
 WIDTH = 1024
 MIB = 2**20
 F32 = jnp.float32
@@ -185,7 +185,7 @@
             pltpu.VMEM((rest, step, columns), BF16),
             pltpu.SemaphoreType.DMA((rest - 1 + len(last_parts(step)),)),
         ],
-        compiler_params=pltpu.CompilerParams(vmem_limit_bytes=36 * MIB),
+        compiler_params=pltpu.CompilerParams(vmem_limit_bytes=40 * MIB),
         cost_estimate=pl.CostEstimate(
             flops=2 * rows * depth * columns,
             bytes_accessed=2 * rest * step * columns,

time: 35.8 us -> 35.8 us (level)
  waiting for transfers between devices: 5.9 us -> 5.06 us
  starting transfers between devices: 7.61 us -> 8.45 us
    pallas_call x1, Pallas kernels: 11.2 us -> 12.4 us  [project(): pl.pallas_call(functools.partial(project_kernel, tensors=tensors, section...]
    pallas_call x1, Pallas kernels: 6.97 us -> 5.78 us  [fetch(): pl.pallas_call(fetch_kernel, out_shape=pltpu.VMEM((rows, columns), weight...]
    ppermute x3, starting transfers between devices: 3.68 us -> 4.51 us  [shifted(): lax.ppermute(array, axis, [(i, (i + shift) % count) for i in range(count)])]
    ppermute x3, waiting for transfers between devices: 3.58 us -> 2.75 us  [shifted(): lax.ppermute(array, axis, [(i, (i + shift) % count) for i in range(count)])]
  transfers between devices with their start and end apart: 6 -> 6, of which waited for: 4 -> 4; matrix products, arithmetic and copies ran while one was open for 2% -> 2% of each run, Pallas kernels for 24% -> 20%
where the time goes in v18:
time: 35.8 us; the launch traced here: 35.7 us
  Pallas kernels  20.7 us (58%)
  starting transfers between devices  8.45 us (24%)
  waiting for transfers between devices  5.06 us (14%)
  between operations  0.74 us (2%)
  local copies, waits for them, and re-layouts  0.66 us (2%)
    pallas_call x1, Pallas kernels, project(): pl.pallas_call(functools.partial(project_kernel, tensors=tensors, section...  12.4 us
    pallas_call x1, Pallas kernels, fetch(): pl.pallas_call(fetch_kernel, out_shape=pltpu.VMEM((rows, columns), weight...  5.78 us
    ppermute x3, starting transfers between devices, shifted(): lax.ppermute(array, axis, [(i, (i + shift) % count) for i in range(count)])  4.51 us
    ppermute x3, starting transfers between devices, across(): return lax.ppermute(array, ('tensor', 'section'), pairs)  3.94 us
    ppermute x3, waiting for transfers between devices, shifted(): lax.ppermute(array, axis, [(i, (i + shift) % count) for i in range(count)])  2.75 us
    ppermute x3, waiting for transfers between devices, across(): return lax.ppermute(array, ('tensor', 'section'), pairs)  2.31 us
    pallas_call x1, Pallas kernels, prepare(): pl.pallas_call(functools.partial(prepare_kernel, slots=slots, owners=owne...  1.23 us
    pallas_call x1, Pallas kernels, finish(): pl.pallas_call(finish_kernel, out_shape=jax.ShapeDtypeStruct((local, 1, M...  0.84 us
  transfers between devices with their start and end apart: 6, of which 4 were waited for; matrix products, arithmetic and copies ran while one was open for 2% of the time, Pallas kernels for 20%

profile of v18, /device:TPU:0, one launch (start us, length us, event | category | flops | bytes accessed | tf_op | source)
XLA Modules:
  0.0 35.7 jit_solution(16518812157226914992)
XLA Ops:
  0.6 0.0 copy-start
  0.6 0.0 copy-start.2
  0.6 3.0 %collective-permute-start = (bf16[16,6656]{1,0:T(8,128)(2,1)}, bf16[16,6656]{1,0:T(8,128)(2,1)S(1)}, u32[]{:S(2)}, u32[]{:S(2)}) collective-permute-start(bf16[16,6656]{1,0:T(8,128)(2,1)} %own_ref.1), channel_id=1, source_target_pairs={{0,2},{2,0},{1,3},{3,1},{4,6},{6,4},{5,7},{7,5},{8,10},{10,8},{9,1... | collective-permute-start | bytes 638984 | tf_op jit(solution)/shard_map/ppermute | solution.py:401
  3.7 5.8 %fetch.1.held_ref = bf16[2048,4096]{1,0:T(8,128)(2,1)S(1)} custom-call(bf16[6656,4096]{1,0:T(8,128)(2,1)} %weight_ref.3), custom_call_target="tpu_custom_call" | custom-call | bytes 16777216 | tf_op jit(solution)/shard_map/fetch/pallas_call | solution.py:38
  9.4 0.0 copy-start.1
  9.4 0.0 copy-start.3
  9.5 0.0 collective-permute-done
  9.5 0.0 copy-done
  9.5 12.4 %project.1 = (f32[32,4096]{1,0:T(8,128)S(1)}, bf16[1,16,4096]{2,1,0:T(8,128)(2,1)S(1)}) custom-call(bf16[16,6656]{1,0:T(8,128)(2,1)S(1)} %copy-done, bf16[1,16,6656]{2,1,0:T(8,128)(2,1)S(1)} %bitcast.5, bf16[2048,4096]{1,0:T(8,128)(2,1)S(1)} %fetch.1.held_ref, bf16[6656,4096]{1,0:T(8,128)(2,1)} %weight_ref.3), custom_call_target="tpu_custom_call" | custom-call | flops 1744830464 | bytes 37748736 | tf_op jit(solution)/shard_map/project/pallas_call | solution.py:175
  21.9 0.1 collective-permute-start.1
  22.0 1.3 %collective-permute-done.1.refs_0_ = bf16[16,4096]{1,0:T(8,128)(2,1)S(1)} collective-permute-done((bf16[16,4096]{1,0:T(8,128)(2,1)S(1)}, bf16[16,4096]{1,0:T(8,128)(2,1)S(1)}, u32[]{:S(2)}, u32[]{:S(2)}) %collective-permute-start.1) | collective-permute-done | bytes 131104 | tf_op jit(solution)/shard_map/ppermute | solution.py:401
  23.4 2.4 %collective-permute-start.2 = (bf16[4,4096]{1,0:T(4,128)(2,1)S(1)}, bf16[4,4096]{1,0:T(4,128)(2,1)S(1)}, u32[]{:S(2)}, u32[]{:S(2)}) collective-permute-start(bf16[4,4096]{1,0:T(4,128)(2,1)S(1)} %get-tuple-element.23), channel_id=1, source_target_pairs={{0,9},{1,8},{4,13},{5,12},{8,5},{9,4},{12,1},{13,0},{2,11},{3,10},... | collective-permute-start | bytes 98312 | tf_op jit(solution)/shard_map/ppermute | solution.py:411
  25.8 1.2 %collective-permute-start.3 = (bf16[4,4096]{1,0:T(4,128)(2,1)S(1)}, bf16[4,4096]{1,0:T(4,128)(2,1)S(1)}, u32[]{:S(2)}, u32[]{:S(2)}) collective-permute-start(bf16[4,4096]{1,0:T(4,128)(2,1)S(1)} %get-tuple-element.24), channel_id=1, source_target_pairs={{0,13},{1,12},{4,9},{5,8},{8,1},{9,0},{12,5},{13,4},{2,15},{3,14},... | collective-permute-start | bytes 98312 | tf_op jit(solution)/shard_map/ppermute | solution.py:411
  27.0 0.3 collective-permute-start.4
  27.3 0.0 copy-done.2
  27.3 1.2 %prepare.1 = (f32[4,4]{1,0:T(4,128)S(1)}, bf16[1,64,8192]{2,1,0:T(8,128)(2,1)S(1)}) custom-call(s32[1,4]{1,0:T(1,128)S(1)} %bitcast.6, bf16[1,64,8192]{2,1,0:T(8,128)(2,1)} %bitcast.9), custom_call_target="tpu_custom_call" | custom-call | tf_op jit(solution)/shard_map/prepare/pallas_call | solution.py:269
  28.6 0.0 collective-permute-done.2.refs_0_
  28.6 1.5 %collective-permute-done.3.refs_1_ = bf16[4,4096]{1,0:T(4,128)(2,1)S(1)} collective-permute-done((bf16[4,4096]{1,0:T(4,128)(2,1)S(1)}, bf16[4,4096]{1,0:T(4,128)(2,1)S(1)}, u32[]{:S(2)}, u32[]{:S(2)}) %collective-permute-start.3) | collective-permute-done | bytes 32800 | tf_op jit(solution)/shard_map/ppermute | solution.py:411
  30.0 0.8 %collective-permute-done.4.refs_2_ = bf16[4,4096]{1,0:T(4,128)(2,1)S(1)} collective-permute-done((bf16[4,4096]{1,0:T(4,128)(2,1)S(1)}, bf16[4,4096]{1,0:T(4,128)(2,1)S(1)}, u32[]{:S(2)}, u32[]{:S(2)}) %collective-permute-start.4) | collective-permute-done | bytes 32800 | tf_op jit(solution)/shard_map/ppermute | solution.py:411
  30.9 0.0 copy-done.1
  30.9 0.1 mix.1
  31.0 1.4 %collective-permute-start.5 = (bf16[2,4096]{1,0:T(2,128)(2,1)S(1)}, bf16[2,4096]{1,0:T(2,128)(2,1)S(1)}, u32[]{:S(2)}, u32[]{:S(2)}) collective-permute-start(bf16[2,4096]{1,0:T(2,128)(2,1)S(1)} %bitcast.8), channel_id=1, source_target_pairs={{0,2},{2,0},{1,3},{3,1},{4,6},{6,4},{5,7},{7,5},{8,10},{10,8},{9,1... | collective-permute-start | bytes 49160 | tf_op jit(solution)/shard_map/ppermute | solution.py:401
  32.4 0.0 copy-done.3
  32.5 0.6 %copy.8 = bf16[4,4096]{1,0:T(4,128)(2,1)} copy(bf16[4,4096]{1,0:T(4,128)(2,1)S(1)} %get-tuple-element.32) | data formatting | bytes 65536
  33.1 0.3 own_half.1
  33.3 1.5 %collective-permute-done.5.refs_0_ = bf16[2,4096]{1,0:T(2,128)(2,1)S(1)} collective-permute-done((bf16[2,4096]{1,0:T(2,128)(2,1)S(1)}, bf16[2,4096]{1,0:T(2,128)(2,1)S(1)}, u32[]{:S(2)}, u32[]{:S(2)}) %collective-permute-start.5) | collective-permute-done | bytes 16416 | tf_op jit(solution)/shard_map/ppermute | solution.py:401
  34.8 0.8 %finish.1 = f32[1,1,2,64]{3,2,1,0:T(2,128)} custom-call(f32[2,64]{1,0:T(2,128)S(1)} %get-tuple-element.29.values_ref, f32[2,64]{1,0:T(2,128)S(1)} %get-tuple-element.30.squares_ref, bf16[1,8192]{1,0:T(2,128)(2,1)S(1)} %broadcast_in_dim.3.gain_ref, bf16[1,64,8192]{2,1,0:T(8,128)(2,1)S(1)} %get-tuple-element.28.shrink_ref, ...), custom_call_target="tpu_custom_call" | custom-call | tf_op jit(solution)/shard_map/finish/pallas_call | solution.py:389
  (3 shorter events, 0.1 us)
Async XLA Ops:
  0.6 8.8 %copy-start = (bf16[16,6656]{1,0:T(8,128)(2,1)S(1)}, bf16[16,6656]{1,0:T(8,128)(2,1)}, u32[]{:S(2)}) copy-start(bf16[16,6656]{1,0:T(8,128)(2,1)} %own_ref.1) | copy-start | bytes 638980
  0.6 26.7 %copy-start.2 = (s32[4,1]{0,1:T(1,128)S(1)}, s32[4,1]{0,1:T(1,128)}, u32[]{:S(2)}) copy-start(s32[4,1]{0,1:T(1,128)} %param.11) | copy-start | bytes 52
  0.6 8.8 %collective-permute-start = (bf16[16,6656]{1,0:T(8,128)(2,1)}, bf16[16,6656]{1,0:T(8,128)(2,1)S(1)}, u32[]{:S(2)}, u32[]{:S(2)}) collective-permute-start(bf16[16,6656]{1,0:T(8,128)(2,1)} %own_ref.1), channel_id=1, source_target_pairs={{0,2},{2,0},{1,3},{3,1},{4,6},{6,4},{5,7},{7,5},{8,10},{10,8},{9,1... | collective-permute-start | bytes 638984 | tf_op jit(solution)/shard_map/ppermute | solution.py:401
  9.4 21.4 %copy-start.1 = (bf16[4,4096]{1,0:T(4,128)(2,1)S(1)}, bf16[4,4096]{1,0:T(4,128)(2,1)}, u32[]{:S(2)}) copy-start(bf16[4,4096]{1,0:T(4,128)(2,1)} %residual_ref.1) | copy-start | bytes 98308
  9.4 23.0 %copy-start.3 = (bf16[8192]{0:T(1024)(128)(2,1)S(1)}, bf16[8192]{0:T(1024)(128)(2,1)}, u32[]{:S(2)}) copy-start(bf16[8192]{0:T(1024)(128)(2,1)} %param.9) | copy-start | bytes 49156
  21.9 1.4 %collective-permute-start.1 = (bf16[16,4096]{1,0:T(8,128)(2,1)S(1)}, bf16[16,4096]{1,0:T(8,128)(2,1)S(1)}, u32[]{:S(2)}, u32[]{:S(2)}) collective-permute-start(bf16[16,4096]{1,0:T(8,128)(2,1)S(1)} %bitcast.7), channel_id=1, source_target_pairs={{0,1},{1,0},{2,3},{3,2},{4,5},{5,4},{6,7},{7,6},{8,9},{9,8},{10,11... | collective-permute-start | bytes 393224 | tf_op jit(solution)/shard_map/ppermute | solution.py:401
  23.4 5.2 %collective-permute-start.2 = (bf16[4,4096]{1,0:T(4,128)(2,1)S(1)}, bf16[4,4096]{1,0:T(4,128)(2,1)S(1)}, u32[]{:S(2)}, u32[]{:S(2)}) collective-permute-start(bf16[4,4096]{1,0:T(4,128)(2,1)S(1)} %get-tuple-element.23), channel_id=1, source_target_pairs={{0,9},{1,8},{4,13},{5,12},{8,5},{9,4},{12,1},{13,0},{2,11},{3,10},... | collective-permute-start | bytes 98312 | tf_op jit(solution)/shard_map/ppermute | solution.py:411
  25.8 4.3 %collective-permute-start.3 = (bf16[4,4096]{1,0:T(4,128)(2,1)S(1)}, bf16[4,4096]{1,0:T(4,128)(2,1)S(1)}, u32[]{:S(2)}, u32[]{:S(2)}) collective-permute-start(bf16[4,4096]{1,0:T(4,128)(2,1)S(1)} %get-tuple-element.24), channel_id=1, source_target_pairs={{0,13},{1,12},{4,9},{5,8},{8,1},{9,0},{12,5},{13,4},{2,15},{3,14},... | collective-permute-start | bytes 98312 | tf_op jit(solution)/shard_map/ppermute | solution.py:411
  27.0 3.9 %collective-permute-start.4 = (bf16[4,4096]{1,0:T(4,128)(2,1)S(1)}, bf16[4,4096]{1,0:T(4,128)(2,1)S(1)}, u32[]{:S(2)}, u32[]{:S(2)}) collective-permute-start(bf16[4,4096]{1,0:T(4,128)(2,1)S(1)} %get-tuple-element.25), channel_id=1, source_target_pairs={{0,5},{1,4},{4,1},{5,0},{8,13},{9,12},{12,9},{13,8},{2,7},{3,6},{6... | collective-permute-start | bytes 98312 | tf_op jit(solution)/shard_map/ppermute | solution.py:411
  31.0 3.8 %collective-permute-start.5 = (bf16[2,4096]{1,0:T(2,128)(2,1)S(1)}, bf16[2,4096]{1,0:T(2,128)(2,1)S(1)}, u32[]{:S(2)}, u32[]{:S(2)}) collective-permute-start(bf16[2,4096]{1,0:T(2,128)(2,1)S(1)} %bitcast.8), channel_id=1, source_target_pairs={{0,2},{2,0},{1,3},{3,1},{4,6},{6,4},{5,7},{7,5},{8,10},{10,8},{9,1... | collective-permute-start | bytes 49160 | tf_op jit(solution)/shard_map/ppermute | solution.py:401

commit v19 on v15

--- a/solution.py
+++ b/solution.py
@@ -62,6 +62,7 @@
     weight_ref,
     total_ref,
     sent_ref,
+    held_rows_ref,
     rows_ref,
     rest_ref,
     sems,
@@ -90,20 +91,20 @@
     for copy in last:
         copy.start()
 
-    for i in range(held + rest):
-        block = slice(i * step, (i + 1) * step)
+    def fill(target, block):
         for shift in range(dp):
             first = pl.multiple_of((me + dp - shift) % dp * own_rows, own_rows)
             source = own_ref[:, block] if shift == 0 else others_ref[shift - 1, :, block]
-            rows_ref[i, pl.ds(first, own_rows), :] = source
+            target[pl.ds(first, own_rows), :] = source
+
+    fill(held_rows_ref, slice(0, held * step))
+    for i in range(rest):
+        fill(rows_ref.at[i], slice((held + i) * step, (held + i + 1) * step))
 
     def held_step(n, _):
         lanes = pl.ds(pl.multiple_of(n * width, width), width)
-        total_ref[:, lanes] = sum(
-            jnp.dot(
-                rows_ref[i], held_ref[i * step : (i + 1) * step, lanes], preferred_element_type=F32
-            )
-            for i in range(held)
+        total_ref[:, lanes] = jnp.dot(
+            held_rows_ref[...], held_ref[:, lanes], preferred_element_type=F32
         )
         return 0
 
@@ -111,7 +112,7 @@
         for n in range(0, columns, width):
             lanes = slice(n, n + width)
             total_ref[:, lanes] += jnp.dot(
-                rows_ref[held + i, :, part], rest_ref[i, part, lanes], preferred_element_type=F32
+                rows_ref[i, :, part], rest_ref[i, part, lanes], preferred_element_type=F32
             )
 
     def rest_step(i, _):
@@ -181,7 +182,8 @@
         in_specs=[whole(), whole(), whole(), pl.BlockSpec(memory_space=pl.ANY)],
         out_specs=(whole(), whole()),
         scratch_shapes=[
-            pltpu.VMEM((depth // step, rows, step), BF16),
+            pltpu.VMEM((rows, held.shape[0]), BF16),
+            pltpu.VMEM((rest, rows, step), BF16),
             pltpu.VMEM((rest, step, columns), BF16),
             pltpu.SemaphoreType.DMA((rest - 1 + len(last_parts(step)),)),
         ],

time: 35.8 us -> 35.8 us (level)
  no operation moved by 1% of the time
where the time goes in v19:
time: 35.8 us; the launch traced here: 35.6 us
  Pallas kernels  20.7 us (58%)
  starting transfers between devices  7.61 us (21%)
  waiting for transfers between devices  5.9 us (16%)
  between operations  0.73 us (2%)
  local copies, waits for them, and re-layouts  0.66 us (2%)
    pallas_call x1, Pallas kernels, project(): pl.pallas_call(functools.partial(project_kernel, tensors=tensors, section...  11.2 us
    pallas_call x1, Pallas kernels, fetch(): pl.pallas_call(fetch_kernel, out_shape=pltpu.VMEM((rows, columns), weight...  6.97 us
    ppermute x3, starting transfers between devices, across(): return lax.ppermute(array, ('tensor', 'section'), pairs)  3.93 us
    ppermute x3, starting transfers between devices, shifted(): lax.ppermute(array, axis, [(i, (i + shift) % count) for i in range(count)])  3.68 us
    ppermute x3, waiting for transfers between devices, shifted(): lax.ppermute(array, axis, [(i, (i + shift) % count) for i in range(count)])  3.58 us
    ppermute x3, waiting for transfers between devices, across(): return lax.ppermute(array, ('tensor', 'section'), pairs)  2.32 us
    pallas_call x1, Pallas kernels, prepare(): pl.pallas_call(functools.partial(prepare_kernel, slots=slots, owners=owne...  1.23 us
    pallas_call x1, Pallas kernels, finish(): pl.pallas_call(finish_kernel, out_shape=jax.ShapeDtypeStruct((local, 1, M...  0.84 us
  transfers between devices with their start and end apart: 6, of which 4 were waited for; matrix products, arithmetic and copies ran while one was open for 2% of the time, Pallas kernels for 24%

profile of v19, /device:TPU:0, one launch (start us, length us, event | category | flops | bytes accessed | tf_op | source)
XLA Modules:
  0.0 35.6 jit_solution(15689710955159621130)
XLA Ops:
  0.6 0.0 copy-start
  0.6 3.0 %collective-permute-start = (bf16[16,6656]{1,0:T(8,128)(2,1)}, bf16[16,6656]{1,0:T(8,128)(2,1)S(1)}, u32[]{:S(2)}, u32[]{:S(2)}) collective-permute-start(bf16[16,6656]{1,0:T(8,128)(2,1)} %own_ref.1), channel_id=1, source_target_pairs={{0,2},{2,0},{1,3},{3,1},{4,6},{6,4},{5,7},{7,5},{8,10},{10,8},{9,1... | collective-permute-start | bytes 638984 | tf_op jit(solution)/shard_map/ppermute | solution.py:403
  3.6 7.0 %fetch.1.held_ref = bf16[2560,4096]{1,0:T(8,128)(2,1)S(1)} custom-call(bf16[6656,4096]{1,0:T(8,128)(2,1)} %weight_ref.3), custom_call_target="tpu_custom_call" | custom-call | bytes 20971520 | tf_op jit(solution)/shard_map/fetch/pallas_call | solution.py:38
  10.6 0.0 copy-start.2
  10.6 0.0 copy-start.1
  10.6 0.0 copy-start.3
  10.7 0.0 collective-permute-done
  10.7 0.0 copy-done
  10.7 11.2 %project.1 = (f32[32,4096]{1,0:T(8,128)S(1)}, bf16[1,16,4096]{2,1,0:T(8,128)(2,1)S(1)}) custom-call(bf16[16,6656]{1,0:T(8,128)(2,1)S(1)} %copy-done, bf16[1,16,6656]{2,1,0:T(8,128)(2,1)S(1)} %bitcast.5, bf16[2560,4096]{1,0:T(8,128)(2,1)S(1)} %fetch.1.held_ref, bf16[6656,4096]{1,0:T(8,128)(2,1)} %weight_ref.3), custom_call_target="tpu_custom_call" | custom-call | flops 1744830464 | bytes 33554432 | tf_op jit(solution)/shard_map/project/pallas_call | solution.py:176
  21.9 0.1 collective-permute-start.1
  22.0 1.3 %collective-permute-done.1.refs_0_ = bf16[16,4096]{1,0:T(8,128)(2,1)S(1)} collective-permute-done((bf16[16,4096]{1,0:T(8,128)(2,1)S(1)}, bf16[16,4096]{1,0:T(8,128)(2,1)S(1)}, u32[]{:S(2)}, u32[]{:S(2)}) %collective-permute-start.1) | collective-permute-done | bytes 131104 | tf_op jit(solution)/shard_map/ppermute | solution.py:403
  23.4 2.4 %collective-permute-start.2 = (bf16[4,4096]{1,0:T(4,128)(2,1)S(1)}, bf16[4,4096]{1,0:T(4,128)(2,1)S(1)}, u32[]{:S(2)}, u32[]{:S(2)}) collective-permute-start(bf16[4,4096]{1,0:T(4,128)(2,1)S(1)} %get-tuple-element.23), channel_id=1, source_target_pairs={{0,9},{1,8},{4,13},{5,12},{8,5},{9,4},{12,1},{13,0},{2,11},{3,10},... | collective-permute-start | bytes 98312 | tf_op jit(solution)/shard_map/ppermute | solution.py:413
  25.8 1.2 %collective-permute-start.3 = (bf16[4,4096]{1,0:T(4,128)(2,1)S(1)}, bf16[4,4096]{1,0:T(4,128)(2,1)S(1)}, u32[]{:S(2)}, u32[]{:S(2)}) collective-permute-start(bf16[4,4096]{1,0:T(4,128)(2,1)S(1)} %get-tuple-element.24), channel_id=1, source_target_pairs={{0,13},{1,12},{4,9},{5,8},{8,1},{9,0},{12,5},{13,4},{2,15},{3,14},... | collective-permute-start | bytes 98312 | tf_op jit(solution)/shard_map/ppermute | solution.py:413
  27.0 0.3 collective-permute-start.4
  27.3 0.0 copy-done.2
  27.3 1.2 %prepare.1 = (f32[4,4]{1,0:T(4,128)S(1)}, bf16[1,64,8192]{2,1,0:T(8,128)(2,1)S(1)}) custom-call(s32[1,4]{1,0:T(1,128)S(1)} %bitcast.6, bf16[1,64,8192]{2,1,0:T(8,128)(2,1)} %bitcast.9), custom_call_target="tpu_custom_call" | custom-call | tf_op jit(solution)/shard_map/prepare/pallas_call | solution.py:271
  28.5 0.0 collective-permute-done.2.refs_0_
  28.6 1.5 %collective-permute-done.3.refs_1_ = bf16[4,4096]{1,0:T(4,128)(2,1)S(1)} collective-permute-done((bf16[4,4096]{1,0:T(4,128)(2,1)S(1)}, bf16[4,4096]{1,0:T(4,128)(2,1)S(1)}, u32[]{:S(2)}, u32[]{:S(2)}) %collective-permute-start.3) | collective-permute-done | bytes 32800 | tf_op jit(solution)/shard_map/ppermute | solution.py:413
  30.0 0.9 %collective-permute-done.4.refs_2_ = bf16[4,4096]{1,0:T(4,128)(2,1)S(1)} collective-permute-done((bf16[4,4096]{1,0:T(4,128)(2,1)S(1)}, bf16[4,4096]{1,0:T(4,128)(2,1)S(1)}, u32[]{:S(2)}, u32[]{:S(2)}) %collective-permute-start.4) | collective-permute-done | bytes 32800 | tf_op jit(solution)/shard_map/ppermute | solution.py:413
  30.9 0.0 copy-done.1
  30.9 0.1 mix.1
  31.0 0.6 %collective-permute-start.5 = (bf16[2,4096]{1,0:T(2,128)(2,1)S(1)}, bf16[2,4096]{1,0:T(2,128)(2,1)S(1)}, u32[]{:S(2)}, u32[]{:S(2)}) collective-permute-start(bf16[2,4096]{1,0:T(2,128)(2,1)S(1)} %bitcast.8), channel_id=1, source_target_pairs={{0,2},{2,0},{1,3},{3,1},{4,6},{6,4},{5,7},{7,5},{8,10},{10,8},{9,1... | collective-permute-start | bytes 49160 | tf_op jit(solution)/shard_map/ppermute | solution.py:403
  31.6 0.0 copy-done.3
  31.6 0.6 %copy.8 = bf16[4,4096]{1,0:T(4,128)(2,1)} copy(bf16[4,4096]{1,0:T(4,128)(2,1)S(1)} %get-tuple-element.32) | data formatting | bytes 65536
  32.3 0.3 own_half.1
  32.5 2.3 %collective-permute-done.5.refs_0_ = bf16[2,4096]{1,0:T(2,128)(2,1)S(1)} collective-permute-done((bf16[2,4096]{1,0:T(2,128)(2,1)S(1)}, bf16[2,4096]{1,0:T(2,128)(2,1)S(1)}, u32[]{:S(2)}, u32[]{:S(2)}) %collective-permute-start.5) | collective-permute-done | bytes 16416 | tf_op jit(solution)/shard_map/ppermute | solution.py:403
  34.8 0.8 %finish.1 = f32[1,1,2,64]{3,2,1,0:T(2,128)} custom-call(f32[2,64]{1,0:T(2,128)S(1)} %get-tuple-element.29.values_ref, f32[2,64]{1,0:T(2,128)S(1)} %get-tuple-element.30.squares_ref, bf16[1,8192]{1,0:T(2,128)(2,1)S(1)} %broadcast_in_dim.3.gain_ref, bf16[1,64,8192]{2,1,0:T(8,128)(2,1)S(1)} %get-tuple-element.28.shrink_ref, ...), custom_call_target="tpu_custom_call" | custom-call | tf_op jit(solution)/shard_map/finish/pallas_call | solution.py:391
  (3 shorter events, 0.1 us)
Async XLA Ops:
  0.6 10.0 %copy-start = (bf16[16,6656]{1,0:T(8,128)(2,1)S(1)}, bf16[16,6656]{1,0:T(8,128)(2,1)}, u32[]{:S(2)}) copy-start(bf16[16,6656]{1,0:T(8,128)(2,1)} %own_ref.1) | copy-start | bytes 638980
  0.6 10.0 %collective-permute-start = (bf16[16,6656]{1,0:T(8,128)(2,1)}, bf16[16,6656]{1,0:T(8,128)(2,1)S(1)}, u32[]{:S(2)}, u32[]{:S(2)}) collective-permute-start(bf16[16,6656]{1,0:T(8,128)(2,1)} %own_ref.1), channel_id=1, source_target_pairs={{0,2},{2,0},{1,3},{3,1},{4,6},{6,4},{5,7},{7,5},{8,10},{10,8},{9,1... | collective-permute-start | bytes 638984 | tf_op jit(solution)/shard_map/ppermute | solution.py:403
  10.6 16.7 %copy-start.2 = (s32[4,1]{0,1:T(1,128)S(1)}, s32[4,1]{0,1:T(1,128)}, u32[]{:S(2)}) copy-start(s32[4,1]{0,1:T(1,128)} %param.11) | copy-start | bytes 52
  10.6 20.2 %copy-start.1 = (bf16[4,4096]{1,0:T(4,128)(2,1)S(1)}, bf16[4,4096]{1,0:T(4,128)(2,1)}, u32[]{:S(2)}) copy-start(bf16[4,4096]{1,0:T(4,128)(2,1)} %residual_ref.1) | copy-start | bytes 98308
  10.6 21.0 %copy-start.3 = (bf16[8192]{0:T(1024)(128)(2,1)S(1)}, bf16[8192]{0:T(1024)(128)(2,1)}, u32[]{:S(2)}) copy-start(bf16[8192]{0:T(1024)(128)(2,1)} %param.9) | copy-start | bytes 49156
  21.9 1.4 %collective-permute-start.1 = (bf16[16,4096]{1,0:T(8,128)(2,1)S(1)}, bf16[16,4096]{1,0:T(8,128)(2,1)S(1)}, u32[]{:S(2)}, u32[]{:S(2)}) collective-permute-start(bf16[16,4096]{1,0:T(8,128)(2,1)S(1)} %bitcast.7), channel_id=1, source_target_pairs={{0,1},{1,0},{2,3},{3,2},{4,5},{5,4},{6,7},{7,6},{8,9},{9,8},{10,11... | collective-permute-start | bytes 393224 | tf_op jit(solution)/shard_map/ppermute | solution.py:403
  23.4 5.2 %collective-permute-start.2 = (bf16[4,4096]{1,0:T(4,128)(2,1)S(1)}, bf16[4,4096]{1,0:T(4,128)(2,1)S(1)}, u32[]{:S(2)}, u32[]{:S(2)}) collective-permute-start(bf16[4,4096]{1,0:T(4,128)(2,1)S(1)} %get-tuple-element.23), channel_id=1, source_target_pairs={{0,9},{1,8},{4,13},{5,12},{8,5},{9,4},{12,1},{13,0},{2,11},{3,10},... | collective-permute-start | bytes 98312 | tf_op jit(solution)/shard_map/ppermute | solution.py:413
  25.8 4.3 %collective-permute-start.3 = (bf16[4,4096]{1,0:T(4,128)(2,1)S(1)}, bf16[4,4096]{1,0:T(4,128)(2,1)S(1)}, u32[]{:S(2)}, u32[]{:S(2)}) collective-permute-start(bf16[4,4096]{1,0:T(4,128)(2,1)S(1)} %get-tuple-element.24), channel_id=1, source_target_pairs={{0,13},{1,12},{4,9},{5,8},{8,1},{9,0},{12,5},{13,4},{2,15},{3,14},... | collective-permute-start | bytes 98312 | tf_op jit(solution)/shard_map/ppermute | solution.py:413
  27.0 3.9 %collective-permute-start.4 = (bf16[4,4096]{1,0:T(4,128)(2,1)S(1)}, bf16[4,4096]{1,0:T(4,128)(2,1)S(1)}, u32[]{:S(2)}, u32[]{:S(2)}) collective-permute-start(bf16[4,4096]{1,0:T(4,128)(2,1)S(1)} %get-tuple-element.25), channel_id=1, source_target_pairs={{0,5},{1,4},{4,1},{5,0},{8,13},{9,12},{12,9},{13,8},{2,7},{3,6},{6... | collective-permute-start | bytes 98312 | tf_op jit(solution)/shard_map/ppermute | solution.py:413
  31.0 3.8 %collective-permute-start.5 = (bf16[2,4096]{1,0:T(2,128)(2,1)S(1)}, bf16[2,4096]{1,0:T(2,128)(2,1)S(1)}, u32[]{:S(2)}, u32[]{:S(2)}) collective-permute-start(bf16[2,4096]{1,0:T(2,128)(2,1)S(1)} %bitcast.8), channel_id=1, source_target_pairs={{0,2},{2,0},{1,3},{3,1},{4,6},{6,4},{5,7},{7,5},{8,10},{10,8},{9,1... | collective-permute-start | bytes 49160 | tf_op jit(solution)/shard_map/ppermute | solution.py:403

commit v20 on v15

--- a/solution.py
+++ b/solution.py
@@ -12,6 +12,7 @@
 DEPTH_STEP = 512
 HELD_BYTES = 21 * 2**20
 WIDTH = 1024
+IN_FLIGHT = 4
 MIB = 2**20
 F32 = jnp.float32
 BF16 = jnp.bfloat16
@@ -85,10 +86,8 @@
 
     parts = last_parts(step)
     last = [copy_of(rest - 1, rest - 1 + k, *part) for k, part in enumerate(parts)]
-    for i in range(rest - 1):
+    for i in range(min(rest - 1, IN_FLIGHT)):
         copy_of(i, i).start()
-    for copy in last:
-        copy.start()
 
     for i in range(held + rest):
         block = slice(i * step, (i + 1) * step)
@@ -120,6 +119,10 @@
         return 0
 
     lax.fori_loop(0, columns // width, held_step, 0)
+    for i in range(IN_FLIGHT, rest - 1):
+        copy_of(i, i).start()
+    for copy in last:
+        copy.start()
     lax.fori_loop(0, rest - 1, rest_step, 0)
     for copy, (first, size) in zip(last, parts):
         copy.wait()

time: 35.8 us -> 36.1 us (level)
  no operation moved by 1% of the time
where the time goes in v20:
time: 36.1 us; the launch traced here: 35.9 us
  Pallas kernels  21 us (58%)
  starting transfers between devices  7.62 us (21%)
  waiting for transfers between devices  5.89 us (16%)
  between operations  0.74 us (2%)
  local copies, waits for them, and re-layouts  0.66 us (2%)
    pallas_call x1, Pallas kernels, project(): pl.pallas_call(functools.partial(project_kernel, tensors=tensors, section...  11.4 us
    pallas_call x1, Pallas kernels, fetch(): pl.pallas_call(fetch_kernel, out_shape=pltpu.VMEM((rows, columns), weight...  6.97 us
    ppermute x3, starting transfers between devices, across(): return lax.ppermute(array, ('tensor', 'section'), pairs)  3.94 us
    ppermute x3, starting transfers between devices, shifted(): lax.ppermute(array, axis, [(i, (i + shift) % count) for i in range(count)])  3.68 us
    ppermute x3, waiting for transfers between devices, shifted(): lax.ppermute(array, axis, [(i, (i + shift) % count) for i in range(count)])  3.59 us
    ppermute x3, waiting for transfers between devices, across(): return lax.ppermute(array, ('tensor', 'section'), pairs)  2.31 us
    pallas_call x1, Pallas kernels, prepare(): pl.pallas_call(functools.partial(prepare_kernel, slots=slots, owners=owne...  1.23 us
    pallas_call x1, Pallas kernels, finish(): pl.pallas_call(finish_kernel, out_shape=jax.ShapeDtypeStruct((local, 1, M...  0.84 us
  transfers between devices with their start and end apart: 6, of which 4 were waited for; matrix products, arithmetic and copies ran while one was open for 2% of the time, Pallas kernels for 24%

profile of v20, /device:TPU:0, one launch (start us, length us, event | category | flops | bytes accessed | tf_op | source)
XLA Modules:
  0.0 35.9 jit_solution(10428683985514948738)
XLA Ops:
  0.6 0.0 copy-start
  0.6 3.0 %collective-permute-start = (bf16[16,6656]{1,0:T(8,128)(2,1)}, bf16[16,6656]{1,0:T(8,128)(2,1)S(1)}, u32[]{:S(2)}, u32[]{:S(2)}) collective-permute-start(bf16[16,6656]{1,0:T(8,128)(2,1)} %own_ref.1), channel_id=1, source_target_pairs={{0,2},{2,0},{1,3},{3,1},{4,6},{6,4},{5,7},{7,5},{8,10},{10,8},{9,1... | collective-permute-start | bytes 638984 | tf_op jit(solution)/shard_map/ppermute | solution.py:404
  3.6 7.0 %fetch.1.held_ref = bf16[2560,4096]{1,0:T(8,128)(2,1)S(1)} custom-call(bf16[6656,4096]{1,0:T(8,128)(2,1)} %weight_ref.3), custom_call_target="tpu_custom_call" | custom-call | bytes 20971520 | tf_op jit(solution)/shard_map/fetch/pallas_call | solution.py:39
  10.6 0.0 copy-start.2
  10.6 0.0 copy-start.1
  10.6 0.0 copy-start.3
  10.7 0.0 collective-permute-done
  10.7 0.0 copy-done
  10.7 11.4 %project.1 = (f32[32,4096]{1,0:T(8,128)S(1)}, bf16[1,16,4096]{2,1,0:T(8,128)(2,1)S(1)}) custom-call(bf16[16,6656]{1,0:T(8,128)(2,1)S(1)} %copy-done, bf16[1,16,6656]{2,1,0:T(8,128)(2,1)S(1)} %bitcast.5, bf16[2560,4096]{1,0:T(8,128)(2,1)S(1)} %fetch.1.held_ref, bf16[6656,4096]{1,0:T(8,128)(2,1)} %weight_ref.3), custom_call_target="tpu_custom_call" | custom-call | flops 1744830464 | bytes 33554432 | tf_op jit(solution)/shard_map/project/pallas_call | solution.py:178
  22.1 0.1 collective-permute-start.1
  22.3 1.3 %collective-permute-done.1.refs_0_ = bf16[16,4096]{1,0:T(8,128)(2,1)S(1)} collective-permute-done((bf16[16,4096]{1,0:T(8,128)(2,1)S(1)}, bf16[16,4096]{1,0:T(8,128)(2,1)S(1)}, u32[]{:S(2)}, u32[]{:S(2)}) %collective-permute-start.1) | collective-permute-done | bytes 131104 | tf_op jit(solution)/shard_map/ppermute | solution.py:404
  23.6 2.4 %collective-permute-start.2 = (bf16[4,4096]{1,0:T(4,128)(2,1)S(1)}, bf16[4,4096]{1,0:T(4,128)(2,1)S(1)}, u32[]{:S(2)}, u32[]{:S(2)}) collective-permute-start(bf16[4,4096]{1,0:T(4,128)(2,1)S(1)} %get-tuple-element.23), channel_id=1, source_target_pairs={{0,9},{1,8},{4,13},{5,12},{8,5},{9,4},{12,1},{13,0},{2,11},{3,10},... | collective-permute-start | bytes 98312 | tf_op jit(solution)/shard_map/ppermute | solution.py:414
  26.0 1.2 %collective-permute-start.3 = (bf16[4,4096]{1,0:T(4,128)(2,1)S(1)}, bf16[4,4096]{1,0:T(4,128)(2,1)S(1)}, u32[]{:S(2)}, u32[]{:S(2)}) collective-permute-start(bf16[4,4096]{1,0:T(4,128)(2,1)S(1)} %get-tuple-element.24), channel_id=1, source_target_pairs={{0,13},{1,12},{4,9},{5,8},{8,1},{9,0},{12,5},{13,4},{2,15},{3,14},... | collective-permute-start | bytes 98312 | tf_op jit(solution)/shard_map/ppermute | solution.py:414
  27.2 0.3 collective-permute-start.4
  27.5 0.0 copy-done.2
  27.5 1.2 %prepare.1 = (f32[4,4]{1,0:T(4,128)S(1)}, bf16[1,64,8192]{2,1,0:T(8,128)(2,1)S(1)}) custom-call(s32[1,4]{1,0:T(1,128)S(1)} %bitcast.6, bf16[1,64,8192]{2,1,0:T(8,128)(2,1)} %bitcast.9), custom_call_target="tpu_custom_call" | custom-call | tf_op jit(solution)/shard_map/prepare/pallas_call | solution.py:272
  28.8 0.0 collective-permute-done.2.refs_0_
  28.8 1.5 %collective-permute-done.3.refs_1_ = bf16[4,4096]{1,0:T(4,128)(2,1)S(1)} collective-permute-done((bf16[4,4096]{1,0:T(4,128)(2,1)S(1)}, bf16[4,4096]{1,0:T(4,128)(2,1)S(1)}, u32[]{:S(2)}, u32[]{:S(2)}) %collective-permute-start.3) | collective-permute-done | bytes 32800 | tf_op jit(solution)/shard_map/ppermute | solution.py:414
  30.2 0.8 %collective-permute-done.4.refs_2_ = bf16[4,4096]{1,0:T(4,128)(2,1)S(1)} collective-permute-done((bf16[4,4096]{1,0:T(4,128)(2,1)S(1)}, bf16[4,4096]{1,0:T(4,128)(2,1)S(1)}, u32[]{:S(2)}, u32[]{:S(2)}) %collective-permute-start.4) | collective-permute-done | bytes 32800 | tf_op jit(solution)/shard_map/ppermute | solution.py:414
  31.1 0.0 copy-done.1
  31.1 0.1 mix.1
  31.2 0.6 %collective-permute-start.5 = (bf16[2,4096]{1,0:T(2,128)(2,1)S(1)}, bf16[2,4096]{1,0:T(2,128)(2,1)S(1)}, u32[]{:S(2)}, u32[]{:S(2)}) collective-permute-start(bf16[2,4096]{1,0:T(2,128)(2,1)S(1)} %bitcast.8), channel_id=1, source_target_pairs={{0,2},{2,0},{1,3},{3,1},{4,6},{6,4},{5,7},{7,5},{8,10},{10,8},{9,1... | collective-permute-start | bytes 49160 | tf_op jit(solution)/shard_map/ppermute | solution.py:404
  31.8 0.0 copy-done.3
  31.9 0.6 %copy.8 = bf16[4,4096]{1,0:T(4,128)(2,1)} copy(bf16[4,4096]{1,0:T(4,128)(2,1)S(1)} %get-tuple-element.32) | data formatting | bytes 65536
  32.5 0.3 own_half.1
  32.7 2.3 %collective-permute-done.5.refs_0_ = bf16[2,4096]{1,0:T(2,128)(2,1)S(1)} collective-permute-done((bf16[2,4096]{1,0:T(2,128)(2,1)S(1)}, bf16[2,4096]{1,0:T(2,128)(2,1)S(1)}, u32[]{:S(2)}, u32[]{:S(2)}) %collective-permute-start.5) | collective-permute-done | bytes 16416 | tf_op jit(solution)/shard_map/ppermute | solution.py:404
  35.0 0.8 %finish.1 = f32[1,1,2,64]{3,2,1,0:T(2,128)} custom-call(f32[2,64]{1,0:T(2,128)S(1)} %get-tuple-element.29.values_ref, f32[2,64]{1,0:T(2,128)S(1)} %get-tuple-element.30.squares_ref, bf16[1,8192]{1,0:T(2,128)(2,1)S(1)} %broadcast_in_dim.3.gain_ref, bf16[1,64,8192]{2,1,0:T(8,128)(2,1)S(1)} %get-tuple-element.28.shrink_ref, ...), custom_call_target="tpu_custom_call" | custom-call | tf_op jit(solution)/shard_map/finish/pallas_call | solution.py:392
  (3 shorter events, 0.1 us)
Async XLA Ops:
  0.6 10.0 %copy-start = (bf16[16,6656]{1,0:T(8,128)(2,1)S(1)}, bf16[16,6656]{1,0:T(8,128)(2,1)}, u32[]{:S(2)}) copy-start(bf16[16,6656]{1,0:T(8,128)(2,1)} %own_ref.1) | copy-start | bytes 638980
  0.6 10.0 %collective-permute-start = (bf16[16,6656]{1,0:T(8,128)(2,1)}, bf16[16,6656]{1,0:T(8,128)(2,1)S(1)}, u32[]{:S(2)}, u32[]{:S(2)}) collective-permute-start(bf16[16,6656]{1,0:T(8,128)(2,1)} %own_ref.1), channel_id=1, source_target_pairs={{0,2},{2,0},{1,3},{3,1},{4,6},{6,4},{5,7},{7,5},{8,10},{10,8},{9,1... | collective-permute-start | bytes 638984 | tf_op jit(solution)/shard_map/ppermute | solution.py:404
  10.6 16.9 %copy-start.2 = (s32[4,1]{0,1:T(1,128)S(1)}, s32[4,1]{0,1:T(1,128)}, u32[]{:S(2)}) copy-start(s32[4,1]{0,1:T(1,128)} %param.11) | copy-start | bytes 52
  10.6 20.5 %copy-start.1 = (bf16[4,4096]{1,0:T(4,128)(2,1)S(1)}, bf16[4,4096]{1,0:T(4,128)(2,1)}, u32[]{:S(2)}) copy-start(bf16[4,4096]{1,0:T(4,128)(2,1)} %residual_ref.1) | copy-start | bytes 98308
  10.6 21.2 %copy-start.3 = (bf16[8192]{0:T(1024)(128)(2,1)S(1)}, bf16[8192]{0:T(1024)(128)(2,1)}, u32[]{:S(2)}) copy-start(bf16[8192]{0:T(1024)(128)(2,1)} %param.9) | copy-start | bytes 49156
  22.1 1.4 %collective-permute-start.1 = (bf16[16,4096]{1,0:T(8,128)(2,1)S(1)}, bf16[16,4096]{1,0:T(8,128)(2,1)S(1)}, u32[]{:S(2)}, u32[]{:S(2)}) collective-permute-start(bf16[16,4096]{1,0:T(8,128)(2,1)S(1)} %bitcast.7), channel_id=1, source_target_pairs={{0,1},{1,0},{2,3},{3,2},{4,5},{5,4},{6,7},{7,6},{8,9},{9,8},{10,11... | collective-permute-start | bytes 393224 | tf_op jit(solution)/shard_map/ppermute | solution.py:404
  23.6 5.2 %collective-permute-start.2 = (bf16[4,4096]{1,0:T(4,128)(2,1)S(1)}, bf16[4,4096]{1,0:T(4,128)(2,1)S(1)}, u32[]{:S(2)}, u32[]{:S(2)}) collective-permute-start(bf16[4,4096]{1,0:T(4,128)(2,1)S(1)} %get-tuple-element.23), channel_id=1, source_target_pairs={{0,9},{1,8},{4,13},{5,12},{8,5},{9,4},{12,1},{13,0},{2,11},{3,10},... | collective-permute-start | bytes 98312 | tf_op jit(solution)/shard_map/ppermute | solution.py:414
  26.0 4.3 %collective-permute-start.3 = (bf16[4,4096]{1,0:T(4,128)(2,1)S(1)}, bf16[4,4096]{1,0:T(4,128)(2,1)S(1)}, u32[]{:S(2)}, u32[]{:S(2)}) collective-permute-start(bf16[4,4096]{1,0:T(4,128)(2,1)S(1)} %get-tuple-element.24), channel_id=1, source_target_pairs={{0,13},{1,12},{4,9},{5,8},{8,1},{9,0},{12,5},{13,4},{2,15},{3,14},... | collective-permute-start | bytes 98312 | tf_op jit(solution)/shard_map/ppermute | solution.py:414
  27.2 3.9 %collective-permute-start.4 = (bf16[4,4096]{1,0:T(4,128)(2,1)S(1)}, bf16[4,4096]{1,0:T(4,128)(2,1)S(1)}, u32[]{:S(2)}, u32[]{:S(2)}) collective-permute-start(bf16[4,4096]{1,0:T(4,128)(2,1)S(1)} %get-tuple-element.25), channel_id=1, source_target_pairs={{0,5},{1,4},{4,1},{5,0},{8,13},{9,12},{12,9},{13,8},{2,7},{3,6},{6... | collective-permute-start | bytes 98312 | tf_op jit(solution)/shard_map/ppermute | solution.py:414
  31.2 3.8 %collective-permute-start.5 = (bf16[2,4096]{1,0:T(2,128)(2,1)S(1)}, bf16[2,4096]{1,0:T(2,128)(2,1)S(1)}, u32[]{:S(2)}, u32[]{:S(2)}) collective-permute-start(bf16[2,4096]{1,0:T(2,128)(2,1)S(1)} %bitcast.8), channel_id=1, source_target_pairs={{0,2},{2,0},{1,3},{3,1},{4,6},{6,4},{5,7},{7,5},{8,10},{10,8},{9,1... | collective-permute-start | bytes 49160 | tf_op jit(solution)/shard_map/ppermute | solution.py:404

commit v21 on v15

--- a/solution.py
+++ b/solution.py
@@ -258,26 +258,38 @@
     return jnp.logical_and(row == adapter, rank_of == slot % MOST).astype(F32)
 
 
-def prepare_kernel(index_ref, shrink_ref, places_ref, out_ref, sem, *, slots, owners):
-    copy = pltpu.make_async_copy(shrink_ref, out_ref, sem)
+def prepare_kernel(
+    index_ref, gain_ref, shrink_ref, places_ref, folded_ref, raw_ref, sem, *, slots, owners
+):
+    copy = pltpu.make_async_copy(shrink_ref, raw_ref, sem)
     copy.start()
     places_ref[...] = places_of(index_ref[...], slots, owners, slots // MOST)
     copy.wait()
-
-
-def prepare(index, shrink, slots, owners):
+    local, rank, features = raw_ref.shape
+    width = min(features, WIDTH)
+    for adapter in range(local):
+        for n in range(0, features, width):
+            lanes = slice(n, n + width)
+            scaled = raw_ref[adapter, :, lanes].astype(F32) * gain_ref[:, lanes].astype(F32)
+            high = scaled.astype(BF16)
+            folded_ref[adapter, :rank, lanes] = high
+            folded_ref[adapter, rank:, lanes] = (scaled - high.astype(F32)).astype(BF16)
+
+
+def prepare(index, gain, shrink, slots, owners):
+    local, rank, features = shrink.shape
     return pl.pallas_call(
         functools.partial(prepare_kernel, slots=slots, owners=owners),
         out_shape=(
             jax.ShapeDtypeStruct((slots * owners, index.shape[1]), F32),
-            pltpu.VMEM(shrink.shape, shrink.dtype),
-        ),
-        in_specs=[whole(), pl.BlockSpec(memory_space=pl.ANY)],
+            pltpu.VMEM((local, 2 * rank, features), shrink.dtype),
+        ),
+        in_specs=[whole(), whole(), pl.BlockSpec(memory_space=pl.ANY)],
         out_specs=(whole(), whole()),
-        scratch_shapes=[pltpu.SemaphoreType.DMA],
-        compiler_params=pltpu.CompilerParams(vmem_limit_bytes=1 * MIB),
+        scratch_shapes=[pltpu.VMEM(shrink.shape, shrink.dtype), pltpu.SemaphoreType.DMA],
+        compiler_params=pltpu.CompilerParams(vmem_limit_bytes=4 * MIB),
         name="prepare",
-    )(index, pltpu.with_memory_space_constraint(shrink, pltpu.HBM))
+    )(index, gain, pltpu.with_memory_space_constraint(shrink, pltpu.HBM))
 
 
 def mix_kernel(residual_ref, places_ref, own_ref, *refs):
@@ -314,86 +326,76 @@
     )(residual, places, own, *arrived)
 
 
-def partial_values(rows, gain_ref, shrink_ref, place, columns, local):
+def partial_values(rows, folded_ref, place):
+    columns = rows.shape[1]
     first = pl.multiple_of(place * columns, columns)
-    squares = jnp.sum(rows * rows, axis=1, keepdims=True)
-    scaled = rows * gain_ref[:, pl.ds(first, columns)].astype(F32)
-    high = scaled.astype(BF16)
-    low = (scaled - high.astype(F32)).astype(BF16)
+    local, rank = folded_ref.shape[0], folded_ref.shape[1] // 2
     values = []
     for adapter in range(local):
-        mine = slice(adapter * MOST, (adapter + 1) * MOST)
-        both = jnp.concatenate([high[mine], low[mine]], axis=0)
         product = lax.dot_general(
-            both,
-            shrink_ref[adapter, :, pl.ds(first, columns)],
+            rows[adapter * MOST : (adapter + 1) * MOST],
+            folded_ref[adapter, :, pl.ds(first, columns)],
             (((1,), (1,)), ((), ())),
             preferred_element_type=F32,
         )
-        values.append(product[:MOST] + product[MOST:])
+        values.append(product[:, :rank] + product[:, rank:])
+    widened = rows.astype(F32)
+    squares = jnp.sum(widened * widened, axis=1, keepdims=True)
     return jnp.concatenate(values, axis=0), squares
 
 
-def own_half_kernel(rows_ref, gain_ref, shrink_ref, values_ref, squares_ref):
-    columns = rows_ref.shape[1]
+def own_half_kernel(rows_ref, folded_ref, values_ref, squares_ref):
     values, squares = partial_values(
-        rows_ref[...], gain_ref, shrink_ref, lax.axis_index("dp"), columns, shrink_ref.shape[0]
+        rows_ref[...].astype(BF16), folded_ref, lax.axis_index("dp")
     )
     values_ref[...] = values
     squares_ref[...] = jnp.broadcast_to(squares, squares_ref.shape)
 
 
-def own_half(rows, gain, shrink):
+def own_half(rows, folded):
     slots = rows.shape[0]
-    rank = shrink.shape[1]
+    rank = folded.shape[1] // 2
     return pl.pallas_call(
         own_half_kernel,
         out_shape=(
             jax.ShapeDtypeStruct((slots, rank), F32),
             jax.ShapeDtypeStruct((slots, rank), F32),
         ),
-        in_specs=[whole()] * 3,
+        in_specs=[whole()] * 2,
         out_specs=(whole(),) * 2,
         compiler_params=pltpu.CompilerParams(vmem_limit_bytes=8 * MIB),
         cost_estimate=pl.CostEstimate(
-            flops=2 * slots * rows.shape[1] * rank, bytes_accessed=2 * MIB, transcendentals=0
+            flops=4 * slots * rows.shape[1] * rank, bytes_accessed=2 * MIB, transcendentals=0
         ),
         name="own_half",
-    )(rows, gain, shrink)
-
-
-def finish_kernel(values_ref, squares_ref, gain_ref, shrink_ref, *refs):
+    )(rows, folded)
+
+
+def finish_kernel(values_ref, squares_ref, folded_ref, *refs):
     arrived, out_ref = refs[:-1], refs[-1]
     dp = 1 + len(arrived)
     me = lax.axis_index("dp")
-    local = shrink_ref.shape[0]
+    local = folded_ref.shape[0]
     columns = arrived[0].shape[1]
     values, squares = values_ref[...], squares_ref[:, :1]
     for shift, piece in enumerate(arrived, start=1):
-        more, more_squares = partial_values(
-            piece[...].astype(F32),
-            gain_ref,
-            shrink_ref,
-            lax.rem(me + dp - shift, dp),
-            columns,
-            local,
-        )
+        more, more_squares = partial_values(piece[...], folded_ref, lax.rem(me + dp - shift, dp))
         values, squares = values + more, squares + more_squares
     result = 2.0 * values * lax.rsqrt(squares / (columns * dp) + EPS)
     for adapter in range(local):
         out_ref[adapter, 0] = result[adapter * MOST : (adapter + 1) * MOST]
 
 
-def finish(values, squares, gain, shrink, arrived):
-    local, rank, _ = shrink.shape
+def finish(values, squares, folded, arrived):
+    local, rank = folded.shape[0], folded.shape[1] // 2
     return pl.pallas_call(
         finish_kernel,
         out_shape=jax.ShapeDtypeStruct((local, 1, MOST, rank), F32),
-        in_specs=[whole()] * (4 + len(arrived)),
+        in_specs=[whole()] * (3 + len(arrived)),
         out_specs=whole(),
         compiler_params=pltpu.CompilerParams(vmem_limit_bytes=8 * MIB),
         name="finish",
-    )(values, squares, gain, shrink, *arrived)
+    )(values, squares, folded, *arrived)
 
 
 def shifted(array, axis, shift):
@@ -430,15 +432,15 @@
     total, sent = project(*in_vmem, down_matrix, tensors, sections)
     index, total = lax.optimization_barrier((adapter_index.reshape(1, -1), total))
     kept = keep(total, tensors, sections)
-    places, shrink = prepare(index, shrink, local * MOST, dp)
+    places, folded = prepare(index, gain, shrink, local * MOST, dp)
     arrived = [shifted(sent[s - 1], "section", s) for s in range(1, sections)]
     plan = exchange_plan(tensors)
     own, *sums = pair(kept, arrived, plan, tensors)
     arrived = [across(x, receivers) for x, receivers in zip(sums, plan)]
     mixed, routed, leaving = mix(residual, places, own, arrived, local * MOST, dp)
     arrived = [shifted(leaving[s - 1], "dp", s) for s in range(1, dp)]
-    values, squares = own_half(routed, gain, shrink)
-    shrunk = finish(values, squares, gain, shrink, arrived)
+    values, squares = own_half(routed, folded)
+    shrunk = finish(values, squares, folded, arrived)
     return (mixed, shrunk)
 
 

time: 35.8 us -> 36 us (level)
  Pallas kernels: 20.7 us -> 21.5 us
  waiting for transfers between devices: 5.9 us -> 5.3 us
    ppermute x3, waiting for transfers between devices: 2.32 us -> 1.87 us  [across(): return lax.ppermute(array, ('tensor', 'section'), pairs)]
    pallas_call x1, Pallas kernels: 1.23 us -> 1.63 us  [prepare(): pl.pallas_call(functools.partial(prepare_kernel, slots=slots, owners=owne...]
  transfers between devices with their start and end apart: 6 -> 6, of which waited for: 4 -> 4; matrix products, arithmetic and copies ran while one was open for 2% -> 2% of each run, Pallas kernels for 24% -> 25%
where the time goes in v21:
time: 36 us; the launch traced here: 35.8 us
  Pallas kernels  21.5 us (60%)
  starting transfers between devices  7.62 us (21%)
  waiting for transfers between devices  5.3 us (15%)
  between operations  0.75 us (2%)
  local copies, waits for them, and re-layouts  0.66 us (2%)
    pallas_call x1, Pallas kernels, project(): pl.pallas_call(functools.partial(project_kernel, tensors=tensors, section...  11.2 us
    pallas_call x1, Pallas kernels, fetch(): pl.pallas_call(fetch_kernel, out_shape=pltpu.VMEM((rows, columns), weight...  6.97 us
    ppermute x3, starting transfers between devices, across(): return lax.ppermute(array, ('tensor', 'section'), pairs)  3.94 us
    ppermute x3, starting transfers between devices, shifted(): lax.ppermute(array, axis, [(i, (i + shift) % count) for i in range(count)])  3.68 us
    ppermute x3, waiting for transfers between devices, shifted(): lax.ppermute(array, axis, [(i, (i + shift) % count) for i in range(count)])  3.42 us
    ppermute x3, waiting for transfers between devices, across(): return lax.ppermute(array, ('tensor', 'section'), pairs)  1.87 us
    pallas_call x1, Pallas kernels, prepare(): pl.pallas_call(functools.partial(prepare_kernel, slots=slots, owners=owne...  1.63 us
    pallas_call x1, Pallas kernels, finish(): pl.pallas_call(finish_kernel, out_shape=jax.ShapeDtypeStruct((local, 1, M...  1.03 us
  transfers between devices with their start and end apart: 6, of which 4 were waited for; matrix products, arithmetic and copies ran while one was open for 2% of the time, Pallas kernels for 25%

profile of v21, /device:TPU:0, one launch (start us, length us, event | category | flops | bytes accessed | tf_op | source)
XLA Modules:
  0.0 35.8 jit_solution(1439292464843396043)
XLA Ops:
  0.6 0.0 copy-start
  0.6 3.0 %collective-permute-start = (bf16[16,6656]{1,0:T(8,128)(2,1)}, bf16[16,6656]{1,0:T(8,128)(2,1)S(1)}, u32[]{:S(2)}, u32[]{:S(2)}) collective-permute-start(bf16[16,6656]{1,0:T(8,128)(2,1)} %own_ref.1), channel_id=1, source_target_pairs={{0,2},{2,0},{1,3},{3,1},{4,6},{6,4},{5,7},{7,5},{8,10},{10,8},{9,1... | collective-permute-start | bytes 638984 | tf_op jit(solution)/shard_map/ppermute | solution.py:403
  3.6 7.0 %fetch.1.held_ref = bf16[2560,4096]{1,0:T(8,128)(2,1)S(1)} custom-call(bf16[6656,4096]{1,0:T(8,128)(2,1)} %weight_ref.3), custom_call_target="tpu_custom_call" | custom-call | bytes 20971520 | tf_op jit(solution)/shard_map/fetch/pallas_call | solution.py:38
  10.6 0.0 collective-permute-done
  10.6 0.0 copy-done
  10.6 0.0 copy-start.3
  10.7 0.0 copy-start.2
  10.7 0.0 copy-start.1
  10.7 11.2 %project.1 = (f32[32,4096]{1,0:T(8,128)S(1)}, bf16[1,16,4096]{2,1,0:T(8,128)(2,1)S(1)}) custom-call(bf16[16,6656]{1,0:T(8,128)(2,1)S(1)} %copy-done, bf16[1,16,6656]{2,1,0:T(8,128)(2,1)S(1)} %bitcast.5, bf16[2560,4096]{1,0:T(8,128)(2,1)S(1)} %fetch.1.held_ref, bf16[6656,4096]{1,0:T(8,128)(2,1)} %weight_ref.3), custom_call_target="tpu_custom_call" | custom-call | flops 1744830464 | bytes 33554432 | tf_op jit(solution)/shard_map/project/pallas_call | solution.py:175
  21.9 0.1 collective-permute-start.1
  22.0 1.3 %collective-permute-done.1.refs_0_ = bf16[16,4096]{1,0:T(8,128)(2,1)S(1)} collective-permute-done((bf16[16,4096]{1,0:T(8,128)(2,1)S(1)}, bf16[16,4096]{1,0:T(8,128)(2,1)S(1)}, u32[]{:S(2)}, u32[]{:S(2)}) %collective-permute-start.1) | collective-permute-done | bytes 131104 | tf_op jit(solution)/shard_map/ppermute | solution.py:403
  23.4 2.4 %collective-permute-start.2 = (bf16[4,4096]{1,0:T(4,128)(2,1)S(1)}, bf16[4,4096]{1,0:T(4,128)(2,1)S(1)}, u32[]{:S(2)}, u32[]{:S(2)}) collective-permute-start(bf16[4,4096]{1,0:T(4,128)(2,1)S(1)} %get-tuple-element.23), channel_id=1, source_target_pairs={{0,9},{1,8},{4,13},{5,12},{8,5},{9,4},{12,1},{13,0},{2,11},{3,10},... | collective-permute-start | bytes 98312 | tf_op jit(solution)/shard_map/ppermute | solution.py:413
  25.8 1.2 %collective-permute-start.3 = (bf16[4,4096]{1,0:T(4,128)(2,1)S(1)}, bf16[4,4096]{1,0:T(4,128)(2,1)S(1)}, u32[]{:S(2)}, u32[]{:S(2)}) collective-permute-start(bf16[4,4096]{1,0:T(4,128)(2,1)S(1)} %get-tuple-element.24), channel_id=1, source_target_pairs={{0,13},{1,12},{4,9},{5,8},{8,1},{9,0},{12,5},{13,4},{2,15},{3,14},... | collective-permute-start | bytes 98312 | tf_op jit(solution)/shard_map/ppermute | solution.py:413
  27.0 0.3 collective-permute-start.4
  27.3 0.0 copy-done.3
  27.3 0.0 copy-done.2
  27.3 1.6 %prepare.1 = (f32[4,4]{1,0:T(4,128)S(1)}, bf16[1,128,8192]{2,1,0:T(8,128)(2,1)S(1)}) custom-call(s32[1,4]{1,0:T(1,128)S(1)} %bitcast.6, bf16[1,8192]{1,0:T(2,128)(2,1)S(1)} %broadcast_in_dim.3.gain_ref, bf16[1,64,8192]{2,1,0:T(8,128)(2,1)} %bitcast.9), custom_call_target="tpu_custom_call" | custom-call | tf_op jit(solution)/shard_map/prepare/pallas_call | solution.py:281
  29.0 0.0 collective-permute-done.2.refs_0_
  29.0 1.0 %collective-permute-done.3.refs_1_ = bf16[4,4096]{1,0:T(4,128)(2,1)S(1)} collective-permute-done((bf16[4,4096]{1,0:T(4,128)(2,1)S(1)}, bf16[4,4096]{1,0:T(4,128)(2,1)S(1)}, u32[]{:S(2)}, u32[]{:S(2)}) %collective-permute-start.3) | collective-permute-done | bytes 32800 | tf_op jit(solution)/shard_map/ppermute | solution.py:413
  30.0 0.8 %collective-permute-done.4.refs_2_ = bf16[4,4096]{1,0:T(4,128)(2,1)S(1)} collective-permute-done((bf16[4,4096]{1,0:T(4,128)(2,1)S(1)}, bf16[4,4096]{1,0:T(4,128)(2,1)S(1)}, u32[]{:S(2)}, u32[]{:S(2)}) %collective-permute-start.4) | collective-permute-done | bytes 32800 | tf_op jit(solution)/shard_map/ppermute | solution.py:413
  30.9 0.0 copy-done.1
  30.9 0.1 mix.1
  31.0 0.6 %collective-permute-start.5 = (bf16[2,4096]{1,0:T(2,128)(2,1)S(1)}, bf16[2,4096]{1,0:T(2,128)(2,1)S(1)}, u32[]{:S(2)}, u32[]{:S(2)}) collective-permute-start(bf16[2,4096]{1,0:T(2,128)(2,1)S(1)} %bitcast.8), channel_id=1, source_target_pairs={{0,2},{2,0},{1,3},{3,1},{4,6},{6,4},{5,7},{7,5},{8,10},{10,8},{9,1... | collective-permute-start | bytes 49160 | tf_op jit(solution)/shard_map/ppermute | solution.py:403
  31.6 0.6 %copy.8 = bf16[4,4096]{1,0:T(4,128)(2,1)} copy(bf16[4,4096]{1,0:T(4,128)(2,1)S(1)} %get-tuple-element.32) | data formatting | bytes 65536
  32.2 0.4 %own_half.1 = (f32[2,64]{1,0:T(2,128)S(1)}, f32[2,64]{1,0:T(2,128)S(1)}) custom-call(f32[2,4096]{1,0:T(2,128)S(1)} %get-tuple-element.27.rows_ref, bf16[1,128,8192]{2,1,0:T(8,128)(2,1)S(1)} %get-tuple-element.28.folded_ref), custom_call_target="tpu_custom_call" | custom-call | flops 2097152 | bytes 2097152 | tf_op jit(solution)/shard_map/own_half/pallas_call | solution.py:358
  32.7 2.1 %collective-permute-done.5.refs_0_ = bf16[2,4096]{1,0:T(2,128)(2,1)S(1)} collective-permute-done((bf16[2,4096]{1,0:T(2,128)(2,1)S(1)}, bf16[2,4096]{1,0:T(2,128)(2,1)S(1)}, u32[]{:S(2)}, u32[]{:S(2)}) %collective-permute-start.5) | collective-permute-done | bytes 16416 | tf_op jit(solution)/shard_map/ppermute | solution.py:403
  34.8 1.0 %finish.1 = f32[1,1,2,64]{3,2,1,0:T(2,128)} custom-call(f32[2,64]{1,0:T(2,128)S(1)} %get-tuple-element.29.values_ref, f32[2,64]{1,0:T(2,128)S(1)} %get-tuple-element.30.squares_ref, bf16[1,128,8192]{2,1,0:T(8,128)(2,1)S(1)} %get-tuple-element.28.folded_ref, bf16[2,4096]{1,0:T(2,128)(2,1)S(1)} %collective-permute-done.5.refs_0_), custom_call_target="tpu_custom_call" | custom-call | tf_op jit(solution)/shard_map/finish/pallas_call | solution.py:391
  (3 shorter events, 0.1 us)
Async XLA Ops:
  0.6 10.0 %copy-start = (bf16[16,6656]{1,0:T(8,128)(2,1)S(1)}, bf16[16,6656]{1,0:T(8,128)(2,1)}, u32[]{:S(2)}) copy-start(bf16[16,6656]{1,0:T(8,128)(2,1)} %own_ref.1) | copy-start | bytes 638980
  0.6 10.0 %collective-permute-start = (bf16[16,6656]{1,0:T(8,128)(2,1)}, bf16[16,6656]{1,0:T(8,128)(2,1)S(1)}, u32[]{:S(2)}, u32[]{:S(2)}) collective-permute-start(bf16[16,6656]{1,0:T(8,128)(2,1)} %own_ref.1), channel_id=1, source_target_pairs={{0,2},{2,0},{1,3},{3,1},{4,6},{6,4},{5,7},{7,5},{8,10},{10,8},{9,1... | collective-permute-start | bytes 638984 | tf_op jit(solution)/shard_map/ppermute | solution.py:403
  10.6 16.7 %copy-start.3 = (bf16[8192]{0:T(1024)(128)(2,1)S(1)}, bf16[8192]{0:T(1024)(128)(2,1)}, u32[]{:S(2)}) copy-start(bf16[8192]{0:T(1024)(128)(2,1)} %param.9) | copy-start | bytes 49156
  10.7 16.7 %copy-start.2 = (s32[4,1]{0,1:T(1,128)S(1)}, s32[4,1]{0,1:T(1,128)}, u32[]{:S(2)}) copy-start(s32[4,1]{0,1:T(1,128)} %param.11) | copy-start | bytes 52
  10.7 20.2 %copy-start.1 = (bf16[4,4096]{1,0:T(4,128)(2,1)S(1)}, bf16[4,4096]{1,0:T(4,128)(2,1)}, u32[]{:S(2)}) copy-start(bf16[4,4096]{1,0:T(4,128)(2,1)} %residual_ref.1) | copy-start | bytes 98308
  21.9 1.4 %collective-permute-start.1 = (bf16[16,4096]{1,0:T(8,128)(2,1)S(1)}, bf16[16,4096]{1,0:T(8,128)(2,1)S(1)}, u32[]{:S(2)}, u32[]{:S(2)}) collective-permute-start(bf16[16,4096]{1,0:T(8,128)(2,1)S(1)} %bitcast.7), channel_id=1, source_target_pairs={{0,1},{1,0},{2,3},{3,2},{4,5},{5,4},{6,7},{7,6},{8,9},{9,8},{10,11... | collective-permute-start | bytes 393224 | tf_op jit(solution)/shard_map/ppermute | solution.py:403
  23.4 5.6 %collective-permute-start.2 = (bf16[4,4096]{1,0:T(4,128)(2,1)S(1)}, bf16[4,4096]{1,0:T(4,128)(2,1)S(1)}, u32[]{:S(2)}, u32[]{:S(2)}) collective-permute-start(bf16[4,4096]{1,0:T(4,128)(2,1)S(1)} %get-tuple-element.23), channel_id=1, source_target_pairs={{0,9},{1,8},{4,13},{5,12},{8,5},{9,4},{12,1},{13,0},{2,11},{3,10},... | collective-permute-start | bytes 98312 | tf_op jit(solution)/shard_map/ppermute | solution.py:413
  25.8 4.3 %collective-permute-start.3 = (bf16[4,4096]{1,0:T(4,128)(2,1)S(1)}, bf16[4,4096]{1,0:T(4,128)(2,1)S(1)}, u32[]{:S(2)}, u32[]{:S(2)}) collective-permute-start(bf16[4,4096]{1,0:T(4,128)(2,1)S(1)} %get-tuple-element.24), channel_id=1, source_target_pairs={{0,13},{1,12},{4,9},{5,8},{8,1},{9,0},{12,5},{13,4},{2,15},{3,14},... | collective-permute-start | bytes 98312 | tf_op jit(solution)/shard_map/ppermute | solution.py:413
  27.0 3.9 %collective-permute-start.4 = (bf16[4,4096]{1,0:T(4,128)(2,1)S(1)}, bf16[4,4096]{1,0:T(4,128)(2,1)S(1)}, u32[]{:S(2)}, u32[]{:S(2)}) collective-permute-start(bf16[4,4096]{1,0:T(4,128)(2,1)S(1)} %get-tuple-element.25), channel_id=1, source_target_pairs={{0,5},{1,4},{4,1},{5,0},{8,13},{9,12},{12,9},{13,8},{2,7},{3,6},{6... | collective-permute-start | bytes 98312 | tf_op jit(solution)/shard_map/ppermute | solution.py:413
  31.0 3.8 %collective-permute-start.5 = (bf16[2,4096]{1,0:T(2,128)(2,1)S(1)}, bf16[2,4096]{1,0:T(2,128)(2,1)S(1)}, u32[]{:S(2)}, u32[]{:S(2)}) collective-permute-start(bf16[2,4096]{1,0:T(2,128)(2,1)S(1)} %bitcast.8), channel_id=1, source_target_pairs={{0,2},{2,0},{1,3},{3,1},{4,6},{6,4},{5,7},{7,5},{8,10},{10,8},{9,1... | collective-permute-start | bytes 49160 | tf_op jit(solution)/shard_map/ppermute | solution.py:403

commit v22 on v15

--- a/solution.py
+++ b/solution.py
@@ -325,11 +325,11 @@
         mine = slice(adapter * MOST, (adapter + 1) * MOST)
         both = jnp.concatenate([high[mine], low[mine]], axis=0)
         product = lax.dot_general(
+            shrink_ref[adapter, :, pl.ds(first, columns)],
             both,
-            shrink_ref[adapter, :, pl.ds(first, columns)],
             (((1,), (1,)), ((), ())),
             preferred_element_type=F32,
-        )
+        ).T
         values.append(product[:MOST] + product[MOST:])
     return jnp.concatenate(values, axis=0), squares
 

time: 35.8 us -> 36 us (level)
  no operation moved by 1% of the time
where the time goes in v22:
time: 36 us; the launch traced here: 35.8 us
  Pallas kernels  21 us (58%)
  starting transfers between devices  7.61 us (21%)
  waiting for transfers between devices  5.8 us (16%)
  between operations  0.73 us (2%)
  local copies, waits for them, and re-layouts  0.66 us (2%)
    pallas_call x1, Pallas kernels, project(): pl.pallas_call(functools.partial(project_kernel, tensors=tensors, section...  11.2 us
    pallas_call x1, Pallas kernels, fetch(): pl.pallas_call(fetch_kernel, out_shape=pltpu.VMEM((rows, columns), weight...  6.97 us
    ppermute x3, starting transfers between devices, across(): return lax.ppermute(array, ('tensor', 'section'), pairs)  3.93 us
    ppermute x3, starting transfers between devices, shifted(): lax.ppermute(array, axis, [(i, (i + shift) % count) for i in range(count)])  3.68 us
    ppermute x3, waiting for transfers between devices, shifted(): lax.ppermute(array, axis, [(i, (i + shift) % count) for i in range(count)])  3.48 us
    ppermute x3, waiting for transfers between devices, across(): return lax.ppermute(array, ('tensor', 'section'), pairs)  2.32 us
    pallas_call x1, Pallas kernels, prepare(): pl.pallas_call(functools.partial(prepare_kernel, slots=slots, owners=owne...  1.23 us
    pallas_call x1, Pallas kernels, finish(): pl.pallas_call(finish_kernel, out_shape=jax.ShapeDtypeStruct((local, 1, M...  0.95 us
  transfers between devices with their start and end apart: 6, of which 4 were waited for; matrix products, arithmetic and copies ran while one was open for 2% of the time, Pallas kernels for 24%

profile of v22, /device:TPU:0, one launch (start us, length us, event | category | flops | bytes accessed | tf_op | source)
XLA Modules:
  0.0 35.8 jit_solution(12703346243394660826)
XLA Ops:
  0.6 0.0 copy-start
  0.6 3.0 %collective-permute-start = (bf16[16,6656]{1,0:T(8,128)(2,1)}, bf16[16,6656]{1,0:T(8,128)(2,1)S(1)}, u32[]{:S(2)}, u32[]{:S(2)}) collective-permute-start(bf16[16,6656]{1,0:T(8,128)(2,1)} %own_ref.1), channel_id=1, source_target_pairs={{0,2},{2,0},{1,3},{3,1},{4,6},{6,4},{5,7},{7,5},{8,10},{10,8},{9,1... | collective-permute-start | bytes 638984 | tf_op jit(solution)/shard_map/ppermute | solution.py:401
  3.6 7.0 %fetch.1.held_ref = bf16[2560,4096]{1,0:T(8,128)(2,1)S(1)} custom-call(bf16[6656,4096]{1,0:T(8,128)(2,1)} %weight_ref.3), custom_call_target="tpu_custom_call" | custom-call | bytes 20971520 | tf_op jit(solution)/shard_map/fetch/pallas_call | solution.py:38
  10.6 0.0 copy-start.2
  10.6 0.0 copy-start.1
  10.6 0.0 copy-start.3
  10.7 0.0 collective-permute-done
  10.7 0.0 copy-done
  10.7 11.2 %project.1 = (f32[32,4096]{1,0:T(8,128)S(1)}, bf16[1,16,4096]{2,1,0:T(8,128)(2,1)S(1)}) custom-call(bf16[16,6656]{1,0:T(8,128)(2,1)S(1)} %copy-done, bf16[1,16,6656]{2,1,0:T(8,128)(2,1)S(1)} %bitcast.5, bf16[2560,4096]{1,0:T(8,128)(2,1)S(1)} %fetch.1.held_ref, bf16[6656,4096]{1,0:T(8,128)(2,1)} %weight_ref.3), custom_call_target="tpu_custom_call" | custom-call | flops 1744830464 | bytes 33554432 | tf_op jit(solution)/shard_map/project/pallas_call | solution.py:175
  21.9 0.1 collective-permute-start.1
  22.0 1.3 %collective-permute-done.1.refs_0_ = bf16[16,4096]{1,0:T(8,128)(2,1)S(1)} collective-permute-done((bf16[16,4096]{1,0:T(8,128)(2,1)S(1)}, bf16[16,4096]{1,0:T(8,128)(2,1)S(1)}, u32[]{:S(2)}, u32[]{:S(2)}) %collective-permute-start.1) | collective-permute-done | bytes 131104 | tf_op jit(solution)/shard_map/ppermute | solution.py:401
  23.4 2.4 %collective-permute-start.2 = (bf16[4,4096]{1,0:T(4,128)(2,1)S(1)}, bf16[4,4096]{1,0:T(4,128)(2,1)S(1)}, u32[]{:S(2)}, u32[]{:S(2)}) collective-permute-start(bf16[4,4096]{1,0:T(4,128)(2,1)S(1)} %get-tuple-element.23), channel_id=1, source_target_pairs={{0,9},{1,8},{4,13},{5,12},{8,5},{9,4},{12,1},{13,0},{2,11},{3,10},... | collective-permute-start | bytes 98312 | tf_op jit(solution)/shard_map/ppermute | solution.py:411
  25.8 1.2 %collective-permute-start.3 = (bf16[4,4096]{1,0:T(4,128)(2,1)S(1)}, bf16[4,4096]{1,0:T(4,128)(2,1)S(1)}, u32[]{:S(2)}, u32[]{:S(2)}) collective-permute-start(bf16[4,4096]{1,0:T(4,128)(2,1)S(1)} %get-tuple-element.24), channel_id=1, source_target_pairs={{0,13},{1,12},{4,9},{5,8},{8,1},{9,0},{12,5},{13,4},{2,15},{3,14},... | collective-permute-start | bytes 98312 | tf_op jit(solution)/shard_map/ppermute | solution.py:411
  27.0 0.3 collective-permute-start.4
  27.3 0.0 copy-done.2
  27.3 1.2 %prepare.1 = (f32[4,4]{1,0:T(4,128)S(1)}, bf16[1,64,8192]{2,1,0:T(8,128)(2,1)S(1)}) custom-call(s32[1,4]{1,0:T(1,128)S(1)} %bitcast.6, bf16[1,64,8192]{2,1,0:T(8,128)(2,1)} %bitcast.9), custom_call_target="tpu_custom_call" | custom-call | tf_op jit(solution)/shard_map/prepare/pallas_call | solution.py:269
  28.5 0.0 collective-permute-done.2.refs_0_
  28.6 1.5 %collective-permute-done.3.refs_1_ = bf16[4,4096]{1,0:T(4,128)(2,1)S(1)} collective-permute-done((bf16[4,4096]{1,0:T(4,128)(2,1)S(1)}, bf16[4,4096]{1,0:T(4,128)(2,1)S(1)}, u32[]{:S(2)}, u32[]{:S(2)}) %collective-permute-start.3) | collective-permute-done | bytes 32800 | tf_op jit(solution)/shard_map/ppermute | solution.py:411
  30.0 0.9 %collective-permute-done.4.refs_2_ = bf16[4,4096]{1,0:T(4,128)(2,1)S(1)} collective-permute-done((bf16[4,4096]{1,0:T(4,128)(2,1)S(1)}, bf16[4,4096]{1,0:T(4,128)(2,1)S(1)}, u32[]{:S(2)}, u32[]{:S(2)}) %collective-permute-start.4) | collective-permute-done | bytes 32800 | tf_op jit(solution)/shard_map/ppermute | solution.py:411
  30.9 0.0 copy-done.1
  30.9 0.1 mix.1
  31.0 0.6 %collective-permute-start.5 = (bf16[2,4096]{1,0:T(2,128)(2,1)S(1)}, bf16[2,4096]{1,0:T(2,128)(2,1)S(1)}, u32[]{:S(2)}, u32[]{:S(2)}) collective-permute-start(bf16[2,4096]{1,0:T(2,128)(2,1)S(1)} %bitcast.8), channel_id=1, source_target_pairs={{0,2},{2,0},{1,3},{3,1},{4,6},{6,4},{5,7},{7,5},{8,10},{10,8},{9,1... | collective-permute-start | bytes 49160 | tf_op jit(solution)/shard_map/ppermute | solution.py:401
  31.6 0.0 copy-done.3
  31.6 0.6 %copy.8 = bf16[4,4096]{1,0:T(4,128)(2,1)} copy(bf16[4,4096]{1,0:T(4,128)(2,1)S(1)} %get-tuple-element.32) | data formatting | bytes 65536
  32.3 0.4 %own_half.1 = (f32[2,64]{1,0:T(2,128)S(1)}, f32[2,64]{1,0:T(2,128)S(1)}) custom-call(f32[2,4096]{1,0:T(2,128)S(1)} %get-tuple-element.27.rows_ref, bf16[1,8192]{1,0:T(2,128)(2,1)S(1)} %broadcast_in_dim.3.gain_ref, bf16[1,64,8192]{2,1,0:T(8,128)(2,1)S(1)} %get-tuple-element.28.shrink_ref), custom_call_target="tpu_custom_call" | custom-call | flops 1048576 | bytes 2097152 | tf_op jit(solution)/shard_map/own_half/pallas_call | solution.py:349
  32.6 2.2 %collective-permute-done.5.refs_0_ = bf16[2,4096]{1,0:T(2,128)(2,1)S(1)} collective-permute-done((bf16[2,4096]{1,0:T(2,128)(2,1)S(1)}, bf16[2,4096]{1,0:T(2,128)(2,1)S(1)}, u32[]{:S(2)}, u32[]{:S(2)}) %collective-permute-start.5) | collective-permute-done | bytes 16416 | tf_op jit(solution)/shard_map/ppermute | solution.py:401
  34.8 1.0 %finish.1 = f32[1,1,2,64]{3,2,1,0:T(2,128)} custom-call(f32[2,64]{1,0:T(2,128)S(1)} %get-tuple-element.29.values_ref, f32[2,64]{1,0:T(2,128)S(1)} %get-tuple-element.30.squares_ref, bf16[1,8192]{1,0:T(2,128)(2,1)S(1)} %broadcast_in_dim.3.gain_ref, bf16[1,64,8192]{2,1,0:T(8,128)(2,1)S(1)} %get-tuple-element.28.shrink_ref, ...), custom_call_target="tpu_custom_call" | custom-call | tf_op jit(solution)/shard_map/finish/pallas_call | solution.py:389
  (3 shorter events, 0.1 us)
Async XLA Ops:
  0.6 10.0 %copy-start = (bf16[16,6656]{1,0:T(8,128)(2,1)S(1)}, bf16[16,6656]{1,0:T(8,128)(2,1)}, u32[]{:S(2)}) copy-start(bf16[16,6656]{1,0:T(8,128)(2,1)} %own_ref.1) | copy-start | bytes 638980
  0.6 10.0 %collective-permute-start = (bf16[16,6656]{1,0:T(8,128)(2,1)}, bf16[16,6656]{1,0:T(8,128)(2,1)S(1)}, u32[]{:S(2)}, u32[]{:S(2)}) collective-permute-start(bf16[16,6656]{1,0:T(8,128)(2,1)} %own_ref.1), channel_id=1, source_target_pairs={{0,2},{2,0},{1,3},{3,1},{4,6},{6,4},{5,7},{7,5},{8,10},{10,8},{9,1... | collective-permute-start | bytes 638984 | tf_op jit(solution)/shard_map/ppermute | solution.py:401
  10.6 16.7 %copy-start.2 = (s32[4,1]{0,1:T(1,128)S(1)}, s32[4,1]{0,1:T(1,128)}, u32[]{:S(2)}) copy-start(s32[4,1]{0,1:T(1,128)} %param.11) | copy-start | bytes 52
  10.6 20.2 %copy-start.1 = (bf16[4,4096]{1,0:T(4,128)(2,1)S(1)}, bf16[4,4096]{1,0:T(4,128)(2,1)}, u32[]{:S(2)}) copy-start(bf16[4,4096]{1,0:T(4,128)(2,1)} %residual_ref.1) | copy-start | bytes 98308
  10.6 21.0 %copy-start.3 = (bf16[8192]{0:T(1024)(128)(2,1)S(1)}, bf16[8192]{0:T(1024)(128)(2,1)}, u32[]{:S(2)}) copy-start(bf16[8192]{0:T(1024)(128)(2,1)} %param.9) | copy-start | bytes 49156
  21.9 1.4 %collective-permute-start.1 = (bf16[16,4096]{1,0:T(8,128)(2,1)S(1)}, bf16[16,4096]{1,0:T(8,128)(2,1)S(1)}, u32[]{:S(2)}, u32[]{:S(2)}) collective-permute-start(bf16[16,4096]{1,0:T(8,128)(2,1)S(1)} %bitcast.7), channel_id=1, source_target_pairs={{0,1},{1,0},{2,3},{3,2},{4,5},{5,4},{6,7},{7,6},{8,9},{9,8},{10,11... | collective-permute-start | bytes 393224 | tf_op jit(solution)/shard_map/ppermute | solution.py:401
  23.4 5.2 %collective-permute-start.2 = (bf16[4,4096]{1,0:T(4,128)(2,1)S(1)}, bf16[4,4096]{1,0:T(4,128)(2,1)S(1)}, u32[]{:S(2)}, u32[]{:S(2)}) collective-permute-start(bf16[4,4096]{1,0:T(4,128)(2,1)S(1)} %get-tuple-element.23), channel_id=1, source_target_pairs={{0,9},{1,8},{4,13},{5,12},{8,5},{9,4},{12,1},{13,0},{2,11},{3,10},... | collective-permute-start | bytes 98312 | tf_op jit(solution)/shard_map/ppermute | solution.py:411
  25.8 4.3 %collective-permute-start.3 = (bf16[4,4096]{1,0:T(4,128)(2,1)S(1)}, bf16[4,4096]{1,0:T(4,128)(2,1)S(1)}, u32[]{:S(2)}, u32[]{:S(2)}) collective-permute-start(bf16[4,4096]{1,0:T(4,128)(2,1)S(1)} %get-tuple-element.24), channel_id=1, source_target_pairs={{0,13},{1,12},{4,9},{5,8},{8,1},{9,0},{12,5},{13,4},{2,15},{3,14},... | collective-permute-start | bytes 98312 | tf_op jit(solution)/shard_map/ppermute | solution.py:411
  27.0 3.9 %collective-permute-start.4 = (bf16[4,4096]{1,0:T(4,128)(2,1)S(1)}, bf16[4,4096]{1,0:T(4,128)(2,1)S(1)}, u32[]{:S(2)}, u32[]{:S(2)}) collective-permute-start(bf16[4,4096]{1,0:T(4,128)(2,1)S(1)} %get-tuple-element.25), channel_id=1, source_target_pairs={{0,5},{1,4},{4,1},{5,0},{8,13},{9,12},{12,9},{13,8},{2,7},{3,6},{6... | collective-permute-start | bytes 98312 | tf_op jit(solution)/shard_map/ppermute | solution.py:411
  31.0 3.8 %collective-permute-start.5 = (bf16[2,4096]{1,0:T(2,128)(2,1)S(1)}, bf16[2,4096]{1,0:T(2,128)(2,1)S(1)}, u32[]{:S(2)}, u32[]{:S(2)}) collective-permute-start(bf16[2,4096]{1,0:T(2,128)(2,1)S(1)} %bitcast.8), channel_id=1, source_target_pairs={{0,2},{2,0},{1,3},{3,1},{4,6},{6,4},{5,7},{7,5},{8,10},{10,8},{9,1... | collective-permute-start | bytes 49160 | tf_op jit(solution)/shard_map/ppermute | solution.py:401

commit v23 on v15

--- a/solution.py
+++ b/solution.py
@@ -258,11 +258,17 @@
     return jnp.logical_and(row == adapter, rank_of == slot % MOST).astype(F32)
 
 
-def prepare_kernel(index_ref, shrink_ref, places_ref, out_ref, sem, *, slots, owners):
-    copy = pltpu.make_async_copy(shrink_ref, out_ref, sem)
+def prepare_kernel(index_ref, shrink_ref, places_ref, out_ref, raw_ref, sem, *, slots, owners):
+    copy = pltpu.make_async_copy(shrink_ref, raw_ref, sem)
     copy.start()
     places_ref[...] = places_of(index_ref[...], slots, owners, slots // MOST)
     copy.wait()
+    local, _, features = raw_ref.shape
+    width = min(features, WIDTH)
+    for adapter in range(local):
+        for n in range(0, features, width):
+            block = raw_ref[adapter, :, n : n + width].astype(F32)
+            out_ref[adapter, n : n + width, :] = block.T.astype(BF16)
 
 
 def prepare(index, shrink, slots, owners):
@@ -270,12 +276,12 @@
         functools.partial(prepare_kernel, slots=slots, owners=owners),
         out_shape=(
             jax.ShapeDtypeStruct((slots * owners, index.shape[1]), F32),
-            pltpu.VMEM(shrink.shape, shrink.dtype),
+            pltpu.VMEM((shrink.shape[0], shrink.shape[2], shrink.shape[1]), shrink.dtype),
         ),
         in_specs=[whole(), pl.BlockSpec(memory_space=pl.ANY)],
         out_specs=(whole(), whole()),
-        scratch_shapes=[pltpu.SemaphoreType.DMA],
-        compiler_params=pltpu.CompilerParams(vmem_limit_bytes=1 * MIB),
+        scratch_shapes=[pltpu.VMEM(shrink.shape, shrink.dtype), pltpu.SemaphoreType.DMA],
+        compiler_params=pltpu.CompilerParams(vmem_limit_bytes=6 * MIB),
         name="prepare",
     )(index, pltpu.with_memory_space_constraint(shrink, pltpu.HBM))
 
@@ -324,11 +330,8 @@
     for adapter in range(local):
         mine = slice(adapter * MOST, (adapter + 1) * MOST)
         both = jnp.concatenate([high[mine], low[mine]], axis=0)
-        product = lax.dot_general(
-            both,
-            shrink_ref[adapter, :, pl.ds(first, columns)],
-            (((1,), (1,)), ((), ())),
-            preferred_element_type=F32,
+        product = jnp.dot(
+            both, shrink_ref[adapter, pl.ds(first, columns), :], preferred_element_type=F32
         )
         values.append(product[:MOST] + product[MOST:])
     return jnp.concatenate(values, axis=0), squares
@@ -345,7 +348,7 @@
 
 def own_half(rows, gain, shrink):
     slots = rows.shape[0]
-    rank = shrink.shape[1]
+    rank = shrink.shape[2]
     return pl.pallas_call(
         own_half_kernel,
         out_shape=(
@@ -385,7 +388,7 @@
 
 
 def finish(values, squares, gain, shrink, arrived):
-    local, rank, _ = shrink.shape
+    local, _, rank = shrink.shape
     return pl.pallas_call(
         finish_kernel,
         out_shape=jax.ShapeDtypeStruct((local, 1, MOST, rank), F32),

time: 35.8 us -> 35.8 us (level)
  Pallas kernels: 20.7 us -> 21.4 us
  waiting for transfers between devices: 5.9 us -> 5.27 us
    ppermute x3, waiting for transfers between devices: 2.32 us -> 1.69 us  [across(): return lax.ppermute(array, ('tensor', 'section'), pairs)]
    pallas_call x1, Pallas kernels: 1.23 us -> 1.85 us  [prepare(): pl.pallas_call(functools.partial(prepare_kernel, slots=slots, owners=owne...]
  transfers between devices with their start and end apart: 6 -> 6, of which waited for: 4 -> 4; matrix products, arithmetic and copies ran while one was open for 2% -> 2% of each run, Pallas kernels for 24% -> 26%
where the time goes in v23:
time: 35.8 us; the launch traced here: 35.7 us
  Pallas kernels  21.4 us (60%)
  starting transfers between devices  7.62 us (21%)
  waiting for transfers between devices  5.27 us (15%)
  between operations  0.74 us (2%)
  local copies, waits for them, and re-layouts  0.66 us (2%)
    pallas_call x1, Pallas kernels, project(): pl.pallas_call(functools.partial(project_kernel, tensors=tensors, section...  11.2 us
    pallas_call x1, Pallas kernels, fetch(): pl.pallas_call(fetch_kernel, out_shape=pltpu.VMEM((rows, columns), weight...  6.97 us
    ppermute x3, starting transfers between devices, across(): return lax.ppermute(array, ('tensor', 'section'), pairs)  3.94 us
    ppermute x3, starting transfers between devices, shifted(): lax.ppermute(array, axis, [(i, (i + shift) % count) for i in range(count)])  3.68 us
    ppermute x3, waiting for transfers between devices, shifted(): lax.ppermute(array, axis, [(i, (i + shift) % count) for i in range(count)])  3.58 us
    pallas_call x1, Pallas kernels, prepare(): pl.pallas_call(functools.partial(prepare_kernel, slots=slots, owners=owne...  1.85 us
    ppermute x3, waiting for transfers between devices, across(): return lax.ppermute(array, ('tensor', 'section'), pairs)  1.69 us
    pallas_call x1, Pallas kernels, finish(): pl.pallas_call(finish_kernel, out_shape=jax.ShapeDtypeStruct((local, 1, M...  0.83 us
  transfers between devices with their start and end apart: 6, of which 4 were waited for; matrix products, arithmetic and copies ran while one was open for 2% of the time, Pallas kernels for 26%

profile of v23, /device:TPU:0, one launch (start us, length us, event | category | flops | bytes accessed | tf_op | source)
XLA Modules:
  0.0 35.7 jit_solution(10129295231750095515)
XLA Ops:
  0.6 0.0 copy-start
  0.6 3.0 %collective-permute-start = (bf16[16,6656]{1,0:T(8,128)(2,1)}, bf16[16,6656]{1,0:T(8,128)(2,1)S(1)}, u32[]{:S(2)}, u32[]{:S(2)}) collective-permute-start(bf16[16,6656]{1,0:T(8,128)(2,1)} %own_ref.1), channel_id=1, source_target_pairs={{0,2},{2,0},{1,3},{3,1},{4,6},{6,4},{5,7},{7,5},{8,10},{10,8},{9,1... | collective-permute-start | bytes 638984 | tf_op jit(solution)/shard_map/ppermute | solution.py:404
  3.6 7.0 %fetch.1.held_ref = bf16[2560,4096]{1,0:T(8,128)(2,1)S(1)} custom-call(bf16[6656,4096]{1,0:T(8,128)(2,1)} %weight_ref.3), custom_call_target="tpu_custom_call" | custom-call | bytes 20971520 | tf_op jit(solution)/shard_map/fetch/pallas_call | solution.py:38
  10.6 0.0 collective-permute-done
  10.6 0.0 copy-done
  10.6 0.0 copy-start.2
  10.7 0.0 copy-start.1
  10.7 0.0 copy-start.3
  10.7 11.2 %project.1 = (f32[32,4096]{1,0:T(8,128)S(1)}, bf16[1,16,4096]{2,1,0:T(8,128)(2,1)S(1)}) custom-call(bf16[16,6656]{1,0:T(8,128)(2,1)S(1)} %copy-done, bf16[1,16,6656]{2,1,0:T(8,128)(2,1)S(1)} %bitcast.5, bf16[2560,4096]{1,0:T(8,128)(2,1)S(1)} %fetch.1.held_ref, bf16[6656,4096]{1,0:T(8,128)(2,1)} %weight_ref.3), custom_call_target="tpu_custom_call" | custom-call | flops 1744830464 | bytes 33554432 | tf_op jit(solution)/shard_map/project/pallas_call | solution.py:175
  21.9 0.1 collective-permute-start.1
  22.0 1.3 %collective-permute-done.1.refs_0_ = bf16[16,4096]{1,0:T(8,128)(2,1)S(1)} collective-permute-done((bf16[16,4096]{1,0:T(8,128)(2,1)S(1)}, bf16[16,4096]{1,0:T(8,128)(2,1)S(1)}, u32[]{:S(2)}, u32[]{:S(2)}) %collective-permute-start.1) | collective-permute-done | bytes 131104 | tf_op jit(solution)/shard_map/ppermute | solution.py:404
  23.4 2.4 %collective-permute-start.2 = (bf16[4,4096]{1,0:T(4,128)(2,1)S(1)}, bf16[4,4096]{1,0:T(4,128)(2,1)S(1)}, u32[]{:S(2)}, u32[]{:S(2)}) collective-permute-start(bf16[4,4096]{1,0:T(4,128)(2,1)S(1)} %get-tuple-element.23), channel_id=1, source_target_pairs={{0,9},{1,8},{4,13},{5,12},{8,5},{9,4},{12,1},{13,0},{2,11},{3,10},... | collective-permute-start | bytes 98312 | tf_op jit(solution)/shard_map/ppermute | solution.py:414
  25.8 1.2 %collective-permute-start.3 = (bf16[4,4096]{1,0:T(4,128)(2,1)S(1)}, bf16[4,4096]{1,0:T(4,128)(2,1)S(1)}, u32[]{:S(2)}, u32[]{:S(2)}) collective-permute-start(bf16[4,4096]{1,0:T(4,128)(2,1)S(1)} %get-tuple-element.24), channel_id=1, source_target_pairs={{0,13},{1,12},{4,9},{5,8},{8,1},{9,0},{12,5},{13,4},{2,15},{3,14},... | collective-permute-start | bytes 98312 | tf_op jit(solution)/shard_map/ppermute | solution.py:414
  27.0 0.3 collective-permute-start.4
  27.3 0.0 copy-done.2
  27.3 1.8 %prepare.1 = (f32[4,4]{1,0:T(4,128)S(1)}, bf16[1,8192,64]{2,1,0:T(8,128)(2,1)S(1)}) custom-call(s32[1,4]{1,0:T(1,128)S(1)} %bitcast.6, bf16[1,64,8192]{2,1,0:T(8,128)(2,1)} %bitcast.9), custom_call_target="tpu_custom_call" | custom-call | tf_op jit(solution)/shard_map/prepare/pallas_call | solution.py:275
  29.2 0.0 collective-permute-done.2.refs_0_
  29.2 0.8 %collective-permute-done.3.refs_1_ = bf16[4,4096]{1,0:T(4,128)(2,1)S(1)} collective-permute-done((bf16[4,4096]{1,0:T(4,128)(2,1)S(1)}, bf16[4,4096]{1,0:T(4,128)(2,1)S(1)}, u32[]{:S(2)}, u32[]{:S(2)}) %collective-permute-start.3) | collective-permute-done | bytes 32800 | tf_op jit(solution)/shard_map/ppermute | solution.py:414
  30.0 0.8 %collective-permute-done.4.refs_2_ = bf16[4,4096]{1,0:T(4,128)(2,1)S(1)} collective-permute-done((bf16[4,4096]{1,0:T(4,128)(2,1)S(1)}, bf16[4,4096]{1,0:T(4,128)(2,1)S(1)}, u32[]{:S(2)}, u32[]{:S(2)}) %collective-permute-start.4) | collective-permute-done | bytes 32800 | tf_op jit(solution)/shard_map/ppermute | solution.py:414
  30.9 0.0 copy-done.1
  30.9 0.1 mix.1
  31.0 0.6 %collective-permute-start.5 = (bf16[2,4096]{1,0:T(2,128)(2,1)S(1)}, bf16[2,4096]{1,0:T(2,128)(2,1)S(1)}, u32[]{:S(2)}, u32[]{:S(2)}) collective-permute-start(bf16[2,4096]{1,0:T(2,128)(2,1)S(1)} %bitcast.8), channel_id=1, source_target_pairs={{0,2},{2,0},{1,3},{3,1},{4,6},{6,4},{5,7},{7,5},{8,10},{10,8},{9,1... | collective-permute-start | bytes 49160 | tf_op jit(solution)/shard_map/ppermute | solution.py:404
  31.6 0.0 copy-done.3
  31.6 0.6 %copy.8 = bf16[4,4096]{1,0:T(4,128)(2,1)} copy(bf16[4,4096]{1,0:T(4,128)(2,1)S(1)} %get-tuple-element.32) | data formatting | bytes 65536
  32.3 0.3 own_half.1
  32.5 2.3 %collective-permute-done.5.refs_0_ = bf16[2,4096]{1,0:T(2,128)(2,1)S(1)} collective-permute-done((bf16[2,4096]{1,0:T(2,128)(2,1)S(1)}, bf16[2,4096]{1,0:T(2,128)(2,1)S(1)}, u32[]{:S(2)}, u32[]{:S(2)}) %collective-permute-start.5) | collective-permute-done | bytes 16416 | tf_op jit(solution)/shard_map/ppermute | solution.py:404
  34.8 0.8 %finish.1 = f32[1,1,2,64]{3,2,1,0:T(2,128)} custom-call(f32[2,64]{1,0:T(2,128)S(1)} %get-tuple-element.29.values_ref, f32[2,64]{1,0:T(2,128)S(1)} %get-tuple-element.30.squares_ref, bf16[1,8192]{1,0:T(2,128)(2,1)S(1)} %broadcast_in_dim.3.gain_ref, bf16[1,8192,64]{2,1,0:T(8,128)(2,1)S(1)} %get-tuple-element.28.shrink_ref, ...), custom_call_target="tpu_custom_call" | custom-call | tf_op jit(solution)/shard_map/finish/pallas_call | solution.py:392
  (3 shorter events, 0.1 us)
Async XLA Ops:
  0.6 10.0 %copy-start = (bf16[16,6656]{1,0:T(8,128)(2,1)S(1)}, bf16[16,6656]{1,0:T(8,128)(2,1)}, u32[]{:S(2)}) copy-start(bf16[16,6656]{1,0:T(8,128)(2,1)} %own_ref.1) | copy-start | bytes 638980
  0.6 10.0 %collective-permute-start = (bf16[16,6656]{1,0:T(8,128)(2,1)}, bf16[16,6656]{1,0:T(8,128)(2,1)S(1)}, u32[]{:S(2)}, u32[]{:S(2)}) collective-permute-start(bf16[16,6656]{1,0:T(8,128)(2,1)} %own_ref.1), channel_id=1, source_target_pairs={{0,2},{2,0},{1,3},{3,1},{4,6},{6,4},{5,7},{7,5},{8,10},{10,8},{9,1... | collective-permute-start | bytes 638984 | tf_op jit(solution)/shard_map/ppermute | solution.py:404
  10.6 16.7 %copy-start.2 = (s32[4,1]{0,1:T(1,128)S(1)}, s32[4,1]{0,1:T(1,128)}, u32[]{:S(2)}) copy-start(s32[4,1]{0,1:T(1,128)} %param.11) | copy-start | bytes 52
  10.7 20.2 %copy-start.1 = (bf16[4,4096]{1,0:T(4,128)(2,1)S(1)}, bf16[4,4096]{1,0:T(4,128)(2,1)}, u32[]{:S(2)}) copy-start(bf16[4,4096]{1,0:T(4,128)(2,1)} %residual_ref.1) | copy-start | bytes 98308
  10.7 21.0 %copy-start.3 = (bf16[8192]{0:T(1024)(128)(2,1)S(1)}, bf16[8192]{0:T(1024)(128)(2,1)}, u32[]{:S(2)}) copy-start(bf16[8192]{0:T(1024)(128)(2,1)} %param.9) | copy-start | bytes 49156
  21.9 1.4 %collective-permute-start.1 = (bf16[16,4096]{1,0:T(8,128)(2,1)S(1)}, bf16[16,4096]{1,0:T(8,128)(2,1)S(1)}, u32[]{:S(2)}, u32[]{:S(2)}) collective-permute-start(bf16[16,4096]{1,0:T(8,128)(2,1)S(1)} %bitcast.7), channel_id=1, source_target_pairs={{0,1},{1,0},{2,3},{3,2},{4,5},{5,4},{6,7},{7,6},{8,9},{9,8},{10,11... | collective-permute-start | bytes 393224 | tf_op jit(solution)/shard_map/ppermute | solution.py:404
  23.4 5.8 %collective-permute-start.2 = (bf16[4,4096]{1,0:T(4,128)(2,1)S(1)}, bf16[4,4096]{1,0:T(4,128)(2,1)S(1)}, u32[]{:S(2)}, u32[]{:S(2)}) collective-permute-start(bf16[4,4096]{1,0:T(4,128)(2,1)S(1)} %get-tuple-element.23), channel_id=1, source_target_pairs={{0,9},{1,8},{4,13},{5,12},{8,5},{9,4},{12,1},{13,0},{2,11},{3,10},... | collective-permute-start | bytes 98312 | tf_op jit(solution)/shard_map/ppermute | solution.py:414
  25.8 4.3 %collective-permute-start.3 = (bf16[4,4096]{1,0:T(4,128)(2,1)S(1)}, bf16[4,4096]{1,0:T(4,128)(2,1)S(1)}, u32[]{:S(2)}, u32[]{:S(2)}) collective-permute-start(bf16[4,4096]{1,0:T(4,128)(2,1)S(1)} %get-tuple-element.24), channel_id=1, source_target_pairs={{0,13},{1,12},{4,9},{5,8},{8,1},{9,0},{12,5},{13,4},{2,15},{3,14},... | collective-permute-start | bytes 98312 | tf_op jit(solution)/shard_map/ppermute | solution.py:414
  27.0 3.9 %collective-permute-start.4 = (bf16[4,4096]{1,0:T(4,128)(2,1)S(1)}, bf16[4,4096]{1,0:T(4,128)(2,1)S(1)}, u32[]{:S(2)}, u32[]{:S(2)}) collective-permute-start(bf16[4,4096]{1,0:T(4,128)(2,1)S(1)} %get-tuple-element.25), channel_id=1, source_target_pairs={{0,5},{1,4},{4,1},{5,0},{8,13},{9,12},{12,9},{13,8},{2,7},{3,6},{6... | collective-permute-start | bytes 98312 | tf_op jit(solution)/shard_map/ppermute | solution.py:414
  31.0 3.8 %collective-permute-start.5 = (bf16[2,4096]{1,0:T(2,128)(2,1)S(1)}, bf16[2,4096]{1,0:T(2,128)(2,1)S(1)}, u32[]{:S(2)}, u32[]{:S(2)}) collective-permute-start(bf16[2,4096]{1,0:T(2,128)(2,1)S(1)} %bitcast.8), channel_id=1, source_target_pairs={{0,2},{2,0},{1,3},{3,1},{4,6},{6,4},{5,7},{7,5},{8,10},{10,8},{9,1... | collective-permute-start | bytes 49160 | tf_op jit(solution)/shard_map/ppermute | solution.py:404

commit v24 on v15

--- a/solution.py
+++ b/solution.py
@@ -50,9 +50,7 @@
 
 
 def last_parts(step):
-    if step % 64:
-        return [(0, step)]
-    return [(0, step // 2), (step // 2, step // 4), (step // 4 * 3, step // 4)]
+    return [(0, step // 2), (step // 2, step // 2)]
 
 
 def project_kernel(

time: 35.8 us -> 35.9 us (level)
  no operation moved by 1% of the time
where the time goes in v24:
time: 35.9 us; the launch traced here: 35.7 us
  Pallas kernels  20.8 us (58%)
  starting transfers between devices  7.62 us (21%)
  waiting for transfers between devices  5.9 us (16%)
  between operations  0.74 us (2%)
  local copies, waits for them, and re-layouts  0.66 us (2%)
    pallas_call x1, Pallas kernels, project(): pl.pallas_call(functools.partial(project_kernel, tensors=tensors, section...  11.3 us
    pallas_call x1, Pallas kernels, fetch(): pl.pallas_call(fetch_kernel, out_shape=pltpu.VMEM((rows, columns), weight...  6.97 us
    ppermute x3, starting transfers between devices, across(): return lax.ppermute(array, ('tensor', 'section'), pairs)  3.94 us
    ppermute x3, starting transfers between devices, shifted(): lax.ppermute(array, axis, [(i, (i + shift) % count) for i in range(count)])  3.68 us
    ppermute x3, waiting for transfers between devices, shifted(): lax.ppermute(array, axis, [(i, (i + shift) % count) for i in range(count)])  3.59 us
    ppermute x3, waiting for transfers between devices, across(): return lax.ppermute(array, ('tensor', 'section'), pairs)  2.31 us
    pallas_call x1, Pallas kernels, prepare(): pl.pallas_call(functools.partial(prepare_kernel, slots=slots, owners=owne...  1.23 us
    pallas_call x1, Pallas kernels, finish(): pl.pallas_call(finish_kernel, out_shape=jax.ShapeDtypeStruct((local, 1, M...  0.84 us
  transfers between devices with their start and end apart: 6, of which 4 were waited for; matrix products, arithmetic and copies ran while one was open for 2% of the time, Pallas kernels for 24%

profile of v24, /device:TPU:0, one launch (start us, length us, event | category | flops | bytes accessed | tf_op | source)
XLA Modules:
  0.0 35.7 jit_solution(10200281301165233015)
XLA Ops:
  0.6 0.0 copy-start
  0.6 3.0 %collective-permute-start = (bf16[16,6656]{1,0:T(8,128)(2,1)}, bf16[16,6656]{1,0:T(8,128)(2,1)S(1)}, u32[]{:S(2)}, u32[]{:S(2)}) collective-permute-start(bf16[16,6656]{1,0:T(8,128)(2,1)} %own_ref.1), channel_id=1, source_target_pairs={{0,2},{2,0},{1,3},{3,1},{4,6},{6,4},{5,7},{7,5},{8,10},{10,8},{9,1... | collective-permute-start | bytes 638984 | tf_op jit(solution)/shard_map/ppermute | solution.py:399
  3.6 7.0 %fetch.1.held_ref = bf16[2560,4096]{1,0:T(8,128)(2,1)S(1)} custom-call(bf16[6656,4096]{1,0:T(8,128)(2,1)} %weight_ref.3), custom_call_target="tpu_custom_call" | custom-call | bytes 20971520 | tf_op jit(solution)/shard_map/fetch/pallas_call | solution.py:38
  10.6 0.0 copy-start.2
  10.6 0.0 copy-start.1
  10.6 0.0 copy-start.3
  10.7 0.0 collective-permute-done
  10.7 0.0 copy-done
  10.7 11.3 %project.1 = (f32[32,4096]{1,0:T(8,128)S(1)}, bf16[1,16,4096]{2,1,0:T(8,128)(2,1)S(1)}) custom-call(bf16[16,6656]{1,0:T(8,128)(2,1)S(1)} %copy-done, bf16[1,16,6656]{2,1,0:T(8,128)(2,1)S(1)} %bitcast.5, bf16[2560,4096]{1,0:T(8,128)(2,1)S(1)} %fetch.1.held_ref, bf16[6656,4096]{1,0:T(8,128)(2,1)} %weight_ref.3), custom_call_target="tpu_custom_call" | custom-call | flops 1744830464 | bytes 33554432 | tf_op jit(solution)/shard_map/project/pallas_call | solution.py:173
  21.9 0.1 collective-permute-start.1
  22.1 1.3 %collective-permute-done.1.refs_0_ = bf16[16,4096]{1,0:T(8,128)(2,1)S(1)} collective-permute-done((bf16[16,4096]{1,0:T(8,128)(2,1)S(1)}, bf16[16,4096]{1,0:T(8,128)(2,1)S(1)}, u32[]{:S(2)}, u32[]{:S(2)}) %collective-permute-start.1) | collective-permute-done | bytes 131104 | tf_op jit(solution)/shard_map/ppermute | solution.py:399
  23.4 2.4 %collective-permute-start.2 = (bf16[4,4096]{1,0:T(4,128)(2,1)S(1)}, bf16[4,4096]{1,0:T(4,128)(2,1)S(1)}, u32[]{:S(2)}, u32[]{:S(2)}) collective-permute-start(bf16[4,4096]{1,0:T(4,128)(2,1)S(1)} %get-tuple-element.23), channel_id=1, source_target_pairs={{0,9},{1,8},{4,13},{5,12},{8,5},{9,4},{12,1},{13,0},{2,11},{3,10},... | collective-permute-start | bytes 98312 | tf_op jit(solution)/shard_map/ppermute | solution.py:409
  25.8 1.2 %collective-permute-start.3 = (bf16[4,4096]{1,0:T(4,128)(2,1)S(1)}, bf16[4,4096]{1,0:T(4,128)(2,1)S(1)}, u32[]{:S(2)}, u32[]{:S(2)}) collective-permute-start(bf16[4,4096]{1,0:T(4,128)(2,1)S(1)} %get-tuple-element.24), channel_id=1, source_target_pairs={{0,13},{1,12},{4,9},{5,8},{8,1},{9,0},{12,5},{13,4},{2,15},{3,14},... | collective-permute-start | bytes 98312 | tf_op jit(solution)/shard_map/ppermute | solution.py:409
  27.0 0.3 collective-permute-start.4
  27.4 0.0 copy-done.2
  27.4 1.2 %prepare.1 = (f32[4,4]{1,0:T(4,128)S(1)}, bf16[1,64,8192]{2,1,0:T(8,128)(2,1)S(1)}) custom-call(s32[1,4]{1,0:T(1,128)S(1)} %bitcast.6, bf16[1,64,8192]{2,1,0:T(8,128)(2,1)} %bitcast.9), custom_call_target="tpu_custom_call" | custom-call | tf_op jit(solution)/shard_map/prepare/pallas_call | solution.py:267
  28.6 0.0 collective-permute-done.2.refs_0_
  28.6 1.5 %collective-permute-done.3.refs_1_ = bf16[4,4096]{1,0:T(4,128)(2,1)S(1)} collective-permute-done((bf16[4,4096]{1,0:T(4,128)(2,1)S(1)}, bf16[4,4096]{1,0:T(4,128)(2,1)S(1)}, u32[]{:S(2)}, u32[]{:S(2)}) %collective-permute-start.3) | collective-permute-done | bytes 32800 | tf_op jit(solution)/shard_map/ppermute | solution.py:409
  30.1 0.8 %collective-permute-done.4.refs_2_ = bf16[4,4096]{1,0:T(4,128)(2,1)S(1)} collective-permute-done((bf16[4,4096]{1,0:T(4,128)(2,1)S(1)}, bf16[4,4096]{1,0:T(4,128)(2,1)S(1)}, u32[]{:S(2)}, u32[]{:S(2)}) %collective-permute-start.4) | collective-permute-done | bytes 32800 | tf_op jit(solution)/shard_map/ppermute | solution.py:409
  30.9 0.0 copy-done.1
  30.9 0.1 mix.1
  31.1 0.6 %collective-permute-start.5 = (bf16[2,4096]{1,0:T(2,128)(2,1)S(1)}, bf16[2,4096]{1,0:T(2,128)(2,1)S(1)}, u32[]{:S(2)}, u32[]{:S(2)}) collective-permute-start(bf16[2,4096]{1,0:T(2,128)(2,1)S(1)} %bitcast.8), channel_id=1, source_target_pairs={{0,2},{2,0},{1,3},{3,1},{4,6},{6,4},{5,7},{7,5},{8,10},{10,8},{9,1... | collective-permute-start | bytes 49160 | tf_op jit(solution)/shard_map/ppermute | solution.py:399
  31.7 0.0 copy-done.3
  31.7 0.6 %copy.8 = bf16[4,4096]{1,0:T(4,128)(2,1)} copy(bf16[4,4096]{1,0:T(4,128)(2,1)S(1)} %get-tuple-element.32) | data formatting | bytes 65536
  32.3 0.3 own_half.1
  32.6 2.3 %collective-permute-done.5.refs_0_ = bf16[2,4096]{1,0:T(2,128)(2,1)S(1)} collective-permute-done((bf16[2,4096]{1,0:T(2,128)(2,1)S(1)}, bf16[2,4096]{1,0:T(2,128)(2,1)S(1)}, u32[]{:S(2)}, u32[]{:S(2)}) %collective-permute-start.5) | collective-permute-done | bytes 16416 | tf_op jit(solution)/shard_map/ppermute | solution.py:399
  34.9 0.8 %finish.1 = f32[1,1,2,64]{3,2,1,0:T(2,128)} custom-call(f32[2,64]{1,0:T(2,128)S(1)} %get-tuple-element.29.values_ref, f32[2,64]{1,0:T(2,128)S(1)} %get-tuple-element.30.squares_ref, bf16[1,8192]{1,0:T(2,128)(2,1)S(1)} %broadcast_in_dim.3.gain_ref, bf16[1,64,8192]{2,1,0:T(8,128)(2,1)S(1)} %get-tuple-element.28.shrink_ref, ...), custom_call_target="tpu_custom_call" | custom-call | tf_op jit(solution)/shard_map/finish/pallas_call | solution.py:387
  (3 shorter events, 0.1 us)
Async XLA Ops:
  0.6 10.0 %copy-start = (bf16[16,6656]{1,0:T(8,128)(2,1)S(1)}, bf16[16,6656]{1,0:T(8,128)(2,1)}, u32[]{:S(2)}) copy-start(bf16[16,6656]{1,0:T(8,128)(2,1)} %own_ref.1) | copy-start | bytes 638980
  0.6 10.0 %collective-permute-start = (bf16[16,6656]{1,0:T(8,128)(2,1)}, bf16[16,6656]{1,0:T(8,128)(2,1)S(1)}, u32[]{:S(2)}, u32[]{:S(2)}) collective-permute-start(bf16[16,6656]{1,0:T(8,128)(2,1)} %own_ref.1), channel_id=1, source_target_pairs={{0,2},{2,0},{1,3},{3,1},{4,6},{6,4},{5,7},{7,5},{8,10},{10,8},{9,1... | collective-permute-start | bytes 638984 | tf_op jit(solution)/shard_map/ppermute | solution.py:399
  10.6 16.7 %copy-start.2 = (s32[4,1]{0,1:T(1,128)S(1)}, s32[4,1]{0,1:T(1,128)}, u32[]{:S(2)}) copy-start(s32[4,1]{0,1:T(1,128)} %param.11) | copy-start | bytes 52
  10.6 20.3 %copy-start.1 = (bf16[4,4096]{1,0:T(4,128)(2,1)S(1)}, bf16[4,4096]{1,0:T(4,128)(2,1)}, u32[]{:S(2)}) copy-start(bf16[4,4096]{1,0:T(4,128)(2,1)} %residual_ref.1) | copy-start | bytes 98308
  10.6 21.0 %copy-start.3 = (bf16[8192]{0:T(1024)(128)(2,1)S(1)}, bf16[8192]{0:T(1024)(128)(2,1)}, u32[]{:S(2)}) copy-start(bf16[8192]{0:T(1024)(128)(2,1)} %param.9) | copy-start | bytes 49156
  21.9 1.4 %collective-permute-start.1 = (bf16[16,4096]{1,0:T(8,128)(2,1)S(1)}, bf16[16,4096]{1,0:T(8,128)(2,1)S(1)}, u32[]{:S(2)}, u32[]{:S(2)}) collective-permute-start(bf16[16,4096]{1,0:T(8,128)(2,1)S(1)} %bitcast.7), channel_id=1, source_target_pairs={{0,1},{1,0},{2,3},{3,2},{4,5},{5,4},{6,7},{7,6},{8,9},{9,8},{10,11... | collective-permute-start | bytes 393224 | tf_op jit(solution)/shard_map/ppermute | solution.py:399
  23.4 5.2 %collective-permute-start.2 = (bf16[4,4096]{1,0:T(4,128)(2,1)S(1)}, bf16[4,4096]{1,0:T(4,128)(2,1)S(1)}, u32[]{:S(2)}, u32[]{:S(2)}) collective-permute-start(bf16[4,4096]{1,0:T(4,128)(2,1)S(1)} %get-tuple-element.23), channel_id=1, source_target_pairs={{0,9},{1,8},{4,13},{5,12},{8,5},{9,4},{12,1},{13,0},{2,11},{3,10},... | collective-permute-start | bytes 98312 | tf_op jit(solution)/shard_map/ppermute | solution.py:409
  25.8 4.3 %collective-permute-start.3 = (bf16[4,4096]{1,0:T(4,128)(2,1)S(1)}, bf16[4,4096]{1,0:T(4,128)(2,1)S(1)}, u32[]{:S(2)}, u32[]{:S(2)}) collective-permute-start(bf16[4,4096]{1,0:T(4,128)(2,1)S(1)} %get-tuple-element.24), channel_id=1, source_target_pairs={{0,13},{1,12},{4,9},{5,8},{8,1},{9,0},{12,5},{13,4},{2,15},{3,14},... | collective-permute-start | bytes 98312 | tf_op jit(solution)/shard_map/ppermute | solution.py:409
  27.0 3.9 %collective-permute-start.4 = (bf16[4,4096]{1,0:T(4,128)(2,1)S(1)}, bf16[4,4096]{1,0:T(4,128)(2,1)S(1)}, u32[]{:S(2)}, u32[]{:S(2)}) collective-permute-start(bf16[4,4096]{1,0:T(4,128)(2,1)S(1)} %get-tuple-element.25), channel_id=1, source_target_pairs={{0,5},{1,4},{4,1},{5,0},{8,13},{9,12},{12,9},{13,8},{2,7},{3,6},{6... | collective-permute-start | bytes 98312 | tf_op jit(solution)/shard_map/ppermute | solution.py:409
  31.1 3.8 %collective-permute-start.5 = (bf16[2,4096]{1,0:T(2,128)(2,1)S(1)}, bf16[2,4096]{1,0:T(2,128)(2,1)S(1)}, u32[]{:S(2)}, u32[]{:S(2)}) collective-permute-start(bf16[2,4096]{1,0:T(2,128)(2,1)S(1)} %bitcast.8), channel_id=1, source_target_pairs={{0,2},{2,0},{1,3},{3,1},{4,6},{6,4},{5,7},{7,5},{8,10},{10,8},{9,1... | collective-permute-start | bytes 49160 | tf_op jit(solution)/shard_map/ppermute | solution.py:399
